TPU v7x, 32 devices: a whole 2x2x4 slice. The times are simulated.
32 devices in a mesh: gx: 4 (over z), gy: 8 (over y, x, core).
Axes of the slice: x: 2, y: 2, z: 4, core: 2. Of those that a mesh axis runs over, the one named last changes fastest.
Arguments:
- source: float32 [32, 64, 512], P('gx', 'gy'), may hold values from -60 to 60
- conductivity: float32 [32, 64, 512], P('gx', 'gy'), may hold values from 0.5 to 5
- robin_flags: int32 [4, 8, 64], P('gx', 'gy'), may hold values from 0 to 63
- htc_class: int32 [4, 8, 64], P('gx', 'gy'), may hold values from 0 to 3
- htc_table: float32 [4], replicated, may hold values from 0.5 to 8
Outputs:
- adjoint: float32 [32, 64, 512], P('gx', 'gy')
- residual: float32 [32, 64, 512], P('gx', 'gy')
Inputs may be any that keep to these rules, and one draw needn't show every extreme that they name: `robin_flags`: bit f (value 2^f) flags face f of the element, in the order x-min, x-max, y-min, y-max, z-min, z-max.
All inputs are finite; a program needn't handle non-finite values.
Results may differ from a plain program's by a relative error of at most 0.0003.
Values sent between devices are 32-bit elements; how exact they have to be, the bound alone decides.
No kernel may reach another device: no remote copies, remote signals or barrier semaphores. Data moves between devices by JAX's collectives and lax.ppermute only.
A program may use at most 64 MiB of HBM per device.

v0:
```python
import jax
import jax.numpy as jnp
import numpy as np
from jax import lax
from jax.sharding import PartitionSpec as P

ITERS = 3


gll_points = (
    -1.0,
    -0.8717401485096066,
    -0.5917001814331423,
    -0.2092992179024789,
    0.2092992179024789,
    0.5917001814331423,
    0.8717401485096066,
    1.0,
)
gll_weights = (
    0.03571428571428571,
    0.21070422714350603,
    0.3411226924835044,
    0.4124587946587038,
    0.4124587946587038,
    0.3411226924835044,
    0.21070422714350603,
    0.03571428571428571,
)
mass_coef = 0.2
scan_speed = 2.0
highest = lax.Precision.HIGHEST


def extended(block, sides, width):
    for axis, dim in sides:
        count = lax.axis_size(axis)
        forward = [(i, i + 1) for i in range(count - 1)]
        backward = [(target, source) for source, target in forward]
        low = lax.ppermute(
            lax.slice_in_dim(block, block.shape[dim] - width, None, axis=dim), axis, forward
        )
        high = lax.ppermute(lax.slice_in_dim(block, 0, width, axis=dim), axis, backward)
        block = jnp.concatenate([low, block, high], axis=dim)
    return block


def lagrange_derivative():
    points = np.array(gll_points)
    barycentric = np.array(
        [1.0 / np.prod([points[j] - points[m] for m in range(8) if m != j]) for j in range(8)]
    )
    derivative = np.zeros((8, 8))
    for a in range(8):
        for b in range(8):
            if a != b:
                derivative[a, b] = barycentric[b] / barycentric[a] / (points[a] - points[b])
        derivative[a, a] = -np.sum(derivative[a])
    return jnp.asarray(derivative, jnp.float32)


def edge_weights(elements):
    return jnp.tile(jnp.asarray(np.array(gll_weights), jnp.float32), elements)


def copies_along(elements, first_element, total_elements):
    node_index = jnp.arange(8 * elements) % 8
    element_index = first_element + jnp.arange(8 * elements) // 8
    shared = (node_index == 7) & (element_index < total_elements - 1) | (node_index == 0) & (
        element_index > 0
    )
    return jnp.where(shared, 2.0, 1.0).astype(jnp.float32)


def fold_inside(values, which_axis):
    moved_field = jnp.moveaxis(values, which_axis, 0)
    extent = moved_field.shape
    blocks = moved_field.reshape((extent[0] // 8, 8) + extent[1:])
    shared = blocks[:-1, 7] + blocks[1:, 0]
    blocks = blocks.at[:-1, 7].set(shared).at[1:, 0].set(shared)
    return jnp.moveaxis(blocks.reshape(extent), 0, which_axis)


def element_expand(elements):
    return (jnp.arange(8 * elements)[None, :] // 8 == jnp.arange(elements)[:, None]).astype(
        jnp.float32
    )


def robin_field(robin_flags, htc_class, htc_table, start_x, start_y, total_x, total_y):
    elems_x, elems_y, elems_z = robin_flags.shape
    class_hits = (htc_class[..., None] == jnp.arange(htc_table.shape[0])).astype(jnp.float32)
    coefficient = jnp.sum(class_hits * htc_table, axis=-1)
    index_x = (start_x + jnp.arange(elems_x))[:, None, None]
    index_y = (start_y + jnp.arange(elems_y))[None, :, None]
    index_z = jnp.arange(elems_z)[None, None, :]
    boundary = [
        index_x == 0,
        index_x == total_x - 1,
        index_y == 0,
        index_y == total_y - 1,
        index_z == 0,
        index_z == elems_z - 1,
    ]
    weight_x = edge_weights(elems_x)
    weight_y = edge_weights(elems_y)
    weight_z = edge_weights(elems_z)
    node_x = (jnp.arange(8 * elems_x) % 8)[:, None, None]
    node_y = (jnp.arange(8 * elems_y) % 8)[None, :, None]
    node_z = (jnp.arange(8 * elems_z) % 8)[None, None, :]
    cross_x = weight_y[None, :, None] * weight_z[None, None, :]
    cross_y = weight_x[:, None, None] * weight_z[None, None, :]
    cross_z = weight_x[:, None, None] * weight_y[None, :, None]
    patterns = [
        (node_x == 0) * cross_x,
        (node_x == 7) * cross_x,
        (node_y == 0) * cross_y,
        (node_y == 7) * cross_y,
        (node_z == 0) * cross_z,
        (node_z == 7) * cross_z,
    ]
    expand_x = element_expand(elems_x)
    expand_y = element_expand(elems_y)
    expand_z = element_expand(elems_z)
    robin_sum = jnp.zeros((8 * elems_x, 8 * elems_y, 8 * elems_z), jnp.float32)
    for face_bit in range(6):
        flag_bit = (robin_flags // (1 << face_bit) % 2).astype(jnp.float32)
        coef_face = (
            coefficient
            * flag_bit
            * jnp.broadcast_to(boundary[face_bit], robin_flags.shape).astype(jnp.float32)
        )
        spread = jnp.einsum("ai,bj,abc->ijc", expand_x, expand_y, coef_face, precision=highest)
        spread = jnp.einsum("ijc,ck->ijk", spread, expand_z, precision=highest)
        robin_sum = robin_sum + spread * patterns[face_bit]
    return robin_sum


def per_device(source, conductivity, robin_flags, htc_class, htc_table):
    elems_x, elems_y, elems_z = robin_flags.shape
    start_x = lax.axis_index("gx") * elems_x
    start_y = lax.axis_index("gy") * elems_y
    total_x = elems_x * lax.axis_size("gx")
    total_y = elems_y * lax.axis_size("gy")
    derivative = lagrange_derivative()
    deriv_x = jnp.kron(jnp.eye(elems_x, dtype=jnp.float32), derivative)
    deriv_y = jnp.kron(jnp.eye(elems_y, dtype=jnp.float32), derivative)
    tile_z = 8 * min(elems_z, 16)
    deriv_z = jnp.kron(jnp.eye(tile_z // 8, dtype=jnp.float32), derivative)
    weight_x = edge_weights(elems_x)
    weight_y = edge_weights(elems_y)
    weight_z = edge_weights(elems_z)
    weights = weight_x[:, None, None] * weight_y[None, :, None] * weight_z[None, None, :]
    copies_x = copies_along(elems_x, start_x, total_x)
    copies_y = copies_along(elems_y, start_y, total_y)
    copies_z = copies_along(elems_z, 0, elems_z)
    inv_copies = 1.0 / (copies_x[:, None, None] * copies_y[None, :, None] * copies_z[None, None, :])
    robin_diag = robin_field(robin_flags, htc_class, htc_table, start_x, start_y, total_x, total_y)
    rows_x, rows_y, rows_z = source.shape
    tiled_shape = (rows_x, rows_y, rows_z // tile_z, tile_z)

    def assemble(values):
        local_sum = fold_inside(fold_inside(fold_inside(values, 0), 1), 2)
        padded = extended(local_sum, (("gx", 0), ("gy", 1)), 1)
        inner_rows = padded[1:-1].at[0].add(padded[0]).at[-1].add(padded[-1])
        return inner_rows[:, 1:-1].at[:, 0].add(inner_rows[:, 0]).at[:, -1].add(inner_rows[:, -1])

    def operate(values):
        grad_x = jnp.einsum("ij,jbc->ibc", deriv_x, values, precision=highest)
        grad_y = jnp.einsum("ij,ajc->aic", deriv_y, values, precision=highest)
        grad_z = jnp.einsum(
            "abkj,ij->abki", values.reshape(tiled_shape), deriv_z, precision=highest
        ).reshape(source.shape)
        flux_x = weights * (conductivity * grad_x - scan_speed * values)
        flux_y = weights * conductivity * grad_y
        flux_z = weights * conductivity * grad_z
        back_x = jnp.einsum("ij,ibc->jbc", deriv_x, flux_x, precision=highest)
        back_y = jnp.einsum("ij,aic->ajc", deriv_y, flux_y, precision=highest)
        back_z = jnp.einsum(
            "abki,ij->abkj", flux_z.reshape(tiled_shape), deriv_z, precision=highest
        ).reshape(source.shape)
        local_terms = mass_coef * weights * values + robin_diag * values + back_x + back_y + back_z
        return assemble(local_terms)

    def local_inner(left, right):
        return jnp.sum(left * right * inv_copies)

    assembled = assemble(weights * source)
    adjoint = jnp.zeros_like(assembled)
    residual = assembled
    direction = assembled
    rho_now = lax.psum(local_inner(assembled, assembled), ("gx", "gy"))
    for iteration in range(ITERS):
        applied = operate(direction)
        alpha_step = rho_now / lax.psum(local_inner(assembled, applied), ("gx", "gy"))
        half_resid = residual - alpha_step * applied
        applied_half = operate(half_resid)
        cross_sum, square_sum, source_half, source_applied = lax.psum(
            (
                local_inner(applied_half, half_resid),
                local_inner(applied_half, applied_half),
                local_inner(assembled, half_resid),
                local_inner(assembled, applied_half),
            ),
            ("gx", "gy"),
        )
        omega_step = cross_sum / square_sum
        rho_next = source_half - omega_step * source_applied
        adjoint = adjoint + alpha_step * direction + omega_step * half_resid
        residual = half_resid - omega_step * applied_half
        if iteration + 1 < ITERS:
            beta_step = rho_next / rho_now * (alpha_step / omega_step)
            direction = residual + beta_step * (direction - omega_step * applied)
            rho_now = rho_next
    return (adjoint, residual)


def solution(mesh):
    return jax.shard_map(
        per_device,
        mesh=mesh,
        in_specs=(
            P("gx", "gy", None),
            P("gx", "gy", None),
            P("gx", "gy", None),
            P("gx", "gy", None),
            P(),
        ),
        out_specs=(P("gx", "gy", None), P("gx", "gy", None)),
        check_vma=False,
    )
```

profile of v0, /device:TPU:0, one launch (start us, length us, event | category | flops | bytes accessed | tf_op | source)
XLA Modules:
  0.0 653.0 jit_solution(2867186665109077588)
XLA Ops:
  5.7 5.1 dynamic-slice_select_fusion.6
  10.8 17.8 %scatter.46 = f32[64,8,8,8]{1,0,3,2:T(8,128)S(1)} dynamic-update-slice(f32[64,8,8,8]{1,0,3,2:T(8,128)S(1)} %reshape.1990, f32[63,1,8,8]{1,0,3,2:T(8,128)} %get-tuple-element.542, s32[]{:T(128)} %bitcast.1, s32[]{:T(128)} %bitcast.2, s32[]{:T(128)} %constant.1113.clone.1, s32[]{:T(128)} %constant.1113.clone.1) | dynamic-update-slice | bytes 32260 | tf_op jit(solution)/shard_map/scatter | solution.py:80
  28.6 10.4 %scatter.49 = f32[64,8,8,8]{1,0,3,2:T(8,128)S(1)} dynamic-update-slice(f32[64,8,8,8]{1,0,3,2:T(8,128)S(1)} %scatter.46, f32[63,1,8,8]{1,0,3,2:T(8,128)} %get-tuple-element.543, s32[]{:T(128)} %constant.1118.clone.1, s32[]{:T(128)} %constant.1113.clone.1, s32[]{:T(128)} %constant.1113.clone.1, s32[]{:T(128)} %constant.1113.clone.1) | dynamic-update-slice | bytes 32260 | tf_op jit(solution)/shard_map/scatter | solution.py:80
  40.2 4.9 collective-permute-start
  45.1 1.3 collective-permute-start.1
  48.6 2.2 collective-permute-done.1
  52.1 1.3 collective-permute-start.3
  53.9 3.0 collective-permute-done.3
  61.0 5.1 dynamic-slice_select_fusion.5
  66.0 17.8 %scatter.50 = f32[64,8,8,8]{1,0,3,2:T(8,128)S(1)} dynamic-update-slice(f32[64,8,8,8]{1,0,3,2:T(8,128)S(1)} %reshape.2005, f32[63,1,8,8]{1,0,3,2:T(8,128)} %get-tuple-element.540, s32[]{:T(128)} %bitcast.1, s32[]{:T(128)} %bitcast.2, s32[]{:T(128)} %constant.1113.clone.1, s32[]{:T(128)} %constant.1113.clone.1) | dynamic-update-slice | bytes 32260 | tf_op jit(solution)/shard_map/scatter | solution.py:80
  83.9 10.4 %scatter.51 = f32[64,8,8,8]{1,0,3,2:T(8,128)S(1)} dynamic-update-slice(f32[64,8,8,8]{1,0,3,2:T(8,128)S(1)} %scatter.50, f32[63,1,8,8]{1,0,3,2:T(8,128)} %get-tuple-element.541, s32[]{:T(128)} %constant.1118.clone.1, s32[]{:T(128)} %constant.1113.clone.1, s32[]{:T(128)} %constant.1113.clone.1, s32[]{:T(128)} %constant.1113.clone.1) | dynamic-update-slice | bytes 32260 | tf_op jit(solution)/shard_map/scatter | solution.py:80
  95.4 3.5 collective-permute-start.4
  98.9 1.3 collective-permute-start.5
  100.3 4.2 collective-permute-done.5
  104.6 3.0 collective-permute-start.6
  107.6 1.3 collective-permute-start.7
  108.9 2.7 collective-permute-done.7
  112.8 43.4 %all-reduce.3 = (f32[]{:T(128)}, f32[]{:T(128)}) all-reduce(f32[]{:T(128)} %get-tuple-element.517, f32[]{:T(128)} %get-tuple-element.516), channel_id=1, replica_groups=mesh['gx'=4,'gy'=8] {'gx','gy'}, use_global_device_ids=true, to_apply=%region_2.3 | all-reduce | flops 2 | bytes 16 | tf_op jit(solution)/shard_map/psum | solution.py:192
  160.6 5.1 dynamic-slice_select_fusion.4
  165.7 17.8 %scatter.54 = f32[64,8,8,8]{1,0,3,2:T(8,128)S(1)} dynamic-update-slice(f32[64,8,8,8]{1,0,3,2:T(8,128)S(1)} %reshape.2011, f32[63,1,8,8]{1,0,3,2:T(8,128)} %get-tuple-element.538, s32[]{:T(128)} %bitcast.1, s32[]{:T(128)} %bitcast.2, s32[]{:T(128)} %constant.1113.clone.1, s32[]{:T(128)} %constant.1113.clone.1) | dynamic-update-slice | bytes 32260 | tf_op jit(solution)/shard_map/scatter | solution.py:80
  183.5 10.4 %scatter.55 = f32[64,8,8,8]{1,0,3,2:T(8,128)S(1)} dynamic-update-slice(f32[64,8,8,8]{1,0,3,2:T(8,128)S(1)} %scatter.54, f32[63,1,8,8]{1,0,3,2:T(8,128)} %get-tuple-element.539, s32[]{:T(128)} %constant.1118.clone.1, s32[]{:T(128)} %constant.1113.clone.1, s32[]{:T(128)} %constant.1113.clone.1, s32[]{:T(128)} %constant.1113.clone.1) | dynamic-update-slice | bytes 32260 | tf_op jit(solution)/shard_map/scatter | solution.py:80
  195.0 2.3 collective-permute-start.8
  197.4 1.3 collective-permute-start.9
  198.8 4.2 collective-permute-done.9
  203.1 1.3 collective-permute-start.10
  204.4 1.3 collective-permute-start.11
  205.7 4.3 collective-permute-done.11
  211.2 42.2 %all-reduce.2 = (f32[]{:T(128)}, f32[]{:T(128)}, f32[]{:T(128)}, f32[]{:T(128)}) all-reduce(f32[]{:T(128)} %get-tuple-element.515, f32[]{:T(128)} %get-tuple-element.514, f32[]{:T(128)} %get-tuple-element.513, f32[]{:T(128)} %get-tuple-element.512), channel_id=1, replica_groups=mesh['gx'=4,'gy'=8] {'gx','gy'}, use_global_device_ids=true, to_apply=%region_11.12 | all-reduce | flops 4 | bytes 32 | tf_op jit(solution)/shard_map/psum | solution.py:198
  262.1 5.1 dynamic-slice_select_fusion.3
  267.2 17.8 %scatter.56 = f32[64,8,8,8]{1,0,3,2:T(8,128)S(1)} dynamic-update-slice(f32[64,8,8,8]{1,0,3,2:T(8,128)S(1)} %reshape.2017, f32[63,1,8,8]{1,0,3,2:T(8,128)} %get-tuple-element.536, s32[]{:T(128)} %bitcast.1, s32[]{:T(128)} %bitcast.2, s32[]{:T(128)} %constant.1113.clone.1, s32[]{:T(128)} %constant.1113.clone.1) | dynamic-update-slice | bytes 32260 | tf_op jit(solution)/shard_map/scatter | solution.py:80
  285.0 10.4 %scatter.59 = f32[64,8,8,8]{1,0,3,2:T(8,128)S(1)} dynamic-update-slice(f32[64,8,8,8]{1,0,3,2:T(8,128)S(1)} %scatter.56, f32[63,1,8,8]{1,0,3,2:T(8,128)} %get-tuple-element.537, s32[]{:T(128)} %constant.1118.clone.1, s32[]{:T(128)} %constant.1113.clone.1, s32[]{:T(128)} %constant.1113.clone.1, s32[]{:T(128)} %constant.1113.clone.1) | dynamic-update-slice | bytes 32260 | tf_op jit(solution)/shard_map/scatter | solution.py:80
  296.6 3.1 collective-permute-start.12
  299.7 1.3 collective-permute-start.13
  301.1 4.2 collective-permute-done.13
  306.6 1.3 collective-permute-start.15
  307.9 4.3 collective-permute-done.15
  313.4 42.1 %psum.104 = f32[]{:T(128)} all-reduce(f32[]{:T(128)} %multiply_reduce_fusion.7), channel_id=1, replica_groups=mesh['gx'=4,'gy'=8] {'gx','gy'}, use_global_device_ids=true, to_apply=%region_15.16 | all-reduce | flops 1 | bytes 8 | tf_op jit(solution)/shard_map/psum | solution.py:195
  359.2 5.1 dynamic-slice_select_fusion.2
  364.3 17.8 %scatter.60 = f32[64,8,8,8]{1,0,3,2:T(8,128)S(1)} dynamic-update-slice(f32[64,8,8,8]{1,0,3,2:T(8,128)S(1)} %reshape.2023, f32[63,1,8,8]{1,0,3,2:T(8,128)} %get-tuple-element.534, s32[]{:T(128)} %bitcast.1, s32[]{:T(128)} %bitcast.2, s32[]{:T(128)} %constant.1113.clone.1, s32[]{:T(128)} %constant.1113.clone.1) | dynamic-update-slice | bytes 32260 | tf_op jit(solution)/shard_map/scatter | solution.py:80
  382.1 10.4 %scatter.61 = f32[64,8,8,8]{1,0,3,2:T(8,128)S(1)} dynamic-update-slice(f32[64,8,8,8]{1,0,3,2:T(8,128)S(1)} %scatter.60, f32[63,1,8,8]{1,0,3,2:T(8,128)} %get-tuple-element.535, s32[]{:T(128)} %constant.1118.clone.1, s32[]{:T(128)} %constant.1113.clone.1, s32[]{:T(128)} %constant.1113.clone.1, s32[]{:T(128)} %constant.1113.clone.1) | dynamic-update-slice | bytes 32260 | tf_op jit(solution)/shard_map/scatter | solution.py:80
  393.7 3.1 collective-permute-start.16
  396.8 1.3 collective-permute-start.17
  398.2 4.2 collective-permute-done.17
  403.7 1.3 collective-permute-start.19
  405.0 4.3 collective-permute-done.19
  410.6 42.5 %all-reduce.1 = (f32[]{:T(128)}, f32[]{:T(128)}, f32[]{:T(128)}, f32[]{:T(128)}) all-reduce(f32[]{:T(128)} %get-tuple-element.511, f32[]{:T(128)} %get-tuple-element.510, f32[]{:T(128)} %get-tuple-element.509, f32[]{:T(128)} %get-tuple-element.508), channel_id=1, replica_groups=mesh['gx'=4,'gy'=8] {'gx','gy'}, use_global_device_ids=true, to_apply=%region_21.22 | all-reduce | flops 4 | bytes 32 | tf_op jit(solution)/shard_map/psum | solution.py:198
  460.5 5.1 dynamic-slice_select_fusion.1
  465.6 17.8 %scatter.64 = f32[64,8,8,8]{1,0,3,2:T(8,128)S(1)} dynamic-update-slice(f32[64,8,8,8]{1,0,3,2:T(8,128)S(1)} %reshape.2029, f32[63,1,8,8]{1,0,3,2:T(8,128)} %get-tuple-element.532, s32[]{:T(128)} %bitcast.1, s32[]{:T(128)} %bitcast.2, s32[]{:T(128)} %constant.1113.clone.1, s32[]{:T(128)} %constant.1113.clone.1) | dynamic-update-slice | bytes 32260 | tf_op jit(solution)/shard_map/scatter | solution.py:80
  483.4 10.4 %scatter.65 = f32[64,8,8,8]{1,0,3,2:T(8,128)S(1)} dynamic-update-slice(f32[64,8,8,8]{1,0,3,2:T(8,128)S(1)} %scatter.64, f32[63,1,8,8]{1,0,3,2:T(8,128)} %get-tuple-element.533, s32[]{:T(128)} %constant.1118.clone.1, s32[]{:T(128)} %constant.1113.clone.1, s32[]{:T(128)} %constant.1113.clone.1, s32[]{:T(128)} %constant.1113.clone.1) | dynamic-update-slice | bytes 32260 | tf_op jit(solution)/shard_map/scatter | solution.py:80
  495.0 3.1 collective-permute-start.20
  498.1 1.3 collective-permute-start.21
  499.5 4.2 collective-permute-done.21
  505.0 1.3 collective-permute-start.23
  506.4 4.3 collective-permute-done.23
  511.8 42.0 %psum.109 = f32[]{:T(128)} all-reduce(f32[]{:T(128)} %multiply_reduce_fusion.2), channel_id=1, replica_groups=mesh['gx'=4,'gy'=8] {'gx','gy'}, use_global_device_ids=true, to_apply=%region_25.26 | all-reduce | flops 1 | bytes 8 | tf_op jit(solution)/shard_map/psum | solution.py:195
  557.5 5.1 dynamic-slice_select_fusion
  562.6 17.8 %scatter.66 = f32[64,8,8,8]{1,0,3,2:T(8,128)S(1)} dynamic-update-slice(f32[64,8,8,8]{1,0,3,2:T(8,128)S(1)} %reshape.2035, f32[63,1,8,8]{1,0,3,2:T(8,128)} %get-tuple-element.530, s32[]{:T(128)} %bitcast.1, s32[]{:T(128)} %bitcast.2, s32[]{:T(128)} %constant.1113.clone.1, s32[]{:T(128)} %constant.1113.clone.1) | dynamic-update-slice | bytes 32260 | tf_op jit(solution)/shard_map/scatter | solution.py:80
  580.4 10.4 %scatter.69 = f32[64,8,8,8]{1,0,3,2:T(8,128)S(1)} dynamic-update-slice(f32[64,8,8,8]{1,0,3,2:T(8,128)S(1)} %scatter.66, f32[63,1,8,8]{1,0,3,2:T(8,128)} %get-tuple-element.531, s32[]{:T(128)} %constant.1118.clone.1, s32[]{:T(128)} %constant.1113.clone.1, s32[]{:T(128)} %constant.1113.clone.1, s32[]{:T(128)} %constant.1113.clone.1) | dynamic-update-slice | bytes 32260 | tf_op jit(solution)/shard_map/scatter | solution.py:80
  592.0 3.1 collective-permute-start.24
  595.1 1.3 collective-permute-start.25
  596.5 4.2 collective-permute-done.25
  602.0 1.3 collective-permute-start.27
  603.4 4.3 collective-permute-done.27
  608.8 41.9 %all-reduce = (f32[]{:T(128)}, f32[]{:T(128)}) all-reduce(f32[]{:T(128)} %get-tuple-element.507, f32[]{:T(128)} %get-tuple-element.506), channel_id=1, replica_groups=mesh['gx'=4,'gy'=8] {'gx','gy'}, use_global_device_ids=true, to_apply=%region_27.28 | all-reduce | flops 2 | bytes 16 | tf_op jit(solution)/shard_map/psum | solution.py:198
  (208 shorter events, 50.0 us)
Async XLA Ops:
  0.6 4.3 copy-start.5
  39.0 7.6 %copy-start.2 = (f32[8]{0:T(128)S(1)}, f32[8]{0:T(128)}, u32[]{:S(2)}) copy-start(f32[8]{0:T(128)} %constant.1135.clone) | copy-start | bytes 100
  39.0 7.7 %copy-start.6 = (f32[4]{0:T(128)S(1)}, f32[4]{0:T(128)}, u32[]{:S(2)}) copy-start(f32[4]{0:T(128)} %param.100) | copy-start | bytes 52
  39.0 7.7 %copy-start.7 = (s32[1,1,64]{2,1,0:T(1,128)S(1)}, s32[1,1,64]{2,1,0:T(1,128)}, u32[]{:S(2)}) copy-start(s32[1,1,64]{2,1,0:T(1,128)} %param.99) | copy-start | bytes 772
  39.0 7.8 %copy-start.4 = (s32[1,1,64]{2,1,0:T(1,128)S(1)}, s32[1,1,64]{2,1,0:T(1,128)}, u32[]{:S(2)}) copy-start(s32[1,1,64]{2,1,0:T(1,128)} %param.98) | copy-start | bytes 772
  39.0 8.9 %copy-start.3 = (f32[8,8]{1,0:T(8,128)S(1)}, f32[8,8]{1,0:T(8,128)}, u32[]{:S(2)}) copy-start(f32[8,8]{1,0:T(8,128)} %constant.1134.clone) | copy-start | bytes 772
  40.2 8.4 %collective-permute-start = (f32[1,8,512]{2,1,0:T(8,128)S(1)}, f32[1,8,512]{2,1,0:T(8,128)S(1)}, u32[]{:S(2)}, u32[]{:S(2)}) collective-permute-start(f32[1,8,512]{2,1,0:T(8,128)S(1)} %get-tuple-element.572), channel_id=1, source_target_pairs={{0,8},{8,16},{16,24},{1,9},{9,17},{17,25},{2,10},{10,18},{18,26},{... | collective-permute-start | bytes 49160 | tf_op jit(solution)/shard_map/ppermute | solution.py:40
  45.1 5.6 collective-permute-start.1
  48.0 9.9 %copy-start.1 = (f32[8,8,1]{1,0,2:T(8,128)S(1)}, f32[8,8,1]{1,0,2:T(8,128)}, u32[]{:S(2)}) copy-start(f32[8,8,1]{1,0,2:T(8,128)} %constant.1138) | copy-start | bytes 772
  48.0 10.2 %copy-start = (f32[8,8,512]{2,1,0:T(8,128)S(1)}, f32[8,8,512]{2,1,0:T(8,128)}, u32[]{:S(2)}) copy-start(f32[8,8,512]{2,1,0:T(8,128)} %param.97) | copy-start | bytes 393220
  50.8 3.1 collective-permute-start.2
  52.1 4.8 collective-permute-start.3
  95.4 4.9 collective-permute-start.4
  98.9 5.6 collective-permute-start.5
  104.6 4.3 collective-permute-start.6
  107.6 4.0 collective-permute-start.7
  195.0 3.8 collective-permute-start.8
  197.4 5.6 collective-permute-start.9
  203.1 2.6 collective-permute-start.10
  204.4 5.6 collective-permute-start.11
  296.6 4.5 collective-permute-start.12
  299.7 5.6 collective-permute-start.13
  305.3 2.6 collective-permute-start.14
  306.6 5.6 collective-permute-start.15
  393.7 4.5 collective-permute-start.16
  396.8 5.6 collective-permute-start.17
  402.4 2.6 collective-permute-start.18
  403.7 5.6 collective-permute-start.19
  495.0 4.5 collective-permute-start.20
  498.1 5.6 collective-permute-start.21
  503.8 2.6 collective-permute-start.22
  505.0 5.6 collective-permute-start.23
  592.0 4.5 collective-permute-start.24
  595.1 5.6 collective-permute-start.25
  600.8 2.6 collective-permute-start.26
  602.0 5.6 collective-permute-start.27
where the time goes:
time: 662 us; the launch traced here: 653 us
  blocking collectives  254 us (38%)
  local copies, waits for them, and re-layouts  218 us (33%)
  waiting for transfers between devices  55.3 us (8%)
  starting transfers between devices  51.9 us (8%)
  other arithmetic  45.8 us (7%)
  between operations  16.3 us (2%)
  matrix products  12 us (2%)
    scatter x14, local copies, waits for them, and re-layouts, fold_inside(): blocks = blocks.at[:-1, 7].set(shared).at[1:, 0].set(shared)  197 us
    psum x3, blocking collectives, per_device(): lax.psum((local_inner(applied_half, half_resid), local_inner(applied_half...  127 us
    psum x2, blocking collectives, per_device(): lax.psum(local_inner(assembled, applied), ('gx', 'gy'))  84 us
    ppermute x14, waiting for transfers between devices, extended(): lax.ppermute(lax.slice_in_dim(block, 0, width, axis=dim), axis, backward)  54.6 us
    psum x1, blocking collectives, per_device(): rho_now = lax.psum(local_inner(assembled, assembled), ('gx', 'gy'))  43.4 us
    another operation x11, other arithmetic  36.2 us
    ppermute x14, starting transfers between devices, extended(): lax.ppermute(lax.slice_in_dim(block, block.shape[dim] - width, None, axis...  33.8 us
    ppermute x14, starting transfers between devices, extended(): lax.ppermute(lax.slice_in_dim(block, 0, width, axis=dim), axis, backward)  18.1 us
  transfers between devices with their start and end apart: 28, of which 20 were waited for; matrix products, arithmetic and copies ran while one was open for 0% of the time, Pallas kernels for 0%

commit v1 on v0

v1 whole, which is shorter than its diff:
```python
import functools

import jax
import jax.numpy as jnp
import numpy as np
from jax import lax
from jax.experimental import pallas as pl
from jax.experimental.pallas import tpu as pltpu
from jax.sharding import PartitionSpec as P

ITERS = 3
N = 8

gll_points = (
    -1.0,
    -0.8717401485096066,
    -0.5917001814331423,
    -0.2092992179024789,
    0.2092992179024789,
    0.5917001814331423,
    0.8717401485096066,
    1.0,
)
gll_weights = (
    0.03571428571428571,
    0.21070422714350603,
    0.3411226924835044,
    0.4124587946587038,
    0.4124587946587038,
    0.3411226924835044,
    0.21070422714350603,
    0.03571428571428571,
)
mass_coef = 0.2
scan_speed = 2.0
f32 = jnp.float32
VMEM = pl.BlockSpec(memory_space=pltpu.VMEM)
SMEM = pl.BlockSpec(memory_space=pltpu.SMEM)
dot = functools.partial(jnp.dot, precision=lax.Precision.HIGHEST, preferred_element_type=f32)


def lagrange_derivative():
    points = np.array(gll_points)
    barycentric = np.array(
        [1.0 / np.prod([points[j] - points[m] for m in range(N) if m != j]) for j in range(N)]
    )
    derivative = np.zeros((N, N))
    for a in range(N):
        for b in range(N):
            if a != b:
                derivative[a, b] = barycentric[b] / barycentric[a] / (points[a] - points[b])
        derivative[a, a] = -np.sum(derivative[a])
    return derivative.astype(np.float32)


def constants(elems_z):
    d = lagrange_derivative()
    w = np.array(gll_weights).astype(np.float32)
    eye = np.eye(N, dtype=np.float32)
    ends = d.T[[0, N - 1]]
    zero = np.zeros((2 * N, N * N), np.float32)
    forward = np.concatenate([np.kron(d, eye), np.kron(eye, d)], 0)
    y_ends = np.concatenate([np.kron(eye, ends[:1]), np.kron(eye, ends[1:])], 0)
    back = np.concatenate(
        [
            np.concatenate([np.kron(d.T, eye), np.kron(eye, d.T)], 1),
            np.concatenate([np.kron(ends, eye), zero], 1),
            np.concatenate([zero, y_ends], 1),
        ],
        0,
    )
    group = min(elems_z, 32)
    z_back = np.kron(np.eye(group, dtype=np.float32), d)
    z_forward = np.ascontiguousarray(z_back.T)
    lane = np.arange(N * elems_z)
    low = (lane % N == 0) & (lane > 0)
    high = (lane % N == N - 1) & (lane < N * elems_z - 1)
    w_z = np.tile(w, elems_z)
    lanes = np.stack([low, high, w_z, 1.0 + low + high] + [0 * lane] * 4).astype(np.float32)
    weights = (w[:, None, None] * w[None, :, None] * w_z).reshape(N * N, N * elems_z)
    w_a = np.repeat(w, N)
    w_b = np.tile(w, N)
    a = np.arange(N * N) // N
    b = np.arange(N * N) % N
    one = np.ones(N * N)
    faces = np.stack(
        [(a == 0) * w_b, (a == 7) * w_b, (b == 0) * w_a, (b == 7) * w_a, w_a * w_b, w_a * w_b, 0 * one, 0 * one],
        1,
    ).astype(np.float32)
    spread = np.kron(np.eye(elems_z), np.ones((1, N))).astype(np.float32)
    return dict(
        forward=forward,
        back=back.astype(np.float32),
        z_forward=z_forward,
        z_back=z_back,
        lanes=lanes,
        weights=weights.astype(np.float32),
        faces=faces,
        spread=spread,
    )


def fold_z(v, lanes_ref):
    size = v.shape[1]
    return (
        v
        + pltpu.roll(v, 1, axis=1) * lanes_ref[0:1, :]
        + pltpu.roll(v, size - 1, axis=1) * lanes_ref[1:2, :]
    )


def y_rows(ref, b):
    return jnp.concatenate([ref[N * a + b : N * a + b + 1, :] for a in range(N)], 0)


def add_y_rows(out, b, values):
    for a in range(N):
        out[N * a + b : N * a + b + 1, :] += values[a : a + 1]


def pick(pos_ref, axis, even, odd):
    return jnp.where(pos_ref[axis] % 2 == 0, even, odd)


def send(pos_ref, axis, low, high, even_ref, odd_ref):
    even_ref[...] = pick(pos_ref, axis, high, low)
    odd_ref[...] = pick(pos_ref, axis, low, high)


def received(pos_ref, axis, count, even, odd):
    low = jnp.where(pos_ref[axis] > 0, pick(pos_ref, axis, odd, even), 0.0)
    high = jnp.where(pos_ref[axis] < count - 1, pick(pos_ref, axis, even, odd), 0.0)
    return low, high


def field_kernel(sizes, pos, table, source, k, flags, classes, weights, faces, lanes, spread,
                 ws_out, wk_out, robin_out, even_out, odd_out):
    elems_z = flags.shape[1]
    ws_out[...] = weights[...] * source[...]
    wk_out[...] = weights[...] * k[...]
    coefficient = jnp.zeros(flags.shape, f32)
    for c in range(table.shape[0]):
        coefficient = jnp.where(classes[...] == c, table[c], coefficient)
    element = lax.broadcasted_iota(jnp.int32, flags.shape, 1)
    sides = [
        pos[0] == 0, pos[0] == sizes[0] - 1, pos[1] == 0, pos[1] == sizes[1] - 1,
        element == 0, element == elems_z - 1,
    ]
    rows = []
    for bit, side in enumerate(sides):
        flagged = (flags[...] >> bit) % 2 == 1
        rows.append(jnp.where(flagged & side, coefficient, 0.0))
    rows += [jnp.zeros(flags.shape, f32)] * 2
    wide = dot(jnp.concatenate(rows, 0), spread[...])
    row = lax.broadcasted_iota(jnp.int32, wide.shape, 0)
    lane = lax.broadcasted_iota(jnp.int32, wide.shape, 1) % N
    along = jnp.where(
        row < 4,
        lanes[2:3, :],
        jnp.where(row == 4, jnp.where(lane == 0, 1.0, 0.0), jnp.where(lane == N - 1, 1.0, 0.0)),
    )
    robin_out[...] = dot(faces[...], wide * along)
    low = jnp.concatenate([y_rows(r, 0) for r in (ws_out, wk_out, robin_out)], 0)
    high = jnp.concatenate([y_rows(r, N - 1) for r in (ws_out, wk_out, robin_out)], 0)
    send(pos, 1, low, high, even_out, odd_out)


def fold_y_kernel(sizes, pos, ws, wk, robin, even, odd, ws_out, wk_out, robin_out, even_out, odd_out):
    low, high = received(pos, 1, sizes[1], even[...], odd[...])
    for i, (field, out) in enumerate(((ws, ws_out), (wk, wk_out), (robin, robin_out))):
        out[...] = field[...]
        add_y_rows(out, 0, low[N * i : N * i + N])
        add_y_rows(out, N - 1, high[N * i : N * i + N])
    fields = (ws_out, wk_out, robin_out, wk)
    last = N * (N - 1)
    send(
        pos, 0,
        jnp.concatenate([r[0:N, :] for r in fields], 0),
        jnp.concatenate([r[last : last + N, :] for r in fields], 0),
        even_out, odd_out,
    )


def copies(sizes, pos, lanes, shape):
    row = lax.broadcasted_iota(jnp.int32, (shape[0], 1), 0)
    a, b = row // N, row % N
    shared_x = ((a == 0) & (pos[0] > 0)) | ((a == N - 1) & (pos[0] < sizes[0] - 1))
    shared_y = ((b == 0) & (pos[1] > 0)) | ((b == N - 1) & (pos[1] < sizes[1] - 1))
    return jnp.where(shared_x, 2.0, 1.0), jnp.where(shared_y, 2.0, 1.0), lanes[3:4, :]


def operate(pos, v, coefs, mats, q_out, sends):
    kx, ky, kz, advect, diagonal = coefs
    forward, back, z_forward, z_back, lanes = mats
    rows, size = v.shape
    group = z_forward.shape[0]
    grad = dot(forward[...], v)
    tiles = [v[:, i : i + group] for i in range(0, size, group)]
    grad_z = dot(jnp.concatenate(tiles, 0), z_forward[...])
    flux_x = kx[...] * grad[:rows] - advect[...] * v
    flux_y = ky[...] * grad[rows:]
    flux = jnp.concatenate([flux_x, flux_y], 0)
    both = dot(back[...], flux)
    send(pos, 0, both[rows : rows + N], both[rows + N : rows + 2 * N], sends[0], sends[1])
    send(pos, 1, both[rows + 2 * N : rows + 3 * N], both[rows + 3 * N :], sends[2], sends[3])
    flux_z = [
        kz[:, i * group : (i + 1) * group] * grad_z[i * rows : (i + 1) * rows]
        for i in range(len(tiles))
    ]
    back_z = dot(jnp.concatenate(flux_z, 0), z_back[...])
    back_z = jnp.concatenate([back_z[i * rows : (i + 1) * rows] for i in range(len(tiles))], 1)
    q_out[...] = both[:rows] + fold_z(back_z, lanes) + diagonal[...] * v


def assemble(sizes, pos, q, recv, out):
    x_even, x_odd, y_even, y_odd = recv
    last = N * (N - 1)
    x_low, x_high = received(pos, 0, sizes[0], x_even[...], x_odd[...])
    y_low, y_high = received(pos, 1, sizes[1], y_even[...], y_odd[...])
    out[...] = q[...]
    out[0:N, :] += x_low
    out[last : last + N, :] += x_high
    add_y_rows(out, 0, y_low)
    add_y_rows(out, N - 1, y_high)


def first_kernel(sizes, pos, ws, wk_y, robin, wk, even, odd, weights, *refs):
    mats, outs = refs[:5], refs[5:]
    b, kx, ky, kz, advect, diagonal, inverse, q = outs[:8]
    sends = outs[8:12]
    lanes = mats[4]
    last = N * (N - 1)
    low, high = received(pos, 0, sizes[0], even[...], odd[...])
    for i, (field, out) in enumerate(((ws, b), (wk_y, kz), (robin, diagonal), (wk, ky))):
        out[...] = field[...]
        out[0:N, :] += low[N * i : N * i + N]
        out[last : last + N, :] += high[N * i : N * i + N]
    copies_x, copies_y, copies_z = copies(sizes, pos, lanes, ws.shape)
    b[...] = fold_z(b[...], lanes)
    kx[...] = fold_z(wk_y[...], lanes)
    ky[...] = fold_z(ky[...], lanes)
    weights_yz = weights[...] * (copies_y * copies_z)
    advect[...] = scan_speed * weights_yz
    diagonal[...] = fold_z(diagonal[...], lanes) + mass_coef * (weights_yz * copies_x)
    inverse[...] = 1.0 / (copies_x * copies_y * copies_z)
    operate(pos, b[...], (kx, ky, kz, advect, diagonal), mats, q, sends)


def dots_row(pairs, inverse, out):
    lane = lax.broadcasted_iota(jnp.int32, (1, out.shape[-1]), 1)
    row = jnp.zeros(lane.shape, f32)
    scaled = {}
    for i, (u, v) in enumerate(pairs):
        if id(u) not in scaled:
            scaled[id(u)] = u * inverse
        product = scaled[id(u)] * v
        total = jnp.sum(jnp.sum(product, axis=0, keepdims=True), axis=1, keepdims=True)
        row = jnp.where(lane == i, total, row)
    for i in range(out.shape[0]):
        out[i] = row


def totals(gathered, count):
    row = jnp.sum(gathered[...], axis=0)
    lane = lax.broadcasted_iota(jnp.int32, row.shape, 1)
    return [jnp.sum(jnp.where(lane == i, row, 0.0), axis=1, keepdims=True) for i in range(count)]


def apply_kernel(sizes, pos, q, *refs):
    recv, coefs, mats, outs = refs[:4], refs[4:9], refs[9:14], refs[14:]
    v, q_next = outs[:2]
    assemble(sizes, pos, q, recv, v)
    operate(pos, v[...], coefs, mats, q_next, outs[2:6])


def inner_pairs(b, r, s, w, z):
    return [(b, r), (b, s), (b, w), (b, z), (w, r), (w, s), (r, z), (s, z), (w, w), (w, z), (z, z)]


def steps(g):
    br, bs, bw, bz, wr, ws, rz, sz, ww, wz, zz = g
    alpha = br / bs
    omega = (wr - alpha * (ws + rz) + alpha * alpha * sz) / (
        ww - 2.0 * alpha * wz + alpha * alpha * zz
    )
    rho_next = (br - alpha * bs) - omega * (bw - alpha * bz)
    beta = rho_next / br * (alpha / omega)
    return alpha, omega, beta


def first_dots_kernel(sizes, pos, b, s, inverse, q, *refs):
    recv, coefs, mats, outs = refs[:4], refs[4:9], refs[9:14], refs[14:]
    z, row, q_next = outs[:3]
    assemble(sizes, pos, q, recv, z)
    b_, s_, z_ = b[...], s[...], z[...]
    dots_row([(b_, b_), (b_, s_), (b_, z_), (s_, s_), (s_, z_), (z_, z_)], inverse[...], row)
    operate(pos, z_, coefs, mats, q_next, outs[3:7])


def update(alpha, omega, r, s, w, z, aw, az):
    half = r - alpha * s
    applied_half = w - alpha * z
    w_next = applied_half - omega * (aw - alpha * az)
    return half, applied_half, w_next


def update_kernel(sizes, first, pos, gathered, q, *refs):
    recv, refs = refs[:4], refs[4:]
    if first:
        b, s, z = refs[:3]
        refs = refs[3:]
        bb, bs, bz, ss, sz, zz = totals(gathered, 6)
        g = (bb, bs, bs, bz, bs, ss, bz, sz, ss, sz, zz)
        r, p, w, aw, x = b, b, s, z, None
    else:
        r, p, s, w, z, aw, x = refs[:7]
        refs = refs[7:]
        g = totals(gathered, 11)
    coefs, mats, outs = refs[:5], refs[5:10], refs[10:]
    x_out, r_out, p_out, s_out, w_out, zpart_out, q_next = outs[:7]
    alpha, omega, beta = steps(g)
    assemble(sizes, pos, q, recv, zpart_out)
    az = zpart_out[...]
    half, applied_half, w_next = update(alpha, omega, r[...], s[...], w[...], z[...], aw[...], az)
    w_out[...] = w_next
    operate(pos, w_next, coefs, mats, q_next, outs[7:11])
    step = alpha * p[...] + omega * half
    x_out[...] = step if x is None else x[...] + step
    r_next = half - omega * applied_half
    r_out[...] = r_next
    p_out[...] = r_next + beta * (p[...] - omega * s[...])
    s_out[...] = w_next + beta * (s[...] - omega * z[...])
    zpart_out[...] = beta * (z[...] - omega * az)


def dots_kernel(sizes, last, pos, b, r, s, w, zpart, inverse, q, *refs):
    recv, refs = refs[:4], refs[4:]
    if last:
        aw, z, row = refs
    else:
        coefs, mats, outs = refs[:5], refs[5:10], refs[10:]
        aw, z, row, q_next = outs[:4]
    assemble(sizes, pos, q, recv, aw)
    z[...] = aw[...] + zpart[...]
    pairs = inner_pairs(b[...], r[...], s[...], w[...], z[...])
    dots_row(pairs, inverse[...], row)
    if not last:
        operate(pos, z[...], coefs, mats, q_next, outs[4:8])


def last_kernel(sizes, gathered, r, p, s, w, z, x, x_out, r_out):
    alpha, omega, _ = steps(totals(gathered, 11))
    half = r[...] - alpha * s[...]
    x_out[...] = x[...] + alpha * p[...] + omega * half
    r_out[...] = half - omega * (w[...] - alpha * z[...])


def pairings(count):
    even = [(i, i ^ 1) for i in range(count)]
    odd = [(i, (i - 1 if i % 2 == 0 else i + 1) % count) for i in range(count)]
    return even, odd


def per_device(sizes, source, conductivity, robin_flags, htc_class, htc_table):
    shape = source.shape
    elems_z = robin_flags.shape[2]
    rows, size = shape[0] * shape[1], shape[2]
    assert robin_flags.shape[:2] == (1, 1) and sizes[0] % 2 == 0 and sizes[1] % 2 == 0
    devices = sizes[0] * sizes[1]
    pos = jnp.stack([lax.axis_index("gx"), lax.axis_index("gy")]).astype(jnp.int32)
    c = {name: jnp.asarray(value) for name, value in constants(elems_z).items()}
    mats = [c[name] for name in ("forward", "back", "z_forward", "z_back", "lanes")]
    x_pairs, y_pairs = pairings(sizes[0]), pairings(sizes[1])

    def struct(n=rows):
        return jax.ShapeDtypeStruct((n, size), f32)

    field = struct()
    faces = [struct(N)] * 4
    row = jax.ShapeDtypeStruct((devices, 1, 128), f32)

    def call(kernel, outs, smem, *operands):
        specs = [SMEM] * smem + [VMEM] * (len(operands) - smem)
        return pl.pallas_call(
            kernel,
            out_shape=outs,
            in_specs=specs,
            out_specs=[VMEM] * len(outs),
            compiler_params=pltpu.CompilerParams(vmem_limit_bytes=32 * 1024 * 1024),
        )(*operands)

    def exchange(axis, pairs, even, odd):
        return lax.ppermute(even, axis, pairs[0]), lax.ppermute(odd, axis, pairs[1])

    def swap(parts):
        return exchange("gx", x_pairs, *parts[:2]) + exchange("gy", y_pairs, *parts[2:])

    def spread(values):
        return lax.all_to_all(values, ("gx", "gy"), 0, 0)

    flat = lambda v: v.reshape(rows, size)
    ws, wk, robin, *parts = call(
        functools.partial(field_kernel, sizes),
        [field] * 3 + [struct(3 * N)] * 2,
        2,
        pos, htc_table, flat(source), flat(conductivity),
        robin_flags.reshape(1, elems_z), htc_class.reshape(1, elems_z),
        c["weights"], c["faces"], c["lanes"], c["spread"],
    )
    parts = exchange("gy", y_pairs, *parts)
    ws, wk_y, robin, *parts = call(
        functools.partial(fold_y_kernel, sizes),
        [field] * 3 + [struct(4 * N)] * 2,
        1,
        pos, ws, wk, robin, *parts,
    )
    parts = exchange("gx", x_pairs, *parts)
    b, *coefs, inverse, q, s0, s1, s2, s3 = call(
        functools.partial(first_kernel, sizes),
        [field] * 8 + faces,
        1,
        pos, ws, wk_y, robin, wk, *parts, c["weights"], *mats,
    )
    recv = swap((s0, s1, s2, s3))
    s, q, *parts = call(
        functools.partial(apply_kernel, sizes), [field] * 2 + faces, 1,
        pos, q, *recv, *coefs, *mats,
    )
    recv = swap(parts)
    z, products, q, *parts = call(
        functools.partial(first_dots_kernel, sizes), [field, row, field] + faces, 1,
        pos, b, s, inverse, q, *recv, *coefs, *mats,
    )
    state = (b, s, z)
    for iteration in range(ITERS - 1):
        recv = swap(parts)
        gathered = spread(products)
        x, r, p, s, w, zpart, q, *parts = call(
            functools.partial(update_kernel, sizes, iteration == 0),
            [field] * 7 + faces,
            1,
            pos, gathered, q, *recv, *state, *coefs, *mats,
        )
        recv = swap(parts)
        last = iteration == ITERS - 2
        aw, z, products, *rest = call(
            functools.partial(dots_kernel, sizes, last),
            [field] * 2 + [row] + ([] if last else [field] + faces),
            1,
            pos, b, r, s, w, zpart, inverse, q, *recv, *(() if last else (*coefs, *mats)),
        )
        if not last:
            q, *parts = rest
            state = (r, p, s, w, z, aw, x)
    gathered = spread(products)
    x, r = call(functools.partial(last_kernel, sizes), [field] * 2, 0, gathered, r, p, s, w, z, x)
    return x.reshape(shape), r.reshape(shape)


def solution(mesh):
    sizes = (mesh.shape["gx"], mesh.shape["gy"])
    field = P("gx", "gy", None)
    return jax.shard_map(
        functools.partial(per_device, sizes),
        mesh=mesh,
        in_specs=(field, field, field, field, P()),
        out_specs=(field, field),
        check_vma=False,
    )
```

time: 662 us -> 96.2 us (0.15); the launches traced: 653 us -> 95.9 us
  blocking collectives: 254 us -> 11.1 us
  local copies, waits for them, and re-layouts: 218 us -> 5.08 us
  other arithmetic: 45.8 us -> 0.08 us
  waiting for transfers between devices: 55.3 us -> 15.9 us
  between operations: 16.3 us -> 0.77 us
  Pallas kernels: 0 us -> 14.5 us
  matrix products: 12 us -> 0 us
    psum x6 -> x0, blocking collectives: 254 us -> none  [the longest x3 127 us: per_device(): lax.psum((local_inner(applied_half, half_resid), local_inner(applied_half...]
    scatter x14 -> x0, local copies, waits for them, and re-layouts: 197 us -> none  [fold_inside(): blocks = blocks.at[:-1, 7].set(shared).at[1:, 0].set(shared)]
    ppermute x28, waiting for transfers between devices: 55.3 us -> 15.9 us  [the longest x14 15.8 us: exchange(): lax.ppermute(odd, axis, pairs[1])]
    another operation x12 -> x1, other arithmetic: 37.2 us -> 0.08 us  [per_device(): jnp.stack([lax.axis_index('gx'), lax.axis_index('gy')]).astype(jnp.int32)]
    reshape x14 -> x0, local copies, waits for them, and re-layouts: 16.3 us -> none  [the longest x7 8.32 us: fold_inside(): return jnp.moveaxis(blocks.reshape(extent), 0, which_axis)]
    pallas_call x0 -> x10, Pallas kernels: none -> 14.5 us  [call(): pl.pallas_call(kernel, out_shape=outs, in_specs=specs, out_specs=[VMEM] *...]
    dot_general x42 -> x0, matrix products: 12 us -> none  [the longest x6 2.02 us: operate(): back_y = jnp.einsum('ij,aic->ajc', deriv_y, flux_y, precision=highest)]
    ppermute x28, starting transfers between devices: 51.9 us -> 40.2 us  [the longest x14 31.7 us: exchange(): lax.ppermute(odd, axis, pairs[1])]
  transfers between devices with their start and end apart: 28 -> 30, of which waited for: 20 -> 12; matrix products, arithmetic and copies ran while one was open for 0% -> 0% of each run, Pallas kernels for 0% -> 0%
where the time goes in v1:
time: 96.2 us; the launch traced here: 95.9 us
  starting transfers between devices  48.5 us (50%)
  waiting for transfers between devices  15.9 us (17%)
  Pallas kernels  14.5 us (15%)
  blocking collectives  11.1 us (12%)
  local copies, waits for them, and re-layouts  5.08 us (5%)
    ppermute x14, starting transfers between devices, exchange(): lax.ppermute(odd, axis, pairs[1])  31.7 us
    ppermute x14, waiting for transfers between devices, exchange(): lax.ppermute(odd, axis, pairs[1])  15.8 us
    pallas_call x10, Pallas kernels, call(): pl.pallas_call(kernel, out_shape=outs, in_specs=specs, out_specs=[VMEM] *...  14.5 us
    all_to_all x1, blocking collectives, spread(): return lax.all_to_all(values, ('gx', 'gy'), 0, 0)  11.1 us
    ppermute x14, starting transfers between devices, exchange(): lax.ppermute(even, axis, pairs[0])  8.45 us
    all_to_all x2, starting transfers between devices, spread(): return lax.all_to_all(values, ('gx', 'gy'), 0, 0)  8.27 us
    unnamed x28, local copies, waits for them, and re-layouts  5.08 us
  transfers between devices with their start and end apart: 30, of which 12 were waited for; matrix products, arithmetic and copies ran while one was open for 0% of the time, Pallas kernels for 0%

profile of v1, /device:TPU:0, one launch (start us, length us, event | category | flops | bytes accessed | tf_op | source)
XLA Modules:
  0.0 95.9 jit_solution(1862076288100301710)
XLA Ops:
  0.6 0.0 copy-start.4
  0.6 0.1 pad_add_fusion.pos
  0.7 0.6 copy-done.4
  1.4 0.0 copy-done.11
  1.4 0.0 copy-done.12
  1.4 0.0 copy-done.13
  1.4 0.9 copy-done.5
  2.3 0.9 copy-done.7
  3.2 0.9 copy-done.8
  4.1 0.9 copy-done.9
  5.0 0.8 copy-done.10
  5.8 1.0 %shard_map.140 = (f32[64,512]{1,0:T(8,128)S(1)}, f32[64,512]{1,0:T(8,128)S(1)}, f32[64,512]{1,0:T(8,128)S(1)}, f32[24,512]{1,0:T(8,128)S(1)}, f32[24,512]{1,0:T(8,128)S(1)}) custom-call(s32[2]{0:T(128)S(1)} %pad_add_fusion.pos, f32[4]{0:T(128)S(1)} %copy-done.11, f32[64,512]{1,0:T(8,128)S(1)} %bitcast.8, f32[64,512]{1,0:T(8,128)S(1)} %bitcast.9, ...), custom_call_target="tpu_custom_call" | custom-call | tf_op jit(solution)/shard_map/pallas_call | solution.py:384
  6.8 0.0 copy-start
  6.8 0.5 collective-permute-start
  7.3 3.6 %collective-permute-start.1 = (f32[24,512]{1,0:T(8,128)S(1)}, f32[24,512]{1,0:T(8,128)S(1)}, u32[]{:S(2)}, u32[]{:S(2)}) collective-permute-start(f32[24,512]{1,0:T(8,128)S(1)} %get-tuple-element.75), channel_id=1, source_target_pairs={{0,7},{1,2},{2,1},{3,4},{4,3},{5,6},{6,5},{7,0},{8,15},{9,10},{10,... | collective-permute-start | bytes 147464 | tf_op jit(solution)/shard_map/ppermute | solution.py:393
  10.9 1.8 %collective-permute-done.1.odd = f32[24,512]{1,0:T(8,128)S(1)} collective-permute-done((f32[24,512]{1,0:T(8,128)S(1)}, f32[24,512]{1,0:T(8,128)S(1)}, u32[]{:S(2)}, u32[]{:S(2)}) %collective-permute-start.1) | collective-permute-done | bytes 49184 | tf_op jit(solution)/shard_map/ppermute | solution.py:393
  12.6 0.6 shard_map.141
  13.3 1.8 %collective-permute-start.2 = (f32[32,512]{1,0:T(8,128)S(1)}, f32[32,512]{1,0:T(8,128)S(1)}, u32[]{:S(2)}, u32[]{:S(2)}) collective-permute-start(f32[32,512]{1,0:T(8,128)S(1)} %get-tuple-element.79), channel_id=1, source_target_pairs={{0,8},{8,0},{16,24},{24,16},{1,9},{9,1},{17,25},{25,17},{2,10},{10... | collective-permute-start | bytes 196616 | tf_op jit(solution)/shard_map/ppermute | solution.py:393
  15.1 2.5 %collective-permute-start.3 = (f32[32,512]{1,0:T(8,128)S(1)}, f32[32,512]{1,0:T(8,128)S(1)}, u32[]{:S(2)}, u32[]{:S(2)}) collective-permute-start(f32[32,512]{1,0:T(8,128)S(1)} %get-tuple-element.80), channel_id=1, source_target_pairs={{0,24},{8,16},{16,8},{24,0},{1,25},{9,17},{17,9},{25,1},{2,26},{10... | collective-permute-start | bytes 196616 | tf_op jit(solution)/shard_map/ppermute | solution.py:393
  17.5 0.1 collective-permute-done.2.even
  17.6 3.7 %collective-permute-done.3.odd = f32[32,512]{1,0:T(8,128)S(1)} collective-permute-done((f32[32,512]{1,0:T(8,128)S(1)}, f32[32,512]{1,0:T(8,128)S(1)}, u32[]{:S(2)}, u32[]{:S(2)}) %collective-permute-start.3) | collective-permute-done | bytes 65568 | tf_op jit(solution)/shard_map/ppermute | solution.py:393
  21.3 1.7 %shard_map.142 = (f32[64,512]{1,0:T(8,128)S(1)}, f32[64,512]{1,0:T(8,128)S(1)}, f32[64,512]{1,0:T(8,128)S(1)}, f32[64,512]{1,0:T(8,128)S(1)}, f32[64,512]{1,0:T(...) custom-call(s32[2]{0:T(128)S(1)} %pad_add_fusion.pos, ...), custom_call_target="tpu_custom_call" | custom-call | tf_op jit(solution)/shard_map/pallas_call | solution.py:384
  23.0 0.6 collective-permute-start.4
  23.6 2.5 %collective-permute-start.5 = (f32[8,512]{1,0:T(8,128)S(1)}, f32[8,512]{1,0:T(8,128)S(1)}, u32[]{:S(2)}, u32[]{:S(2)}) collective-permute-start(f32[8,512]{1,0:T(8,128)S(1)} %get-tuple-element.84), channel_id=1, source_target_pairs={{0,24},{8,16},{16,8},{24,0},{1,25},{9,17},{17,9},{25,1},{2,26},{10... | collective-permute-start | bytes 49160 | tf_op jit(solution)/shard_map/ppermute | solution.py:393
  26.1 0.0 collective-permute-start.6
  26.1 2.7 %collective-permute-start.7 = (f32[8,512]{1,0:T(8,128)S(1)}, f32[8,512]{1,0:T(8,128)S(1)}, u32[]{:S(2)}, u32[]{:S(2)}) collective-permute-start(f32[8,512]{1,0:T(8,128)S(1)} %get-tuple-element.86), channel_id=1, source_target_pairs={{0,7},{1,2},{2,1},{3,4},{4,3},{5,6},{6,5},{7,0},{8,15},{9,10},{10,... | collective-permute-start | bytes 49160 | tf_op jit(solution)/shard_map/ppermute | solution.py:393
  28.8 0.3 collective-permute-done.5.refs_1_
  29.1 0.0 collective-permute-done.6.refs_2_
  29.1 1.1 %collective-permute-done.7.refs_3_ = f32[8,512]{1,0:T(8,128)S(1)} collective-permute-done((f32[8,512]{1,0:T(8,128)S(1)}, f32[8,512]{1,0:T(8,128)S(1)}, u32[]{:S(2)}, u32[]{:S(2)}) %collective-permute-start.7) | collective-permute-done | bytes 16416 | tf_op jit(solution)/shard_map/ppermute | solution.py:393
  30.3 1.5 %shard_map.143 = (f32[64,512]{1,0:T(8,128)S(1)}, f32[64,512]{1,0:T(8,128)S(1)}, f32[8,512]{1,0:T(8,128)S(1)}, f32[8,512]{1,0:T(8,128)S(1)}, f32[8,512]{1,0:T(8,128)S(1)}, /*index=5*/f32[8,512]{1,0:T(8,128)S(1)}) custom-call(s32[2]{0:T(128)S(1)} %pad_add_fusion.pos, f32[64,512]{1,0:T(8,128)S(1)} %get-tuple-element.82.q, ...), custom_call_target="tpu_custom_call" | custom-call | tf_op jit(solution)/shard_map/pallas_call | solution.py:384
  31.8 0.5 collective-permute-start.8
  32.2 1.4 %collective-permute-start.9 = (f32[8,512]{1,0:T(8,128)S(1)}, f32[8,512]{1,0:T(8,128)S(1)}, u32[]{:S(2)}, u32[]{:S(2)}) collective-permute-start(f32[8,512]{1,0:T(8,128)S(1)} %get-tuple-element.96), channel_id=1, source_target_pairs={{0,24},{8,16},{16,8},{24,0},{1,25},{9,17},{17,9},{25,1},{2,26},{10... | collective-permute-start | bytes 49160 | tf_op jit(solution)/shard_map/ppermute | solution.py:393
  33.7 2.4 %collective-permute-start.11 = (f32[8,512]{1,0:T(8,128)S(1)}, f32[8,512]{1,0:T(8,128)S(1)}, u32[]{:S(2)}, u32[]{:S(2)}) collective-permute-start(f32[8,512]{1,0:T(8,128)S(1)} %get-tuple-element.98), channel_id=1, source_target_pairs={{0,7},{1,2},{2,1},{3,4},{4,3},{5,6},{6,5},{7,0},{8,15},{9,10},{10,... | collective-permute-start | bytes 49160 | tf_op jit(solution)/shard_map/ppermute | solution.py:393
  36.0 0.0 collective-permute-done.8.refs_0_
  36.0 1.8 %collective-permute-done.9.refs_1_ = f32[8,512]{1,0:T(8,128)S(1)} collective-permute-done((f32[8,512]{1,0:T(8,128)S(1)}, f32[8,512]{1,0:T(8,128)S(1)}, u32[]{:S(2)}, u32[]{:S(2)}) %collective-permute-start.9) | collective-permute-done | bytes 16416 | tf_op jit(solution)/shard_map/ppermute | solution.py:393
  37.8 2.0 %shard_map.144 = (f32[64,512]{1,0:T(8,128)S(1)}, f32[32,1,128]{2,1,0:T(1,128)}, f32[64,512]{1,0:T(8,128)S(1)}, f32[8,512]{1,0:T(8,128)S(1)}, f32[8,512]{1,0:T(8,...) custom-call(s32[2]{0:T(128)S(1)} %pad_add_fusion.pos, f32[64,512]{1,0:T(8,128)S(1)} %get-tuple-element.81.b.refs_4_, ...), custom_call_target="tpu_custom_call" | custom-call | tf_op jit(solution)/shard_map/pallas_call | solution.py:384
  39.8 4.2 %all-to-all-start = ((f32[32,1,128]{2,1,0:T(1,128)}), f32[32,1,128]{2,1,0:T(1,128)S(1)}, u32[]{:S(2)}, u32[]{:S(2)}) async-start(f32[32,1,128]{2,1,0:T(1,128)} %get-tuple-element.99), calls=%async_computation | async-start | bytes 32768 | tf_op jit(solution)/shard_map/all_to_all | solution.py:399
  44.0 1.8 %collective-permute-start.12 = (f32[8,512]{1,0:T(8,128)S(1)}, f32[8,512]{1,0:T(8,128)S(1)}, u32[]{:S(2)}, u32[]{:S(2)}) collective-permute-start(f32[8,512]{1,0:T(8,128)S(1)} %get-tuple-element.101), channel_id=1, source_target_pairs={{0,8},{8,0},{16,24},{24,16},{1,9},{9,1},{17,25},{25,17},{2,10},{10... | collective-permute-start | bytes 49160 | tf_op jit(solution)/shard_map/ppermute | solution.py:393
  45.8 2.4 %collective-permute-start.13 = (f32[8,512]{1,0:T(8,128)S(1)}, f32[8,512]{1,0:T(8,128)S(1)}, u32[]{:S(2)}, u32[]{:S(2)}) collective-permute-start(f32[8,512]{1,0:T(8,128)S(1)} %get-tuple-element.102), channel_id=1, source_target_pairs={{0,24},{8,16},{16,8},{24,0},{1,25},{9,17},{17,9},{25,1},{2,26},{10... | collective-permute-start | bytes 49160 | tf_op jit(solution)/shard_map/ppermute | solution.py:393
  48.2 0.0 collective-permute-start.14
  48.2 2.5 %collective-permute-start.15 = (f32[8,512]{1,0:T(8,128)S(1)}, f32[8,512]{1,0:T(8,128)S(1)}, u32[]{:S(2)}, u32[]{:S(2)}) collective-permute-start(f32[8,512]{1,0:T(8,128)S(1)} %get-tuple-element.104), channel_id=1, source_target_pairs={{0,7},{1,2},{2,1},{3,4},{4,3},{5,6},{6,5},{7,0},{8,15},{9,10},{10,... | collective-permute-start | bytes 49160 | tf_op jit(solution)/shard_map/ppermute | solution.py:393
  50.7 0.7 collective-permute-done.13.refs_1_
  51.4 0.0 collective-permute-done.14.refs_2_
  51.4 0.9 collective-permute-done.15.refs_3_
  52.3 1.6 %shard_map.145 = (f32[64,512]{1,0:T(8,128)S(1)}, f32[64,512]{1,0:T(8,128)S(1)}, f32[64,512]{1,0:T(8,128)S(1)}, f32[64,512]{1,0:T(8,128)S(1)}, f32[64,512]{1,0:T(...) custom-call(s32[2]{0:T(128)S(1)} %pad_add_fusion.pos, ...), custom_call_target="tpu_custom_call" | custom-call | tf_op jit(solution)/shard_map/pallas_call | solution.py:384
  53.9 0.7 collective-permute-start.16
  54.6 1.0 %collective-permute-start.17 = (f32[8,512]{1,0:T(8,128)S(1)}, f32[8,512]{1,0:T(8,128)S(1)}, u32[]{:S(2)}, u32[]{:S(2)}) collective-permute-start(f32[8,512]{1,0:T(8,128)S(1)} %get-tuple-element.112), channel_id=1, source_target_pairs={{0,24},{8,16},{16,8},{24,0},{1,25},{9,17},{17,9},{25,1},{2,26},{10... | collective-permute-start | bytes 49160 | tf_op jit(solution)/shard_map/ppermute | solution.py:393
  55.6 2.5 %collective-permute-start.19 = (f32[8,512]{1,0:T(8,128)S(1)}, f32[8,512]{1,0:T(8,128)S(1)}, u32[]{:S(2)}, u32[]{:S(2)}) collective-permute-start(f32[8,512]{1,0:T(8,128)S(1)} %get-tuple-element.114), channel_id=1, source_target_pairs={{0,7},{1,2},{2,1},{3,4},{4,3},{5,6},{6,5},{7,0},{8,15},{9,10},{10,... | collective-permute-start | bytes 49160 | tf_op jit(solution)/shard_map/ppermute | solution.py:393
  58.1 2.0 %collective-permute-done.17.refs_1_ = f32[8,512]{1,0:T(8,128)S(1)} collective-permute-done((f32[8,512]{1,0:T(8,128)S(1)}, f32[8,512]{1,0:T(8,128)S(1)}, u32[]{:S(2)}, u32[]{:S(2)}) %collective-permute-start.17) | collective-permute-done | bytes 16416 | tf_op jit(solution)/shard_map/ppermute | solution.py:393
  60.1 2.1 %shard_map.146 = (f32[64,512]{1,0:T(8,128)S(1)}, f32[64,512]{1,0:T(8,128)S(1)}, f32[32,1,128]{2,1,0:T(1,128)}, f32[64,512]{1,0:T(8,128)S(1)}, f32[8,512]{1,0:T(8...) custom-call(s32[2]{0:T(128)S(1)} %pad_add_fusion.pos, ...), custom_call_target="tpu_custom_call" | custom-call | tf_op jit(solution)/shard_map/pallas_call | solution.py:384
  62.3 4.1 %all-to-all-start.1 = ((f32[32,1,128]{2,1,0:T(1,128)}), f32[32,1,128]{2,1,0:T(1,128)S(1)}, u32[]{:S(2)}, u32[]{:S(2)}) async-start(f32[32,1,128]{2,1,0:T(1,128)} %get-tuple-element.115), calls=%async_computation.1 | async-start | bytes 32768 | tf_op jit(solution)/shard_map/all_to_all | solution.py:399
  66.4 1.8 %collective-permute-start.20 = (f32[8,512]{1,0:T(8,128)S(1)}, f32[8,512]{1,0:T(8,128)S(1)}, u32[]{:S(2)}, u32[]{:S(2)}) collective-permute-start(f32[8,512]{1,0:T(8,128)S(1)} %get-tuple-element.117), channel_id=1, source_target_pairs={{0,8},{8,0},{16,24},{24,16},{1,9},{9,1},{17,25},{25,17},{2,10},{10... | collective-permute-start | bytes 49160 | tf_op jit(solution)/shard_map/ppermute | solution.py:393
  68.2 2.4 %collective-permute-start.21 = (f32[8,512]{1,0:T(8,128)S(1)}, f32[8,512]{1,0:T(8,128)S(1)}, u32[]{:S(2)}, u32[]{:S(2)}) collective-permute-start(f32[8,512]{1,0:T(8,128)S(1)} %get-tuple-element.118), channel_id=1, source_target_pairs={{0,24},{8,16},{16,8},{24,0},{1,25},{9,17},{17,9},{25,1},{2,26},{10... | collective-permute-start | bytes 49160 | tf_op jit(solution)/shard_map/ppermute | solution.py:393
  70.6 2.5 %collective-permute-start.23 = (f32[8,512]{1,0:T(8,128)S(1)}, f32[8,512]{1,0:T(8,128)S(1)}, u32[]{:S(2)}, u32[]{:S(2)}) collective-permute-start(f32[8,512]{1,0:T(8,128)S(1)} %get-tuple-element.120), channel_id=1, source_target_pairs={{0,7},{1,2},{2,1},{3,4},{4,3},{5,6},{6,5},{7,0},{8,15},{9,10},{10,... | collective-permute-start | bytes 49160 | tf_op jit(solution)/shard_map/ppermute | solution.py:393
  73.1 0.7 collective-permute-done.21.refs_1_
  73.8 0.9 collective-permute-done.23.refs_3_
  74.7 1.6 %shard_map.147 = (f32[64,512]{1,0:T(8,128)S(1)}, f32[64,512]{1,0:T(8,128)S(1)}, f32[64,512]{1,0:T(8,128)S(1)}, f32[64,512]{1,0:T(8,128)S(1)}, f32[64,512]{1,0:T(...) custom-call(s32[2]{0:T(128)S(1)} %pad_add_fusion.pos, ...), custom_call_target="tpu_custom_call" | custom-call | tf_op jit(solution)/shard_map/pallas_call | solution.py:384
  76.3 0.7 collective-permute-start.24
  77.0 1.0 %collective-permute-start.25 = (f32[8,512]{1,0:T(8,128)S(1)}, f32[8,512]{1,0:T(8,128)S(1)}, u32[]{:S(2)}, u32[]{:S(2)}) collective-permute-start(f32[8,512]{1,0:T(8,128)S(1)} %get-tuple-element.131), channel_id=1, source_target_pairs={{0,24},{8,16},{16,8},{24,0},{1,25},{9,17},{17,9},{25,1},{2,26},{10... | collective-permute-start | bytes 49160 | tf_op jit(solution)/shard_map/ppermute | solution.py:393
  78.0 2.5 %collective-permute-start.27 = (f32[8,512]{1,0:T(8,128)S(1)}, f32[8,512]{1,0:T(8,128)S(1)}, u32[]{:S(2)}, u32[]{:S(2)}) collective-permute-start(f32[8,512]{1,0:T(8,128)S(1)} %get-tuple-element.133), channel_id=1, source_target_pairs={{0,7},{1,2},{2,1},{3,4},{4,3},{5,6},{6,5},{7,0},{8,15},{9,10},{10,... | collective-permute-start | bytes 49160 | tf_op jit(solution)/shard_map/ppermute | solution.py:393
  80.5 2.0 %collective-permute-done.25.refs_1_ = f32[8,512]{1,0:T(8,128)S(1)} collective-permute-done((f32[8,512]{1,0:T(8,128)S(1)}, f32[8,512]{1,0:T(8,128)S(1)}, u32[]{:S(2)}, u32[]{:S(2)}) %collective-permute-start.25) | collective-permute-done | bytes 16416 | tf_op jit(solution)/shard_map/ppermute | solution.py:393
  82.5 1.4 %shard_map.148 = (f32[64,512]{1,0:T(8,128)}, f32[64,512]{1,0:T(8,128)S(1)}, f32[32,1,128]{2,1,0:T(1,128)S(1)}) custom-call(s32[2]{0:T(128)S(1)} %pad_add_fusion.pos, f32[64,512]{1,0:T(8,128)S(1)} %get-tuple-element.81.b.refs_4_, f32[64,512]{1,0:T(8,128)S(1)} %get-tuple-element.125.r, f32[64,512]{1,0:T(8,128)S(1)} %get-tuple-element.126.s, ...), custom_call_target="tpu_custom_call" | custom-call | tf_op jit(solution)/shard_map/pallas_call | solution.py:384
  84.0 11.1 %all_to_all.15.gathered = f32[32,1,128]{2,1,0:T(1,128)S(1)} all-to-all(f32[32,1,128]{2,1,0:T(1,128)S(1)} %get-tuple-element.134), channel_id=1, replica_groups=mesh['gx'=4,'gy'=8] {'gx','gy'}, dimensions={0} | all-to-all | bytes 32768 | tf_op jit(solution)/shard_map/all_to_all | solution.py:399
  95.0 0.9 shard_map.149
  (36 shorter events, 0.1 us)
Async XLA Ops:
  0.6 0.7 copy-start.4
  0.7 0.7 copy-start.11
  0.7 0.7 copy-start.12
  0.7 0.7 copy-start.13
  1.4 0.9 copy-start.5
  2.3 0.9 copy-start.7
  3.2 0.9 copy-start.8
  4.1 0.9 copy-start.9
  5.0 0.8 copy-start.10
  5.8 15.5 %copy-start.1 = (f32[256,256]{1,0:T(8,128)S(1)}, f32[256,256]{1,0:T(8,128)}, u32[]{:S(2)}) copy-start(f32[256,256]{1,0:T(8,128)} %constant.26.clone.refs_2_.refs_11_.refs_14_.refs_18_) | copy-start | bytes 786436
  6.8 14.5 %copy-start = (f32[256,256]{1,0:T(8,128)S(1)}, f32[256,256]{1,0:T(8,128)}, u32[]{:S(2)}) copy-start(f32[256,256]{1,0:T(8,128)} %constant.27.clone.refs_3_.refs_12_.refs_15_.refs_19_) | copy-start | bytes 786436
  6.8 4.1 %collective-permute-start = (f32[24,512]{1,0:T(8,128)S(1)}, f32[24,512]{1,0:T(8,128)S(1)}, u32[]{:S(2)}, u32[]{:S(2)}) collective-permute-start(f32[24,512]{1,0:T(8,128)S(1)} %get-tuple-element.74), channel_id=1, source_target_pairs={{0,1},{1,0},{2,3},{3,2},{4,5},{5,4},{6,7},{7,6},{8,9},{9,8},{10,11... | collective-permute-start | bytes 147464 | tf_op jit(solution)/shard_map/ppermute | solution.py:393
  7.3 5.3 %collective-permute-start.1 = (f32[24,512]{1,0:T(8,128)S(1)}, f32[24,512]{1,0:T(8,128)S(1)}, u32[]{:S(2)}, u32[]{:S(2)}) collective-permute-start(f32[24,512]{1,0:T(8,128)S(1)} %get-tuple-element.75), channel_id=1, source_target_pairs={{0,7},{1,2},{2,1},{3,4},{4,3},{5,6},{6,5},{7,0},{8,15},{9,10},{10,... | collective-permute-start | bytes 147464 | tf_op jit(solution)/shard_map/ppermute | solution.py:393
  12.6 8.7 %copy-start.2 = (f32[128,64]{1,0:T(8,128)S(1)}, f32[128,64]{1,0:T(8,128)}, u32[]{:S(2)}) copy-start(f32[128,64]{1,0:T(8,128)} %constant.24.clone.refs_0_.refs_9_.refs_12_.refs_16_) | copy-start | bytes 98308
  12.6 8.7 %copy-start.3 = (f32[96,128]{1,0:T(8,128)S(1)}, f32[96,128]{1,0:T(8,128)}, u32[]{:S(2)}) copy-start(f32[96,128]{1,0:T(8,128)} %constant.25.clone.refs_1_.refs_10_.refs_13_.refs_17_) | copy-start | bytes 147460
  12.6 8.7 %copy-start.6 = (f32[64,512]{1,0:T(8,128)S(1)}, f32[64,512]{1,0:T(8,128)}, u32[]{:S(2)}) copy-start(f32[64,512]{1,0:T(8,128)} %constant.29.clone.weights) | copy-start | bytes 393220
  13.3 4.3 %collective-permute-start.2 = (f32[32,512]{1,0:T(8,128)S(1)}, f32[32,512]{1,0:T(8,128)S(1)}, u32[]{:S(2)}, u32[]{:S(2)}) collective-permute-start(f32[32,512]{1,0:T(8,128)S(1)} %get-tuple-element.79), channel_id=1, source_target_pairs={{0,8},{8,0},{16,24},{24,16},{1,9},{9,1},{17,25},{25,17},{2,10},{10... | collective-permute-start | bytes 196616 | tf_op jit(solution)/shard_map/ppermute | solution.py:393
  15.1 6.2 %collective-permute-start.3 = (f32[32,512]{1,0:T(8,128)S(1)}, f32[32,512]{1,0:T(8,128)S(1)}, u32[]{:S(2)}, u32[]{:S(2)}) collective-permute-start(f32[32,512]{1,0:T(8,128)S(1)} %get-tuple-element.80), channel_id=1, source_target_pairs={{0,24},{8,16},{16,8},{24,0},{1,25},{9,17},{17,9},{25,1},{2,26},{10... | collective-permute-start | bytes 196616 | tf_op jit(solution)/shard_map/ppermute | solution.py:393
  23.0 5.8 %collective-permute-start.4 = (f32[8,512]{1,0:T(8,128)S(1)}, f32[8,512]{1,0:T(8,128)S(1)}, u32[]{:S(2)}, u32[]{:S(2)}) collective-permute-start(f32[8,512]{1,0:T(8,128)S(1)} %get-tuple-element.83), channel_id=1, source_target_pairs={{0,8},{8,0},{16,24},{24,16},{1,9},{9,1},{17,25},{25,17},{2,10},{10... | collective-permute-start | bytes 49160 | tf_op jit(solution)/shard_map/ppermute | solution.py:393
  23.6 5.5 %collective-permute-start.5 = (f32[8,512]{1,0:T(8,128)S(1)}, f32[8,512]{1,0:T(8,128)S(1)}, u32[]{:S(2)}, u32[]{:S(2)}) collective-permute-start(f32[8,512]{1,0:T(8,128)S(1)} %get-tuple-element.84), channel_id=1, source_target_pairs={{0,24},{8,16},{16,8},{24,0},{1,25},{9,17},{17,9},{25,1},{2,26},{10... | collective-permute-start | bytes 49160 | tf_op jit(solution)/shard_map/ppermute | solution.py:393
  26.1 3.1 %collective-permute-start.6 = (f32[8,512]{1,0:T(8,128)S(1)}, f32[8,512]{1,0:T(8,128)S(1)}, u32[]{:S(2)}, u32[]{:S(2)}) collective-permute-start(f32[8,512]{1,0:T(8,128)S(1)} %get-tuple-element.85), channel_id=1, source_target_pairs={{0,1},{1,0},{2,3},{3,2},{4,5},{5,4},{6,7},{7,6},{8,9},{9,8},{10,11... | collective-permute-start | bytes 49160 | tf_op jit(solution)/shard_map/ppermute | solution.py:393
  26.1 4.2 %collective-permute-start.7 = (f32[8,512]{1,0:T(8,128)S(1)}, f32[8,512]{1,0:T(8,128)S(1)}, u32[]{:S(2)}, u32[]{:S(2)}) collective-permute-start(f32[8,512]{1,0:T(8,128)S(1)} %get-tuple-element.86), channel_id=1, source_target_pairs={{0,7},{1,2},{2,1},{3,4},{4,3},{5,6},{6,5},{7,0},{8,15},{9,10},{10,... | collective-permute-start | bytes 49160 | tf_op jit(solution)/shard_map/ppermute | solution.py:393
  31.8 4.2 %collective-permute-start.8 = (f32[8,512]{1,0:T(8,128)S(1)}, f32[8,512]{1,0:T(8,128)S(1)}, u32[]{:S(2)}, u32[]{:S(2)}) collective-permute-start(f32[8,512]{1,0:T(8,128)S(1)} %get-tuple-element.95), channel_id=1, source_target_pairs={{0,8},{8,0},{16,24},{24,16},{1,9},{9,1},{17,25},{25,17},{2,10},{10... | collective-permute-start | bytes 49160 | tf_op jit(solution)/shard_map/ppermute | solution.py:393
  32.2 5.5 %collective-permute-start.9 = (f32[8,512]{1,0:T(8,128)S(1)}, f32[8,512]{1,0:T(8,128)S(1)}, u32[]{:S(2)}, u32[]{:S(2)}) collective-permute-start(f32[8,512]{1,0:T(8,128)S(1)} %get-tuple-element.96), channel_id=1, source_target_pairs={{0,24},{8,16},{16,8},{24,0},{1,25},{9,17},{17,9},{25,1},{2,26},{10... | collective-permute-start | bytes 49160 | tf_op jit(solution)/shard_map/ppermute | solution.py:393
  33.6 4.1 %collective-permute-start.10 = (f32[8,512]{1,0:T(8,128)S(1)}, f32[8,512]{1,0:T(8,128)S(1)}, u32[]{:S(2)}, u32[]{:S(2)}) collective-permute-start(f32[8,512]{1,0:T(8,128)S(1)} %get-tuple-element.97), channel_id=1, source_target_pairs={{0,1},{1,0},{2,3},{3,2},{4,5},{5,4},{6,7},{7,6},{8,9},{9,8},{10,11... | collective-permute-start | bytes 49160 | tf_op jit(solution)/shard_map/ppermute | solution.py:393
  33.7 4.1 %collective-permute-start.11 = (f32[8,512]{1,0:T(8,128)S(1)}, f32[8,512]{1,0:T(8,128)S(1)}, u32[]{:S(2)}, u32[]{:S(2)}) collective-permute-start(f32[8,512]{1,0:T(8,128)S(1)} %get-tuple-element.98), channel_id=1, source_target_pairs={{0,7},{1,2},{2,1},{3,4},{4,3},{5,6},{6,5},{7,0},{8,15},{9,10},{10,... | collective-permute-start | bytes 49160 | tf_op jit(solution)/shard_map/ppermute | solution.py:393
  39.8 12.4 %all-to-all-start = ((f32[32,1,128]{2,1,0:T(1,128)}), f32[32,1,128]{2,1,0:T(1,128)S(1)}, u32[]{:S(2)}, u32[]{:S(2)}) async-start(f32[32,1,128]{2,1,0:T(1,128)} %get-tuple-element.99), calls=%async_computation | async-start | bytes 32768 | tf_op jit(solution)/shard_map/all_to_all | solution.py:399
  44.0 6.7 %collective-permute-start.12 = (f32[8,512]{1,0:T(8,128)S(1)}, f32[8,512]{1,0:T(8,128)S(1)}, u32[]{:S(2)}, u32[]{:S(2)}) collective-permute-start(f32[8,512]{1,0:T(8,128)S(1)} %get-tuple-element.101), channel_id=1, source_target_pairs={{0,8},{8,0},{16,24},{24,16},{1,9},{9,1},{17,25},{25,17},{2,10},{10... | collective-permute-start | bytes 49160 | tf_op jit(solution)/shard_map/ppermute | solution.py:393
  45.8 5.5 %collective-permute-start.13 = (f32[8,512]{1,0:T(8,128)S(1)}, f32[8,512]{1,0:T(8,128)S(1)}, u32[]{:S(2)}, u32[]{:S(2)}) collective-permute-start(f32[8,512]{1,0:T(8,128)S(1)} %get-tuple-element.102), channel_id=1, source_target_pairs={{0,24},{8,16},{16,8},{24,0},{1,25},{9,17},{17,9},{25,1},{2,26},{10... | collective-permute-start | bytes 49160 | tf_op jit(solution)/shard_map/ppermute | solution.py:393
  48.2 3.2 %collective-permute-start.14 = (f32[8,512]{1,0:T(8,128)S(1)}, f32[8,512]{1,0:T(8,128)S(1)}, u32[]{:S(2)}, u32[]{:S(2)}) collective-permute-start(f32[8,512]{1,0:T(8,128)S(1)} %get-tuple-element.103), channel_id=1, source_target_pairs={{0,1},{1,0},{2,3},{3,2},{4,5},{5,4},{6,7},{7,6},{8,9},{9,8},{10,11... | collective-permute-start | bytes 49160 | tf_op jit(solution)/shard_map/ppermute | solution.py:393
  48.2 4.1 %collective-permute-start.15 = (f32[8,512]{1,0:T(8,128)S(1)}, f32[8,512]{1,0:T(8,128)S(1)}, u32[]{:S(2)}, u32[]{:S(2)}) collective-permute-start(f32[8,512]{1,0:T(8,128)S(1)} %get-tuple-element.104), channel_id=1, source_target_pairs={{0,7},{1,2},{2,1},{3,4},{4,3},{5,6},{6,5},{7,0},{8,15},{9,10},{10,... | collective-permute-start | bytes 49160 | tf_op jit(solution)/shard_map/ppermute | solution.py:393
  53.9 4.2 %collective-permute-start.16 = (f32[8,512]{1,0:T(8,128)S(1)}, f32[8,512]{1,0:T(8,128)S(1)}, u32[]{:S(2)}, u32[]{:S(2)}) collective-permute-start(f32[8,512]{1,0:T(8,128)S(1)} %get-tuple-element.111), channel_id=1, source_target_pairs={{0,8},{8,0},{16,24},{24,16},{1,9},{9,1},{17,25},{25,17},{2,10},{10... | collective-permute-start | bytes 49160 | tf_op jit(solution)/shard_map/ppermute | solution.py:393
  54.6 5.5 %collective-permute-start.17 = (f32[8,512]{1,0:T(8,128)S(1)}, f32[8,512]{1,0:T(8,128)S(1)}, u32[]{:S(2)}, u32[]{:S(2)}) collective-permute-start(f32[8,512]{1,0:T(8,128)S(1)} %get-tuple-element.112), channel_id=1, source_target_pairs={{0,24},{8,16},{16,8},{24,0},{1,25},{9,17},{17,9},{25,1},{2,26},{10... | collective-permute-start | bytes 49160 | tf_op jit(solution)/shard_map/ppermute | solution.py:393
  55.6 4.6 %collective-permute-start.18 = (f32[8,512]{1,0:T(8,128)S(1)}, f32[8,512]{1,0:T(8,128)S(1)}, u32[]{:S(2)}, u32[]{:S(2)}) collective-permute-start(f32[8,512]{1,0:T(8,128)S(1)} %get-tuple-element.113), channel_id=1, source_target_pairs={{0,1},{1,0},{2,3},{3,2},{4,5},{5,4},{6,7},{7,6},{8,9},{9,8},{10,11... | collective-permute-start | bytes 49160 | tf_op jit(solution)/shard_map/ppermute | solution.py:393
  55.6 4.6 %collective-permute-start.19 = (f32[8,512]{1,0:T(8,128)S(1)}, f32[8,512]{1,0:T(8,128)S(1)}, u32[]{:S(2)}, u32[]{:S(2)}) collective-permute-start(f32[8,512]{1,0:T(8,128)S(1)} %get-tuple-element.114), channel_id=1, source_target_pairs={{0,7},{1,2},{2,1},{3,4},{4,3},{5,6},{6,5},{7,0},{8,15},{9,10},{10,... | collective-permute-start | bytes 49160 | tf_op jit(solution)/shard_map/ppermute | solution.py:393
  62.3 12.4 %all-to-all-start.1 = ((f32[32,1,128]{2,1,0:T(1,128)}), f32[32,1,128]{2,1,0:T(1,128)S(1)}, u32[]{:S(2)}, u32[]{:S(2)}) async-start(f32[32,1,128]{2,1,0:T(1,128)} %get-tuple-element.115), calls=%async_computation.1 | async-start | bytes 32768 | tf_op jit(solution)/shard_map/all_to_all | solution.py:399
  66.4 6.7 %collective-permute-start.20 = (f32[8,512]{1,0:T(8,128)S(1)}, f32[8,512]{1,0:T(8,128)S(1)}, u32[]{:S(2)}, u32[]{:S(2)}) collective-permute-start(f32[8,512]{1,0:T(8,128)S(1)} %get-tuple-element.117), channel_id=1, source_target_pairs={{0,8},{8,0},{16,24},{24,16},{1,9},{9,1},{17,25},{25,17},{2,10},{10... | collective-permute-start | bytes 49160 | tf_op jit(solution)/shard_map/ppermute | solution.py:393
  68.2 5.5 %collective-permute-start.21 = (f32[8,512]{1,0:T(8,128)S(1)}, f32[8,512]{1,0:T(8,128)S(1)}, u32[]{:S(2)}, u32[]{:S(2)}) collective-permute-start(f32[8,512]{1,0:T(8,128)S(1)} %get-tuple-element.118), channel_id=1, source_target_pairs={{0,24},{8,16},{16,8},{24,0},{1,25},{9,17},{17,9},{25,1},{2,26},{10... | collective-permute-start | bytes 49160 | tf_op jit(solution)/shard_map/ppermute | solution.py:393
  70.6 3.2 %collective-permute-start.22 = (f32[8,512]{1,0:T(8,128)S(1)}, f32[8,512]{1,0:T(8,128)S(1)}, u32[]{:S(2)}, u32[]{:S(2)}) collective-permute-start(f32[8,512]{1,0:T(8,128)S(1)} %get-tuple-element.119), channel_id=1, source_target_pairs={{0,1},{1,0},{2,3},{3,2},{4,5},{5,4},{6,7},{7,6},{8,9},{9,8},{10,11... | collective-permute-start | bytes 49160 | tf_op jit(solution)/shard_map/ppermute | solution.py:393
  70.6 4.1 %collective-permute-start.23 = (f32[8,512]{1,0:T(8,128)S(1)}, f32[8,512]{1,0:T(8,128)S(1)}, u32[]{:S(2)}, u32[]{:S(2)}) collective-permute-start(f32[8,512]{1,0:T(8,128)S(1)} %get-tuple-element.120), channel_id=1, source_target_pairs={{0,7},{1,2},{2,1},{3,4},{4,3},{5,6},{6,5},{7,0},{8,15},{9,10},{10,... | collective-permute-start | bytes 49160 | tf_op jit(solution)/shard_map/ppermute | solution.py:393
  76.3 4.2 %collective-permute-start.24 = (f32[8,512]{1,0:T(8,128)S(1)}, f32[8,512]{1,0:T(8,128)S(1)}, u32[]{:S(2)}, u32[]{:S(2)}) collective-permute-start(f32[8,512]{1,0:T(8,128)S(1)} %get-tuple-element.130), channel_id=1, source_target_pairs={{0,8},{8,0},{16,24},{24,16},{1,9},{9,1},{17,25},{25,17},{2,10},{10... | collective-permute-start | bytes 49160 | tf_op jit(solution)/shard_map/ppermute | solution.py:393
  77.0 5.5 %collective-permute-start.25 = (f32[8,512]{1,0:T(8,128)S(1)}, f32[8,512]{1,0:T(8,128)S(1)}, u32[]{:S(2)}, u32[]{:S(2)}) collective-permute-start(f32[8,512]{1,0:T(8,128)S(1)} %get-tuple-element.131), channel_id=1, source_target_pairs={{0,24},{8,16},{16,8},{24,0},{1,25},{9,17},{17,9},{25,1},{2,26},{10... | collective-permute-start | bytes 49160 | tf_op jit(solution)/shard_map/ppermute | solution.py:393
  78.0 4.5 %collective-permute-start.26 = (f32[8,512]{1,0:T(8,128)S(1)}, f32[8,512]{1,0:T(8,128)S(1)}, u32[]{:S(2)}, u32[]{:S(2)}) collective-permute-start(f32[8,512]{1,0:T(8,128)S(1)} %get-tuple-element.132), channel_id=1, source_target_pairs={{0,1},{1,0},{2,3},{3,2},{4,5},{5,4},{6,7},{7,6},{8,9},{9,8},{10,11... | collective-permute-start | bytes 49160 | tf_op jit(solution)/shard_map/ppermute | solution.py:393
  78.0 4.5 %collective-permute-start.27 = (f32[8,512]{1,0:T(8,128)S(1)}, f32[8,512]{1,0:T(8,128)S(1)}, u32[]{:S(2)}, u32[]{:S(2)}) collective-permute-start(f32[8,512]{1,0:T(8,128)S(1)} %get-tuple-element.133), channel_id=1, source_target_pairs={{0,7},{1,2},{2,1},{3,4},{4,3},{5,6},{6,5},{7,0},{8,15},{9,10},{10,... | collective-permute-start | bytes 49160 | tf_op jit(solution)/shard_map/ppermute | solution.py:393

commit v2 on v1

--- a/solution.py
+++ b/solution.py
@@ -355,10 +355,18 @@
     r_out[...] = half - omega * (w[...] - alpha * z[...])
 
 
-def pairings(count):
-    even = [(i, i ^ 1) for i in range(count)]
-    odd = [(i, (i - 1 if i % 2 == 0 else i + 1) % count) for i in range(count)]
-    return even, odd
+def pairings(sizes):
+    count_x, count_y = sizes
+    grid = [(i, j) for i in range(count_x) for j in range(count_y)]
+    number = lambda i, j: i * count_y + j
+    step = lambda i: i + 1 if i % 2 else i - 1
+    x_even = [(number(i, j), number(i ^ 1, j)) for i, j in grid]
+    x_odd = [
+        (number(i, j), number(step(i), j) if 0 < i < count_x - 1 else number(i, j ^ 1)) for i, j in grid
+    ]
+    y_even = [(number(i, j), number(i, j ^ 1)) for i, j in grid]
+    y_odd = [(number(i, j), number(i, step(j) % count_y)) for i, j in grid]
+    return (x_even, x_odd), (y_even, y_odd)
 
 
 def per_device(sizes, source, conductivity, robin_flags, htc_class, htc_table):
@@ -370,7 +378,7 @@
     pos = jnp.stack([lax.axis_index("gx"), lax.axis_index("gy")]).astype(jnp.int32)
     c = {name: jnp.asarray(value) for name, value in constants(elems_z).items()}
     mats = [c[name] for name in ("forward", "back", "z_forward", "z_back", "lanes")]
-    x_pairs, y_pairs = pairings(sizes[0]), pairings(sizes[1])
+    x_pairs, y_pairs = pairings(sizes)
 
     def struct(n=rows):
         return jax.ShapeDtypeStruct((n, size), f32)
@@ -389,11 +397,18 @@
             compiler_params=pltpu.CompilerParams(vmem_limit_bytes=32 * 1024 * 1024),
         )(*operands)
 
-    def exchange(axis, pairs, even, odd):
-        return lax.ppermute(even, axis, pairs[0]), lax.ppermute(odd, axis, pairs[1])
+    def permute(values, pairs):
+        return lax.ppermute(values, ("gx", "gy"), pairs)
+
+    def exchange(pairs, even, odd):
+        odd = permute(odd, pairs[1])
+        return permute(even, pairs[0]), odd
 
     def swap(parts):
-        return exchange("gx", x_pairs, *parts[:2]) + exchange("gy", y_pairs, *parts[2:])
+        x_odd = permute(parts[1], x_pairs[1])
+        y_odd = permute(parts[3], y_pairs[1])
+        x_even = permute(parts[0], x_pairs[0])
+        return x_even, x_odd, permute(parts[2], y_pairs[0]), y_odd
 
     def spread(values):
         return lax.all_to_all(values, ("gx", "gy"), 0, 0)
@@ -407,14 +422,14 @@
         robin_flags.reshape(1, elems_z), htc_class.reshape(1, elems_z),
         c["weights"], c["faces"], c["lanes"], c["spread"],
     )
-    parts = exchange("gy", y_pairs, *parts)
+    parts = exchange(y_pairs, *parts)
     ws, wk_y, robin, *parts = call(
         functools.partial(fold_y_kernel, sizes),
         [field] * 3 + [struct(4 * N)] * 2,
         1,
         pos, ws, wk, robin, *parts,
     )
-    parts = exchange("gx", x_pairs, *parts)
+    parts = exchange(x_pairs, *parts)
     b, *coefs, inverse, q, s0, s1, s2, s3 = call(
         functools.partial(first_kernel, sizes),
         [field] * 8 + faces,

time: 96.2 us -> 88.3 us (0.918)
  starting transfers between devices: 48.5 us -> 39.5 us
  waiting for transfers between devices: 15.9 us -> 18 us
  blocking collectives: 11.1 us -> 10 us
    ppermute x28, starting transfers between devices: 40.2 us -> 33 us  [permute(): return lax.ppermute(values, ('gx', 'gy'), pairs)]
    all_to_all x2, starting transfers between devices: 8.27 us -> 6.52 us  [spread(): return lax.all_to_all(values, ('gx', 'gy'), 0, 0)]
    all_to_all x2, waiting for transfers between devices: 0.01 us -> 1.33 us  [spread(): return lax.all_to_all(values, ('gx', 'gy'), 0, 0)]
    all_to_all x1, blocking collectives: 11.1 us -> 10 us  [spread(): return lax.all_to_all(values, ('gx', 'gy'), 0, 0)]
  transfers between devices with their start and end apart: 30 -> 30, of which waited for: 12 -> 10; matrix products, arithmetic and copies ran while one was open for 0% -> 0% of each run, Pallas kernels for 0% -> 0%
where the time goes in v2:
time: 88.3 us; the launch traced here: 87.9 us
  starting transfers between devices  39.5 us (45%)
  waiting for transfers between devices  18 us (20%)
  Pallas kernels  14.5 us (16%)
  blocking collectives  10 us (11%)
  local copies, waits for them, and re-layouts  5.08 us (6%)
    ppermute x28, starting transfers between devices, permute(): return lax.ppermute(values, ('gx', 'gy'), pairs)  33 us
    ppermute x28, waiting for transfers between devices, permute(): return lax.ppermute(values, ('gx', 'gy'), pairs)  16.6 us
    pallas_call x10, Pallas kernels, call(): pl.pallas_call(kernel, out_shape=outs, in_specs=specs, out_specs=[VMEM] *...  14.5 us
    all_to_all x1, blocking collectives, spread(): return lax.all_to_all(values, ('gx', 'gy'), 0, 0)  10 us
    all_to_all x2, starting transfers between devices, spread(): return lax.all_to_all(values, ('gx', 'gy'), 0, 0)  6.52 us
    unnamed x28, local copies, waits for them, and re-layouts  5.08 us
  transfers between devices with their start and end apart: 30, of which 10 were waited for; matrix products, arithmetic and copies ran while one was open for 0% of the time, Pallas kernels for 0%

profile of v2, /device:TPU:0, one launch (start us, length us, event | category | flops | bytes accessed | tf_op | source)
XLA Modules:
  0.0 87.9 jit_solution(12689359911622795348)
XLA Ops:
  0.6 0.0 copy-start.4
  0.6 0.1 pad_add_fusion.pos
  0.7 0.6 copy-done.4
  1.4 0.0 copy-done.11
  1.4 0.0 copy-done.12
  1.4 0.0 copy-done.13
  1.4 0.9 %copy-done.5 = f32[64,512]{1,0:T(8,128)S(1)} copy-done((f32[64,512]{1,0:T(8,128)S(1)}, f32[64,512]{1,0:T(8,128)}, u32[]{:S(2)}) %copy-start.5) | copy-done | bytes 131096
  2.3 0.9 %copy-done.7 = f32[8,8,512]{2,1,0:T(8,128)S(1)} copy-done((f32[8,8,512]{2,1,0:T(8,128)S(1)}, f32[8,8,512]{2,1,0:T(8,128)}, u32[]{:S(2)}) %copy-start.7) | copy-done | bytes 131096
  3.2 0.9 %copy-done.8 = f32[8,8,512]{2,1,0:T(8,128)S(1)} copy-done((f32[8,8,512]{2,1,0:T(8,128)S(1)}, f32[8,8,512]{2,1,0:T(8,128)}, u32[]{:S(2)}) %copy-start.8) | copy-done | bytes 131096
  4.1 0.9 %copy-done.9 = f32[64,512]{1,0:T(8,128)S(1)} copy-done((f32[64,512]{1,0:T(8,128)S(1)}, f32[64,512]{1,0:T(8,128)}, u32[]{:S(2)}) %copy-start.9) | copy-done | bytes 131096
  5.0 0.8 copy-done.10
  5.8 1.0 %shard_map.140 = (f32[64,512]{1,0:T(8,128)S(1)}, f32[64,512]{1,0:T(8,128)S(1)}, f32[64,512]{1,0:T(8,128)S(1)}, f32[24,512]{1,0:T(8,128)S(1)}, f32[24,512]{1,0:T(8,128)S(1)}) custom-call(s32[2]{0:T(128)S(1)} %pad_add_fusion.pos, f32[4]{0:T(128)S(1)} %copy-done.11, f32[64,512]{1,0:T(8,128)S(1)} %bitcast.8, f32[64,512]{1,0:T(8,128)S(1)} %bitcast.9, ...), custom_call_target="tpu_custom_call" | custom-call | tf_op jit(solution)/shard_map/pallas_call | solution.py:392
  6.8 0.0 copy-start
  6.8 0.5 collective-permute-start
  7.3 3.6 %collective-permute-start.1 = (f32[24,512]{1,0:T(8,128)S(1)}, f32[24,512]{1,0:T(8,128)S(1)}, u32[]{:S(2)}, u32[]{:S(2)}) collective-permute-start(f32[24,512]{1,0:T(8,128)S(1)} %get-tuple-element.75), channel_id=1, source_target_pairs={{0,7},{1,2},{2,1},{3,4},{4,3},{5,6},{6,5},{7,0},{8,15},{9,10},{10,... | collective-permute-start | bytes 147464 | tf_op jit(solution)/shard_map/ppermute | solution.py:401
  10.9 1.8 %collective-permute-done.1.odd = f32[24,512]{1,0:T(8,128)S(1)} collective-permute-done((f32[24,512]{1,0:T(8,128)S(1)}, f32[24,512]{1,0:T(8,128)S(1)}, u32[]{:S(2)}, u32[]{:S(2)}) %collective-permute-start.1) | collective-permute-done | bytes 49184 | tf_op jit(solution)/shard_map/ppermute | solution.py:401
  12.6 0.6 shard_map.141
  13.3 1.8 %collective-permute-start.2 = (f32[32,512]{1,0:T(8,128)S(1)}, f32[32,512]{1,0:T(8,128)S(1)}, u32[]{:S(2)}, u32[]{:S(2)}) collective-permute-start(f32[32,512]{1,0:T(8,128)S(1)} %get-tuple-element.79), channel_id=1, source_target_pairs={{0,8},{1,9},{2,10},{3,11},{4,12},{5,13},{6,14},{7,15},{8,0},{9,1},... | collective-permute-start | bytes 196616 | tf_op jit(solution)/shard_map/ppermute | solution.py:401
  15.1 2.5 %collective-permute-done.2.even = f32[32,512]{1,0:T(8,128)S(1)} collective-permute-done((f32[32,512]{1,0:T(8,128)S(1)}, f32[32,512]{1,0:T(8,128)S(1)}, u32[]{:S(2)}, u32[]{:S(2)}) %collective-permute-start.2) | collective-permute-done | bytes 65568 | tf_op jit(solution)/shard_map/ppermute | solution.py:401
  17.6 1.7 %shard_map.142 = (f32[64,512]{1,0:T(8,128)S(1)}, f32[64,512]{1,0:T(8,128)S(1)}, f32[64,512]{1,0:T(8,128)S(1)}, f32[64,512]{1,0:T(8,128)S(1)}, f32[64,512]{1,0:T(...) custom-call(s32[2]{0:T(128)S(1)} %pad_add_fusion.pos, ...), custom_call_target="tpu_custom_call" | custom-call | tf_op jit(solution)/shard_map/pallas_call | solution.py:392
  19.3 2.9 %collective-permute-start.4 = (f32[8,512]{1,0:T(8,128)S(1)}, f32[8,512]{1,0:T(8,128)S(1)}, u32[]{:S(2)}, u32[]{:S(2)}) collective-permute-start(f32[8,512]{1,0:T(8,128)S(1)} %get-tuple-element.83), channel_id=1, source_target_pairs={{0,8},{1,9},{2,10},{3,11},{4,12},{5,13},{6,14},{7,15},{8,0},{9,1},... | collective-permute-start | bytes 49160 | tf_op jit(solution)/shard_map/ppermute | solution.py:401
  22.2 0.5 collective-permute-start.6
  22.7 1.6 %collective-permute-start.7 = (f32[8,512]{1,0:T(8,128)S(1)}, f32[8,512]{1,0:T(8,128)S(1)}, u32[]{:S(2)}, u32[]{:S(2)}) collective-permute-start(f32[8,512]{1,0:T(8,128)S(1)} %get-tuple-element.86), channel_id=1, source_target_pairs={{0,7},{1,2},{2,1},{3,4},{4,3},{5,6},{6,5},{7,0},{8,15},{9,10},{10,... | collective-permute-start | bytes 49160 | tf_op jit(solution)/shard_map/ppermute | solution.py:401
  24.3 0.0 collective-permute-done.5.refs_1_
  24.3 0.0 collective-permute-done.6.refs_2_
  24.3 2.5 %collective-permute-done.7.refs_3_ = f32[8,512]{1,0:T(8,128)S(1)} collective-permute-done((f32[8,512]{1,0:T(8,128)S(1)}, f32[8,512]{1,0:T(8,128)S(1)}, u32[]{:S(2)}, u32[]{:S(2)}) %collective-permute-start.7) | collective-permute-done | bytes 16416 | tf_op jit(solution)/shard_map/ppermute | solution.py:401
  26.8 1.5 %shard_map.143 = (f32[64,512]{1,0:T(8,128)S(1)}, f32[64,512]{1,0:T(8,128)S(1)}, f32[8,512]{1,0:T(8,128)S(1)}, f32[8,512]{1,0:T(8,128)S(1)}, f32[8,512]{1,0:T(8,128)S(1)}, /*index=5*/f32[8,512]{1,0:T(8,128)S(1)}) custom-call(s32[2]{0:T(128)S(1)} %pad_add_fusion.pos, f32[64,512]{1,0:T(8,128)S(1)} %get-tuple-element.82.q, ...), custom_call_target="tpu_custom_call" | custom-call | tf_op jit(solution)/shard_map/pallas_call | solution.py:392
  28.3 1.7 %collective-permute-start.8 = (f32[8,512]{1,0:T(8,128)S(1)}, f32[8,512]{1,0:T(8,128)S(1)}, u32[]{:S(2)}, u32[]{:S(2)}) collective-permute-start(f32[8,512]{1,0:T(8,128)S(1)} %get-tuple-element.95), channel_id=1, source_target_pairs={{0,8},{1,9},{2,10},{3,11},{4,12},{5,13},{6,14},{7,15},{8,0},{9,1},... | collective-permute-start | bytes 49160 | tf_op jit(solution)/shard_map/ppermute | solution.py:401
  30.0 0.5 collective-permute-start.10
  30.5 2.0 %collective-permute-start.11 = (f32[8,512]{1,0:T(8,128)S(1)}, f32[8,512]{1,0:T(8,128)S(1)}, u32[]{:S(2)}, u32[]{:S(2)}) collective-permute-start(f32[8,512]{1,0:T(8,128)S(1)} %get-tuple-element.98), channel_id=1, source_target_pairs={{0,7},{1,2},{2,1},{3,4},{4,3},{5,6},{6,5},{7,0},{8,15},{9,10},{10,... | collective-permute-start | bytes 49160 | tf_op jit(solution)/shard_map/ppermute | solution.py:401
  32.5 0.0 collective-permute-done.8.refs_0_
  32.5 0.0 collective-permute-done.9.refs_1_
  32.5 0.0 collective-permute-done.10.refs_2_
  32.5 2.1 %collective-permute-done.11.refs_3_ = f32[8,512]{1,0:T(8,128)S(1)} collective-permute-done((f32[8,512]{1,0:T(8,128)S(1)}, f32[8,512]{1,0:T(8,128)S(1)}, u32[]{:S(2)}, u32[]{:S(2)}) %collective-permute-start.11) | collective-permute-done | bytes 16416 | tf_op jit(solution)/shard_map/ppermute | solution.py:401
  34.5 2.0 %shard_map.144 = (f32[64,512]{1,0:T(8,128)S(1)}, f32[32,1,128]{2,1,0:T(1,128)}, f32[64,512]{1,0:T(8,128)S(1)}, f32[8,512]{1,0:T(8,128)S(1)}, f32[8,512]{1,0:T(8,...) custom-call(s32[2]{0:T(128)S(1)} %pad_add_fusion.pos, f32[64,512]{1,0:T(8,128)S(1)} %get-tuple-element.81.b.refs_4_, ...), custom_call_target="tpu_custom_call" | custom-call | tf_op jit(solution)/shard_map/pallas_call | solution.py:392
  36.6 3.4 %all-to-all-start = ((f32[32,1,128]{2,1,0:T(1,128)}), f32[32,1,128]{2,1,0:T(1,128)S(1)}, u32[]{:S(2)}, u32[]{:S(2)}) async-start(f32[32,1,128]{2,1,0:T(1,128)} %get-tuple-element.99), calls=%async_computation | async-start | bytes 32768 | tf_op jit(solution)/shard_map/all_to_all | solution.py:414
  40.0 1.8 %collective-permute-start.12 = (f32[8,512]{1,0:T(8,128)S(1)}, f32[8,512]{1,0:T(8,128)S(1)}, u32[]{:S(2)}, u32[]{:S(2)}) collective-permute-start(f32[8,512]{1,0:T(8,128)S(1)} %get-tuple-element.101), channel_id=1, source_target_pairs={{0,8},{1,9},{2,10},{3,11},{4,12},{5,13},{6,14},{7,15},{8,0},{9,1},... | collective-permute-start | bytes 49160 | tf_op jit(solution)/shard_map/ppermute | solution.py:401
  41.9 0.5 collective-permute-start.14
  42.4 2.0 %collective-permute-start.15 = (f32[8,512]{1,0:T(8,128)S(1)}, f32[8,512]{1,0:T(8,128)S(1)}, u32[]{:S(2)}, u32[]{:S(2)}) collective-permute-start(f32[8,512]{1,0:T(8,128)S(1)} %get-tuple-element.104), channel_id=1, source_target_pairs={{0,7},{1,2},{2,1},{3,4},{4,3},{5,6},{6,5},{7,0},{8,15},{9,10},{10,... | collective-permute-start | bytes 49160 | tf_op jit(solution)/shard_map/ppermute | solution.py:401
  44.4 2.1 %collective-permute-done.15.refs_3_ = f32[8,512]{1,0:T(8,128)S(1)} collective-permute-done((f32[8,512]{1,0:T(8,128)S(1)}, f32[8,512]{1,0:T(8,128)S(1)}, u32[]{:S(2)}, u32[]{:S(2)}) %collective-permute-start.15) | collective-permute-done | bytes 16416 | tf_op jit(solution)/shard_map/ppermute | solution.py:401
  46.4 0.7 all-to-all-done.gathered
  47.1 1.6 %shard_map.145 = (f32[64,512]{1,0:T(8,128)S(1)}, f32[64,512]{1,0:T(8,128)S(1)}, f32[64,512]{1,0:T(8,128)S(1)}, f32[64,512]{1,0:T(8,128)S(1)}, f32[64,512]{1,0:T(...) custom-call(s32[2]{0:T(128)S(1)} %pad_add_fusion.pos, ...), custom_call_target="tpu_custom_call" | custom-call | tf_op jit(solution)/shard_map/pallas_call | solution.py:392
  48.8 1.9 %collective-permute-start.16 = (f32[8,512]{1,0:T(8,128)S(1)}, f32[8,512]{1,0:T(8,128)S(1)}, u32[]{:S(2)}, u32[]{:S(2)}) collective-permute-start(f32[8,512]{1,0:T(8,128)S(1)} %get-tuple-element.111), channel_id=1, source_target_pairs={{0,8},{1,9},{2,10},{3,11},{4,12},{5,13},{6,14},{7,15},{8,0},{9,1},... | collective-permute-start | bytes 49160 | tf_op jit(solution)/shard_map/ppermute | solution.py:401
  50.6 0.5 collective-permute-start.18
  51.1 2.2 %collective-permute-start.19 = (f32[8,512]{1,0:T(8,128)S(1)}, f32[8,512]{1,0:T(8,128)S(1)}, u32[]{:S(2)}, u32[]{:S(2)}) collective-permute-start(f32[8,512]{1,0:T(8,128)S(1)} %get-tuple-element.114), channel_id=1, source_target_pairs={{0,7},{1,2},{2,1},{3,4},{4,3},{5,6},{6,5},{7,0},{8,15},{9,10},{10,... | collective-permute-start | bytes 49160 | tf_op jit(solution)/shard_map/ppermute | solution.py:401
  53.4 1.8 %collective-permute-done.19.refs_3_ = f32[8,512]{1,0:T(8,128)S(1)} collective-permute-done((f32[8,512]{1,0:T(8,128)S(1)}, f32[8,512]{1,0:T(8,128)S(1)}, u32[]{:S(2)}, u32[]{:S(2)}) %collective-permute-start.19) | collective-permute-done | bytes 16416 | tf_op jit(solution)/shard_map/ppermute | solution.py:401
  55.2 2.1 %shard_map.146 = (f32[64,512]{1,0:T(8,128)S(1)}, f32[64,512]{1,0:T(8,128)S(1)}, f32[32,1,128]{2,1,0:T(1,128)}, f32[64,512]{1,0:T(8,128)S(1)}, f32[8,512]{1,0:T(8...) custom-call(s32[2]{0:T(128)S(1)} %pad_add_fusion.pos, ...), custom_call_target="tpu_custom_call" | custom-call | tf_op jit(solution)/shard_map/pallas_call | solution.py:392
  57.3 3.1 %all-to-all-start.1 = ((f32[32,1,128]{2,1,0:T(1,128)}), f32[32,1,128]{2,1,0:T(1,128)S(1)}, u32[]{:S(2)}, u32[]{:S(2)}) async-start(f32[32,1,128]{2,1,0:T(1,128)} %get-tuple-element.115), calls=%async_computation.1 | async-start | bytes 32768 | tf_op jit(solution)/shard_map/all_to_all | solution.py:414
  60.4 1.8 %collective-permute-start.20 = (f32[8,512]{1,0:T(8,128)S(1)}, f32[8,512]{1,0:T(8,128)S(1)}, u32[]{:S(2)}, u32[]{:S(2)}) collective-permute-start(f32[8,512]{1,0:T(8,128)S(1)} %get-tuple-element.117), channel_id=1, source_target_pairs={{0,8},{1,9},{2,10},{3,11},{4,12},{5,13},{6,14},{7,15},{8,0},{9,1},... | collective-permute-start | bytes 49160 | tf_op jit(solution)/shard_map/ppermute | solution.py:401
  62.2 0.0 collective-permute-start.21
  62.2 0.5 collective-permute-start.22
  62.8 2.0 %collective-permute-start.23 = (f32[8,512]{1,0:T(8,128)S(1)}, f32[8,512]{1,0:T(8,128)S(1)}, u32[]{:S(2)}, u32[]{:S(2)}) collective-permute-start(f32[8,512]{1,0:T(8,128)S(1)} %get-tuple-element.120), channel_id=1, source_target_pairs={{0,7},{1,2},{2,1},{3,4},{4,3},{5,6},{6,5},{7,0},{8,15},{9,10},{10,... | collective-permute-start | bytes 49160 | tf_op jit(solution)/shard_map/ppermute | solution.py:401
  64.7 0.0 collective-permute-done.20.refs_0_
  64.7 0.0 collective-permute-done.21.refs_1_
  64.7 2.1 %collective-permute-done.23.refs_3_ = f32[8,512]{1,0:T(8,128)S(1)} collective-permute-done((f32[8,512]{1,0:T(8,128)S(1)}, f32[8,512]{1,0:T(8,128)S(1)}, u32[]{:S(2)}, u32[]{:S(2)}) %collective-permute-start.23) | collective-permute-done | bytes 16416 | tf_op jit(solution)/shard_map/ppermute | solution.py:401
  66.8 0.7 all-to-all-done.1.gathered
  67.5 1.6 %shard_map.147 = (f32[64,512]{1,0:T(8,128)S(1)}, f32[64,512]{1,0:T(8,128)S(1)}, f32[64,512]{1,0:T(8,128)S(1)}, f32[64,512]{1,0:T(8,128)S(1)}, f32[64,512]{1,0:T(...) custom-call(s32[2]{0:T(128)S(1)} %pad_add_fusion.pos, ...), custom_call_target="tpu_custom_call" | custom-call | tf_op jit(solution)/shard_map/pallas_call | solution.py:392
  69.1 1.9 %collective-permute-start.24 = (f32[8,512]{1,0:T(8,128)S(1)}, f32[8,512]{1,0:T(8,128)S(1)}, u32[]{:S(2)}, u32[]{:S(2)}) collective-permute-start(f32[8,512]{1,0:T(8,128)S(1)} %get-tuple-element.130), channel_id=1, source_target_pairs={{0,8},{1,9},{2,10},{3,11},{4,12},{5,13},{6,14},{7,15},{8,0},{9,1},... | collective-permute-start | bytes 49160 | tf_op jit(solution)/shard_map/ppermute | solution.py:401
  71.0 0.5 collective-permute-start.26
  71.5 2.2 %collective-permute-start.27 = (f32[8,512]{1,0:T(8,128)S(1)}, f32[8,512]{1,0:T(8,128)S(1)}, u32[]{:S(2)}, u32[]{:S(2)}) collective-permute-start(f32[8,512]{1,0:T(8,128)S(1)} %get-tuple-element.133), channel_id=1, source_target_pairs={{0,7},{1,2},{2,1},{3,4},{4,3},{5,6},{6,5},{7,0},{8,15},{9,10},{10,... | collective-permute-start | bytes 49160 | tf_op jit(solution)/shard_map/ppermute | solution.py:401
  73.8 1.8 %collective-permute-done.27.refs_3_ = f32[8,512]{1,0:T(8,128)S(1)} collective-permute-done((f32[8,512]{1,0:T(8,128)S(1)}, f32[8,512]{1,0:T(8,128)S(1)}, u32[]{:S(2)}, u32[]{:S(2)}) %collective-permute-start.27) | collective-permute-done | bytes 16416 | tf_op jit(solution)/shard_map/ppermute | solution.py:401
  75.6 1.4 %shard_map.148 = (f32[64,512]{1,0:T(8,128)}, f32[64,512]{1,0:T(8,128)S(1)}, f32[32,1,128]{2,1,0:T(1,128)S(1)}) custom-call(s32[2]{0:T(128)S(1)} %pad_add_fusion.pos, f32[64,512]{1,0:T(8,128)S(1)} %get-tuple-element.81.b.refs_4_, f32[64,512]{1,0:T(8,128)S(1)} %get-tuple-element.125.r, f32[64,512]{1,0:T(8,128)S(1)} %get-tuple-element.126.s, ...), custom_call_target="tpu_custom_call" | custom-call | tf_op jit(solution)/shard_map/pallas_call | solution.py:392
  77.0 10.0 %all_to_all.15.gathered = f32[32,1,128]{2,1,0:T(1,128)S(1)} all-to-all(f32[32,1,128]{2,1,0:T(1,128)S(1)} %get-tuple-element.134), channel_id=1, replica_groups=mesh['gx'=4,'gy'=8] {'gx','gy'}, dimensions={0} | all-to-all | bytes 32768 | tf_op jit(solution)/shard_map/all_to_all | solution.py:414
  87.0 0.9 shard_map.149
  (36 shorter events, 0.1 us)
Async XLA Ops:
  0.6 0.7 copy-start.4
  0.7 0.7 copy-start.11
  0.7 0.7 copy-start.12
  0.7 0.7 copy-start.13
  1.4 0.9 %copy-start.5 = (f32[64,512]{1,0:T(8,128)S(1)}, f32[64,512]{1,0:T(8,128)}, u32[]{:S(2)}) copy-start(f32[64,512]{1,0:T(8,128)} %constant.29.clone.weights) | copy-start | bytes 393220
  2.3 0.9 %copy-start.7 = (f32[8,8,512]{2,1,0:T(8,128)S(1)}, f32[8,8,512]{2,1,0:T(8,128)}, u32[]{:S(2)}) copy-start(f32[8,8,512]{2,1,0:T(8,128)} %param.13) | copy-start | bytes 393220
  3.2 0.9 %copy-start.8 = (f32[8,8,512]{2,1,0:T(8,128)S(1)}, f32[8,8,512]{2,1,0:T(8,128)}, u32[]{:S(2)}) copy-start(f32[8,8,512]{2,1,0:T(8,128)} %param.14) | copy-start | bytes 393220
  4.1 0.9 %copy-start.9 = (f32[64,512]{1,0:T(8,128)S(1)}, f32[64,512]{1,0:T(8,128)}, u32[]{:S(2)}) copy-start(f32[64,512]{1,0:T(8,128)} %constant.31.clone.spread) | copy-start | bytes 393220
  5.0 0.8 copy-start.10
  5.8 11.8 %copy-start.1 = (f32[256,256]{1,0:T(8,128)S(1)}, f32[256,256]{1,0:T(8,128)}, u32[]{:S(2)}) copy-start(f32[256,256]{1,0:T(8,128)} %constant.26.clone.refs_2_.refs_11_.refs_14_.refs_18_) | copy-start | bytes 786436
  6.8 10.8 %copy-start = (f32[256,256]{1,0:T(8,128)S(1)}, f32[256,256]{1,0:T(8,128)}, u32[]{:S(2)}) copy-start(f32[256,256]{1,0:T(8,128)} %constant.27.clone.refs_3_.refs_12_.refs_15_.refs_19_) | copy-start | bytes 786436
  6.8 4.1 %collective-permute-start = (f32[24,512]{1,0:T(8,128)S(1)}, f32[24,512]{1,0:T(8,128)S(1)}, u32[]{:S(2)}, u32[]{:S(2)}) collective-permute-start(f32[24,512]{1,0:T(8,128)S(1)} %get-tuple-element.74), channel_id=1, source_target_pairs={{0,1},{1,0},{2,3},{3,2},{4,5},{5,4},{6,7},{7,6},{8,9},{9,8},{10,11... | collective-permute-start | bytes 147464 | tf_op jit(solution)/shard_map/ppermute | solution.py:401
  7.3 5.3 %collective-permute-start.1 = (f32[24,512]{1,0:T(8,128)S(1)}, f32[24,512]{1,0:T(8,128)S(1)}, u32[]{:S(2)}, u32[]{:S(2)}) collective-permute-start(f32[24,512]{1,0:T(8,128)S(1)} %get-tuple-element.75), channel_id=1, source_target_pairs={{0,7},{1,2},{2,1},{3,4},{4,3},{5,6},{6,5},{7,0},{8,15},{9,10},{10,... | collective-permute-start | bytes 147464 | tf_op jit(solution)/shard_map/ppermute | solution.py:401
  12.6 5.0 %copy-start.2 = (f32[128,64]{1,0:T(8,128)S(1)}, f32[128,64]{1,0:T(8,128)}, u32[]{:S(2)}) copy-start(f32[128,64]{1,0:T(8,128)} %constant.24.clone.refs_0_.refs_9_.refs_12_.refs_16_) | copy-start | bytes 98308
  12.6 5.0 %copy-start.3 = (f32[96,128]{1,0:T(8,128)S(1)}, f32[96,128]{1,0:T(8,128)}, u32[]{:S(2)}) copy-start(f32[96,128]{1,0:T(8,128)} %constant.25.clone.refs_1_.refs_10_.refs_13_.refs_17_) | copy-start | bytes 147460
  12.6 5.0 %copy-start.6 = (f32[64,512]{1,0:T(8,128)S(1)}, f32[64,512]{1,0:T(8,128)}, u32[]{:S(2)}) copy-start(f32[64,512]{1,0:T(8,128)} %constant.29.clone.weights) | copy-start | bytes 393220
  13.3 4.3 %collective-permute-start.2 = (f32[32,512]{1,0:T(8,128)S(1)}, f32[32,512]{1,0:T(8,128)S(1)}, u32[]{:S(2)}, u32[]{:S(2)}) collective-permute-start(f32[32,512]{1,0:T(8,128)S(1)} %get-tuple-element.79), channel_id=1, source_target_pairs={{0,8},{1,9},{2,10},{3,11},{4,12},{5,13},{6,14},{7,15},{8,0},{9,1},... | collective-permute-start | bytes 196616 | tf_op jit(solution)/shard_map/ppermute | solution.py:401
  15.1 2.5 %collective-permute-start.3 = (f32[32,512]{1,0:T(8,128)S(1)}, f32[32,512]{1,0:T(8,128)S(1)}, u32[]{:S(2)}, u32[]{:S(2)}) collective-permute-start(f32[32,512]{1,0:T(8,128)S(1)} %get-tuple-element.80), channel_id=1, source_target_pairs={{0,1},{1,0},{2,3},{3,2},{4,5},{5,4},{6,7},{7,6},{8,16},{9,17},{10,... | collective-permute-start | bytes 196616 | tf_op jit(solution)/shard_map/ppermute | solution.py:401
  19.3 5.0 %collective-permute-start.4 = (f32[8,512]{1,0:T(8,128)S(1)}, f32[8,512]{1,0:T(8,128)S(1)}, u32[]{:S(2)}, u32[]{:S(2)}) collective-permute-start(f32[8,512]{1,0:T(8,128)S(1)} %get-tuple-element.83), channel_id=1, source_target_pairs={{0,8},{1,9},{2,10},{3,11},{4,12},{5,13},{6,14},{7,15},{8,0},{9,1},... | collective-permute-start | bytes 49160 | tf_op jit(solution)/shard_map/ppermute | solution.py:401
  22.2 2.1 %collective-permute-start.5 = (f32[8,512]{1,0:T(8,128)S(1)}, f32[8,512]{1,0:T(8,128)S(1)}, u32[]{:S(2)}, u32[]{:S(2)}) collective-permute-start(f32[8,512]{1,0:T(8,128)S(1)} %get-tuple-element.84), channel_id=1, source_target_pairs={{0,1},{1,0},{2,3},{3,2},{4,5},{5,4},{6,7},{7,6},{8,16},{9,17},{10,... | collective-permute-start | bytes 49160 | tf_op jit(solution)/shard_map/ppermute | solution.py:401
  22.2 2.1 %collective-permute-start.6 = (f32[8,512]{1,0:T(8,128)S(1)}, f32[8,512]{1,0:T(8,128)S(1)}, u32[]{:S(2)}, u32[]{:S(2)}) collective-permute-start(f32[8,512]{1,0:T(8,128)S(1)} %get-tuple-element.85), channel_id=1, source_target_pairs={{0,1},{1,0},{2,3},{3,2},{4,5},{5,4},{6,7},{7,6},{8,9},{9,8},{10,11... | collective-permute-start | bytes 49160 | tf_op jit(solution)/shard_map/ppermute | solution.py:401
  22.7 4.1 %collective-permute-start.7 = (f32[8,512]{1,0:T(8,128)S(1)}, f32[8,512]{1,0:T(8,128)S(1)}, u32[]{:S(2)}, u32[]{:S(2)}) collective-permute-start(f32[8,512]{1,0:T(8,128)S(1)} %get-tuple-element.86), channel_id=1, source_target_pairs={{0,7},{1,2},{2,1},{3,4},{4,3},{5,6},{6,5},{7,0},{8,15},{9,10},{10,... | collective-permute-start | bytes 49160 | tf_op jit(solution)/shard_map/ppermute | solution.py:401
  28.3 4.2 %collective-permute-start.8 = (f32[8,512]{1,0:T(8,128)S(1)}, f32[8,512]{1,0:T(8,128)S(1)}, u32[]{:S(2)}, u32[]{:S(2)}) collective-permute-start(f32[8,512]{1,0:T(8,128)S(1)} %get-tuple-element.95), channel_id=1, source_target_pairs={{0,8},{1,9},{2,10},{3,11},{4,12},{5,13},{6,14},{7,15},{8,0},{9,1},... | collective-permute-start | bytes 49160 | tf_op jit(solution)/shard_map/ppermute | solution.py:401
  30.0 2.5 %collective-permute-start.9 = (f32[8,512]{1,0:T(8,128)S(1)}, f32[8,512]{1,0:T(8,128)S(1)}, u32[]{:S(2)}, u32[]{:S(2)}) collective-permute-start(f32[8,512]{1,0:T(8,128)S(1)} %get-tuple-element.96), channel_id=1, source_target_pairs={{0,1},{1,0},{2,3},{3,2},{4,5},{5,4},{6,7},{7,6},{8,16},{9,17},{10,... | collective-permute-start | bytes 49160 | tf_op jit(solution)/shard_map/ppermute | solution.py:401
  30.0 2.5 %collective-permute-start.10 = (f32[8,512]{1,0:T(8,128)S(1)}, f32[8,512]{1,0:T(8,128)S(1)}, u32[]{:S(2)}, u32[]{:S(2)}) collective-permute-start(f32[8,512]{1,0:T(8,128)S(1)} %get-tuple-element.97), channel_id=1, source_target_pairs={{0,1},{1,0},{2,3},{3,2},{4,5},{5,4},{6,7},{7,6},{8,9},{9,8},{10,11... | collective-permute-start | bytes 49160 | tf_op jit(solution)/shard_map/ppermute | solution.py:401
  30.5 4.1 %collective-permute-start.11 = (f32[8,512]{1,0:T(8,128)S(1)}, f32[8,512]{1,0:T(8,128)S(1)}, u32[]{:S(2)}, u32[]{:S(2)}) collective-permute-start(f32[8,512]{1,0:T(8,128)S(1)} %get-tuple-element.98), channel_id=1, source_target_pairs={{0,7},{1,2},{2,1},{3,4},{4,3},{5,6},{6,5},{7,0},{8,15},{9,10},{10,... | collective-permute-start | bytes 49160 | tf_op jit(solution)/shard_map/ppermute | solution.py:401
  36.6 10.5 %all-to-all-start = ((f32[32,1,128]{2,1,0:T(1,128)}), f32[32,1,128]{2,1,0:T(1,128)S(1)}, u32[]{:S(2)}, u32[]{:S(2)}) async-start(f32[32,1,128]{2,1,0:T(1,128)} %get-tuple-element.99), calls=%async_computation | async-start | bytes 32768 | tf_op jit(solution)/shard_map/all_to_all | solution.py:414
  40.0 4.3 %collective-permute-start.12 = (f32[8,512]{1,0:T(8,128)S(1)}, f32[8,512]{1,0:T(8,128)S(1)}, u32[]{:S(2)}, u32[]{:S(2)}) collective-permute-start(f32[8,512]{1,0:T(8,128)S(1)} %get-tuple-element.101), channel_id=1, source_target_pairs={{0,8},{1,9},{2,10},{3,11},{4,12},{5,13},{6,14},{7,15},{8,0},{9,1},... | collective-permute-start | bytes 49160 | tf_op jit(solution)/shard_map/ppermute | solution.py:401
  41.9 2.5 %collective-permute-start.13 = (f32[8,512]{1,0:T(8,128)S(1)}, f32[8,512]{1,0:T(8,128)S(1)}, u32[]{:S(2)}, u32[]{:S(2)}) collective-permute-start(f32[8,512]{1,0:T(8,128)S(1)} %get-tuple-element.102), channel_id=1, source_target_pairs={{0,1},{1,0},{2,3},{3,2},{4,5},{5,4},{6,7},{7,6},{8,16},{9,17},{10,... | collective-permute-start | bytes 49160 | tf_op jit(solution)/shard_map/ppermute | solution.py:401
  41.9 2.5 %collective-permute-start.14 = (f32[8,512]{1,0:T(8,128)S(1)}, f32[8,512]{1,0:T(8,128)S(1)}, u32[]{:S(2)}, u32[]{:S(2)}) collective-permute-start(f32[8,512]{1,0:T(8,128)S(1)} %get-tuple-element.103), channel_id=1, source_target_pairs={{0,1},{1,0},{2,3},{3,2},{4,5},{5,4},{6,7},{7,6},{8,9},{9,8},{10,11... | collective-permute-start | bytes 49160 | tf_op jit(solution)/shard_map/ppermute | solution.py:401
  42.4 4.1 %collective-permute-start.15 = (f32[8,512]{1,0:T(8,128)S(1)}, f32[8,512]{1,0:T(8,128)S(1)}, u32[]{:S(2)}, u32[]{:S(2)}) collective-permute-start(f32[8,512]{1,0:T(8,128)S(1)} %get-tuple-element.104), channel_id=1, source_target_pairs={{0,7},{1,2},{2,1},{3,4},{4,3},{5,6},{6,5},{7,0},{8,15},{9,10},{10,... | collective-permute-start | bytes 49160 | tf_op jit(solution)/shard_map/ppermute | solution.py:401
  48.8 4.6 %collective-permute-start.16 = (f32[8,512]{1,0:T(8,128)S(1)}, f32[8,512]{1,0:T(8,128)S(1)}, u32[]{:S(2)}, u32[]{:S(2)}) collective-permute-start(f32[8,512]{1,0:T(8,128)S(1)} %get-tuple-element.111), channel_id=1, source_target_pairs={{0,8},{1,9},{2,10},{3,11},{4,12},{5,13},{6,14},{7,15},{8,0},{9,1},... | collective-permute-start | bytes 49160 | tf_op jit(solution)/shard_map/ppermute | solution.py:401
  50.6 2.8 %collective-permute-start.17 = (f32[8,512]{1,0:T(8,128)S(1)}, f32[8,512]{1,0:T(8,128)S(1)}, u32[]{:S(2)}, u32[]{:S(2)}) collective-permute-start(f32[8,512]{1,0:T(8,128)S(1)} %get-tuple-element.112), channel_id=1, source_target_pairs={{0,1},{1,0},{2,3},{3,2},{4,5},{5,4},{6,7},{7,6},{8,16},{9,17},{10,... | collective-permute-start | bytes 49160 | tf_op jit(solution)/shard_map/ppermute | solution.py:401
  50.6 2.8 %collective-permute-start.18 = (f32[8,512]{1,0:T(8,128)S(1)}, f32[8,512]{1,0:T(8,128)S(1)}, u32[]{:S(2)}, u32[]{:S(2)}) collective-permute-start(f32[8,512]{1,0:T(8,128)S(1)} %get-tuple-element.113), channel_id=1, source_target_pairs={{0,1},{1,0},{2,3},{3,2},{4,5},{5,4},{6,7},{7,6},{8,9},{9,8},{10,11... | collective-permute-start | bytes 49160 | tf_op jit(solution)/shard_map/ppermute | solution.py:401
  51.1 4.1 %collective-permute-start.19 = (f32[8,512]{1,0:T(8,128)S(1)}, f32[8,512]{1,0:T(8,128)S(1)}, u32[]{:S(2)}, u32[]{:S(2)}) collective-permute-start(f32[8,512]{1,0:T(8,128)S(1)} %get-tuple-element.114), channel_id=1, source_target_pairs={{0,7},{1,2},{2,1},{3,4},{4,3},{5,6},{6,5},{7,0},{8,15},{9,10},{10,... | collective-permute-start | bytes 49160 | tf_op jit(solution)/shard_map/ppermute | solution.py:401
  57.3 10.2 %all-to-all-start.1 = ((f32[32,1,128]{2,1,0:T(1,128)}), f32[32,1,128]{2,1,0:T(1,128)S(1)}, u32[]{:S(2)}, u32[]{:S(2)}) async-start(f32[32,1,128]{2,1,0:T(1,128)} %get-tuple-element.115), calls=%async_computation.1 | async-start | bytes 32768 | tf_op jit(solution)/shard_map/all_to_all | solution.py:414
  60.4 4.3 %collective-permute-start.20 = (f32[8,512]{1,0:T(8,128)S(1)}, f32[8,512]{1,0:T(8,128)S(1)}, u32[]{:S(2)}, u32[]{:S(2)}) collective-permute-start(f32[8,512]{1,0:T(8,128)S(1)} %get-tuple-element.117), channel_id=1, source_target_pairs={{0,8},{1,9},{2,10},{3,11},{4,12},{5,13},{6,14},{7,15},{8,0},{9,1},... | collective-permute-start | bytes 49160 | tf_op jit(solution)/shard_map/ppermute | solution.py:401
  62.2 2.5 %collective-permute-start.21 = (f32[8,512]{1,0:T(8,128)S(1)}, f32[8,512]{1,0:T(8,128)S(1)}, u32[]{:S(2)}, u32[]{:S(2)}) collective-permute-start(f32[8,512]{1,0:T(8,128)S(1)} %get-tuple-element.118), channel_id=1, source_target_pairs={{0,1},{1,0},{2,3},{3,2},{4,5},{5,4},{6,7},{7,6},{8,16},{9,17},{10,... | collective-permute-start | bytes 49160 | tf_op jit(solution)/shard_map/ppermute | solution.py:401
  62.2 2.5 %collective-permute-start.22 = (f32[8,512]{1,0:T(8,128)S(1)}, f32[8,512]{1,0:T(8,128)S(1)}, u32[]{:S(2)}, u32[]{:S(2)}) collective-permute-start(f32[8,512]{1,0:T(8,128)S(1)} %get-tuple-element.119), channel_id=1, source_target_pairs={{0,1},{1,0},{2,3},{3,2},{4,5},{5,4},{6,7},{7,6},{8,9},{9,8},{10,11... | collective-permute-start | bytes 49160 | tf_op jit(solution)/shard_map/ppermute | solution.py:401
  62.8 4.1 %collective-permute-start.23 = (f32[8,512]{1,0:T(8,128)S(1)}, f32[8,512]{1,0:T(8,128)S(1)}, u32[]{:S(2)}, u32[]{:S(2)}) collective-permute-start(f32[8,512]{1,0:T(8,128)S(1)} %get-tuple-element.120), channel_id=1, source_target_pairs={{0,7},{1,2},{2,1},{3,4},{4,3},{5,6},{6,5},{7,0},{8,15},{9,10},{10,... | collective-permute-start | bytes 49160 | tf_op jit(solution)/shard_map/ppermute | solution.py:401
  69.1 4.6 %collective-permute-start.24 = (f32[8,512]{1,0:T(8,128)S(1)}, f32[8,512]{1,0:T(8,128)S(1)}, u32[]{:S(2)}, u32[]{:S(2)}) collective-permute-start(f32[8,512]{1,0:T(8,128)S(1)} %get-tuple-element.130), channel_id=1, source_target_pairs={{0,8},{1,9},{2,10},{3,11},{4,12},{5,13},{6,14},{7,15},{8,0},{9,1},... | collective-permute-start | bytes 49160 | tf_op jit(solution)/shard_map/ppermute | solution.py:401
  71.0 2.8 %collective-permute-start.25 = (f32[8,512]{1,0:T(8,128)S(1)}, f32[8,512]{1,0:T(8,128)S(1)}, u32[]{:S(2)}, u32[]{:S(2)}) collective-permute-start(f32[8,512]{1,0:T(8,128)S(1)} %get-tuple-element.131), channel_id=1, source_target_pairs={{0,1},{1,0},{2,3},{3,2},{4,5},{5,4},{6,7},{7,6},{8,16},{9,17},{10,... | collective-permute-start | bytes 49160 | tf_op jit(solution)/shard_map/ppermute | solution.py:401
  71.0 2.8 %collective-permute-start.26 = (f32[8,512]{1,0:T(8,128)S(1)}, f32[8,512]{1,0:T(8,128)S(1)}, u32[]{:S(2)}, u32[]{:S(2)}) collective-permute-start(f32[8,512]{1,0:T(8,128)S(1)} %get-tuple-element.132), channel_id=1, source_target_pairs={{0,1},{1,0},{2,3},{3,2},{4,5},{5,4},{6,7},{7,6},{8,9},{9,8},{10,11... | collective-permute-start | bytes 49160 | tf_op jit(solution)/shard_map/ppermute | solution.py:401
  71.5 4.1 %collective-permute-start.27 = (f32[8,512]{1,0:T(8,128)S(1)}, f32[8,512]{1,0:T(8,128)S(1)}, u32[]{:S(2)}, u32[]{:S(2)}) collective-permute-start(f32[8,512]{1,0:T(8,128)S(1)} %get-tuple-element.133), channel_id=1, source_target_pairs={{0,7},{1,2},{2,1},{3,4},{4,3},{5,6},{6,5},{7,0},{8,15},{9,10},{10,... | collective-permute-start | bytes 49160 | tf_op jit(solution)/shard_map/ppermute | solution.py:401

commit v3 on v2

v3 whole, which is shorter than its diff:
```python
import functools

import jax
import jax.numpy as jnp
import numpy as np
from jax import lax
from jax.experimental import pallas as pl
from jax.experimental.pallas import tpu as pltpu
from jax.sharding import PartitionSpec as P

ITERS = 3
N = 8

gll_points = (
    -1.0,
    -0.8717401485096066,
    -0.5917001814331423,
    -0.2092992179024789,
    0.2092992179024789,
    0.5917001814331423,
    0.8717401485096066,
    1.0,
)
gll_weights = (
    0.03571428571428571,
    0.21070422714350603,
    0.3411226924835044,
    0.4124587946587038,
    0.4124587946587038,
    0.3411226924835044,
    0.21070422714350603,
    0.03571428571428571,
)
mass_coef = 0.2
scan_speed = 2.0
f32 = jnp.float32
VMEM = pl.BlockSpec(memory_space=pltpu.VMEM)
HBM = pl.BlockSpec(memory_space=pl.ANY)
COST = 1 << 20
dot = functools.partial(jnp.dot, precision=lax.Precision.HIGHEST, preferred_element_type=f32)


def lagrange_derivative():
    points = np.array(gll_points)
    barycentric = np.array(
        [1.0 / np.prod([points[j] - points[m] for m in range(N) if m != j]) for j in range(N)]
    )
    derivative = np.zeros((N, N))
    for a in range(N):
        for b in range(N):
            if a != b:
                derivative[a, b] = barycentric[b] / barycentric[a] / (points[a] - points[b])
        derivative[a, a] = -np.sum(derivative[a])
    return derivative.astype(np.float32)


def constants(elems_z):
    group = min(elems_z, 32)
    z_back = np.kron(np.eye(group, dtype=np.float32), lagrange_derivative())
    lane = np.arange(N * elems_z)
    low = (lane % N == 0) & (lane > 0)
    high = (lane % N == N - 1) & (lane < N * elems_z - 1)
    lanes = np.stack([low, high] + [0 * lane] * 6).astype(np.float32)
    return np.ascontiguousarray(z_back.T), z_back, lanes


def weights_1d():
    return [float(np.float32(x)) for x in gll_weights]


def position():
    return lax.axis_index("gx"), lax.axis_index("gy")


def tiles(ref):
    return [ref[N * a : N * a + N, :] for a in range(N)]


def store(ref, values):
    for a in range(N):
        ref[N * a : N * a + N, :] = values[a]


def row_index(shape):
    return lax.broadcasted_iota(jnp.int32, shape, 0)


def along(shape, values, index):
    out = jnp.full(shape, values[0], f32)
    for i in range(1, len(values)):
        out = jnp.where(index == i, values[i], out)
    return out


def fold_z(v, lanes):
    size = v.shape[1]
    return (
        v
        + pltpu.roll(v, 1, axis=1) * lanes[0:1, :]
        + pltpu.roll(v, size - 1, axis=1) * lanes[1:2, :]
    )


def pick(pos, axis, even, odd):
    return jnp.where(pos[axis] % 2 == 0, even, odd)


def send(pos, axis, low, high, even_ref, odd_ref):
    even_ref[...] = pick(pos, axis, high, low)
    odd_ref[...] = pick(pos, axis, low, high)


def received(sizes, pos, axis, even, odd):
    low = jnp.where(pos[axis] > 0, pick(pos, axis, odd, even), 0.0)
    high = jnp.where(pos[axis] < sizes[axis] - 1, pick(pos, axis, even, odd), 0.0)
    return low, high


def place(low, high, a, row):
    return jnp.where(row == 0, low[a : a + 1], jnp.where(row == N - 1, high[a : a + 1], 0.0))


def robin_tiles(sizes, pos, table, flags, classes, size):
    elems_z = flags.shape[1]
    coefficient = jnp.zeros(flags.shape, f32)
    for c in range(table.shape[1]):
        coefficient = jnp.where(classes[...] == c, table[:, c : c + 1], coefficient)
    element = lax.broadcasted_iota(jnp.int32, flags.shape, 1)
    sides = [
        pos[0] == 0, pos[0] == sizes[0] - 1, pos[1] == 0, pos[1] == sizes[1] - 1,
        element == 0, element == elems_z - 1,
    ]
    rows = []
    for bit, side in enumerate(sides):
        flagged = (flags[...] >> bit) % 2 == 1
        rows.append(jnp.where(flagged & side, coefficient, 0.0))
    rows += [jnp.zeros(flags.shape, f32)] * 2
    spread = lax.broadcasted_iota(jnp.int32, (elems_z, size), 1) // N == row_index((elems_z, size))
    faces = dot(jnp.concatenate(rows, 0), spread.astype(f32))
    node = lax.broadcasted_iota(jnp.int32, (1, size), 1) % N
    w = weights_1d()
    w_z = along((1, size), w, node)
    row = row_index((N, size))
    w_b = along((N, size), w, row)
    w_bz = w_b * w_z
    ends_z = jnp.where(node == 0, faces[4:5], 0.0) + jnp.where(node == N - 1, faces[5:6], 0.0)
    common = place(faces[2:3] * w_z, faces[3:4] * w_z, 0, row) + w_b * ends_z
    robin = [w[a] * common for a in range(N)]
    robin[0] += w_bz * faces[0:1]
    robin[N - 1] += w_bz * faces[1:2]
    return robin, w_bz


def field_kernel(sizes, source, k, flags, classes, table, even_out, odd_out,
                 v_ref, k_ref, flags_ref, classes_ref, table_ref, low, high, sems):
    pairs = (
        (flags, flags_ref), (classes, classes_ref), (table, table_ref), (source, v_ref), (k, k_ref),
    )
    copies = [pltpu.make_async_copy(*pair, sems.at[i]) for i, pair in enumerate(pairs)]
    for copy in copies:
        copy.start()
    for copy in copies[:3]:
        copy.wait()
    pos = position()
    robin, w_bz = robin_tiles(sizes, pos, table_ref, flags_ref, classes_ref, source.shape[1])
    for copy in copies[3:]:
        copy.wait()
    w = weights_1d()
    ws = [w[a] * w_bz * v for a, v in enumerate(tiles(v_ref))]
    wk = [w[a] * w_bz * v for a, v in enumerate(tiles(k_ref))]
    for i, field in enumerate((ws, wk, robin)):
        for a in range(N):
            low[N * i + a : N * i + a + 1, :] = field[a][0:1]
            high[N * i + a : N * i + a + 1, :] = field[a][N - 1 : N]
    send(pos, 1, low[...], high[...], even_out, odd_out)


def whole_field_kernel(sizes, source, k, flags, classes, table, ws_out, wk_out, robin_out):
    robin, w_bz = robin_tiles(sizes, position(), table, flags, classes, source.shape[1])
    w = weights_1d()
    store(robin_out, robin)
    store(ws_out, [w[a] * w_bz * v for a, v in enumerate(tiles(source))])
    store(wk_out, [w[a] * w_bz * v for a, v in enumerate(tiles(k))])


def fold_y_kernel(sizes, ws, wk, robin, even, odd, even_out, odd_out):
    pos = position()
    low, high = received(sizes, pos, 1, even[...], odd[...])
    row = row_index((N, ws.shape[1]))
    sides = []
    for a in (0, N - 1):
        part = [
            field[N * a : N * a + N, :] + place(low, high, N * i + a, row)
            for i, field in enumerate((ws, wk, robin))
        ]
        sides.append(jnp.concatenate(part + [wk[N * a : N * a + N, :]], 0))
    send(pos, 0, sides[0], sides[1], even_out, odd_out)


def prepare_kernel(sizes, ws, wk, robin, even, odd, lanes,
                   b_out, kx_out, ky_out, kz_out, advect_out, diagonal_out, inverse_out):
    pos = position()
    low, high = received(sizes, pos, 1, even[...], odd[...])
    shape = (N, ws.shape[1])
    row = row_index(shape)
    w = weights_1d()
    node = lax.broadcasted_iota(jnp.int32, (1, shape[1]), 1) % N
    copies_z = 1.0 + lanes[0:1, :] + lanes[1:2, :]
    shared_y = ((row == 0) & (pos[1] > 0)) | ((row == N - 1) & (pos[1] < sizes[1] - 1))
    copies_yz = jnp.where(shared_y, 2.0, 1.0) * copies_z
    weights_yz = along(shape, w, row) * along((1, shape[1]), w, node) * copies_yz
    inverse_yz = 1.0 / copies_yz
    for a in range(N):
        at = slice(N * a, N * a + N)
        summed = [
            field[at, :] + place(low, high, N * i + a, row) for i, field in enumerate((ws, wk, robin))
        ]
        b_out[at, :] = fold_z(summed[0], lanes)
        kz_out[at, :] = summed[1]
        kx_out[at, :] = fold_z(summed[1], lanes)
        ky_out[at, :] = fold_z(wk[at, :], lanes)
        copies_x = 1.0
        if a == 0:
            copies_x = jnp.where(pos[0] > 0, 2.0, 1.0)
        if a == N - 1:
            copies_x = jnp.where(pos[0] < sizes[0] - 1, 2.0, 1.0)
        weights_a = w[a] * weights_yz
        advect_out[at, :] = scan_speed * weights_a
        diagonal_out[at, :] = fold_z(summed[2], lanes) + mass_coef * copies_x * weights_a
        inverse_out[at, :] = inverse_yz * (1.0 / copies_x)


def contract(m, values):
    half = N // 2
    total = [values[b] + values[N - 1 - b] for b in range(half)]
    apart = [values[b] - values[N - 1 - b] for b in range(half)]
    out = [None] * N
    for a in range(half):
        even = sum(float((m[a][b] + m[a][N - 1 - b]) / 2) * total[b] for b in range(half))
        odd = sum(float((m[a][b] - m[a][N - 1 - b]) / 2) * apart[b] for b in range(half))
        out[a] = even + odd
        out[N - 1 - a] = odd - even
    return out


def rotations(m, row):
    return [along(row.shape, [float(m[b][(b + s) % N]) for b in range(N)], row) for s in range(N)]


def contract_rows(coefs, v):
    out = coefs[0] * v
    for s in range(1, N):
        out += coefs[s] * pltpu.roll(v, N - s, axis=0)
    return out


def operate(pos, v, kx, ky, advect, xy_out, sends, low, high):
    d = lagrange_derivative()
    k, speed = tiles(kx), tiles(advect)
    flux = [k[a] * g - speed[a] * v[a] for a, g in enumerate(contract(d, v))]
    x = contract(d.T, flux)
    send(pos, 0, x[0], x[N - 1], sends[0], sends[1])
    row = row_index(v[0].shape)
    forward, back = rotations(d, row), rotations(d.T, row)
    for a in range(N):
        at = slice(N * a, N * a + N)
        y = contract_rows(back, ky[at, :] * contract_rows(forward, v[a]))
        low[a : a + 1, :] = y[0:1]
        high[a : a + 1, :] = y[N - 1 : N]
        xy_out[at, :] = x[a] + y
    send(pos, 1, low[...], high[...], sends[2], sends[3])


def along_z(v, xy, kz, diagonal, z_forward, z_back, lanes, q_out):
    group = z_forward.shape[0]
    rows, size = v.shape
    columns = [slice(i, i + group) for i in range(0, size, group)]
    grad = dot(jnp.concatenate([v[:, c] for c in columns], 0), z_forward[...])
    flux = [kz[:, c] * grad[i * rows : (i + 1) * rows] for i, c in enumerate(columns)]
    back = dot(jnp.concatenate(flux, 0), z_back[...])
    back = jnp.concatenate([back[i * rows : (i + 1) * rows] for i in range(len(columns))], 1)
    q_out[...] = fold_z(back, lanes) + (xy[...] + diagonal[...] * v[...])


def assemble(sizes, pos, q, recv):
    x_even, x_odd, y_even, y_odd = recv
    x_low, x_high = received(sizes, pos, 0, x_even[...], x_odd[...])
    y_low, y_high = received(sizes, pos, 1, y_even[...], y_odd[...])
    row = row_index(y_low.shape)
    out = [q[N * a : N * a + N, :] + place(y_low, y_high, a, row) for a in range(N)]
    out[0] += x_low
    out[N - 1] += x_high
    return out


def first_kernel(sizes, b_in, kx, ky_in, advect, even, odd, lanes,
                 b_out, ky_out, xy_out, *refs):
    pos = position()
    low, high = received(sizes, pos, 0, even[...], odd[...])
    b, ky = tiles(b_in), tiles(ky_in)
    for a, side in ((0, low), (N - 1, high)):
        b[a] += fold_z(side[0:N], lanes)
        ky[a] += fold_z(side[3 * N : 4 * N], lanes)
    store(b_out, b)
    store(ky_out, ky)
    operate(pos, b, kx, ky_out, advect, xy_out, refs[:4], *refs[4:])


def first_z_kernel(sizes, b, xy, kz_in, diagonal_in, even, odd, z_forward, z_back, lanes,
                   kz_out, diagonal_out, q_out):
    pos = position()
    low, high = received(sizes, pos, 0, even[...], odd[...])
    kz_out[...] = kz_in[...]
    diagonal_out[...] = diagonal_in[...]
    for a, side in ((0, low), (N - 1, high)):
        at = slice(N * a, N * a + N)
        kz_out[at, :] += side[N : 2 * N]
        diagonal_out[at, :] += fold_z(side[2 * N : 3 * N], lanes)
    along_z(b, xy, kz_out, diagonal_out, z_forward, z_back, lanes, q_out)


def dots_row(pairs, inverse, out):
    width = out.shape[-1]
    rows = []
    for u, v in pairs:
        product = sum(x * (y * m) for x, y, m in zip(u, v, inverse))
        product = sum(product[:, i : i + width] for i in range(0, product.shape[1], width))
        rows.append(jnp.sum(product, axis=0, keepdims=True))
    rows += [jnp.zeros_like(rows[0])] * (-len(rows) % N)
    sums = jnp.sum(jnp.concatenate(rows, 0), axis=1, keepdims=True)
    shape = (len(rows), width)
    lane = lax.broadcasted_iota(jnp.int32, shape, 1)
    row = jnp.sum(jnp.where(lane == row_index(shape), sums, 0.0), axis=0, keepdims=True)
    for i in range(out.shape[0]):
        out[i] = row


def totals(gathered, count):
    row = jnp.sum(gathered[...], axis=0)
    return [jnp.broadcast_to(row[:, i : i + 1], row.shape) for i in range(count)]


def wide(scalar, like):
    return jnp.concatenate([scalar] * (like.shape[1] // scalar.shape[1]), 1)


def inner_pairs(b, r, s, w, z):
    return [(b, r), (b, s), (b, w), (b, z), (w, r), (w, s), (r, z), (s, z), (w, w), (w, z), (z, z)]


def steps(g):
    br, bs, bw, bz, wr, ws, rz, sz, ww, wz, zz = g
    alpha = br / bs
    omega = (wr - alpha * (ws + rz) + alpha * alpha * sz) / (
        ww - 2.0 * alpha * wz + alpha * alpha * zz
    )
    rho_next = (br - alpha * bs) - omega * (bw - alpha * bz)
    beta = rho_next / br * (alpha / omega)
    return alpha, omega, beta


def apply_kernel(sizes, q, x0, x1, y0, y1, kx, ky, advect, s_out, xy_out, *refs):
    pos = position()
    s = assemble(sizes, pos, q, (x0, x1, y0, y1))
    store(s_out, s)
    operate(pos, s, kx, ky, advect, xy_out, refs[:4], *refs[4:])


def z_kernel(v, xy, kz, diagonal, z_forward, z_back, lanes, q_out):
    along_z(v, xy, kz, diagonal, z_forward, z_back, lanes, q_out)


def first_dots_kernel(sizes, b, s, inverse, q, x0, x1, y0, y1, kx, ky, advect,
                      z_out, row, xy_out, *refs):
    pos = position()
    z = assemble(sizes, pos, q, (x0, x1, y0, y1))
    store(z_out, z)
    b, s = tiles(b), tiles(s)
    dots_row([(b, b), (b, s), (b, z), (s, s), (s, z), (z, z)], tiles(inverse), row)
    operate(pos, z, kx, ky, advect, xy_out, refs[:4], *refs[4:])


def update_kernel(sizes, first, gathered, s, w, z, aw, q, x0, x1, y0, y1, kx, ky, advect,
                  w_out, az_out, scalars, xy_out, *refs):
    pos = position()
    if first:
        bb, bs, bz, ss, sz, zz = totals(gathered, 6)
        g = (bb, bs, bs, bz, bs, ss, bz, sz, ss, sz, zz)
    else:
        g = totals(gathered, 11)
    values = steps(g)
    for i, value in enumerate(values):
        scalars[i : i + 1, :] = value
    alpha, omega, _ = (wide(value, s) for value in values)
    az = assemble(sizes, pos, q, (x0, x1, y0, y1))
    store(az_out, az)
    w_next = [
        (w_ - alpha * z_) - omega * (aw_ - alpha * az_)
        for w_, z_, aw_, az_ in zip(tiles(w), tiles(z), tiles(aw), az)
    ]
    store(w_out, w_next)
    operate(pos, w_next, kx, ky, advect, xy_out, refs[:4], *refs[4:])


def update_rest_kernel(first, scalars, r, p, s, w, z, az, w_next, xy, kz, diagonal, z_forward, z_back,
                       lanes, *refs):
    x, outs = (None, refs) if first else (refs[0], refs[1:])
    x_out, r_out, p_out, s_out, zpart_out, q_out = outs
    along_z(w_next, xy, kz, diagonal, z_forward, z_back, lanes, q_out)
    alpha, omega, beta = (wide(scalars[i : i + 1, :], s) for i in range(3))
    half = r[...] - alpha * s[...]
    step = alpha * p[...] + omega * half
    x_out[...] = step if first else x[...] + step
    r_next = half - omega * (w[...] - alpha * z[...])
    r_out[...] = r_next
    p_out[...] = r_next + beta * (p[...] - omega * s[...])
    s_out[...] = w_next[...] + beta * (s[...] - omega * z[...])
    zpart_out[...] = beta * (z[...] - omega * az[...])


def dots_kernel(sizes, last, b, r, s, w, zpart, inverse, q, x0, x1, y0, y1, *refs):
    pos = position()
    aw = assemble(sizes, pos, q, (x0, x1, y0, y1))
    z = [u + v for u, v in zip(aw, tiles(zpart))]
    if last:
        z_out, row = refs
    else:
        kx, ky, advect, z_out, row, aw_out, xy_out, *refs = refs
        store(aw_out, aw)
    store(z_out, z)
    pairs = inner_pairs(tiles(b), tiles(r), tiles(s), tiles(w), z)
    dots_row(pairs, tiles(inverse), row)
    if not last:
        operate(pos, z, kx, ky, advect, xy_out, refs[:4], *refs[4:])


def last_kernel(gathered, r, p, s, w, z, x, x_out, r_out):
    alpha, omega, _ = steps(totals(gathered, 11))
    alpha, omega = wide(alpha, s), wide(omega, s)
    half = r[...] - alpha * s[...]
    x_out[...] = x[...] + alpha * p[...] + omega * half
    r_out[...] = half - omega * (w[...] - alpha * z[...])


def pairings(sizes):
    count_x, count_y = sizes
    grid = [(i, j) for i in range(count_x) for j in range(count_y)]
    number = lambda i, j: i * count_y + j
    step = lambda i: i + 1 if i % 2 else i - 1
    x_even = [(number(i, j), number(i ^ 1, j)) for i, j in grid]
    x_odd = [
        (number(i, j), number(step(i), j) if 0 < i < count_x - 1 else number(i, j ^ 1)) for i, j in grid
    ]
    y_even = [(number(i, j), number(i, j ^ 1)) for i, j in grid]
    y_odd = [(number(i, j), number(i, step(j) % count_y)) for i, j in grid]
    return (x_even, x_odd), (y_even, y_odd)


def per_device(sizes, source, conductivity, robin_flags, htc_class, htc_table):
    shape = source.shape
    elems_z = robin_flags.shape[2]
    rows, size = shape[0] * shape[1], shape[2]
    assert robin_flags.shape[:2] == (1, 1) and sizes[0] % 2 == 0 and sizes[1] % 2 == 0
    devices = sizes[0] * sizes[1]
    z_forward, z_back, lanes = (jnp.asarray(value) for value in constants(elems_z))
    x_pairs, y_pairs = pairings(sizes)

    def struct(n=rows):
        return jax.ShapeDtypeStruct((n, size), f32)

    field = struct()
    faces = [struct(N)] * 4
    row = jax.ShapeDtypeStruct((devices, 1, 128), f32)
    scalars = jax.ShapeDtypeStruct((N, 128), f32)
    side = [pltpu.VMEM((N, size), f32)] * 2

    def call(kernel, outs, *operands, scratch=(), hbm=0, limit=32, cost=0):
        specs = [HBM] * hbm + [VMEM] * (len(operands) - hbm)
        return pl.pallas_call(
            kernel,
            out_shape=outs,
            in_specs=specs,
            out_specs=[VMEM] * len(outs),
            scratch_shapes=list(scratch),
            compiler_params=pltpu.CompilerParams(vmem_limit_bytes=limit * 1024 * 1024),
            cost_estimate=pl.CostEstimate(flops=cost, bytes_accessed=cost, transcendentals=0)
            if cost
            else None,
        )(*operands)

    def permute(values, pairs):
        return lax.ppermute(values, ("gx", "gy"), pairs)

    def exchange(pairs, even, odd):
        odd = permute(odd, pairs[1])
        return permute(even, pairs[0]), odd

    def swap(parts):
        x_odd = permute(parts[1], x_pairs[1])
        y_odd = permute(parts[3], y_pairs[1])
        x_even = permute(parts[0], x_pairs[0])
        return x_even, x_odd, permute(parts[2], y_pairs[0]), y_odd

    def spread(values):
        return lax.all_to_all(values, ("gx", "gy"), 0, 0)

    given = (
        source.reshape(rows, size), conductivity.reshape(rows, size),
        robin_flags.reshape(1, elems_z), htc_class.reshape(1, elems_z), htc_table.reshape(1, -1),
    )
    parts = call(
        functools.partial(field_kernel, sizes), [struct(3 * N)] * 2, *given,
        hbm=5,
        limit=60,
        scratch=[pltpu.VMEM(v.shape, v.dtype) for v in given]
        + [pltpu.VMEM((3 * N, size), f32)] * 2
        + [pltpu.SemaphoreType.DMA((5,))],
    )
    recv = exchange(y_pairs, *parts)
    ws, wk, robin = call(functools.partial(whole_field_kernel, sizes), [field] * 3, *given, cost=COST)
    parts = call(
        functools.partial(fold_y_kernel, sizes), [struct(4 * N)] * 2, ws, wk, robin, *recv
    )
    b, kx, ky, kz, advect, diagonal, inverse = call(
        functools.partial(prepare_kernel, sizes), [field] * 7, ws, wk, robin, *recv, lanes,
        cost=COST,
    )
    recv = exchange(x_pairs, *parts)
    b, ky, xy, *parts = call(
        functools.partial(first_kernel, sizes), [field] * 3 + faces,
        b, kx, ky, advect, *recv, lanes, scratch=side,
    )
    kz, diagonal, q = call(
        functools.partial(first_z_kernel, sizes), [field] * 3,
        b, xy, kz, diagonal, *recv, z_forward, z_back, lanes, cost=COST,
    )
    coefs = (kx, ky, advect)
    z_args = (kz, diagonal, z_forward, z_back, lanes)
    recv = swap(parts)
    s, xy, *parts = call(
        functools.partial(apply_kernel, sizes), [field] * 2 + faces,
        q, *recv, *coefs, scratch=side,
    )
    (q,) = call(z_kernel, [field], s, xy, *z_args, cost=COST)
    recv = swap(parts)
    z, products, xy, *parts = call(
        functools.partial(first_dots_kernel, sizes), [field, row, field] + faces,
        b, s, inverse, q, *recv, *coefs, scratch=side,
    )
    (q,) = call(z_kernel, [field], z, xy, *z_args, cost=COST)
    r, p, w, aw, x = b, b, s, z, ()
    for iteration in range(ITERS - 1):
        gathered = spread(products)
        recv = swap(parts)
        first, last = iteration == 0, iteration == ITERS - 2
        w_next, az, values, xy, *parts = call(
            functools.partial(update_kernel, sizes, first),
            [field] * 2 + [scalars, field] + faces,
            gathered, s, w, z, aw, q, *recv, *coefs, scratch=side,
        )
        x, r, p, s, zpart, q = call(
            functools.partial(update_rest_kernel, first), [field] * 6,
            values, r, p, s, w, z, az, w_next, xy, *z_args, *(() if first else (x,)), cost=COST,
        )
        w = w_next
        recv = swap(parts)
        z, products, *rest = call(
            functools.partial(dots_kernel, sizes, last),
            [field, row] + ([] if last else [field] * 2 + faces),
            b, r, s, w, zpart, inverse, q, *recv, *(() if last else coefs),
            scratch=() if last else side,
        )
        if not last:
            aw, xy, *parts = rest
            (q,) = call(z_kernel, [field], z, xy, *z_args, cost=COST)
    gathered = spread(products)
    x, r = call(last_kernel, [field] * 2, gathered, r, p, s, w, z, x)
    return x.reshape(shape), r.reshape(shape)


def solution(mesh):
    sizes = (mesh.shape["gx"], mesh.shape["gy"])
    field = P("gx", "gy", None)
    return jax.shard_map(
        functools.partial(per_device, sizes),
        mesh=mesh,
        in_specs=(field, field, field, field, P()),
        out_specs=(field, field),
        check_vma=False,
    )
```

time: 88.3 us -> 75.1 us (0.85)
  waiting for transfers between devices: 18 us -> 12.8 us
  local copies, waits for them, and re-layouts: 5.08 us -> 0.04 us
  Pallas kernels: 14.5 us -> 11.8 us
    ppermute x28, waiting for transfers between devices: 16.6 us -> 11.5 us  [permute(): return lax.ppermute(values, ('gx', 'gy'), pairs)]
    unnamed x28 -> x16, local copies, waits for them, and re-layouts: 5.08 us -> 0.04 us
    pallas_call x10 -> x18, Pallas kernels: 14.5 us -> 11.8 us  [call(): pl.pallas_call(kernel, out_shape=outs, in_specs=specs, out_specs=[VMEM] *...]
  transfers between devices with their start and end apart: 30 -> 30, of which waited for: 10 -> 10; matrix products, arithmetic and copies ran while one was open for 0% -> 0% of each run, Pallas kernels for 0% -> 7%
where the time goes in v3:
time: 75.1 us; the launch traced here: 74.9 us
  starting transfers between devices  39.3 us (52%)
  waiting for transfers between devices  12.8 us (17%)
  Pallas kernels  11.8 us (16%)
  blocking collectives  10 us (13%)
  between operations  0.95 us (1%)
    ppermute x28, starting transfers between devices, permute(): return lax.ppermute(values, ('gx', 'gy'), pairs)  32.8 us
    pallas_call x18, Pallas kernels, call(): pl.pallas_call(kernel, out_shape=outs, in_specs=specs, out_specs=[VMEM] *...  11.8 us
    ppermute x28, waiting for transfers between devices, permute(): return lax.ppermute(values, ('gx', 'gy'), pairs)  11.5 us
    all_to_all x1, blocking collectives, spread(): return lax.all_to_all(values, ('gx', 'gy'), 0, 0)  10 us
    all_to_all x2, starting transfers between devices, spread(): return lax.all_to_all(values, ('gx', 'gy'), 0, 0)  6.53 us
  transfers between devices with their start and end apart: 30, of which 10 were waited for; matrix products, arithmetic and copies ran while one was open for 0% of the time, Pallas kernels for 7%

profile of v3, /device:TPU:0, one launch (start us, length us, event | category | flops | bytes accessed | tf_op | source)
XLA Modules:
  0.0 74.9 jit_solution(6145578273502338131)
XLA Ops:
  0.6 1.8 %shard_map.96 = (f32[24,512]{1,0:T(8,128)}, f32[24,512]{1,0:T(8,128)}) custom-call(f32[64,512]{1,0:T(8,128)} %bitcast.7, f32[64,512]{1,0:T(8,128)} %bitcast.9, s32[1,64]{1,0:T(1,128)} %bitcast.11, s32[1,64]{1,0:T(1,128)} %bitcast.13, f32[1,4]{1,0:T(1,128)} %bitcast.15), custom_call_target="tpu_custom_call" | custom-call | tf_op jit(solution)/shard_map/pallas_call | solution.py:479
  2.5 0.0 copy-start.5
  2.5 0.0 copy-start.6
  2.5 0.0 copy-start.7
  2.5 0.5 collective-permute-start
  3.0 3.6 %collective-permute-start.1 = (f32[24,512]{1,0:T(8,128)}, f32[24,512]{1,0:T(8,128)S(1)}, u32[]{:S(2)}, u32[]{:S(2)}) collective-permute-start(f32[24,512]{1,0:T(8,128)} %get-tuple-element.83), channel_id=1, source_target_pairs={{0,7},{1,2},{2,1},{3,4},{4,3},{5,6},{6,5},{7,0},{8,15},{9,10},{10,... | collective-permute-start | bytes 147464 | tf_op jit(solution)/shard_map/ppermute | solution.py:492
  6.6 0.3 shard_map.95
  6.9 0.0 collective-permute-done.even
  6.9 1.8 %collective-permute-done.1.odd = f32[24,512]{1,0:T(8,128)S(1)} collective-permute-done((f32[24,512]{1,0:T(8,128)}, f32[24,512]{1,0:T(8,128)S(1)}, u32[]{:S(2)}, u32[]{:S(2)}) %collective-permute-start.1) | collective-permute-done | bytes 49184 | tf_op jit(solution)/shard_map/ppermute | solution.py:492
  8.7 1.7 %collective-permute-start.2 = (f32[32,512]{1,0:T(8,128)S(1)}, f32[32,512]{1,0:T(8,128)S(1)}, u32[]{:S(2)}, u32[]{:S(2)}) collective-permute-start(f32[32,512]{1,0:T(8,128)S(1)} %get-tuple-element.88), channel_id=1, source_target_pairs={{0,8},{1,9},{2,10},{3,11},{4,12},{5,13},{6,14},{7,15},{8,0},{9,1},... | collective-permute-start | bytes 196616 | tf_op jit(solution)/shard_map/ppermute | solution.py:492
  10.4 0.4 shard_map.97
  10.8 2.2 %collective-permute-done.2.even = f32[32,512]{1,0:T(8,128)S(1)} collective-permute-done((f32[32,512]{1,0:T(8,128)S(1)}, f32[32,512]{1,0:T(8,128)S(1)}, u32[]{:S(2)}, u32[]{:S(2)}) %collective-permute-start.2) | collective-permute-done | bytes 65568 | tf_op jit(solution)/shard_map/ppermute | solution.py:492
  13.0 0.4 shard_map.99
  13.4 2.8 %collective-permute-start.4 = (f32[8,512]{1,0:T(8,128)S(1)}, f32[8,512]{1,0:T(8,128)S(1)}, u32[]{:S(2)}, u32[]{:S(2)}) collective-permute-start(f32[8,512]{1,0:T(8,128)S(1)} %get-tuple-element.95), channel_id=1, source_target_pairs={{0,8},{1,9},{2,10},{3,11},{4,12},{5,13},{6,14},{7,15},{8,0},{9,1},... | collective-permute-start | bytes 49160 | tf_op jit(solution)/shard_map/ppermute | solution.py:492
  16.3 0.5 collective-permute-start.6
  16.8 1.6 %collective-permute-start.7 = (f32[8,512]{1,0:T(8,128)S(1)}, f32[8,512]{1,0:T(8,128)S(1)}, u32[]{:S(2)}, u32[]{:S(2)}) collective-permute-start(f32[8,512]{1,0:T(8,128)S(1)} %get-tuple-element.98), channel_id=1, source_target_pairs={{0,7},{1,2},{2,1},{3,4},{4,3},{5,6},{6,5},{7,0},{8,15},{9,10},{10,... | collective-permute-start | bytes 49160 | tf_op jit(solution)/shard_map/ppermute | solution.py:492
  18.4 0.8 %shard_map.100 = (f32[64,512]{1,0:T(8,128)S(1)}, f32[64,512]{1,0:T(8,128)S(1)}, f32[64,512]{1,0:T(8,128)S(1)}) custom-call(f32[64,512]{1,0:T(8,128)S(1)} %get-tuple-element.90.b.r.p, f32[64,512]{1,0:T(8,128)S(1)} %get-tuple-element.91.xy, f32[64,512]{1,0:T(8,128)S(1)} %get-tuple-element.92.kz_in, f32[64,512]{1,0:T(8,128)S(1)} %get-tuple-element.93.diagonal_in, ...), custom_call_target="tpu_custom_call" | custom-call | flops 1048576 | bytes 1048576 | tf_op jit(solution)/shard_map/pallas_call | solution.py:479
  19.1 0.0 collective-permute-done.4.x0
  19.1 0.0 collective-permute-done.5.x1
  19.2 1.7 %collective-permute-done.7.y1 = f32[8,512]{1,0:T(8,128)S(1)} collective-permute-done((f32[8,512]{1,0:T(8,128)S(1)}, f32[8,512]{1,0:T(8,128)S(1)}, u32[]{:S(2)}, u32[]{:S(2)}) %collective-permute-start.7) | collective-permute-done | bytes 16416 | tf_op jit(solution)/shard_map/ppermute | solution.py:492
  20.8 0.4 shard_map.101
  21.2 1.7 %collective-permute-start.8 = (f32[8,512]{1,0:T(8,128)S(1)}, f32[8,512]{1,0:T(8,128)S(1)}, u32[]{:S(2)}, u32[]{:S(2)}) collective-permute-start(f32[8,512]{1,0:T(8,128)S(1)} %get-tuple-element.105), channel_id=1, source_target_pairs={{0,8},{1,9},{2,10},{3,11},{4,12},{5,13},{6,14},{7,15},{8,0},{9,1},... | collective-permute-start | bytes 49160 | tf_op jit(solution)/shard_map/ppermute | solution.py:492
  22.9 0.5 collective-permute-start.10
  23.4 2.0 %collective-permute-start.11 = (f32[8,512]{1,0:T(8,128)S(1)}, f32[8,512]{1,0:T(8,128)S(1)}, u32[]{:S(2)}, u32[]{:S(2)}) collective-permute-start(f32[8,512]{1,0:T(8,128)S(1)} %get-tuple-element.108), channel_id=1, source_target_pairs={{0,7},{1,2},{2,1},{3,4},{4,3},{5,6},{6,5},{7,0},{8,15},{9,10},{10,... | collective-permute-start | bytes 49160 | tf_op jit(solution)/shard_map/ppermute | solution.py:492
  25.4 0.8 %shard_map.102.q = f32[64,512]{1,0:T(8,128)S(1)} custom-call(f32[64,512]{1,0:T(8,128)S(1)} %get-tuple-element.100.v.s.w, f32[64,512]{1,0:T(8,128)S(1)} %get-tuple-element.102.xy, f32[64,512]{1,0:T(8,128)S(1)} %get-tuple-element.103.kz, f32[64,512]{1,0:T(8,128)S(1)} %get-tuple-element.104.diagonal, f32[256,256]{1,0:T(8,128)S(1)} %copy-done.1, ...), custom_call_target="tpu_custom_call" | custom-call | flops 1048576 | bytes 1048576 | tf_op jit(solution)/shard_map/pallas_call | solution.py:479
  26.1 0.0 collective-permute-done.8.x0
  26.2 0.0 collective-permute-done.10.y0
  26.2 1.3 %collective-permute-done.11.y1 = f32[8,512]{1,0:T(8,128)S(1)} collective-permute-done((f32[8,512]{1,0:T(8,128)S(1)}, f32[8,512]{1,0:T(8,128)S(1)}, u32[]{:S(2)}, u32[]{:S(2)}) %collective-permute-start.11) | collective-permute-done | bytes 16416 | tf_op jit(solution)/shard_map/ppermute | solution.py:492
  27.4 0.8 %shard_map.103 = (f32[64,512]{1,0:T(8,128)S(1)}, f32[32,1,128]{2,1,0:T(1,128)}, f32[64,512]{1,0:T(8,128)S(1)}, f32[8,512]{1,0:T(8,128)S(1)}, f32[8,512]{1,0:T(8,...) custom-call(f32[64,512]{1,0:T(8,128)S(1)} %get-tuple-element.90.b.r.p, f32[64,512]{1,0:T(8,128)S(1)} %get-tuple-element.100.v.s.w, ...), custom_call_target="tpu_custom_call" | custom-call | tf_op jit(solution)/shard_map/pallas_call | solution.py:479
  28.3 3.5 %all-to-all-start = ((f32[32,1,128]{2,1,0:T(1,128)}), f32[32,1,128]{2,1,0:T(1,128)S(1)}, u32[]{:S(2)}, u32[]{:S(2)}) async-start(f32[32,1,128]{2,1,0:T(1,128)} %get-tuple-element.109), calls=%async_computation | async-start | bytes 32768 | tf_op jit(solution)/shard_map/all_to_all | solution.py:505
  31.7 1.8 %collective-permute-start.12 = (f32[8,512]{1,0:T(8,128)S(1)}, f32[8,512]{1,0:T(8,128)S(1)}, u32[]{:S(2)}, u32[]{:S(2)}) collective-permute-start(f32[8,512]{1,0:T(8,128)S(1)} %get-tuple-element.112), channel_id=1, source_target_pairs={{0,8},{1,9},{2,10},{3,11},{4,12},{5,13},{6,14},{7,15},{8,0},{9,1},... | collective-permute-start | bytes 49160 | tf_op jit(solution)/shard_map/ppermute | solution.py:492
  33.6 0.5 collective-permute-start.14
  34.1 2.0 %collective-permute-start.15 = (f32[8,512]{1,0:T(8,128)S(1)}, f32[8,512]{1,0:T(8,128)S(1)}, u32[]{:S(2)}, u32[]{:S(2)}) collective-permute-start(f32[8,512]{1,0:T(8,128)S(1)} %get-tuple-element.115), channel_id=1, source_target_pairs={{0,7},{1,2},{2,1},{3,4},{4,3},{5,6},{6,5},{7,0},{8,15},{9,10},{10,... | collective-permute-start | bytes 49160 | tf_op jit(solution)/shard_map/ppermute | solution.py:492
  36.1 0.8 %shard_map.104.q = f32[64,512]{1,0:T(8,128)S(1)} custom-call(f32[64,512]{1,0:T(8,128)S(1)} %get-tuple-element.110.v.z.aw, f32[64,512]{1,0:T(8,128)S(1)} %get-tuple-element.111.xy, f32[64,512]{1,0:T(8,128)S(1)} %get-tuple-element.103.kz, f32[64,512]{1,0:T(8,128)S(1)} %get-tuple-element.104.diagonal, f32[256,256]{1,0:T(8,128)S(1)} %copy-done.1, ...), custom_call_target="tpu_custom_call" | custom-call | flops 1048576 | bytes 1048576 | tf_op jit(solution)/shard_map/pallas_call | solution.py:479
  36.8 0.0 collective-permute-done.12.x0
  36.8 0.0 collective-permute-done.13.x1
  36.8 1.3 %collective-permute-done.15.y1 = f32[8,512]{1,0:T(8,128)S(1)} collective-permute-done((f32[8,512]{1,0:T(8,128)S(1)}, f32[8,512]{1,0:T(8,128)S(1)}, u32[]{:S(2)}, u32[]{:S(2)}) %collective-permute-start.15) | collective-permute-done | bytes 16416 | tf_op jit(solution)/shard_map/ppermute | solution.py:492
  38.1 0.7 all-to-all-done.gathered
  38.8 0.5 shard_map.105
  39.3 1.9 %collective-permute-start.16 = (f32[8,512]{1,0:T(8,128)S(1)}, f32[8,512]{1,0:T(8,128)S(1)}, u32[]{:S(2)}, u32[]{:S(2)}) collective-permute-start(f32[8,512]{1,0:T(8,128)S(1)} %get-tuple-element.124), channel_id=1, source_target_pairs={{0,8},{1,9},{2,10},{3,11},{4,12},{5,13},{6,14},{7,15},{8,0},{9,1},... | collective-permute-start | bytes 49160 | tf_op jit(solution)/shard_map/ppermute | solution.py:492
  41.2 0.0 collective-permute-start.17
  41.2 0.5 collective-permute-start.18
  41.7 2.2 %collective-permute-start.19 = (f32[8,512]{1,0:T(8,128)S(1)}, f32[8,512]{1,0:T(8,128)S(1)}, u32[]{:S(2)}, u32[]{:S(2)}) collective-permute-start(f32[8,512]{1,0:T(8,128)S(1)} %get-tuple-element.127), channel_id=1, source_target_pairs={{0,7},{1,2},{2,1},{3,4},{4,3},{5,6},{6,5},{7,0},{8,15},{9,10},{10,... | collective-permute-start | bytes 49160 | tf_op jit(solution)/shard_map/ppermute | solution.py:492
  43.9 0.9 %shard_map.106 = (f32[64,512]{1,0:T(8,128)S(1)}, f32[64,512]{1,0:T(8,128)S(1)}, f32[64,512]{1,0:T(8,128)S(1)}, f32[64,512]{1,0:T(8,128)S(1)}, f32[64,512]{1,0:T(8,128)S(1)}, /*index=5*/f32[64,512]{1,0:T(8,128)S(1)}) custom-call(f32[8,128]{1,0:T(8,128)S(1)} %get-tuple-element.116.scalars, f32[64,512]{1,0:T(8,128)S(1)} %get-tuple-element.90.b.r.p, ...), custom_call_target="tpu_custom_call" | custom-call | flops 1048576 | bytes 1048576 | tf_op jit(solution)/shard_map/pallas_call | solution.py:479
  44.8 0.0 collective-permute-done.17.x1
  44.8 0.9 %collective-permute-done.19.y1 = f32[8,512]{1,0:T(8,128)S(1)} collective-permute-done((f32[8,512]{1,0:T(8,128)S(1)}, f32[8,512]{1,0:T(8,128)S(1)}, u32[]{:S(2)}, u32[]{:S(2)}) %collective-permute-start.19) | collective-permute-done | bytes 16416 | tf_op jit(solution)/shard_map/ppermute | solution.py:492
  45.7 0.9 %shard_map.107 = (f32[64,512]{1,0:T(8,128)S(1)}, f32[32,1,128]{2,1,0:T(1,128)}, f32[64,512]{1,0:T(8,128)S(1)}, f32[64,512]{1,0:T(8,128)S(1)}, f32[8,512]{1,0:T(8...) custom-call(f32[64,512]{1,0:T(8,128)S(1)} %get-tuple-element.90.b.r.p, ...), custom_call_target="tpu_custom_call" | custom-call | tf_op jit(solution)/shard_map/pallas_call | solution.py:479
  46.7 3.1 %all-to-all-start.1 = ((f32[32,1,128]{2,1,0:T(1,128)}), f32[32,1,128]{2,1,0:T(1,128)S(1)}, u32[]{:S(2)}, u32[]{:S(2)}) async-start(f32[32,1,128]{2,1,0:T(1,128)} %get-tuple-element.128), calls=%async_computation.1 | async-start | bytes 32768 | tf_op jit(solution)/shard_map/all_to_all | solution.py:505
  49.7 1.8 %collective-permute-start.20 = (f32[8,512]{1,0:T(8,128)S(1)}, f32[8,512]{1,0:T(8,128)S(1)}, u32[]{:S(2)}, u32[]{:S(2)}) collective-permute-start(f32[8,512]{1,0:T(8,128)S(1)} %get-tuple-element.132), channel_id=1, source_target_pairs={{0,8},{1,9},{2,10},{3,11},{4,12},{5,13},{6,14},{7,15},{8,0},{9,1},... | collective-permute-start | bytes 49160 | tf_op jit(solution)/shard_map/ppermute | solution.py:492
  51.6 0.0 collective-permute-start.21
  51.6 0.5 collective-permute-start.22
  52.1 2.0 %collective-permute-start.23 = (f32[8,512]{1,0:T(8,128)S(1)}, f32[8,512]{1,0:T(8,128)S(1)}, u32[]{:S(2)}, u32[]{:S(2)}) collective-permute-start(f32[8,512]{1,0:T(8,128)S(1)} %get-tuple-element.135), channel_id=1, source_target_pairs={{0,7},{1,2},{2,1},{3,4},{4,3},{5,6},{6,5},{7,0},{8,15},{9,10},{10,... | collective-permute-start | bytes 49160 | tf_op jit(solution)/shard_map/ppermute | solution.py:492
  54.1 0.8 %shard_map.108.q = f32[64,512]{1,0:T(8,128)S(1)} custom-call(f32[64,512]{1,0:T(8,128)S(1)} %get-tuple-element.129.v.z, f32[64,512]{1,0:T(8,128)S(1)} %get-tuple-element.131.xy, f32[64,512]{1,0:T(8,128)S(1)} %get-tuple-element.103.kz, f32[64,512]{1,0:T(8,128)S(1)} %get-tuple-element.104.diagonal, f32[256,256]{1,0:T(8,128)S(1)} %copy-done.1, ...), custom_call_target="tpu_custom_call" | custom-call | flops 1048576 | bytes 1048576 | tf_op jit(solution)/shard_map/pallas_call | solution.py:479
  54.9 1.3 %collective-permute-done.23.y1 = f32[8,512]{1,0:T(8,128)S(1)} collective-permute-done((f32[8,512]{1,0:T(8,128)S(1)}, f32[8,512]{1,0:T(8,128)S(1)}, u32[]{:S(2)}, u32[]{:S(2)}) %collective-permute-start.23) | collective-permute-done | bytes 16416 | tf_op jit(solution)/shard_map/ppermute | solution.py:492
  56.2 0.7 all-to-all-done.1.gathered
  56.8 0.5 shard_map.109
  57.3 1.9 %collective-permute-start.24 = (f32[8,512]{1,0:T(8,128)S(1)}, f32[8,512]{1,0:T(8,128)S(1)}, u32[]{:S(2)}, u32[]{:S(2)}) collective-permute-start(f32[8,512]{1,0:T(8,128)S(1)} %get-tuple-element.146), channel_id=1, source_target_pairs={{0,8},{1,9},{2,10},{3,11},{4,12},{5,13},{6,14},{7,15},{8,0},{9,1},... | collective-permute-start | bytes 49160 | tf_op jit(solution)/shard_map/ppermute | solution.py:492
  59.2 0.5 collective-permute-start.26
  59.7 2.2 %collective-permute-start.27 = (f32[8,512]{1,0:T(8,128)S(1)}, f32[8,512]{1,0:T(8,128)S(1)}, u32[]{:S(2)}, u32[]{:S(2)}) collective-permute-start(f32[8,512]{1,0:T(8,128)S(1)} %get-tuple-element.149), channel_id=1, source_target_pairs={{0,7},{1,2},{2,1},{3,4},{4,3},{5,6},{6,5},{7,0},{8,15},{9,10},{10,... | collective-permute-start | bytes 49160 | tf_op jit(solution)/shard_map/ppermute | solution.py:492
  61.9 0.9 %shard_map.110 = (f32[64,512]{1,0:T(8,128)S(1)}, f32[64,512]{1,0:T(8,128)S(1)}, f32[64,512]{1,0:T(8,128)S(1)}, f32[64,512]{1,0:T(8,128)S(1)}, f32[64,512]{1,0:T(8,128)S(1)}, /*index=5*/f32[64,512]{1,0:T(8,128)S(1)}) custom-call(f32[8,128]{1,0:T(8,128)S(1)} %get-tuple-element.136.scalars, f32[64,512]{1,0:T(8,128)S(1)} %get-tuple-element.120.r, ...), custom_call_target="tpu_custom_call" | custom-call | flops 1048576 | bytes 1048576 | tf_op jit(solution)/shard_map/pallas_call | solution.py:479
  62.8 0.9 %collective-permute-done.27.y1 = f32[8,512]{1,0:T(8,128)S(1)} collective-permute-done((f32[8,512]{1,0:T(8,128)S(1)}, f32[8,512]{1,0:T(8,128)S(1)}, u32[]{:S(2)}, u32[]{:S(2)}) %collective-permute-start.27) | collective-permute-done | bytes 16416 | tf_op jit(solution)/shard_map/ppermute | solution.py:492
  63.8 0.3 shard_map.111
  64.0 10.0 %all_to_all.15.gathered = f32[32,1,128]{2,1,0:T(1,128)S(1)} all-to-all(f32[32,1,128]{2,1,0:T(1,128)S(1)} %get-tuple-element.150), channel_id=1, replica_groups=mesh['gx'=4,'gy'=8] {'gx','gy'}, dimensions={0} | all-to-all | bytes 32768 | tf_op jit(solution)/shard_map/all_to_all | solution.py:505
  74.1 0.8 %shard_map.112 = (f32[64,512]{1,0:T(8,128)}, f32[64,512]{1,0:T(8,128)}) custom-call(f32[32,1,128]{2,1,0:T(1,128)S(1)} %all_to_all.15.gathered, f32[64,512]{1,0:T(8,128)S(1)} %get-tuple-element.142.r, f32[64,512]{1,0:T(8,128)S(1)} %get-tuple-element.151.p, f32[64,512]{1,0:T(8,128)S(1)} %get-tuple-element.143.s, f32[64,512]{1,0:T(8,128)S(1)} %get-tuple-element.139.w_next.w, ...), custom_call_target="tpu_custom_call" | custom-call | tf_op jit(solution)/shard_map/pallas_call | solution.py:479
  (31 shorter events, 0.1 us)
Async XLA Ops:
  0.6 6.0 %copy-start.3 = (f32[8,8,512]{2,1,0:T(8,128)S(1)}, f32[8,8,512]{2,1,0:T(8,128)}, u32[]{:S(2)}) copy-start(f32[8,8,512]{2,1,0:T(8,128)} %param.8) | copy-start | bytes 393220
  0.6 5.9 %copy-start.4 = (f32[8,8,512]{2,1,0:T(8,128)S(1)}, f32[8,8,512]{2,1,0:T(8,128)}, u32[]{:S(2)}) copy-start(f32[8,8,512]{2,1,0:T(8,128)} %param.9) | copy-start | bytes 393220
  2.5 4.1 %copy-start.5 = (s32[1,1,64]{2,1,0:T(1,128)S(1)}, s32[1,1,64]{2,1,0:T(1,128)}, u32[]{:S(2)}) copy-start(s32[1,1,64]{2,1,0:T(1,128)} %param.10) | copy-start | bytes 772
  2.5 4.1 %copy-start.6 = (s32[1,1,64]{2,1,0:T(1,128)S(1)}, s32[1,1,64]{2,1,0:T(1,128)}, u32[]{:S(2)}) copy-start(s32[1,1,64]{2,1,0:T(1,128)} %param.11) | copy-start | bytes 772
  2.5 4.1 %copy-start.7 = (f32[4]{0:T(128)S(1)}, f32[4]{0:T(128)}, u32[]{:S(2)}) copy-start(f32[4]{0:T(128)} %param.12) | copy-start | bytes 52
  2.5 4.4 %collective-permute-start = (f32[24,512]{1,0:T(8,128)}, f32[24,512]{1,0:T(8,128)S(1)}, u32[]{:S(2)}, u32[]{:S(2)}) collective-permute-start(f32[24,512]{1,0:T(8,128)} %get-tuple-element.82), channel_id=1, source_target_pairs={{0,1},{1,0},{2,3},{3,2},{4,5},{5,4},{6,7},{7,6},{8,9},{9,8},{10,11... | collective-permute-start | bytes 147464 | tf_op jit(solution)/shard_map/ppermute | solution.py:492
  3.0 5.6 %collective-permute-start.1 = (f32[24,512]{1,0:T(8,128)}, f32[24,512]{1,0:T(8,128)S(1)}, u32[]{:S(2)}, u32[]{:S(2)}) collective-permute-start(f32[24,512]{1,0:T(8,128)} %get-tuple-element.83), channel_id=1, source_target_pairs={{0,7},{1,2},{2,1},{3,4},{4,3},{5,6},{6,5},{7,0},{8,15},{9,10},{10,... | collective-permute-start | bytes 147464 | tf_op jit(solution)/shard_map/ppermute | solution.py:492
  8.6 1.8 %copy-start.2 = (f32[8,512]{1,0:T(8,128)S(1)}, f32[8,512]{1,0:T(8,128)}, u32[]{:S(2)}) copy-start(f32[8,512]{1,0:T(8,128)} %constant.8.clone.lanes) | copy-start | bytes 49156
  8.7 4.3 %collective-permute-start.2 = (f32[32,512]{1,0:T(8,128)S(1)}, f32[32,512]{1,0:T(8,128)S(1)}, u32[]{:S(2)}, u32[]{:S(2)}) collective-permute-start(f32[32,512]{1,0:T(8,128)S(1)} %get-tuple-element.88), channel_id=1, source_target_pairs={{0,8},{1,9},{2,10},{3,11},{4,12},{5,13},{6,14},{7,15},{8,0},{9,1},... | collective-permute-start | bytes 196616 | tf_op jit(solution)/shard_map/ppermute | solution.py:492
  10.4 2.6 %collective-permute-start.3 = (f32[32,512]{1,0:T(8,128)S(1)}, f32[32,512]{1,0:T(8,128)S(1)}, u32[]{:S(2)}, u32[]{:S(2)}) collective-permute-start(f32[32,512]{1,0:T(8,128)S(1)} %get-tuple-element.89), channel_id=1, source_target_pairs={{0,1},{1,0},{2,3},{3,2},{4,5},{5,4},{6,7},{7,6},{8,16},{9,17},{10,... | collective-permute-start | bytes 196616 | tf_op jit(solution)/shard_map/ppermute | solution.py:492
  13.0 5.3 %copy-start = (f32[256,256]{1,0:T(8,128)S(1)}, f32[256,256]{1,0:T(8,128)}, u32[]{:S(2)}) copy-start(f32[256,256]{1,0:T(8,128)} %constant.7.clone.z_back) | copy-start | bytes 786436
  13.0 5.3 %copy-start.1 = (f32[256,256]{1,0:T(8,128)S(1)}, f32[256,256]{1,0:T(8,128)}, u32[]{:S(2)}) copy-start(f32[256,256]{1,0:T(8,128)} %constant.6.clone.z_forward) | copy-start | bytes 786436
  13.4 5.7 %collective-permute-start.4 = (f32[8,512]{1,0:T(8,128)S(1)}, f32[8,512]{1,0:T(8,128)S(1)}, u32[]{:S(2)}, u32[]{:S(2)}) collective-permute-start(f32[8,512]{1,0:T(8,128)S(1)} %get-tuple-element.95), channel_id=1, source_target_pairs={{0,8},{1,9},{2,10},{3,11},{4,12},{5,13},{6,14},{7,15},{8,0},{9,1},... | collective-permute-start | bytes 49160 | tf_op jit(solution)/shard_map/ppermute | solution.py:492
  16.3 2.9 %collective-permute-start.5 = (f32[8,512]{1,0:T(8,128)S(1)}, f32[8,512]{1,0:T(8,128)S(1)}, u32[]{:S(2)}, u32[]{:S(2)}) collective-permute-start(f32[8,512]{1,0:T(8,128)S(1)} %get-tuple-element.96), channel_id=1, source_target_pairs={{0,1},{1,0},{2,3},{3,2},{4,5},{5,4},{6,7},{7,6},{8,16},{9,17},{10,... | collective-permute-start | bytes 49160 | tf_op jit(solution)/shard_map/ppermute | solution.py:492
  16.3 2.9 %collective-permute-start.6 = (f32[8,512]{1,0:T(8,128)S(1)}, f32[8,512]{1,0:T(8,128)S(1)}, u32[]{:S(2)}, u32[]{:S(2)}) collective-permute-start(f32[8,512]{1,0:T(8,128)S(1)} %get-tuple-element.97), channel_id=1, source_target_pairs={{0,1},{1,0},{2,3},{3,2},{4,5},{5,4},{6,7},{7,6},{8,9},{9,8},{10,11... | collective-permute-start | bytes 49160 | tf_op jit(solution)/shard_map/ppermute | solution.py:492
  16.8 4.1 %collective-permute-start.7 = (f32[8,512]{1,0:T(8,128)S(1)}, f32[8,512]{1,0:T(8,128)S(1)}, u32[]{:S(2)}, u32[]{:S(2)}) collective-permute-start(f32[8,512]{1,0:T(8,128)S(1)} %get-tuple-element.98), channel_id=1, source_target_pairs={{0,7},{1,2},{2,1},{3,4},{4,3},{5,6},{6,5},{7,0},{8,15},{9,10},{10,... | collective-permute-start | bytes 49160 | tf_op jit(solution)/shard_map/ppermute | solution.py:492
  21.2 4.9 %collective-permute-start.8 = (f32[8,512]{1,0:T(8,128)S(1)}, f32[8,512]{1,0:T(8,128)S(1)}, u32[]{:S(2)}, u32[]{:S(2)}) collective-permute-start(f32[8,512]{1,0:T(8,128)S(1)} %get-tuple-element.105), channel_id=1, source_target_pairs={{0,8},{1,9},{2,10},{3,11},{4,12},{5,13},{6,14},{7,15},{8,0},{9,1},... | collective-permute-start | bytes 49160 | tf_op jit(solution)/shard_map/ppermute | solution.py:492
  22.9 3.3 %collective-permute-start.9 = (f32[8,512]{1,0:T(8,128)S(1)}, f32[8,512]{1,0:T(8,128)S(1)}, u32[]{:S(2)}, u32[]{:S(2)}) collective-permute-start(f32[8,512]{1,0:T(8,128)S(1)} %get-tuple-element.106), channel_id=1, source_target_pairs={{0,1},{1,0},{2,3},{3,2},{4,5},{5,4},{6,7},{7,6},{8,16},{9,17},{10,... | collective-permute-start | bytes 49160 | tf_op jit(solution)/shard_map/ppermute | solution.py:492
  22.9 3.3 %collective-permute-start.10 = (f32[8,512]{1,0:T(8,128)S(1)}, f32[8,512]{1,0:T(8,128)S(1)}, u32[]{:S(2)}, u32[]{:S(2)}) collective-permute-start(f32[8,512]{1,0:T(8,128)S(1)} %get-tuple-element.107), channel_id=1, source_target_pairs={{0,1},{1,0},{2,3},{3,2},{4,5},{5,4},{6,7},{7,6},{8,9},{9,8},{10,11... | collective-permute-start | bytes 49160 | tf_op jit(solution)/shard_map/ppermute | solution.py:492
  23.4 4.1 %collective-permute-start.11 = (f32[8,512]{1,0:T(8,128)S(1)}, f32[8,512]{1,0:T(8,128)S(1)}, u32[]{:S(2)}, u32[]{:S(2)}) collective-permute-start(f32[8,512]{1,0:T(8,128)S(1)} %get-tuple-element.108), channel_id=1, source_target_pairs={{0,7},{1,2},{2,1},{3,4},{4,3},{5,6},{6,5},{7,0},{8,15},{9,10},{10,... | collective-permute-start | bytes 49160 | tf_op jit(solution)/shard_map/ppermute | solution.py:492
  28.3 10.5 %all-to-all-start = ((f32[32,1,128]{2,1,0:T(1,128)}), f32[32,1,128]{2,1,0:T(1,128)S(1)}, u32[]{:S(2)}, u32[]{:S(2)}) async-start(f32[32,1,128]{2,1,0:T(1,128)} %get-tuple-element.109), calls=%async_computation | async-start | bytes 32768 | tf_op jit(solution)/shard_map/all_to_all | solution.py:505
  31.7 5.1 %collective-permute-start.12 = (f32[8,512]{1,0:T(8,128)S(1)}, f32[8,512]{1,0:T(8,128)S(1)}, u32[]{:S(2)}, u32[]{:S(2)}) collective-permute-start(f32[8,512]{1,0:T(8,128)S(1)} %get-tuple-element.112), channel_id=1, source_target_pairs={{0,8},{1,9},{2,10},{3,11},{4,12},{5,13},{6,14},{7,15},{8,0},{9,1},... | collective-permute-start | bytes 49160 | tf_op jit(solution)/shard_map/ppermute | solution.py:492
  33.6 3.3 %collective-permute-start.13 = (f32[8,512]{1,0:T(8,128)S(1)}, f32[8,512]{1,0:T(8,128)S(1)}, u32[]{:S(2)}, u32[]{:S(2)}) collective-permute-start(f32[8,512]{1,0:T(8,128)S(1)} %get-tuple-element.113), channel_id=1, source_target_pairs={{0,1},{1,0},{2,3},{3,2},{4,5},{5,4},{6,7},{7,6},{8,16},{9,17},{10,... | collective-permute-start | bytes 49160 | tf_op jit(solution)/shard_map/ppermute | solution.py:492
  33.6 3.3 %collective-permute-start.14 = (f32[8,512]{1,0:T(8,128)S(1)}, f32[8,512]{1,0:T(8,128)S(1)}, u32[]{:S(2)}, u32[]{:S(2)}) collective-permute-start(f32[8,512]{1,0:T(8,128)S(1)} %get-tuple-element.114), channel_id=1, source_target_pairs={{0,1},{1,0},{2,3},{3,2},{4,5},{5,4},{6,7},{7,6},{8,9},{9,8},{10,11... | collective-permute-start | bytes 49160 | tf_op jit(solution)/shard_map/ppermute | solution.py:492
  34.1 4.1 %collective-permute-start.15 = (f32[8,512]{1,0:T(8,128)S(1)}, f32[8,512]{1,0:T(8,128)S(1)}, u32[]{:S(2)}, u32[]{:S(2)}) collective-permute-start(f32[8,512]{1,0:T(8,128)S(1)} %get-tuple-element.115), channel_id=1, source_target_pairs={{0,7},{1,2},{2,1},{3,4},{4,3},{5,6},{6,5},{7,0},{8,15},{9,10},{10,... | collective-permute-start | bytes 49160 | tf_op jit(solution)/shard_map/ppermute | solution.py:492
  39.3 5.5 %collective-permute-start.16 = (f32[8,512]{1,0:T(8,128)S(1)}, f32[8,512]{1,0:T(8,128)S(1)}, u32[]{:S(2)}, u32[]{:S(2)}) collective-permute-start(f32[8,512]{1,0:T(8,128)S(1)} %get-tuple-element.124), channel_id=1, source_target_pairs={{0,8},{1,9},{2,10},{3,11},{4,12},{5,13},{6,14},{7,15},{8,0},{9,1},... | collective-permute-start | bytes 49160 | tf_op jit(solution)/shard_map/ppermute | solution.py:492
  41.2 3.6 %collective-permute-start.17 = (f32[8,512]{1,0:T(8,128)S(1)}, f32[8,512]{1,0:T(8,128)S(1)}, u32[]{:S(2)}, u32[]{:S(2)}) collective-permute-start(f32[8,512]{1,0:T(8,128)S(1)} %get-tuple-element.125), channel_id=1, source_target_pairs={{0,1},{1,0},{2,3},{3,2},{4,5},{5,4},{6,7},{7,6},{8,16},{9,17},{10,... | collective-permute-start | bytes 49160 | tf_op jit(solution)/shard_map/ppermute | solution.py:492
  41.2 3.6 %collective-permute-start.18 = (f32[8,512]{1,0:T(8,128)S(1)}, f32[8,512]{1,0:T(8,128)S(1)}, u32[]{:S(2)}, u32[]{:S(2)}) collective-permute-start(f32[8,512]{1,0:T(8,128)S(1)} %get-tuple-element.126), channel_id=1, source_target_pairs={{0,1},{1,0},{2,3},{3,2},{4,5},{5,4},{6,7},{7,6},{8,9},{9,8},{10,11... | collective-permute-start | bytes 49160 | tf_op jit(solution)/shard_map/ppermute | solution.py:492
  41.7 4.1 %collective-permute-start.19 = (f32[8,512]{1,0:T(8,128)S(1)}, f32[8,512]{1,0:T(8,128)S(1)}, u32[]{:S(2)}, u32[]{:S(2)}) collective-permute-start(f32[8,512]{1,0:T(8,128)S(1)} %get-tuple-element.127), channel_id=1, source_target_pairs={{0,7},{1,2},{2,1},{3,4},{4,3},{5,6},{6,5},{7,0},{8,15},{9,10},{10,... | collective-permute-start | bytes 49160 | tf_op jit(solution)/shard_map/ppermute | solution.py:492
  46.7 10.2 %all-to-all-start.1 = ((f32[32,1,128]{2,1,0:T(1,128)}), f32[32,1,128]{2,1,0:T(1,128)S(1)}, u32[]{:S(2)}, u32[]{:S(2)}) async-start(f32[32,1,128]{2,1,0:T(1,128)} %get-tuple-element.128), calls=%async_computation.1 | async-start | bytes 32768 | tf_op jit(solution)/shard_map/all_to_all | solution.py:505
  49.7 5.1 %collective-permute-start.20 = (f32[8,512]{1,0:T(8,128)S(1)}, f32[8,512]{1,0:T(8,128)S(1)}, u32[]{:S(2)}, u32[]{:S(2)}) collective-permute-start(f32[8,512]{1,0:T(8,128)S(1)} %get-tuple-element.132), channel_id=1, source_target_pairs={{0,8},{1,9},{2,10},{3,11},{4,12},{5,13},{6,14},{7,15},{8,0},{9,1},... | collective-permute-start | bytes 49160 | tf_op jit(solution)/shard_map/ppermute | solution.py:492
  51.6 3.3 %collective-permute-start.21 = (f32[8,512]{1,0:T(8,128)S(1)}, f32[8,512]{1,0:T(8,128)S(1)}, u32[]{:S(2)}, u32[]{:S(2)}) collective-permute-start(f32[8,512]{1,0:T(8,128)S(1)} %get-tuple-element.133), channel_id=1, source_target_pairs={{0,1},{1,0},{2,3},{3,2},{4,5},{5,4},{6,7},{7,6},{8,16},{9,17},{10,... | collective-permute-start | bytes 49160 | tf_op jit(solution)/shard_map/ppermute | solution.py:492
  51.6 3.3 %collective-permute-start.22 = (f32[8,512]{1,0:T(8,128)S(1)}, f32[8,512]{1,0:T(8,128)S(1)}, u32[]{:S(2)}, u32[]{:S(2)}) collective-permute-start(f32[8,512]{1,0:T(8,128)S(1)} %get-tuple-element.134), channel_id=1, source_target_pairs={{0,1},{1,0},{2,3},{3,2},{4,5},{5,4},{6,7},{7,6},{8,9},{9,8},{10,11... | collective-permute-start | bytes 49160 | tf_op jit(solution)/shard_map/ppermute | solution.py:492
  52.1 4.1 %collective-permute-start.23 = (f32[8,512]{1,0:T(8,128)S(1)}, f32[8,512]{1,0:T(8,128)S(1)}, u32[]{:S(2)}, u32[]{:S(2)}) collective-permute-start(f32[8,512]{1,0:T(8,128)S(1)} %get-tuple-element.135), channel_id=1, source_target_pairs={{0,7},{1,2},{2,1},{3,4},{4,3},{5,6},{6,5},{7,0},{8,15},{9,10},{10,... | collective-permute-start | bytes 49160 | tf_op jit(solution)/shard_map/ppermute | solution.py:492
  57.3 5.5 %collective-permute-start.24 = (f32[8,512]{1,0:T(8,128)S(1)}, f32[8,512]{1,0:T(8,128)S(1)}, u32[]{:S(2)}, u32[]{:S(2)}) collective-permute-start(f32[8,512]{1,0:T(8,128)S(1)} %get-tuple-element.146), channel_id=1, source_target_pairs={{0,8},{1,9},{2,10},{3,11},{4,12},{5,13},{6,14},{7,15},{8,0},{9,1},... | collective-permute-start | bytes 49160 | tf_op jit(solution)/shard_map/ppermute | solution.py:492
  59.2 3.6 %collective-permute-start.25 = (f32[8,512]{1,0:T(8,128)S(1)}, f32[8,512]{1,0:T(8,128)S(1)}, u32[]{:S(2)}, u32[]{:S(2)}) collective-permute-start(f32[8,512]{1,0:T(8,128)S(1)} %get-tuple-element.147), channel_id=1, source_target_pairs={{0,1},{1,0},{2,3},{3,2},{4,5},{5,4},{6,7},{7,6},{8,16},{9,17},{10,... | collective-permute-start | bytes 49160 | tf_op jit(solution)/shard_map/ppermute | solution.py:492
  59.2 3.6 %collective-permute-start.26 = (f32[8,512]{1,0:T(8,128)S(1)}, f32[8,512]{1,0:T(8,128)S(1)}, u32[]{:S(2)}, u32[]{:S(2)}) collective-permute-start(f32[8,512]{1,0:T(8,128)S(1)} %get-tuple-element.148), channel_id=1, source_target_pairs={{0,1},{1,0},{2,3},{3,2},{4,5},{5,4},{6,7},{7,6},{8,9},{9,8},{10,11... | collective-permute-start | bytes 49160 | tf_op jit(solution)/shard_map/ppermute | solution.py:492
  59.7 4.1 %collective-permute-start.27 = (f32[8,512]{1,0:T(8,128)S(1)}, f32[8,512]{1,0:T(8,128)S(1)}, u32[]{:S(2)}, u32[]{:S(2)}) collective-permute-start(f32[8,512]{1,0:T(8,128)S(1)} %get-tuple-element.149), channel_id=1, source_target_pairs={{0,7},{1,2},{2,1},{3,4},{4,3},{5,6},{6,5},{7,0},{8,15},{9,10},{10,... | collective-permute-start | bytes 49160 | tf_op jit(solution)/shard_map/ppermute | solution.py:492

commit v4 on v3

--- a/solution.py
+++ b/solution.py
@@ -359,79 +359,97 @@
     return alpha, omega, beta
 
 
-def apply_kernel(sizes, q, x0, x1, y0, y1, kx, ky, advect, s_out, xy_out, *refs):
-    pos = position()
-    s = assemble(sizes, pos, q, (x0, x1, y0, y1))
-    store(s_out, s)
-    operate(pos, s, kx, ky, advect, xy_out, refs[:4], *refs[4:])
+def apply_kernel(sizes, q, x0, x1, y0, y1, kx, ky, advect, v_out, xy_out, *refs):
+    pos = position()
+    v = assemble(sizes, pos, q, (x0, x1, y0, y1))
+    store(v_out, v)
+    operate(pos, v, kx, ky, advect, xy_out, refs[:4], *refs[4:])
 
 
 def z_kernel(v, xy, kz, diagonal, z_forward, z_back, lanes, q_out):
     along_z(v, xy, kz, diagonal, z_forward, z_back, lanes, q_out)
 
 
-def first_dots_kernel(sizes, b, s, inverse, q, x0, x1, y0, y1, kx, ky, advect,
-                      z_out, row, xy_out, *refs):
-    pos = position()
-    z = assemble(sizes, pos, q, (x0, x1, y0, y1))
-    store(z_out, z)
-    b, s = tiles(b), tiles(s)
+def first_dots_kernel(b, s, z, inverse, row):
+    b, s, z = tiles(b), tiles(s), tiles(z)
     dots_row([(b, b), (b, s), (b, z), (s, s), (s, z), (z, z)], tiles(inverse), row)
-    operate(pos, z, kx, ky, advect, xy_out, refs[:4], *refs[4:])
-
-
-def update_kernel(sizes, first, gathered, s, w, z, aw, q, x0, x1, y0, y1, kx, ky, advect,
-                  w_out, az_out, scalars, xy_out, *refs):
-    pos = position()
-    if first:
-        bb, bs, bz, ss, sz, zz = totals(gathered, 6)
-        g = (bb, bs, bs, bz, bs, ss, bz, sz, ss, sz, zz)
-    else:
-        g = totals(gathered, 11)
-    values = steps(g)
+
+
+def update_kernel(sizes, gathered, s, z, az, q, x0, x1, y0, y1, kx, ky, advect,
+                  z_out, aw_out, scalars, z_xy_out, aw_xy_out, *refs):
+    pos = position()
+    bb, bs, bz, ss, sz, zz = totals(gathered, 6)
+    values = steps((bb, bs, bs, bz, bs, ss, bz, sz, ss, sz, zz))
     for i, value in enumerate(values):
         scalars[i : i + 1, :] = value
-    alpha, omega, _ = (wide(value, s) for value in values)
-    az = assemble(sizes, pos, q, (x0, x1, y0, y1))
+    alpha, omega, beta = (wide(value, s) for value in values)
+    aaz = assemble(sizes, pos, q, (x0, x1, y0, y1))
+    z, az = tiles(z), tiles(az)
+    aw = [(z[i] - alpha * az[i]) - omega * (az[i] - alpha * aaz[i]) for i in range(N)]
+    z_next = [aw[i] + beta * (z[i] - omega * az[i]) for i in range(N)]
+    store(aw_out, aw)
+    store(z_out, z_next)
+    sends, sides = refs[:4], refs[4:]
+    halves = [[ref.at[pl.ds(i * N, N)] for ref in sends] for i in range(2)]
+    operate(pos, z_next, kx, ky, advect, z_xy_out, halves[0], *sides)
+    operate(pos, aw, kx, ky, advect, aw_xy_out, halves[1], *sides)
+
+
+def update_rest_kernel(scalars, b, s, z, az, z_next, inverse, x_out, r_out, p_out, s_out, w_out, row):
+    alpha, omega, beta = (wide(scalars[i : i + 1, :], s) for i in range(3))
+    fields = [], [], [], []
+    for i in range(N):
+        at = slice(N * i, N * i + N)
+        b_, s_, z_, az_ = b[at, :], s[at, :], z[at, :], az[at, :]
+        half, applied_half = b_ - alpha * s_, s_ - alpha * z_
+        x_out[at, :] = alpha * b_ + omega * half
+        r = half - omega * applied_half
+        w = applied_half - omega * (z_ - alpha * az_)
+        s_next = w + beta * (s_ - omega * z_)
+        p_out[at, :] = r + beta * (b_ - omega * s_)
+        r_out[at, :], w_out[at, :], s_out[at, :] = r, w, s_next
+        for values, value in zip(fields, (b_, r, s_next, w)):
+            values.append(value)
+    dots_row(inner_pairs(*fields, tiles(z_next)), tiles(inverse), row)
+
+
+def two_z_kernel(z, z_xy, aw, aw_xy, kz, diagonal, z_forward, z_back, lanes, z_q_out, aw_q_out):
+    along_z(z, z_xy, kz, diagonal, z_forward, z_back, lanes, z_q_out)
+    along_z(aw, aw_xy, kz, diagonal, z_forward, z_back, lanes, aw_q_out)
+
+
+def apply_two_kernel(sizes, z_q, aw_q, x0, x1, y0, y1, kx, ky, advect, az_out, aaw_out, xy_out, *refs):
+    pos = position()
+    halves = [[ref.at[pl.ds(i * N, N)] for ref in (x0, x1, y0, y1)] for i in range(2)]
+    az = assemble(sizes, pos, z_q, halves[0])
     store(az_out, az)
-    w_next = [
-        (w_ - alpha * z_) - omega * (aw_ - alpha * az_)
-        for w_, z_, aw_, az_ in zip(tiles(w), tiles(z), tiles(aw), az)
-    ]
-    store(w_out, w_next)
-    operate(pos, w_next, kx, ky, advect, xy_out, refs[:4], *refs[4:])
-
-
-def update_rest_kernel(first, scalars, r, p, s, w, z, az, w_next, xy, kz, diagonal, z_forward, z_back,
-                       lanes, *refs):
-    x, outs = (None, refs) if first else (refs[0], refs[1:])
-    x_out, r_out, p_out, s_out, zpart_out, q_out = outs
-    along_z(w_next, xy, kz, diagonal, z_forward, z_back, lanes, q_out)
-    alpha, omega, beta = (wide(scalars[i : i + 1, :], s) for i in range(3))
-    half = r[...] - alpha * s[...]
-    step = alpha * p[...] + omega * half
-    x_out[...] = step if first else x[...] + step
-    r_next = half - omega * (w[...] - alpha * z[...])
-    r_out[...] = r_next
-    p_out[...] = r_next + beta * (p[...] - omega * s[...])
-    s_out[...] = w_next[...] + beta * (s[...] - omega * z[...])
-    zpart_out[...] = beta * (z[...] - omega * az[...])
-
-
-def dots_kernel(sizes, last, b, r, s, w, zpart, inverse, q, x0, x1, y0, y1, *refs):
-    pos = position()
-    aw = assemble(sizes, pos, q, (x0, x1, y0, y1))
-    z = [u + v for u, v in zip(aw, tiles(zpart))]
-    if last:
-        z_out, row = refs
-    else:
-        kx, ky, advect, z_out, row, aw_out, xy_out, *refs = refs
-        store(aw_out, aw)
-    store(z_out, z)
-    pairs = inner_pairs(tiles(b), tiles(r), tiles(s), tiles(w), z)
-    dots_row(pairs, tiles(inverse), row)
-    if not last:
-        operate(pos, z, kx, ky, advect, xy_out, refs[:4], *refs[4:])
+    operate(pos, az, kx, ky, advect, xy_out, refs[:4], *refs[4:])
+    store(aaw_out, assemble(sizes, pos, aw_q, halves[1]))
+
+
+def second_kernel(sizes, gathered, b, x, r, p, s, w, z, az, aw, aaw, inverse, q, x0, x1, y0, y1,
+                  x_out, r_out, p_out, s_out, w_out, z_out, row):
+    pos = position()
+    alpha, omega, beta = (wide(value, s) for value in steps(totals(gathered, 11)))
+    aaz = assemble(sizes, pos, q, (x0, x1, y0, y1))
+    fields = [], [], [], []
+    for i in range(N):
+        at = slice(N * i, N * i + N)
+        r_, s_, w_, z_, az_ = r[at, :], s[at, :], w[at, :], z[at, :], az[at, :]
+        applied_half = w_ - alpha * z_
+        applied_twice = aw[at, :] - alpha * az_
+        half = r_ - alpha * s_
+        r_next = half - omega * applied_half
+        x_out[at, :] = x[at, :] + alpha * p[at, :] + omega * half
+        p_out[at, :] = r_next + beta * (p[at, :] - omega * s_)
+        w_next = applied_half - omega * applied_twice
+        aw_next = applied_twice - omega * (aaw[at, :] - alpha * aaz[i])
+        s_next = w_next + beta * (s_ - omega * z_)
+        z_next = aw_next + beta * (z_ - omega * az_)
+        r_out[at, :], w_out[at, :], s_out[at, :], z_out[at, :] = r_next, w_next, s_next, z_next
+        for values, value in zip(fields, (r_next, s_next, w_next, z_next)):
+            values.append(value)
+    dots_row(inner_pairs(tiles(b), *fields), tiles(inverse), row)
 
 
 def last_kernel(gathered, r, p, s, w, z, x, x_out, r_out):
@@ -537,44 +555,43 @@
     coefs = (kx, ky, advect)
     z_args = (kz, diagonal, z_forward, z_back, lanes)
     recv = swap(parts)
-    s, xy, *parts = call(
-        functools.partial(apply_kernel, sizes), [field] * 2 + faces,
-        q, *recv, *coefs, scratch=side,
-    )
-    (q,) = call(z_kernel, [field], s, xy, *z_args, cost=COST)
+
+    def apply(q, recv):
+        v, xy, *parts = call(
+            functools.partial(apply_kernel, sizes), [field] * 2 + faces, q, *recv, *coefs, scratch=side
+        )
+        recv = swap(parts)
+        (q,) = call(z_kernel, [field], v, xy, *z_args, cost=COST)
+        return v, q, recv
+
+    s, q, recv = apply(q, recv)
+    z, q, recv = apply(q, recv)
+    (products,) = call(first_dots_kernel, [row], b, s, z, inverse, cost=COST)
+    gathered = spread(products)
+    az, q, recv = apply(q, recv)
+    z_next, aw, values, z_xy, aw_xy, *parts = call(
+        functools.partial(update_kernel, sizes),
+        [field] * 2 + [scalars] + [field] * 2 + [struct(2 * N)] * 4,
+        gathered, s, z, az, q, *recv, *coefs, scratch=side,
+    )
     recv = swap(parts)
-    z, products, xy, *parts = call(
-        functools.partial(first_dots_kernel, sizes), [field, row, field] + faces,
-        b, s, inverse, q, *recv, *coefs, scratch=side,
-    )
-    (q,) = call(z_kernel, [field], z, xy, *z_args, cost=COST)
-    r, p, w, aw, x = b, b, s, z, ()
-    for iteration in range(ITERS - 1):
-        gathered = spread(products)
-        recv = swap(parts)
-        first, last = iteration == 0, iteration == ITERS - 2
-        w_next, az, values, xy, *parts = call(
-            functools.partial(update_kernel, sizes, first),
-            [field] * 2 + [scalars, field] + faces,
-            gathered, s, w, z, aw, q, *recv, *coefs, scratch=side,
-        )
-        x, r, p, s, zpart, q = call(
-            functools.partial(update_rest_kernel, first), [field] * 6,
-            values, r, p, s, w, z, az, w_next, xy, *z_args, *(() if first else (x,)), cost=COST,
-        )
-        w = w_next
-        recv = swap(parts)
-        z, products, *rest = call(
-            functools.partial(dots_kernel, sizes, last),
-            [field, row] + ([] if last else [field] * 2 + faces),
-            b, r, s, w, zpart, inverse, q, *recv, *(() if last else coefs),
-            scratch=() if last else side,
-        )
-        if not last:
-            aw, xy, *parts = rest
-            (q,) = call(z_kernel, [field], z, xy, *z_args, cost=COST)
+    x, r, p, s, w, products = call(
+        update_rest_kernel, [field] * 5 + [row], values, b, s, z, az, z_next, inverse, cost=COST
+    )
     gathered = spread(products)
-    x, r = call(last_kernel, [field] * 2, gathered, r, p, s, w, z, x)
+    z = z_next
+    z_q, aw_q = call(two_z_kernel, [field] * 2, z, z_xy, aw, aw_xy, *z_args, cost=COST)
+    az, aaw, xy, *parts = call(
+        functools.partial(apply_two_kernel, sizes), [field] * 3 + faces,
+        z_q, aw_q, *recv, *coefs, scratch=side,
+    )
+    recv = swap(parts)
+    (q,) = call(z_kernel, [field], az, xy, *z_args, cost=COST)
+    x, r, p, s, w, z, products = call(
+        functools.partial(second_kernel, sizes), [field] * 6 + [row],
+        gathered, b, x, r, p, s, w, z, az, aw, aaw, inverse, q, *recv,
+    )
+    x, r = call(last_kernel, [field] * 2, spread(products), r, p, s, w, z, x)
     return x.reshape(shape), r.reshape(shape)
 
 

time: 75.1 us -> 73.6 us (0.980)
  waiting for transfers between devices: 12.8 us -> 9.6 us
  blocking collectives: 10 us -> 11.8 us
  starting transfers between devices: 39.3 us -> 38 us
  Pallas kernels: 11.8 us -> 13 us
    ppermute x28, waiting for transfers between devices: 11.5 us -> 8.21 us  [permute(): return lax.ppermute(values, ('gx', 'gy'), pairs)]
    all_to_all x1, blocking collectives: 10 us -> 11.8 us  [spread(): return lax.all_to_all(values, ('gx', 'gy'), 0, 0)]
    pallas_call x18 -> x20, Pallas kernels: 11.8 us -> 13 us  [call(): pl.pallas_call(kernel, out_shape=outs, in_specs=specs, out_specs=[VMEM] *...]
    all_to_all x2, starting transfers between devices: 6.53 us -> 5.5 us  [spread(): return lax.all_to_all(values, ('gx', 'gy'), 0, 0)]
  transfers between devices with their start and end apart: 30 -> 30, of which waited for: 10 -> 8; matrix products, arithmetic and copies ran while one was open for 0% -> 0% of each run, Pallas kernels for 7% -> 11%
where the time goes in v4:
time: 73.6 us; the launch traced here: 73.3 us
  starting transfers between devices  38 us (52%)
  Pallas kernels  13 us (18%)
  blocking collectives  11.8 us (16%)
  waiting for transfers between devices  9.6 us (13%)
  between operations  0.94 us (1%)
    ppermute x28, starting transfers between devices, permute(): return lax.ppermute(values, ('gx', 'gy'), pairs)  32.5 us
    pallas_call x20, Pallas kernels, call(): pl.pallas_call(kernel, out_shape=outs, in_specs=specs, out_specs=[VMEM] *...  13 us
    all_to_all x1, blocking collectives, spread(): return lax.all_to_all(values, ('gx', 'gy'), 0, 0)  11.8 us
    ppermute x28, waiting for transfers between devices, permute(): return lax.ppermute(values, ('gx', 'gy'), pairs)  8.21 us
    all_to_all x2, starting transfers between devices, spread(): return lax.all_to_all(values, ('gx', 'gy'), 0, 0)  5.5 us
  transfers between devices with their start and end apart: 30, of which 8 were waited for; matrix products, arithmetic and copies ran while one was open for 0% of the time, Pallas kernels for 11%

profile of v4, /device:TPU:0, one launch (start us, length us, event | category | flops | bytes accessed | tf_op | source)
XLA Modules:
  0.0 73.3 jit_solution(6700170335772990739)
XLA Ops:
  0.6 1.8 %shard_map.96 = (f32[24,512]{1,0:T(8,128)}, f32[24,512]{1,0:T(8,128)}) custom-call(f32[64,512]{1,0:T(8,128)} %bitcast.7, f32[64,512]{1,0:T(8,128)} %bitcast.9, s32[1,64]{1,0:T(1,128)} %bitcast.11, s32[1,64]{1,0:T(1,128)} %bitcast.13, f32[1,4]{1,0:T(1,128)} %bitcast.15), custom_call_target="tpu_custom_call" | custom-call | tf_op jit(solution)/shard_map/pallas_call | solution.py:497
  2.5 0.0 copy-start.5
  2.5 0.0 copy-start.6
  2.5 0.0 copy-start.7
  2.5 0.5 collective-permute-start
  3.0 3.6 %collective-permute-start.1 = (f32[24,512]{1,0:T(8,128)}, f32[24,512]{1,0:T(8,128)S(1)}, u32[]{:S(2)}, u32[]{:S(2)}) collective-permute-start(f32[24,512]{1,0:T(8,128)} %get-tuple-element.81), channel_id=1, source_target_pairs={{0,7},{1,2},{2,1},{3,4},{4,3},{5,6},{6,5},{7,0},{8,15},{9,10},{10,... | collective-permute-start | bytes 147464 | tf_op jit(solution)/shard_map/ppermute | solution.py:510
  6.6 0.3 shard_map.95
  6.9 0.0 collective-permute-done.even
  6.9 1.8 %collective-permute-done.1.odd = f32[24,512]{1,0:T(8,128)S(1)} collective-permute-done((f32[24,512]{1,0:T(8,128)}, f32[24,512]{1,0:T(8,128)S(1)}, u32[]{:S(2)}, u32[]{:S(2)}) %collective-permute-start.1) | collective-permute-done | bytes 49184 | tf_op jit(solution)/shard_map/ppermute | solution.py:510
  8.7 1.7 %collective-permute-start.2 = (f32[32,512]{1,0:T(8,128)S(1)}, f32[32,512]{1,0:T(8,128)S(1)}, u32[]{:S(2)}, u32[]{:S(2)}) collective-permute-start(f32[32,512]{1,0:T(8,128)S(1)} %get-tuple-element.86), channel_id=1, source_target_pairs={{0,8},{1,9},{2,10},{3,11},{4,12},{5,13},{6,14},{7,15},{8,0},{9,1},... | collective-permute-start | bytes 196616 | tf_op jit(solution)/shard_map/ppermute | solution.py:510
  10.4 0.4 shard_map.97
  10.8 2.2 %collective-permute-done.2.even = f32[32,512]{1,0:T(8,128)S(1)} collective-permute-done((f32[32,512]{1,0:T(8,128)S(1)}, f32[32,512]{1,0:T(8,128)S(1)}, u32[]{:S(2)}, u32[]{:S(2)}) %collective-permute-start.2) | collective-permute-done | bytes 65568 | tf_op jit(solution)/shard_map/ppermute | solution.py:510
  13.0 0.4 shard_map.99
  13.4 2.8 %collective-permute-start.4 = (f32[8,512]{1,0:T(8,128)S(1)}, f32[8,512]{1,0:T(8,128)S(1)}, u32[]{:S(2)}, u32[]{:S(2)}) collective-permute-start(f32[8,512]{1,0:T(8,128)S(1)} %get-tuple-element.93), channel_id=1, source_target_pairs={{0,8},{1,9},{2,10},{3,11},{4,12},{5,13},{6,14},{7,15},{8,0},{9,1},... | collective-permute-start | bytes 49160 | tf_op jit(solution)/shard_map/ppermute | solution.py:510
  16.3 0.5 collective-permute-start.6
  16.8 1.6 %collective-permute-start.7 = (f32[8,512]{1,0:T(8,128)S(1)}, f32[8,512]{1,0:T(8,128)S(1)}, u32[]{:S(2)}, u32[]{:S(2)}) collective-permute-start(f32[8,512]{1,0:T(8,128)S(1)} %get-tuple-element.96), channel_id=1, source_target_pairs={{0,7},{1,2},{2,1},{3,4},{4,3},{5,6},{6,5},{7,0},{8,15},{9,10},{10,... | collective-permute-start | bytes 49160 | tf_op jit(solution)/shard_map/ppermute | solution.py:510
  18.4 0.8 %shard_map.100 = (f32[64,512]{1,0:T(8,128)S(1)}, f32[64,512]{1,0:T(8,128)S(1)}, f32[64,512]{1,0:T(8,128)S(1)}) custom-call(f32[64,512]{1,0:T(8,128)S(1)} %get-tuple-element.88.b, f32[64,512]{1,0:T(8,128)S(1)} %get-tuple-element.89.xy, f32[64,512]{1,0:T(8,128)S(1)} %get-tuple-element.90.kz_in, f32[64,512]{1,0:T(8,128)S(1)} %get-tuple-element.91.diagonal_in, ...), custom_call_target="tpu_custom_call" | custom-call | flops 1048576 | bytes 1048576 | tf_op jit(solution)/shard_map/pallas_call | solution.py:497
  19.1 0.0 collective-permute-done.4.x0
  19.1 0.0 collective-permute-done.5.x1
  19.2 1.7 %collective-permute-done.7.y1 = f32[8,512]{1,0:T(8,128)S(1)} collective-permute-done((f32[8,512]{1,0:T(8,128)S(1)}, f32[8,512]{1,0:T(8,128)S(1)}, u32[]{:S(2)}, u32[]{:S(2)}) %collective-permute-start.7) | collective-permute-done | bytes 16416 | tf_op jit(solution)/shard_map/ppermute | solution.py:510
  20.8 0.4 shard_map.101
  21.2 1.7 %collective-permute-start.8 = (f32[8,512]{1,0:T(8,128)S(1)}, f32[8,512]{1,0:T(8,128)S(1)}, u32[]{:S(2)}, u32[]{:S(2)}) collective-permute-start(f32[8,512]{1,0:T(8,128)S(1)} %get-tuple-element.102), channel_id=1, source_target_pairs={{0,8},{1,9},{2,10},{3,11},{4,12},{5,13},{6,14},{7,15},{8,0},{9,1},... | collective-permute-start | bytes 49160 | tf_op jit(solution)/shard_map/ppermute | solution.py:510
  22.9 0.5 collective-permute-start.10
  23.4 2.0 %collective-permute-start.11 = (f32[8,512]{1,0:T(8,128)S(1)}, f32[8,512]{1,0:T(8,128)S(1)}, u32[]{:S(2)}, u32[]{:S(2)}) collective-permute-start(f32[8,512]{1,0:T(8,128)S(1)} %get-tuple-element.105), channel_id=1, source_target_pairs={{0,7},{1,2},{2,1},{3,4},{4,3},{5,6},{6,5},{7,0},{8,15},{9,10},{10,... | collective-permute-start | bytes 49160 | tf_op jit(solution)/shard_map/ppermute | solution.py:510
  25.4 0.8 %shard_map.102.q = f32[64,512]{1,0:T(8,128)S(1)} custom-call(f32[64,512]{1,0:T(8,128)S(1)} %get-tuple-element.98.v.s, f32[64,512]{1,0:T(8,128)S(1)} %get-tuple-element.99.xy, f32[64,512]{1,0:T(8,128)S(1)} %get-tuple-element.100.kz, f32[64,512]{1,0:T(8,128)S(1)} %get-tuple-element.101.diagonal, f32[256,256]{1,0:T(8,128)S(1)} %copy-done.1, ...), custom_call_target="tpu_custom_call" | custom-call | flops 1048576 | bytes 1048576 | tf_op jit(solution)/shard_map/pallas_call | solution.py:497
  26.1 0.0 collective-permute-done.8.x0
  26.2 0.0 collective-permute-done.10.y0
  26.2 1.3 %collective-permute-done.11.y1 = f32[8,512]{1,0:T(8,128)S(1)} collective-permute-done((f32[8,512]{1,0:T(8,128)S(1)}, f32[8,512]{1,0:T(8,128)S(1)}, u32[]{:S(2)}, u32[]{:S(2)}) %collective-permute-start.11) | collective-permute-done | bytes 16416 | tf_op jit(solution)/shard_map/ppermute | solution.py:510
  27.4 0.4 shard_map.103
  27.8 2.0 %collective-permute-start.12 = (f32[8,512]{1,0:T(8,128)S(1)}, f32[8,512]{1,0:T(8,128)S(1)}, u32[]{:S(2)}, u32[]{:S(2)}) collective-permute-start(f32[8,512]{1,0:T(8,128)S(1)} %get-tuple-element.109), channel_id=1, source_target_pairs={{0,8},{1,9},{2,10},{3,11},{4,12},{5,13},{6,14},{7,15},{8,0},{9,1},... | collective-permute-start | bytes 49160 | tf_op jit(solution)/shard_map/ppermute | solution.py:510
  29.8 0.0 collective-permute-start.13
  29.8 0.5 collective-permute-start.14
  30.3 1.2 %collective-permute-start.15 = (f32[8,512]{1,0:T(8,128)S(1)}, f32[8,512]{1,0:T(8,128)S(1)}, u32[]{:S(2)}, u32[]{:S(2)}) collective-permute-start(f32[8,512]{1,0:T(8,128)S(1)} %get-tuple-element.112), channel_id=1, source_target_pairs={{0,7},{1,2},{2,1},{3,4},{4,3},{5,6},{6,5},{7,0},{8,15},{9,10},{10,... | collective-permute-start | bytes 49160 | tf_op jit(solution)/shard_map/ppermute | solution.py:510
  31.5 0.8 %shard_map.104 = f32[32,1,128]{2,1,0:T(1,128)} custom-call(f32[64,512]{1,0:T(8,128)S(1)} %get-tuple-element.88.b, f32[64,512]{1,0:T(8,128)S(1)} %get-tuple-element.98.v.s, f32[64,512]{1,0:T(8,128)S(1)} %get-tuple-element.106.z.v, f32[64,512]{1,0:T(8,128)S(1)} %get-tuple-element.107.inverse), custom_call_target="tpu_custom_call" | custom-call | flops 1048576 | bytes 1048576 | tf_op jit(solution)/shard_map/pallas_call | solution.py:497
  32.3 3.0 %all-to-all-start = ((f32[32,1,128]{2,1,0:T(1,128)}), f32[32,1,128]{2,1,0:T(1,128)S(1)}, u32[]{:S(2)}, u32[]{:S(2)}) async-start(f32[32,1,128]{2,1,0:T(1,128)} %shard_map.104), calls=%async_computation | async-start | bytes 32768 | tf_op jit(solution)/shard_map/all_to_all | solution.py:523
  35.2 0.8 %shard_map.105.q = f32[64,512]{1,0:T(8,128)S(1)} custom-call(f32[64,512]{1,0:T(8,128)S(1)} %get-tuple-element.106.z.v, f32[64,512]{1,0:T(8,128)S(1)} %get-tuple-element.108.xy, f32[64,512]{1,0:T(8,128)S(1)} %get-tuple-element.100.kz, f32[64,512]{1,0:T(8,128)S(1)} %get-tuple-element.101.diagonal, f32[256,256]{1,0:T(8,128)S(1)} %copy-done.1, ...), custom_call_target="tpu_custom_call" | custom-call | flops 1048576 | bytes 1048576 | tf_op jit(solution)/shard_map/pallas_call | solution.py:497
  36.0 0.0 collective-permute-done.12.x0
  36.0 0.0 collective-permute-done.15.y1
  36.0 0.4 shard_map.106
  36.4 1.8 %collective-permute-start.16 = (f32[8,512]{1,0:T(8,128)S(1)}, f32[8,512]{1,0:T(8,128)S(1)}, u32[]{:S(2)}, u32[]{:S(2)}) collective-permute-start(f32[8,512]{1,0:T(8,128)S(1)} %get-tuple-element.115), channel_id=1, source_target_pairs={{0,8},{1,9},{2,10},{3,11},{4,12},{5,13},{6,14},{7,15},{8,0},{9,1},... | collective-permute-start | bytes 49160 | tf_op jit(solution)/shard_map/ppermute | solution.py:510
  38.3 0.5 collective-permute-start.18
  38.8 2.0 %collective-permute-start.19 = (f32[8,512]{1,0:T(8,128)S(1)}, f32[8,512]{1,0:T(8,128)S(1)}, u32[]{:S(2)}, u32[]{:S(2)}) collective-permute-start(f32[8,512]{1,0:T(8,128)S(1)} %get-tuple-element.118), channel_id=1, source_target_pairs={{0,7},{1,2},{2,1},{3,4},{4,3},{5,6},{6,5},{7,0},{8,15},{9,10},{10,... | collective-permute-start | bytes 49160 | tf_op jit(solution)/shard_map/ppermute | solution.py:510
  40.8 0.8 %shard_map.107.q = f32[64,512]{1,0:T(8,128)S(1)} custom-call(f32[64,512]{1,0:T(8,128)S(1)} %get-tuple-element.113.v.az, f32[64,512]{1,0:T(8,128)S(1)} %get-tuple-element.114.xy, f32[64,512]{1,0:T(8,128)S(1)} %get-tuple-element.100.kz, f32[64,512]{1,0:T(8,128)S(1)} %get-tuple-element.101.diagonal, f32[256,256]{1,0:T(8,128)S(1)} %copy-done.1, ...), custom_call_target="tpu_custom_call" | custom-call | flops 1048576 | bytes 1048576 | tf_op jit(solution)/shard_map/pallas_call | solution.py:497
  41.5 0.8 %all-to-all-done.gathered = f32[32,1,128]{2,1,0:T(1,128)S(1)} async-done(((f32[32,1,128]{2,1,0:T(1,128)}), f32[32,1,128]{2,1,0:T(1,128)S(1)}, u32[]{:S(2)}, u32[]{:S(2)}) %all-to-all-start) | async-done | bytes 16416 | tf_op jit(solution)/shard_map/all_to_all | solution.py:523
  42.3 0.0 collective-permute-done.16.x0
  42.3 0.0 collective-permute-done.17.x1
  42.3 0.5 collective-permute-done.19.y1
  42.8 0.8 %shard_map.108 = (f32[64,512]{1,0:T(8,128)S(1)}, f32[64,512]{1,0:T(8,128)S(1)}, f32[8,128]{1,0:T(8,128)S(1)}, f32[64,512]{1,0:T(8,128)S(1)}, f32[64,512]{1,0:T(8...) custom-call(f32[32,1,128]{2,1,0:T(1,128)S(1)} %all-to-all-done.gathere, ...), custom_call_target="tpu_custom_call" | custom-call | tf_op jit(solution)/shard_map/pallas_call | solution.py:497
  43.7 2.5 %collective-permute-start.20 = (f32[16,512]{1,0:T(8,128)S(1)}, f32[16,512]{1,0:T(8,128)S(1)}, u32[]{:S(2)}, u32[]{:S(2)}) collective-permute-start(f32[16,512]{1,0:T(8,128)S(1)} %get-tuple-element.132), channel_id=1, source_target_pairs={{0,8},{1,9},{2,10},{3,11},{4,12},{5,13},{6,14},{7,15},{8,0},{9,1},... | collective-permute-start | bytes 98312 | tf_op jit(solution)/shard_map/ppermute | solution.py:510
  46.2 0.5 collective-permute-start.22
  46.7 2.2 %collective-permute-start.23 = (f32[16,512]{1,0:T(8,128)S(1)}, f32[16,512]{1,0:T(8,128)S(1)}, u32[]{:S(2)}, u32[]{:S(2)}) collective-permute-start(f32[16,512]{1,0:T(8,128)S(1)} %get-tuple-element.135), channel_id=1, source_target_pairs={{0,7},{1,2},{2,1},{3,4},{4,3},{5,6},{6,5},{7,0},{8,15},{9,10},{10,... | collective-permute-start | bytes 98312 | tf_op jit(solution)/shard_map/ppermute | solution.py:510
  48.9 0.9 %shard_map.109 = (f32[64,512]{1,0:T(8,128)S(1)}, f32[64,512]{1,0:T(8,128)S(1)}, f32[64,512]{1,0:T(8,128)S(1)}, f32[64,512]{1,0:T(8,128)S(1)}, f32[64,512]{1,0:T(8,128)S(1)}, /*index=5*/f32[32,1,128]{2,1,0:T(1,128)}) custom-call(f32[8,128]{1,0:T(8,128)S(1)} %get-tuple-element.119.scalars, f32[64,512]{1,0:T(8,128)S(1)} %get-tuple-element.88.b, ...), custom_call_target="tpu_custom_call" | custom-call | flops 1048576 | bytes 1048576 | tf_op jit(solution)/shard_map/pallas_call | solution.py:497
  49.9 2.5 %all-to-all-start.1 = ((f32[32,1,128]{2,1,0:T(1,128)}), f32[32,1,128]{2,1,0:T(1,128)S(1)}, u32[]{:S(2)}, u32[]{:S(2)}) async-start(f32[32,1,128]{2,1,0:T(1,128)} %get-tuple-element.121), calls=%async_computation.1 | async-start | bytes 32768 | tf_op jit(solution)/shard_map/all_to_all | solution.py:523
  52.4 1.0 %shard_map.110 = (f32[64,512]{1,0:T(8,128)S(1)}, f32[64,512]{1,0:T(8,128)S(1)}) custom-call(f32[64,512]{1,0:T(8,128)S(1)} %get-tuple-element.120.z_next.z, f32[64,512]{1,0:T(8,128)S(1)} %get-tuple-element.127.z_xy, f32[64,512]{1,0:T(8,128)S(1)} %get-tuple-element.128.aw, f32[64,512]{1,0:T(8,128)S(1)} %get-tuple-element.129.aw_xy, ...), custom_call_target="tpu_custom_call" | custom-call | flops 1048576 | bytes 1048576 | tf_op jit(solution)/shard_map/pallas_call | solution.py:497
  53.4 0.4 shard_map.111
  53.8 1.8 %collective-permute-start.24 = (f32[8,512]{1,0:T(8,128)S(1)}, f32[8,512]{1,0:T(8,128)S(1)}, u32[]{:S(2)}, u32[]{:S(2)}) collective-permute-start(f32[8,512]{1,0:T(8,128)S(1)} %get-tuple-element.139), channel_id=1, source_target_pairs={{0,8},{1,9},{2,10},{3,11},{4,12},{5,13},{6,14},{7,15},{8,0},{9,1},... | collective-permute-start | bytes 49160 | tf_op jit(solution)/shard_map/ppermute | solution.py:510
  55.6 0.5 collective-permute-start.26
  56.1 2.0 %collective-permute-start.27 = (f32[8,512]{1,0:T(8,128)S(1)}, f32[8,512]{1,0:T(8,128)S(1)}, u32[]{:S(2)}, u32[]{:S(2)}) collective-permute-start(f32[8,512]{1,0:T(8,128)S(1)} %get-tuple-element.142), channel_id=1, source_target_pairs={{0,7},{1,2},{2,1},{3,4},{4,3},{5,6},{6,5},{7,0},{8,15},{9,10},{10,... | collective-permute-start | bytes 49160 | tf_op jit(solution)/shard_map/ppermute | solution.py:510
  58.1 0.8 %shard_map.112.q = f32[64,512]{1,0:T(8,128)S(1)} custom-call(f32[64,512]{1,0:T(8,128)S(1)} %get-tuple-element.136.v.az, f32[64,512]{1,0:T(8,128)S(1)} %get-tuple-element.138.xy, f32[64,512]{1,0:T(8,128)S(1)} %get-tuple-element.100.kz, f32[64,512]{1,0:T(8,128)S(1)} %get-tuple-element.101.diagonal, f32[256,256]{1,0:T(8,128)S(1)} %copy-done.1, ...), custom_call_target="tpu_custom_call" | custom-call | flops 1048576 | bytes 1048576 | tf_op jit(solution)/shard_map/pallas_call | solution.py:497
  58.9 0.6 all-to-all-done.1.gathered
  59.5 0.7 collective-permute-done.27.y1
  60.2 0.5 shard_map.113
  60.7 11.8 %all_to_all.15.gathered = f32[32,1,128]{2,1,0:T(1,128)S(1)} all-to-all(f32[32,1,128]{2,1,0:T(1,128)S(1)} %get-tuple-element.143), channel_id=1, replica_groups=mesh['gx'=4,'gy'=8] {'gx','gy'}, dimensions={0} | all-to-all | bytes 32768 | tf_op jit(solution)/shard_map/all_to_all | solution.py:523
  72.5 0.8 %shard_map.114 = (f32[64,512]{1,0:T(8,128)}, f32[64,512]{1,0:T(8,128)}) custom-call(f32[32,1,128]{2,1,0:T(1,128)S(1)} %all_to_all.15.gathered, f32[64,512]{1,0:T(8,128)S(1)} %get-tuple-element.144.r, f32[64,512]{1,0:T(8,128)S(1)} %get-tuple-element.145.p, f32[64,512]{1,0:T(8,128)S(1)} %get-tuple-element.146.s, f32[64,512]{1,0:T(8,128)S(1)} %get-tuple-element.147.w, ...), custom_call_target="tpu_custom_call" | custom-call | tf_op jit(solution)/shard_map/pallas_call | solution.py:497
  (33 shorter events, 0.1 us)
Async XLA Ops:
  0.6 6.0 %copy-start.3 = (f32[8,8,512]{2,1,0:T(8,128)S(1)}, f32[8,8,512]{2,1,0:T(8,128)}, u32[]{:S(2)}) copy-start(f32[8,8,512]{2,1,0:T(8,128)} %param.8) | copy-start | bytes 393220
  0.6 5.9 %copy-start.4 = (f32[8,8,512]{2,1,0:T(8,128)S(1)}, f32[8,8,512]{2,1,0:T(8,128)}, u32[]{:S(2)}) copy-start(f32[8,8,512]{2,1,0:T(8,128)} %param.9) | copy-start | bytes 393220
  2.5 4.1 %copy-start.5 = (s32[1,1,64]{2,1,0:T(1,128)S(1)}, s32[1,1,64]{2,1,0:T(1,128)}, u32[]{:S(2)}) copy-start(s32[1,1,64]{2,1,0:T(1,128)} %param.10) | copy-start | bytes 772
  2.5 4.1 %copy-start.6 = (s32[1,1,64]{2,1,0:T(1,128)S(1)}, s32[1,1,64]{2,1,0:T(1,128)}, u32[]{:S(2)}) copy-start(s32[1,1,64]{2,1,0:T(1,128)} %param.11) | copy-start | bytes 772
  2.5 4.1 %copy-start.7 = (f32[4]{0:T(128)S(1)}, f32[4]{0:T(128)}, u32[]{:S(2)}) copy-start(f32[4]{0:T(128)} %param.12) | copy-start | bytes 52
  2.5 4.4 %collective-permute-start = (f32[24,512]{1,0:T(8,128)}, f32[24,512]{1,0:T(8,128)S(1)}, u32[]{:S(2)}, u32[]{:S(2)}) collective-permute-start(f32[24,512]{1,0:T(8,128)} %get-tuple-element.80), channel_id=1, source_target_pairs={{0,1},{1,0},{2,3},{3,2},{4,5},{5,4},{6,7},{7,6},{8,9},{9,8},{10,11... | collective-permute-start | bytes 147464 | tf_op jit(solution)/shard_map/ppermute | solution.py:510
  3.0 5.6 %collective-permute-start.1 = (f32[24,512]{1,0:T(8,128)}, f32[24,512]{1,0:T(8,128)S(1)}, u32[]{:S(2)}, u32[]{:S(2)}) collective-permute-start(f32[24,512]{1,0:T(8,128)} %get-tuple-element.81), channel_id=1, source_target_pairs={{0,7},{1,2},{2,1},{3,4},{4,3},{5,6},{6,5},{7,0},{8,15},{9,10},{10,... | collective-permute-start | bytes 147464 | tf_op jit(solution)/shard_map/ppermute | solution.py:510
  8.6 1.8 %copy-start.2 = (f32[8,512]{1,0:T(8,128)S(1)}, f32[8,512]{1,0:T(8,128)}, u32[]{:S(2)}) copy-start(f32[8,512]{1,0:T(8,128)} %constant.8.clone.lanes) | copy-start | bytes 49156
  8.7 4.3 %collective-permute-start.2 = (f32[32,512]{1,0:T(8,128)S(1)}, f32[32,512]{1,0:T(8,128)S(1)}, u32[]{:S(2)}, u32[]{:S(2)}) collective-permute-start(f32[32,512]{1,0:T(8,128)S(1)} %get-tuple-element.86), channel_id=1, source_target_pairs={{0,8},{1,9},{2,10},{3,11},{4,12},{5,13},{6,14},{7,15},{8,0},{9,1},... | collective-permute-start | bytes 196616 | tf_op jit(solution)/shard_map/ppermute | solution.py:510
  10.4 2.6 %collective-permute-start.3 = (f32[32,512]{1,0:T(8,128)S(1)}, f32[32,512]{1,0:T(8,128)S(1)}, u32[]{:S(2)}, u32[]{:S(2)}) collective-permute-start(f32[32,512]{1,0:T(8,128)S(1)} %get-tuple-element.87), channel_id=1, source_target_pairs={{0,1},{1,0},{2,3},{3,2},{4,5},{5,4},{6,7},{7,6},{8,16},{9,17},{10,... | collective-permute-start | bytes 196616 | tf_op jit(solution)/shard_map/ppermute | solution.py:510
  13.0 5.3 %copy-start = (f32[256,256]{1,0:T(8,128)S(1)}, f32[256,256]{1,0:T(8,128)}, u32[]{:S(2)}) copy-start(f32[256,256]{1,0:T(8,128)} %constant.7.clone.z_back) | copy-start | bytes 786436
  13.0 5.3 %copy-start.1 = (f32[256,256]{1,0:T(8,128)S(1)}, f32[256,256]{1,0:T(8,128)}, u32[]{:S(2)}) copy-start(f32[256,256]{1,0:T(8,128)} %constant.6.clone.z_forward) | copy-start | bytes 786436
  13.4 5.7 %collective-permute-start.4 = (f32[8,512]{1,0:T(8,128)S(1)}, f32[8,512]{1,0:T(8,128)S(1)}, u32[]{:S(2)}, u32[]{:S(2)}) collective-permute-start(f32[8,512]{1,0:T(8,128)S(1)} %get-tuple-element.93), channel_id=1, source_target_pairs={{0,8},{1,9},{2,10},{3,11},{4,12},{5,13},{6,14},{7,15},{8,0},{9,1},... | collective-permute-start | bytes 49160 | tf_op jit(solution)/shard_map/ppermute | solution.py:510
  16.3 2.9 %collective-permute-start.5 = (f32[8,512]{1,0:T(8,128)S(1)}, f32[8,512]{1,0:T(8,128)S(1)}, u32[]{:S(2)}, u32[]{:S(2)}) collective-permute-start(f32[8,512]{1,0:T(8,128)S(1)} %get-tuple-element.94), channel_id=1, source_target_pairs={{0,1},{1,0},{2,3},{3,2},{4,5},{5,4},{6,7},{7,6},{8,16},{9,17},{10,... | collective-permute-start | bytes 49160 | tf_op jit(solution)/shard_map/ppermute | solution.py:510
  16.3 2.9 %collective-permute-start.6 = (f32[8,512]{1,0:T(8,128)S(1)}, f32[8,512]{1,0:T(8,128)S(1)}, u32[]{:S(2)}, u32[]{:S(2)}) collective-permute-start(f32[8,512]{1,0:T(8,128)S(1)} %get-tuple-element.95), channel_id=1, source_target_pairs={{0,1},{1,0},{2,3},{3,2},{4,5},{5,4},{6,7},{7,6},{8,9},{9,8},{10,11... | collective-permute-start | bytes 49160 | tf_op jit(solution)/shard_map/ppermute | solution.py:510
  16.8 4.1 %collective-permute-start.7 = (f32[8,512]{1,0:T(8,128)S(1)}, f32[8,512]{1,0:T(8,128)S(1)}, u32[]{:S(2)}, u32[]{:S(2)}) collective-permute-start(f32[8,512]{1,0:T(8,128)S(1)} %get-tuple-element.96), channel_id=1, source_target_pairs={{0,7},{1,2},{2,1},{3,4},{4,3},{5,6},{6,5},{7,0},{8,15},{9,10},{10,... | collective-permute-start | bytes 49160 | tf_op jit(solution)/shard_map/ppermute | solution.py:510
  21.2 4.9 %collective-permute-start.8 = (f32[8,512]{1,0:T(8,128)S(1)}, f32[8,512]{1,0:T(8,128)S(1)}, u32[]{:S(2)}, u32[]{:S(2)}) collective-permute-start(f32[8,512]{1,0:T(8,128)S(1)} %get-tuple-element.102), channel_id=1, source_target_pairs={{0,8},{1,9},{2,10},{3,11},{4,12},{5,13},{6,14},{7,15},{8,0},{9,1},... | collective-permute-start | bytes 49160 | tf_op jit(solution)/shard_map/ppermute | solution.py:510
  22.9 3.3 %collective-permute-start.9 = (f32[8,512]{1,0:T(8,128)S(1)}, f32[8,512]{1,0:T(8,128)S(1)}, u32[]{:S(2)}, u32[]{:S(2)}) collective-permute-start(f32[8,512]{1,0:T(8,128)S(1)} %get-tuple-element.103), channel_id=1, source_target_pairs={{0,1},{1,0},{2,3},{3,2},{4,5},{5,4},{6,7},{7,6},{8,16},{9,17},{10,... | collective-permute-start | bytes 49160 | tf_op jit(solution)/shard_map/ppermute | solution.py:510
  22.9 3.3 %collective-permute-start.10 = (f32[8,512]{1,0:T(8,128)S(1)}, f32[8,512]{1,0:T(8,128)S(1)}, u32[]{:S(2)}, u32[]{:S(2)}) collective-permute-start(f32[8,512]{1,0:T(8,128)S(1)} %get-tuple-element.104), channel_id=1, source_target_pairs={{0,1},{1,0},{2,3},{3,2},{4,5},{5,4},{6,7},{7,6},{8,9},{9,8},{10,11... | collective-permute-start | bytes 49160 | tf_op jit(solution)/shard_map/ppermute | solution.py:510
  23.4 4.1 %collective-permute-start.11 = (f32[8,512]{1,0:T(8,128)S(1)}, f32[8,512]{1,0:T(8,128)S(1)}, u32[]{:S(2)}, u32[]{:S(2)}) collective-permute-start(f32[8,512]{1,0:T(8,128)S(1)} %get-tuple-element.105), channel_id=1, source_target_pairs={{0,7},{1,2},{2,1},{3,4},{4,3},{5,6},{6,5},{7,0},{8,15},{9,10},{10,... | collective-permute-start | bytes 49160 | tf_op jit(solution)/shard_map/ppermute | solution.py:510
  27.8 8.2 %collective-permute-start.12 = (f32[8,512]{1,0:T(8,128)S(1)}, f32[8,512]{1,0:T(8,128)S(1)}, u32[]{:S(2)}, u32[]{:S(2)}) collective-permute-start(f32[8,512]{1,0:T(8,128)S(1)} %get-tuple-element.109), channel_id=1, source_target_pairs={{0,8},{1,9},{2,10},{3,11},{4,12},{5,13},{6,14},{7,15},{8,0},{9,1},... | collective-permute-start | bytes 49160 | tf_op jit(solution)/shard_map/ppermute | solution.py:510
  29.8 6.2 %collective-permute-start.13 = (f32[8,512]{1,0:T(8,128)S(1)}, f32[8,512]{1,0:T(8,128)S(1)}, u32[]{:S(2)}, u32[]{:S(2)}) collective-permute-start(f32[8,512]{1,0:T(8,128)S(1)} %get-tuple-element.110), channel_id=1, source_target_pairs={{0,1},{1,0},{2,3},{3,2},{4,5},{5,4},{6,7},{7,6},{8,16},{9,17},{10,... | collective-permute-start | bytes 49160 | tf_op jit(solution)/shard_map/ppermute | solution.py:510
  29.8 6.2 %collective-permute-start.14 = (f32[8,512]{1,0:T(8,128)S(1)}, f32[8,512]{1,0:T(8,128)S(1)}, u32[]{:S(2)}, u32[]{:S(2)}) collective-permute-start(f32[8,512]{1,0:T(8,128)S(1)} %get-tuple-element.111), channel_id=1, source_target_pairs={{0,1},{1,0},{2,3},{3,2},{4,5},{5,4},{6,7},{7,6},{8,9},{9,8},{10,11... | collective-permute-start | bytes 49160 | tf_op jit(solution)/shard_map/ppermute | solution.py:510
  30.3 5.7 %collective-permute-start.15 = (f32[8,512]{1,0:T(8,128)S(1)}, f32[8,512]{1,0:T(8,128)S(1)}, u32[]{:S(2)}, u32[]{:S(2)}) collective-permute-start(f32[8,512]{1,0:T(8,128)S(1)} %get-tuple-element.112), channel_id=1, source_target_pairs={{0,7},{1,2},{2,1},{3,4},{4,3},{5,6},{6,5},{7,0},{8,15},{9,10},{10,... | collective-permute-start | bytes 49160 | tf_op jit(solution)/shard_map/ppermute | solution.py:510
  32.3 10.0 %all-to-all-start = ((f32[32,1,128]{2,1,0:T(1,128)}), f32[32,1,128]{2,1,0:T(1,128)S(1)}, u32[]{:S(2)}, u32[]{:S(2)}) async-start(f32[32,1,128]{2,1,0:T(1,128)} %shard_map.104), calls=%async_computation | async-start | bytes 32768 | tf_op jit(solution)/shard_map/all_to_all | solution.py:523
  36.4 5.9 %collective-permute-start.16 = (f32[8,512]{1,0:T(8,128)S(1)}, f32[8,512]{1,0:T(8,128)S(1)}, u32[]{:S(2)}, u32[]{:S(2)}) collective-permute-start(f32[8,512]{1,0:T(8,128)S(1)} %get-tuple-element.115), channel_id=1, source_target_pairs={{0,8},{1,9},{2,10},{3,11},{4,12},{5,13},{6,14},{7,15},{8,0},{9,1},... | collective-permute-start | bytes 49160 | tf_op jit(solution)/shard_map/ppermute | solution.py:510
  38.3 4.0 %collective-permute-start.17 = (f32[8,512]{1,0:T(8,128)S(1)}, f32[8,512]{1,0:T(8,128)S(1)}, u32[]{:S(2)}, u32[]{:S(2)}) collective-permute-start(f32[8,512]{1,0:T(8,128)S(1)} %get-tuple-element.116), channel_id=1, source_target_pairs={{0,1},{1,0},{2,3},{3,2},{4,5},{5,4},{6,7},{7,6},{8,16},{9,17},{10,... | collective-permute-start | bytes 49160 | tf_op jit(solution)/shard_map/ppermute | solution.py:510
  38.3 4.0 %collective-permute-start.18 = (f32[8,512]{1,0:T(8,128)S(1)}, f32[8,512]{1,0:T(8,128)S(1)}, u32[]{:S(2)}, u32[]{:S(2)}) collective-permute-start(f32[8,512]{1,0:T(8,128)S(1)} %get-tuple-element.117), channel_id=1, source_target_pairs={{0,1},{1,0},{2,3},{3,2},{4,5},{5,4},{6,7},{7,6},{8,9},{9,8},{10,11... | collective-permute-start | bytes 49160 | tf_op jit(solution)/shard_map/ppermute | solution.py:510
  38.8 4.1 %collective-permute-start.19 = (f32[8,512]{1,0:T(8,128)S(1)}, f32[8,512]{1,0:T(8,128)S(1)}, u32[]{:S(2)}, u32[]{:S(2)}) collective-permute-start(f32[8,512]{1,0:T(8,128)S(1)} %get-tuple-element.118), channel_id=1, source_target_pairs={{0,7},{1,2},{2,1},{3,4},{4,3},{5,6},{6,5},{7,0},{8,15},{9,10},{10,... | collective-permute-start | bytes 49160 | tf_op jit(solution)/shard_map/ppermute | solution.py:510
  43.7 9.7 %collective-permute-start.20 = (f32[16,512]{1,0:T(8,128)S(1)}, f32[16,512]{1,0:T(8,128)S(1)}, u32[]{:S(2)}, u32[]{:S(2)}) collective-permute-start(f32[16,512]{1,0:T(8,128)S(1)} %get-tuple-element.132), channel_id=1, source_target_pairs={{0,8},{1,9},{2,10},{3,11},{4,12},{5,13},{6,14},{7,15},{8,0},{9,1},... | collective-permute-start | bytes 98312 | tf_op jit(solution)/shard_map/ppermute | solution.py:510
  46.2 7.2 %collective-permute-start.21 = (f32[16,512]{1,0:T(8,128)S(1)}, f32[16,512]{1,0:T(8,128)S(1)}, u32[]{:S(2)}, u32[]{:S(2)}) collective-permute-start(f32[16,512]{1,0:T(8,128)S(1)} %get-tuple-element.133), channel_id=1, source_target_pairs={{0,1},{1,0},{2,3},{3,2},{4,5},{5,4},{6,7},{7,6},{8,16},{9,17},{10,... | collective-permute-start | bytes 98312 | tf_op jit(solution)/shard_map/ppermute | solution.py:510
  46.2 7.2 %collective-permute-start.22 = (f32[16,512]{1,0:T(8,128)S(1)}, f32[16,512]{1,0:T(8,128)S(1)}, u32[]{:S(2)}, u32[]{:S(2)}) collective-permute-start(f32[16,512]{1,0:T(8,128)S(1)} %get-tuple-element.134), channel_id=1, source_target_pairs={{0,1},{1,0},{2,3},{3,2},{4,5},{5,4},{6,7},{7,6},{8,9},{9,8},{10,11... | collective-permute-start | bytes 98312 | tf_op jit(solution)/shard_map/ppermute | solution.py:510
  46.7 6.7 %collective-permute-start.23 = (f32[16,512]{1,0:T(8,128)S(1)}, f32[16,512]{1,0:T(8,128)S(1)}, u32[]{:S(2)}, u32[]{:S(2)}) collective-permute-start(f32[16,512]{1,0:T(8,128)S(1)} %get-tuple-element.135), channel_id=1, source_target_pairs={{0,7},{1,2},{2,1},{3,4},{4,3},{5,6},{6,5},{7,0},{8,15},{9,10},{10,... | collective-permute-start | bytes 98312 | tf_op jit(solution)/shard_map/ppermute | solution.py:510
  49.9 9.6 %all-to-all-start.1 = ((f32[32,1,128]{2,1,0:T(1,128)}), f32[32,1,128]{2,1,0:T(1,128)S(1)}, u32[]{:S(2)}, u32[]{:S(2)}) async-start(f32[32,1,128]{2,1,0:T(1,128)} %get-tuple-element.121), calls=%async_computation.1 | async-start | bytes 32768 | tf_op jit(solution)/shard_map/all_to_all | solution.py:523
  53.8 5.6 %collective-permute-start.24 = (f32[8,512]{1,0:T(8,128)S(1)}, f32[8,512]{1,0:T(8,128)S(1)}, u32[]{:S(2)}, u32[]{:S(2)}) collective-permute-start(f32[8,512]{1,0:T(8,128)S(1)} %get-tuple-element.139), channel_id=1, source_target_pairs={{0,8},{1,9},{2,10},{3,11},{4,12},{5,13},{6,14},{7,15},{8,0},{9,1},... | collective-permute-start | bytes 49160 | tf_op jit(solution)/shard_map/ppermute | solution.py:510
  55.6 3.9 %collective-permute-start.25 = (f32[8,512]{1,0:T(8,128)S(1)}, f32[8,512]{1,0:T(8,128)S(1)}, u32[]{:S(2)}, u32[]{:S(2)}) collective-permute-start(f32[8,512]{1,0:T(8,128)S(1)} %get-tuple-element.140), channel_id=1, source_target_pairs={{0,1},{1,0},{2,3},{3,2},{4,5},{5,4},{6,7},{7,6},{8,16},{9,17},{10,... | collective-permute-start | bytes 49160 | tf_op jit(solution)/shard_map/ppermute | solution.py:510
  55.6 3.9 %collective-permute-start.26 = (f32[8,512]{1,0:T(8,128)S(1)}, f32[8,512]{1,0:T(8,128)S(1)}, u32[]{:S(2)}, u32[]{:S(2)}) collective-permute-start(f32[8,512]{1,0:T(8,128)S(1)} %get-tuple-element.141), channel_id=1, source_target_pairs={{0,1},{1,0},{2,3},{3,2},{4,5},{5,4},{6,7},{7,6},{8,9},{9,8},{10,11... | collective-permute-start | bytes 49160 | tf_op jit(solution)/shard_map/ppermute | solution.py:510
  56.1 4.1 %collective-permute-start.27 = (f32[8,512]{1,0:T(8,128)S(1)}, f32[8,512]{1,0:T(8,128)S(1)}, u32[]{:S(2)}, u32[]{:S(2)}) collective-permute-start(f32[8,512]{1,0:T(8,128)S(1)} %get-tuple-element.142), channel_id=1, source_target_pairs={{0,7},{1,2},{2,1},{3,4},{4,3},{5,6},{6,5},{7,0},{8,15},{9,10},{10,... | collective-permute-start | bytes 49160 | tf_op jit(solution)/shard_map/ppermute | solution.py:510

commit v5 on v4

--- a/solution.py
+++ b/solution.py
@@ -37,6 +37,8 @@
 VMEM = pl.BlockSpec(memory_space=pltpu.VMEM)
 HBM = pl.BlockSpec(memory_space=pl.ANY)
 COST = 1 << 20
+LANES = 128
+ORDER = (3, 0, 1, 2)
 dot = functools.partial(jnp.dot, precision=lax.Precision.HIGHEST, preferred_element_type=f32)
 
 
@@ -54,14 +56,39 @@
     return derivative.astype(np.float32)
 
 
+def pieces(v):
+    high = v.astype(jnp.bfloat16)
+    rest = v - high.astype(f32)
+    middle = rest.astype(jnp.bfloat16)
+    return high, middle, (rest - middle.astype(f32)).astype(jnp.bfloat16)
+
+
+def stacked(m):
+    high = m.astype(jnp.bfloat16).astype(np.float32)
+    middle = (m - high).astype(jnp.bfloat16).astype(np.float32)
+    low = m - high - middle
+    both = np.concatenate([high, middle], 1)
+    return [
+        jnp.asarray(np.concatenate([both, both], 0), jnp.bfloat16),
+        jnp.asarray(np.concatenate([low, high], 0), jnp.bfloat16),
+    ]
+
+
 def constants(elems_z):
-    group = min(elems_z, 32)
-    z_back = np.kron(np.eye(group, dtype=np.float32), lagrange_derivative())
+    z_back = np.kron(np.eye(LANES // N, dtype=np.float32), lagrange_derivative())
     lane = np.arange(N * elems_z)
     low = (lane % N == 0) & (lane > 0)
     high = (lane % N == N - 1) & (lane < N * elems_z - 1)
     lanes = np.stack([low, high] + [0 * lane] * 6).astype(np.float32)
-    return np.ascontiguousarray(z_back.T), z_back, lanes
+    return stacked(z_back.T) + stacked(z_back) + [jnp.asarray(lanes)]
+
+
+def times(v, first, second):
+    high, middle, low = pieces(v)
+    product = functools.partial(jnp.dot, preferred_element_type=f32)
+    large = product(jnp.concatenate([high, middle], 1), first[...])
+    small = product(jnp.concatenate([high, low], 1), second[...])
+    return (large[:, :LANES] + large[:, LANES:]) + small
 
 
 def weights_1d():
@@ -183,7 +210,7 @@
     store(wk_out, [w[a] * w_bz * v for a, v in enumerate(tiles(k))])
 
 
-def fold_y_kernel(sizes, ws, wk, robin, even, odd, even_out, odd_out):
+def fold_y_kernel(sizes, ws, wk, robin, odd, even, even_out, odd_out):
     pos = position()
     low, high = received(sizes, pos, 1, even[...], odd[...])
     row = row_index((N, ws.shape[1]))
@@ -197,7 +224,7 @@
     send(pos, 0, sides[0], sides[1], even_out, odd_out)
 
 
-def prepare_kernel(sizes, ws, wk, robin, even, odd, lanes,
+def prepare_kernel(sizes, ws, wk, robin, odd, even, lanes,
                    b_out, kx_out, ky_out, kz_out, advect_out, diagonal_out, inverse_out):
     pos = position()
     low, high = received(sizes, pos, 1, even[...], odd[...])
@@ -271,19 +298,18 @@
     send(pos, 1, low[...], high[...], sends[2], sends[3])
 
 
-def along_z(v, xy, kz, diagonal, z_forward, z_back, lanes, q_out):
-    group = z_forward.shape[0]
+def along_z(v, xy, kz, diagonal, forward_1, forward_2, back_1, back_2, lanes, q_out):
     rows, size = v.shape
-    columns = [slice(i, i + group) for i in range(0, size, group)]
-    grad = dot(jnp.concatenate([v[:, c] for c in columns], 0), z_forward[...])
+    columns = [slice(i, i + LANES) for i in range(0, size, LANES)]
+    grad = times(jnp.concatenate([v[:, c] for c in columns], 0), forward_1, forward_2)
     flux = [kz[:, c] * grad[i * rows : (i + 1) * rows] for i, c in enumerate(columns)]
-    back = dot(jnp.concatenate(flux, 0), z_back[...])
+    back = times(jnp.concatenate(flux, 0), back_1, back_2)
     back = jnp.concatenate([back[i * rows : (i + 1) * rows] for i in range(len(columns))], 1)
     q_out[...] = fold_z(back, lanes) + (xy[...] + diagonal[...] * v[...])
 
 
 def assemble(sizes, pos, q, recv):
-    x_even, x_odd, y_even, y_odd = recv
+    x_even, x_odd, y_even, y_odd = (recv[ORDER.index(i)] for i in range(4))
     x_low, x_high = received(sizes, pos, 0, x_even[...], x_odd[...])
     y_low, y_high = received(sizes, pos, 1, y_even[...], y_odd[...])
     row = row_index(y_low.shape)
@@ -293,7 +319,7 @@
     return out
 
 
-def first_kernel(sizes, b_in, kx, ky_in, advect, even, odd, lanes,
+def first_kernel(sizes, b_in, kx, ky_in, advect, odd, even, lanes,
                  b_out, ky_out, xy_out, *refs):
     pos = position()
     low, high = received(sizes, pos, 0, even[...], odd[...])
@@ -306,7 +332,7 @@
     operate(pos, b, kx, ky_out, advect, xy_out, refs[:4], *refs[4:])
 
 
-def first_z_kernel(sizes, b, xy, kz_in, diagonal_in, even, odd, z_forward, z_back, lanes,
+def first_z_kernel(sizes, b, xy, kz_in, diagonal_in, odd, even, f1, f2, b1, b2, lanes,
                    kz_out, diagonal_out, q_out):
     pos = position()
     low, high = received(sizes, pos, 0, even[...], odd[...])
@@ -316,7 +342,7 @@
         at = slice(N * a, N * a + N)
         kz_out[at, :] += side[N : 2 * N]
         diagonal_out[at, :] += fold_z(side[2 * N : 3 * N], lanes)
-    along_z(b, xy, kz_out, diagonal_out, z_forward, z_back, lanes, q_out)
+    along_z(b, xy, kz_out, diagonal_out, f1, f2, b1, b2, lanes, q_out)
 
 
 def dots_row(pairs, inverse, out):
@@ -366,8 +392,8 @@
     operate(pos, v, kx, ky, advect, xy_out, refs[:4], *refs[4:])
 
 
-def z_kernel(v, xy, kz, diagonal, z_forward, z_back, lanes, q_out):
-    along_z(v, xy, kz, diagonal, z_forward, z_back, lanes, q_out)
+def z_kernel(*refs):
+    along_z(*refs)
 
 
 def first_dots_kernel(b, s, z, inverse, row):
@@ -413,9 +439,10 @@
     dots_row(inner_pairs(*fields, tiles(z_next)), tiles(inverse), row)
 
 
-def two_z_kernel(z, z_xy, aw, aw_xy, kz, diagonal, z_forward, z_back, lanes, z_q_out, aw_q_out):
-    along_z(z, z_xy, kz, diagonal, z_forward, z_back, lanes, z_q_out)
-    along_z(aw, aw_xy, kz, diagonal, z_forward, z_back, lanes, aw_q_out)
+def two_z_kernel(z, z_xy, aw, aw_xy, *refs):
+    *shared, z_q_out, aw_q_out = refs
+    along_z(z, z_xy, *shared, z_q_out)
+    along_z(aw, aw_xy, *shared, aw_q_out)
 
 
 def apply_two_kernel(sizes, z_q, aw_q, x0, x1, y0, y1, kx, ky, advect, az_out, aaw_out, xy_out, *refs):
@@ -470,7 +497,9 @@
         (number(i, j), number(step(i), j) if 0 < i < count_x - 1 else number(i, j ^ 1)) for i, j in grid
     ]
     y_even = [(number(i, j), number(i, j ^ 1)) for i, j in grid]
-    y_odd = [(number(i, j), number(i, step(j) % count_y)) for i, j in grid]
+    y_odd = [
+        (number(i, j), number(i, step(j)) if 0 < j < count_y - 1 else number(i ^ 1, j)) for i, j in grid
+    ]
     return (x_even, x_odd), (y_even, y_odd)
 
 
@@ -478,9 +507,10 @@
     shape = source.shape
     elems_z = robin_flags.shape[2]
     rows, size = shape[0] * shape[1], shape[2]
-    assert robin_flags.shape[:2] == (1, 1) and sizes[0] % 2 == 0 and sizes[1] % 2 == 0
+    assert robin_flags.shape[:2] == (1, 1) and size % LANES == 0
+    assert sizes[0] % 2 == 0 and sizes[1] % 2 == 0
     devices = sizes[0] * sizes[1]
-    z_forward, z_back, lanes = (jnp.asarray(value) for value in constants(elems_z))
+    *z_mats, lanes = constants(elems_z)
     x_pairs, y_pairs = pairings(sizes)
 
     def struct(n=rows):
@@ -510,14 +540,14 @@
         return lax.ppermute(values, ("gx", "gy"), pairs)
 
     def exchange(pairs, even, odd):
-        odd = permute(odd, pairs[1])
-        return permute(even, pairs[0]), odd
+        return permute(odd, pairs[1]), permute(even, pairs[0])
 
     def swap(parts):
         x_odd = permute(parts[1], x_pairs[1])
         y_odd = permute(parts[3], y_pairs[1])
         x_even = permute(parts[0], x_pairs[0])
-        return x_even, x_odd, permute(parts[2], y_pairs[0]), y_odd
+        recv = x_even, x_odd, permute(parts[2], y_pairs[0]), y_odd
+        return tuple(recv[i] for i in ORDER)
 
     def spread(values):
         return lax.all_to_all(values, ("gx", "gy"), 0, 0)
@@ -550,10 +580,10 @@
     )
     kz, diagonal, q = call(
         functools.partial(first_z_kernel, sizes), [field] * 3,
-        b, xy, kz, diagonal, *recv, z_forward, z_back, lanes, cost=COST,
+        b, xy, kz, diagonal, *recv, *z_mats, lanes, cost=COST,
     )
     coefs = (kx, ky, advect)
-    z_args = (kz, diagonal, z_forward, z_back, lanes)
+    z_args = (kz, diagonal, *z_mats, lanes)
     recv = swap(parts)
 
     def apply(q, recv):

time: 73.6 us -> 69.7 us (0.947)
  starting transfers between devices: 38 us -> 32.5 us
  waiting for transfers between devices: 9.6 us -> 13.3 us
  Pallas kernels: 13 us -> 11.2 us
    ppermute x28, starting transfers between devices: 32.5 us -> 24.5 us  [permute(): return lax.ppermute(values, ('gx', 'gy'), pairs)]
    all_to_all x2, waiting for transfers between devices: 1.39 us -> 4.92 us  [spread(): return lax.all_to_all(values, ('gx', 'gy'), 0, 0)]
    all_to_all x2, starting transfers between devices: 5.5 us -> 8.02 us  [spread(): return lax.all_to_all(values, ('gx', 'gy'), 0, 0)]
    pallas_call x20, Pallas kernels: 13 us -> 11.2 us  [call(): pl.pallas_call(kernel, out_shape=outs, in_specs=specs, out_specs=[VMEM] *...]
  transfers between devices with their start and end apart: 30 -> 30, of which waited for: 8 -> 7; matrix products, arithmetic and copies ran while one was open for 0% -> 0% of each run, Pallas kernels for 11% -> 9%
where the time goes in v5:
time: 69.7 us; the launch traced here: 69.5 us
  starting transfers between devices  32.5 us (47%)
  waiting for transfers between devices  13.3 us (19%)
  blocking collectives  11.5 us (16%)
  Pallas kernels  11.2 us (16%)
  between operations  0.95 us (1%)
    ppermute x28, starting transfers between devices, permute(): return lax.ppermute(values, ('gx', 'gy'), pairs)  24.5 us
    all_to_all x1, blocking collectives, spread(): return lax.all_to_all(values, ('gx', 'gy'), 0, 0)  11.5 us
    pallas_call x20, Pallas kernels, call(): pl.pallas_call(kernel, out_shape=outs, in_specs=specs, out_specs=[VMEM] *...  11.2 us
    ppermute x28, waiting for transfers between devices, permute(): return lax.ppermute(values, ('gx', 'gy'), pairs)  8.4 us
    all_to_all x2, starting transfers between devices, spread(): return lax.all_to_all(values, ('gx', 'gy'), 0, 0)  8.02 us
    all_to_all x2, waiting for transfers between devices, spread(): return lax.all_to_all(values, ('gx', 'gy'), 0, 0)  4.92 us
  transfers between devices with their start and end apart: 30, of which 7 were waited for; matrix products, arithmetic and copies ran while one was open for 0% of the time, Pallas kernels for 9%

profile of v5, /device:TPU:0, one launch (start us, length us, event | category | flops | bytes accessed | tf_op | source)
XLA Modules:
  0.0 69.5 jit_solution(17523736810372913929)
XLA Ops:
  0.6 1.8 %shard_map.114 = (f32[24,512]{1,0:T(8,128)}, f32[24,512]{1,0:T(8,128)}) custom-call(f32[64,512]{1,0:T(8,128)} %bitcast.7, f32[64,512]{1,0:T(8,128)} %bitcast.9, s32[1,64]{1,0:T(1,128)} %bitcast.11, s32[1,64]{1,0:T(1,128)} %bitcast.13, f32[1,4]{1,0:T(1,128)} %bitcast.15), custom_call_target="tpu_custom_call" | custom-call | tf_op jit(solution)/shard_map/pallas_call | solution.py:527
  2.5 0.0 copy-start.7
  2.5 0.0 copy-start.8
  2.5 0.0 copy-start.9
  2.5 3.1 %collective-permute-start = (f32[24,512]{1,0:T(8,128)}, f32[24,512]{1,0:T(8,128)S(1)}, u32[]{:S(2)}, u32[]{:S(2)}) collective-permute-start(f32[24,512]{1,0:T(8,128)} %get-tuple-element.80), channel_id=1, source_target_pairs={{0,8},{1,2},{2,1},{3,4},{4,3},{5,6},{6,5},{7,15},{8,0},{9,10},{10,... | collective-permute-start | bytes 147464 | tf_op jit(solution)/shard_map/ppermute | solution.py:540
  5.6 0.0 collective-permute-start.1
  5.6 0.3 shard_map.113
  5.9 2.0 %collective-permute-done.odd = f32[24,512]{1,0:T(8,128)S(1)} collective-permute-done((f32[24,512]{1,0:T(8,128)}, f32[24,512]{1,0:T(8,128)S(1)}, u32[]{:S(2)}, u32[]{:S(2)}) %collective-permute-start) | collective-permute-done | bytes 49184 | tf_op jit(solution)/shard_map/ppermute | solution.py:540
  7.9 0.0 collective-permute-done.1.even
  7.9 0.1 collective-permute-start.2
  8.0 3.6 %collective-permute-start.3 = (f32[32,512]{1,0:T(8,128)S(1)}, f32[32,512]{1,0:T(8,128)S(1)}, u32[]{:S(2)}, u32[]{:S(2)}) collective-permute-start(f32[32,512]{1,0:T(8,128)S(1)} %get-tuple-element.87), channel_id=1, source_target_pairs={{0,8},{1,9},{2,10},{3,11},{4,12},{5,13},{6,14},{7,15},{8,0},{9,1},... | collective-permute-start | bytes 196616 | tf_op jit(solution)/shard_map/ppermute | solution.py:540
  11.6 0.4 shard_map.115
  12.0 1.9 %collective-permute-done.3.even = f32[32,512]{1,0:T(8,128)S(1)} collective-permute-done((f32[32,512]{1,0:T(8,128)S(1)}, f32[32,512]{1,0:T(8,128)S(1)}, u32[]{:S(2)}, u32[]{:S(2)}) %collective-permute-start.3) | collective-permute-done | bytes 65568 | tf_op jit(solution)/shard_map/ppermute | solution.py:540
  13.8 0.4 shard_map.117
  14.2 2.1 %collective-permute-start.4 = (f32[8,512]{1,0:T(8,128)S(1)}, f32[8,512]{1,0:T(8,128)S(1)}, u32[]{:S(2)}, u32[]{:S(2)}) collective-permute-start(f32[8,512]{1,0:T(8,128)S(1)} %get-tuple-element.93), channel_id=1, source_target_pairs={{0,8},{1,2},{2,1},{3,4},{4,3},{5,6},{6,5},{7,15},{8,0},{9,10},{10,... | collective-permute-start | bytes 49160 | tf_op jit(solution)/shard_map/ppermute | solution.py:540
  16.3 0.1 collective-permute-start.5
  16.4 1.3 %collective-permute-start.6 = (f32[8,512]{1,0:T(8,128)S(1)}, f32[8,512]{1,0:T(8,128)S(1)}, u32[]{:S(2)}, u32[]{:S(2)}) collective-permute-start(f32[8,512]{1,0:T(8,128)S(1)} %get-tuple-element.95), channel_id=1, source_target_pairs={{0,1},{1,0},{2,3},{3,2},{4,5},{5,4},{6,7},{7,6},{8,16},{9,17},{10,... | collective-permute-start | bytes 49160 | tf_op jit(solution)/shard_map/ppermute | solution.py:540
  17.7 0.0 collective-permute-start.7
  17.8 0.5 shard_map.118
  18.2 1.8 %collective-permute-done.5.x1 = f32[8,512]{1,0:T(8,128)S(1)} collective-permute-done((f32[8,512]{1,0:T(8,128)S(1)}, f32[8,512]{1,0:T(8,128)S(1)}, u32[]{:S(2)}, u32[]{:S(2)}) %collective-permute-start.5) | collective-permute-done | bytes 16416 | tf_op jit(solution)/shard_map/ppermute | solution.py:540
  20.1 0.0 collective-permute-done.6.y0
  20.1 0.0 collective-permute-done.7.y1
  20.1 0.4 shard_map.119
  20.5 2.1 %collective-permute-start.8 = (f32[8,512]{1,0:T(8,128)S(1)}, f32[8,512]{1,0:T(8,128)S(1)}, u32[]{:S(2)}, u32[]{:S(2)}) collective-permute-start(f32[8,512]{1,0:T(8,128)S(1)} %get-tuple-element.102), channel_id=1, source_target_pairs={{0,8},{1,2},{2,1},{3,4},{4,3},{5,6},{6,5},{7,15},{8,0},{9,10},{10,... | collective-permute-start | bytes 49160 | tf_op jit(solution)/shard_map/ppermute | solution.py:540
  22.5 0.1 collective-permute-start.9
  22.6 0.5 collective-permute-start.11
  23.1 0.4 shard_map.120.q
  23.6 0.7 collective-permute-done.8.x0
  24.3 2.0 %collective-permute-done.9.x1 = f32[8,512]{1,0:T(8,128)S(1)} collective-permute-done((f32[8,512]{1,0:T(8,128)S(1)}, f32[8,512]{1,0:T(8,128)S(1)}, u32[]{:S(2)}, u32[]{:S(2)}) %collective-permute-start.9) | collective-permute-done | bytes 16416 | tf_op jit(solution)/shard_map/ppermute | solution.py:540
  26.3 0.4 shard_map.121
  26.7 2.1 %collective-permute-start.12 = (f32[8,512]{1,0:T(8,128)S(1)}, f32[8,512]{1,0:T(8,128)S(1)}, u32[]{:S(2)}, u32[]{:S(2)}) collective-permute-start(f32[8,512]{1,0:T(8,128)S(1)} %get-tuple-element.109), channel_id=1, source_target_pairs={{0,8},{1,2},{2,1},{3,4},{4,3},{5,6},{6,5},{7,15},{8,0},{9,10},{10,... | collective-permute-start | bytes 49160 | tf_op jit(solution)/shard_map/ppermute | solution.py:540
  28.7 0.1 collective-permute-start.13
  28.8 0.0 collective-permute-start.14
  28.8 0.5 collective-permute-start.15
  29.3 0.8 %shard_map.122 = f32[32,1,128]{2,1,0:T(1,128)} custom-call(f32[64,512]{1,0:T(8,128)S(1)} %get-tuple-element.88.b, f32[64,512]{1,0:T(8,128)S(1)} %get-tuple-element.98.refs_0_.s, f32[64,512]{1,0:T(8,128)S(1)} %get-tuple-element.106.z.refs_0_, f32[64,512]{1,0:T(8,128)S(1)} %get-tuple-element.107.inverse), custom_call_target="tpu_custom_call" | custom-call | flops 1048576 | bytes 1048576 | tf_op jit(solution)/shard_map/pallas_call | solution.py:527
  30.1 3.4 %all-to-all-start = ((f32[32,1,128]{2,1,0:T(1,128)}), f32[32,1,128]{2,1,0:T(1,128)S(1)}, u32[]{:S(2)}, u32[]{:S(2)}) async-start(f32[32,1,128]{2,1,0:T(1,128)} %shard_map.122), calls=%async_computation | async-start | bytes 32768 | tf_op jit(solution)/shard_map/all_to_all | solution.py:553
  33.5 0.5 shard_map.123.q
  34.0 0.0 collective-permute-done.13.x1
  34.0 0.0 collective-permute-done.14.y0
  34.0 0.4 shard_map.124
  34.4 1.8 %collective-permute-start.16 = (f32[8,512]{1,0:T(8,128)S(1)}, f32[8,512]{1,0:T(8,128)S(1)}, u32[]{:S(2)}, u32[]{:S(2)}) collective-permute-start(f32[8,512]{1,0:T(8,128)S(1)} %get-tuple-element.115), channel_id=1, source_target_pairs={{0,8},{1,2},{2,1},{3,4},{4,3},{5,6},{6,5},{7,15},{8,0},{9,10},{10,... | collective-permute-start | bytes 49160 | tf_op jit(solution)/shard_map/ppermute | solution.py:540
  36.2 0.3 collective-permute-start.17
  36.5 1.0 %collective-permute-start.18 = (f32[8,512]{1,0:T(8,128)S(1)}, f32[8,512]{1,0:T(8,128)S(1)}, u32[]{:S(2)}, u32[]{:S(2)}) collective-permute-start(f32[8,512]{1,0:T(8,128)S(1)} %get-tuple-element.117), channel_id=1, source_target_pairs={{0,1},{1,0},{2,3},{3,2},{4,5},{5,4},{6,7},{7,6},{8,16},{9,17},{10,... | collective-permute-start | bytes 49160 | tf_op jit(solution)/shard_map/ppermute | solution.py:540
  37.5 0.4 shard_map.125.q
  38.0 2.6 %all-to-all-done.gathered = f32[32,1,128]{2,1,0:T(1,128)S(1)} async-done(((f32[32,1,128]{2,1,0:T(1,128)}), f32[32,1,128]{2,1,0:T(1,128)S(1)}, u32[]{:S(2)}, u32[]{:S(2)}) %all-to-all-start) | async-done | bytes 16416 | tf_op jit(solution)/shard_map/all_to_all | solution.py:553
  40.6 0.0 collective-permute-done.16.x0
  40.6 0.0 collective-permute-done.17.x1
  40.6 0.0 collective-permute-done.18.y0
  40.6 0.8 %shard_map.126 = (f32[64,512]{1,0:T(8,128)S(1)}, f32[64,512]{1,0:T(8,128)S(1)}, f32[8,128]{1,0:T(8,128)S(1)}, f32[64,512]{1,0:T(8,128)S(1)}, f32[64,512]{1,0:T(8...) custom-call(f32[32,1,128]{2,1,0:T(1,128)S(1)} %all-to-all-done.gathere, ...), custom_call_target="tpu_custom_call" | custom-call | tf_op jit(solution)/shard_map/pallas_call | solution.py:527
  41.4 1.4 %collective-permute-start.20 = (f32[16,512]{1,0:T(8,128)S(1)}, f32[16,512]{1,0:T(8,128)S(1)}, u32[]{:S(2)}, u32[]{:S(2)}) collective-permute-start(f32[16,512]{1,0:T(8,128)S(1)} %get-tuple-element.132), channel_id=1, source_target_pairs={{0,8},{1,2},{2,1},{3,4},{4,3},{5,6},{6,5},{7,15},{8,0},{9,10},{10,... | collective-permute-start | bytes 98312 | tf_op jit(solution)/shard_map/ppermute | solution.py:540
  42.9 0.6 collective-permute-start.21
  43.5 0.5 collective-permute-start.23
  44.0 0.9 %shard_map.127 = (f32[64,512]{1,0:T(8,128)S(1)}, f32[64,512]{1,0:T(8,128)S(1)}, f32[64,512]{1,0:T(8,128)S(1)}, f32[64,512]{1,0:T(8,128)S(1)}, f32[64,512]{1,0:T(8,128)S(1)}, /*index=5*/f32[32,1,128]{2,1,0:T(1,128)}) custom-call(f32[8,128]{1,0:T(8,128)S(1)} %get-tuple-element.119.scalars, f32[64,512]{1,0:T(8,128)S(1)} %get-tuple-element.88.b, ...), custom_call_target="tpu_custom_call" | custom-call | flops 1048576 | bytes 1048576 | tf_op jit(solution)/shard_map/pallas_call | solution.py:527
  44.9 4.6 %all-to-all-start.1 = ((f32[32,1,128]{2,1,0:T(1,128)}), f32[32,1,128]{2,1,0:T(1,128)S(1)}, u32[]{:S(2)}, u32[]{:S(2)}) async-start(f32[32,1,128]{2,1,0:T(1,128)} %get-tuple-element.121), calls=%async_computation.1 | async-start | bytes 32768 | tf_op jit(solution)/shard_map/all_to_all | solution.py:553
  49.6 0.7 shard_map.128
  50.3 0.4 shard_map.129
  50.7 1.8 %collective-permute-start.24 = (f32[8,512]{1,0:T(8,128)S(1)}, f32[8,512]{1,0:T(8,128)S(1)}, u32[]{:S(2)}, u32[]{:S(2)}) collective-permute-start(f32[8,512]{1,0:T(8,128)S(1)} %get-tuple-element.139), channel_id=1, source_target_pairs={{0,8},{1,2},{2,1},{3,4},{4,3},{5,6},{6,5},{7,15},{8,0},{9,10},{10,... | collective-permute-start | bytes 49160 | tf_op jit(solution)/shard_map/ppermute | solution.py:540
  52.6 0.3 collective-permute-start.25
  52.8 1.0 %collective-permute-start.26 = (f32[8,512]{1,0:T(8,128)S(1)}, f32[8,512]{1,0:T(8,128)S(1)}, u32[]{:S(2)}, u32[]{:S(2)}) collective-permute-start(f32[8,512]{1,0:T(8,128)S(1)} %get-tuple-element.141), channel_id=1, source_target_pairs={{0,1},{1,0},{2,3},{3,2},{4,5},{5,4},{6,7},{7,6},{8,16},{9,17},{10,... | collective-permute-start | bytes 49160 | tf_op jit(solution)/shard_map/ppermute | solution.py:540
  53.9 0.4 shard_map.130.q
  54.3 2.3 %all-to-all-done.1.gathered = f32[32,1,128]{2,1,0:T(1,128)S(1)} async-done(((f32[32,1,128]{2,1,0:T(1,128)}), f32[32,1,128]{2,1,0:T(1,128)S(1)}, u32[]{:S(2)}, u32[]{:S(2)}) %all-to-all-start.1) | async-done | bytes 16416 | tf_op jit(solution)/shard_map/all_to_all | solution.py:553
  56.7 0.5 shard_map.131
  57.2 11.5 %all_to_all.15.gathered = f32[32,1,128]{2,1,0:T(1,128)S(1)} all-to-all(f32[32,1,128]{2,1,0:T(1,128)S(1)} %get-tuple-element.143), channel_id=1, replica_groups=mesh['gx'=4,'gy'=8] {'gx','gy'}, dimensions={0} | all-to-all | bytes 32768 | tf_op jit(solution)/shard_map/all_to_all | solution.py:553
  68.7 0.8 %shard_map.132 = (f32[64,512]{1,0:T(8,128)}, f32[64,512]{1,0:T(8,128)}) custom-call(f32[32,1,128]{2,1,0:T(1,128)S(1)} %all_to_all.15.gathered, f32[64,512]{1,0:T(8,128)S(1)} %get-tuple-element.144.r, f32[64,512]{1,0:T(8,128)S(1)} %get-tuple-element.145.p, f32[64,512]{1,0:T(8,128)S(1)} %get-tuple-element.146.s, f32[64,512]{1,0:T(8,128)S(1)} %get-tuple-element.147.w, ...), custom_call_target="tpu_custom_call" | custom-call | tf_op jit(solution)/shard_map/pallas_call | solution.py:527
  (37 shorter events, 0.1 us)
Async XLA Ops:
  0.6 5.0 %copy-start.5 = (f32[8,8,512]{2,1,0:T(8,128)S(1)}, f32[8,8,512]{2,1,0:T(8,128)}, u32[]{:S(2)}) copy-start(f32[8,8,512]{2,1,0:T(8,128)} %param.10) | copy-start | bytes 393220
  0.6 5.0 %copy-start.6 = (f32[8,8,512]{2,1,0:T(8,128)S(1)}, f32[8,8,512]{2,1,0:T(8,128)}, u32[]{:S(2)}) copy-start(f32[8,8,512]{2,1,0:T(8,128)} %param.11) | copy-start | bytes 393220
  2.5 3.2 %copy-start.7 = (s32[1,1,64]{2,1,0:T(1,128)S(1)}, s32[1,1,64]{2,1,0:T(1,128)}, u32[]{:S(2)}) copy-start(s32[1,1,64]{2,1,0:T(1,128)} %param.12) | copy-start | bytes 772
  2.5 3.2 %copy-start.8 = (s32[1,1,64]{2,1,0:T(1,128)S(1)}, s32[1,1,64]{2,1,0:T(1,128)}, u32[]{:S(2)}) copy-start(s32[1,1,64]{2,1,0:T(1,128)} %param.13) | copy-start | bytes 772
  2.5 3.1 %copy-start.9 = (f32[4]{0:T(128)S(1)}, f32[4]{0:T(128)}, u32[]{:S(2)}) copy-start(f32[4]{0:T(128)} %param.14) | copy-start | bytes 52
  2.5 5.4 %collective-permute-start = (f32[24,512]{1,0:T(8,128)}, f32[24,512]{1,0:T(8,128)S(1)}, u32[]{:S(2)}, u32[]{:S(2)}) collective-permute-start(f32[24,512]{1,0:T(8,128)} %get-tuple-element.80), channel_id=1, source_target_pairs={{0,8},{1,2},{2,1},{3,4},{4,3},{5,6},{6,5},{7,15},{8,0},{9,10},{10,... | collective-permute-start | bytes 147464 | tf_op jit(solution)/shard_map/ppermute | solution.py:540
  5.6 2.3 %collective-permute-start.1 = (f32[24,512]{1,0:T(8,128)}, f32[24,512]{1,0:T(8,128)S(1)}, u32[]{:S(2)}, u32[]{:S(2)}) collective-permute-start(f32[24,512]{1,0:T(8,128)} %get-tuple-element.81), channel_id=1, source_target_pairs={{0,1},{1,0},{2,3},{3,2},{4,5},{5,4},{6,7},{7,6},{8,9},{9,8},{10,11... | collective-permute-start | bytes 147464 | tf_op jit(solution)/shard_map/ppermute | solution.py:540
  7.9 3.7 %copy-start.4 = (f32[8,512]{1,0:T(8,128)S(1)}, f32[8,512]{1,0:T(8,128)}, u32[]{:S(2)}) copy-start(f32[8,512]{1,0:T(8,128)} %constant.14.clone.lanes.refs_8_.refs_6_) | copy-start | bytes 49156
  7.9 4.0 %collective-permute-start.2 = (f32[32,512]{1,0:T(8,128)S(1)}, f32[32,512]{1,0:T(8,128)S(1)}, u32[]{:S(2)}, u32[]{:S(2)}) collective-permute-start(f32[32,512]{1,0:T(8,128)S(1)} %get-tuple-element.86), channel_id=1, source_target_pairs={{0,1},{1,0},{2,3},{3,2},{4,5},{5,4},{6,7},{7,6},{8,16},{9,17},{10,... | collective-permute-start | bytes 196616 | tf_op jit(solution)/shard_map/ppermute | solution.py:540
  8.0 5.8 %collective-permute-start.3 = (f32[32,512]{1,0:T(8,128)S(1)}, f32[32,512]{1,0:T(8,128)S(1)}, u32[]{:S(2)}, u32[]{:S(2)}) collective-permute-start(f32[32,512]{1,0:T(8,128)S(1)} %get-tuple-element.87), channel_id=1, source_target_pairs={{0,8},{1,9},{2,10},{3,11},{4,12},{5,13},{6,14},{7,15},{8,0},{9,1},... | collective-permute-start | bytes 196616 | tf_op jit(solution)/shard_map/ppermute | solution.py:540
  13.8 3.9 %copy-start = (bf16[256,256]{1,0:T(8,128)(2,1)S(1)}, bf16[256,256]{1,0:T(8,128)(2,1)}, u32[]{:S(2)}) copy-start(bf16[256,256]{1,0:T(8,128)(2,1)} %constant.12.clone.b1.refs_6_.refs_4_) | copy-start | bytes 393220
  13.8 3.9 %copy-start.1 = (bf16[256,256]{1,0:T(8,128)(2,1)S(1)}, bf16[256,256]{1,0:T(8,128)(2,1)}, u32[]{:S(2)}) copy-start(bf16[256,256]{1,0:T(8,128)(2,1)} %constant.10.clone.f1.refs_4_.refs_2_) | copy-start | bytes 393220
  13.8 3.9 %copy-start.2 = (bf16[256,128]{1,0:T(8,128)(2,1)S(1)}, bf16[256,128]{1,0:T(8,128)(2,1)}, u32[]{:S(2)}) copy-start(bf16[256,128]{1,0:T(8,128)(2,1)} %constant.13.clone.b2.refs_7_.refs_5_) | copy-start | bytes 196612
  13.8 3.9 %copy-start.3 = (bf16[256,128]{1,0:T(8,128)(2,1)S(1)}, bf16[256,128]{1,0:T(8,128)(2,1)}, u32[]{:S(2)}) copy-start(bf16[256,128]{1,0:T(8,128)(2,1)} %constant.11.clone.f2.refs_5_.refs_3_) | copy-start | bytes 196612
  14.2 4.0 %collective-permute-start.4 = (f32[8,512]{1,0:T(8,128)S(1)}, f32[8,512]{1,0:T(8,128)S(1)}, u32[]{:S(2)}, u32[]{:S(2)}) collective-permute-start(f32[8,512]{1,0:T(8,128)S(1)} %get-tuple-element.93), channel_id=1, source_target_pairs={{0,8},{1,2},{2,1},{3,4},{4,3},{5,6},{6,5},{7,15},{8,0},{9,10},{10,... | collective-permute-start | bytes 49160 | tf_op jit(solution)/shard_map/ppermute | solution.py:540
  16.3 3.7 %collective-permute-start.5 = (f32[8,512]{1,0:T(8,128)S(1)}, f32[8,512]{1,0:T(8,128)S(1)}, u32[]{:S(2)}, u32[]{:S(2)}) collective-permute-start(f32[8,512]{1,0:T(8,128)S(1)} %get-tuple-element.94), channel_id=1, source_target_pairs={{0,8},{1,9},{2,10},{3,11},{4,12},{5,13},{6,14},{7,15},{8,0},{9,1},... | collective-permute-start | bytes 49160 | tf_op jit(solution)/shard_map/ppermute | solution.py:540
  16.4 3.7 %collective-permute-start.6 = (f32[8,512]{1,0:T(8,128)S(1)}, f32[8,512]{1,0:T(8,128)S(1)}, u32[]{:S(2)}, u32[]{:S(2)}) collective-permute-start(f32[8,512]{1,0:T(8,128)S(1)} %get-tuple-element.95), channel_id=1, source_target_pairs={{0,1},{1,0},{2,3},{3,2},{4,5},{5,4},{6,7},{7,6},{8,16},{9,17},{10,... | collective-permute-start | bytes 49160 | tf_op jit(solution)/shard_map/ppermute | solution.py:540
  17.7 2.3 %collective-permute-start.7 = (f32[8,512]{1,0:T(8,128)S(1)}, f32[8,512]{1,0:T(8,128)S(1)}, u32[]{:S(2)}, u32[]{:S(2)}) collective-permute-start(f32[8,512]{1,0:T(8,128)S(1)} %get-tuple-element.96), channel_id=1, source_target_pairs={{0,1},{1,0},{2,3},{3,2},{4,5},{5,4},{6,7},{7,6},{8,9},{9,8},{10,11... | collective-permute-start | bytes 49160 | tf_op jit(solution)/shard_map/ppermute | solution.py:540
  20.5 3.8 %collective-permute-start.8 = (f32[8,512]{1,0:T(8,128)S(1)}, f32[8,512]{1,0:T(8,128)S(1)}, u32[]{:S(2)}, u32[]{:S(2)}) collective-permute-start(f32[8,512]{1,0:T(8,128)S(1)} %get-tuple-element.102), channel_id=1, source_target_pairs={{0,8},{1,2},{2,1},{3,4},{4,3},{5,6},{6,5},{7,15},{8,0},{9,10},{10,... | collective-permute-start | bytes 49160 | tf_op jit(solution)/shard_map/ppermute | solution.py:540
  22.5 3.7 %collective-permute-start.9 = (f32[8,512]{1,0:T(8,128)S(1)}, f32[8,512]{1,0:T(8,128)S(1)}, u32[]{:S(2)}, u32[]{:S(2)}) collective-permute-start(f32[8,512]{1,0:T(8,128)S(1)} %get-tuple-element.103), channel_id=1, source_target_pairs={{0,8},{1,9},{2,10},{3,11},{4,12},{5,13},{6,14},{7,15},{8,0},{9,1},... | collective-permute-start | bytes 49160 | tf_op jit(solution)/shard_map/ppermute | solution.py:540
  22.6 3.7 %collective-permute-start.10 = (f32[8,512]{1,0:T(8,128)S(1)}, f32[8,512]{1,0:T(8,128)S(1)}, u32[]{:S(2)}, u32[]{:S(2)}) collective-permute-start(f32[8,512]{1,0:T(8,128)S(1)} %get-tuple-element.104), channel_id=1, source_target_pairs={{0,1},{1,0},{2,3},{3,2},{4,5},{5,4},{6,7},{7,6},{8,16},{9,17},{10,... | collective-permute-start | bytes 49160 | tf_op jit(solution)/shard_map/ppermute | solution.py:540
  22.6 3.7 %collective-permute-start.11 = (f32[8,512]{1,0:T(8,128)S(1)}, f32[8,512]{1,0:T(8,128)S(1)}, u32[]{:S(2)}, u32[]{:S(2)}) collective-permute-start(f32[8,512]{1,0:T(8,128)S(1)} %get-tuple-element.105), channel_id=1, source_target_pairs={{0,1},{1,0},{2,3},{3,2},{4,5},{5,4},{6,7},{7,6},{8,9},{9,8},{10,11... | collective-permute-start | bytes 49160 | tf_op jit(solution)/shard_map/ppermute | solution.py:540
  26.7 7.3 %collective-permute-start.12 = (f32[8,512]{1,0:T(8,128)S(1)}, f32[8,512]{1,0:T(8,128)S(1)}, u32[]{:S(2)}, u32[]{:S(2)}) collective-permute-start(f32[8,512]{1,0:T(8,128)S(1)} %get-tuple-element.109), channel_id=1, source_target_pairs={{0,8},{1,2},{2,1},{3,4},{4,3},{5,6},{6,5},{7,15},{8,0},{9,10},{10,... | collective-permute-start | bytes 49160 | tf_op jit(solution)/shard_map/ppermute | solution.py:540
  28.7 5.2 %collective-permute-start.13 = (f32[8,512]{1,0:T(8,128)S(1)}, f32[8,512]{1,0:T(8,128)S(1)}, u32[]{:S(2)}, u32[]{:S(2)}) collective-permute-start(f32[8,512]{1,0:T(8,128)S(1)} %get-tuple-element.110), channel_id=1, source_target_pairs={{0,8},{1,9},{2,10},{3,11},{4,12},{5,13},{6,14},{7,15},{8,0},{9,1},... | collective-permute-start | bytes 49160 | tf_op jit(solution)/shard_map/ppermute | solution.py:540
  28.8 5.2 %collective-permute-start.14 = (f32[8,512]{1,0:T(8,128)S(1)}, f32[8,512]{1,0:T(8,128)S(1)}, u32[]{:S(2)}, u32[]{:S(2)}) collective-permute-start(f32[8,512]{1,0:T(8,128)S(1)} %get-tuple-element.111), channel_id=1, source_target_pairs={{0,1},{1,0},{2,3},{3,2},{4,5},{5,4},{6,7},{7,6},{8,16},{9,17},{10,... | collective-permute-start | bytes 49160 | tf_op jit(solution)/shard_map/ppermute | solution.py:540
  28.8 5.2 %collective-permute-start.15 = (f32[8,512]{1,0:T(8,128)S(1)}, f32[8,512]{1,0:T(8,128)S(1)}, u32[]{:S(2)}, u32[]{:S(2)}) collective-permute-start(f32[8,512]{1,0:T(8,128)S(1)} %get-tuple-element.112), channel_id=1, source_target_pairs={{0,1},{1,0},{2,3},{3,2},{4,5},{5,4},{6,7},{7,6},{8,9},{9,8},{10,11... | collective-permute-start | bytes 49160 | tf_op jit(solution)/shard_map/ppermute | solution.py:540
  30.1 10.5 %all-to-all-start = ((f32[32,1,128]{2,1,0:T(1,128)}), f32[32,1,128]{2,1,0:T(1,128)S(1)}, u32[]{:S(2)}, u32[]{:S(2)}) async-start(f32[32,1,128]{2,1,0:T(1,128)} %shard_map.122), calls=%async_computation | async-start | bytes 32768 | tf_op jit(solution)/shard_map/all_to_all | solution.py:553
  34.4 6.2 %collective-permute-start.16 = (f32[8,512]{1,0:T(8,128)S(1)}, f32[8,512]{1,0:T(8,128)S(1)}, u32[]{:S(2)}, u32[]{:S(2)}) collective-permute-start(f32[8,512]{1,0:T(8,128)S(1)} %get-tuple-element.115), channel_id=1, source_target_pairs={{0,8},{1,2},{2,1},{3,4},{4,3},{5,6},{6,5},{7,15},{8,0},{9,10},{10,... | collective-permute-start | bytes 49160 | tf_op jit(solution)/shard_map/ppermute | solution.py:540
  36.2 4.4 %collective-permute-start.17 = (f32[8,512]{1,0:T(8,128)S(1)}, f32[8,512]{1,0:T(8,128)S(1)}, u32[]{:S(2)}, u32[]{:S(2)}) collective-permute-start(f32[8,512]{1,0:T(8,128)S(1)} %get-tuple-element.116), channel_id=1, source_target_pairs={{0,8},{1,9},{2,10},{3,11},{4,12},{5,13},{6,14},{7,15},{8,0},{9,1},... | collective-permute-start | bytes 49160 | tf_op jit(solution)/shard_map/ppermute | solution.py:540
  36.5 4.1 %collective-permute-start.18 = (f32[8,512]{1,0:T(8,128)S(1)}, f32[8,512]{1,0:T(8,128)S(1)}, u32[]{:S(2)}, u32[]{:S(2)}) collective-permute-start(f32[8,512]{1,0:T(8,128)S(1)} %get-tuple-element.117), channel_id=1, source_target_pairs={{0,1},{1,0},{2,3},{3,2},{4,5},{5,4},{6,7},{7,6},{8,16},{9,17},{10,... | collective-permute-start | bytes 49160 | tf_op jit(solution)/shard_map/ppermute | solution.py:540
  37.5 3.1 %collective-permute-start.19 = (f32[8,512]{1,0:T(8,128)S(1)}, f32[8,512]{1,0:T(8,128)S(1)}, u32[]{:S(2)}, u32[]{:S(2)}) collective-permute-start(f32[8,512]{1,0:T(8,128)S(1)} %get-tuple-element.118), channel_id=1, source_target_pairs={{0,1},{1,0},{2,3},{3,2},{4,5},{5,4},{6,7},{7,6},{8,9},{9,8},{10,11... | collective-permute-start | bytes 49160 | tf_op jit(solution)/shard_map/ppermute | solution.py:540
  41.4 8.9 %collective-permute-start.20 = (f32[16,512]{1,0:T(8,128)S(1)}, f32[16,512]{1,0:T(8,128)S(1)}, u32[]{:S(2)}, u32[]{:S(2)}) collective-permute-start(f32[16,512]{1,0:T(8,128)S(1)} %get-tuple-element.132), channel_id=1, source_target_pairs={{0,8},{1,2},{2,1},{3,4},{4,3},{5,6},{6,5},{7,15},{8,0},{9,10},{10,... | collective-permute-start | bytes 98312 | tf_op jit(solution)/shard_map/ppermute | solution.py:540
  42.9 7.4 %collective-permute-start.21 = (f32[16,512]{1,0:T(8,128)S(1)}, f32[16,512]{1,0:T(8,128)S(1)}, u32[]{:S(2)}, u32[]{:S(2)}) collective-permute-start(f32[16,512]{1,0:T(8,128)S(1)} %get-tuple-element.133), channel_id=1, source_target_pairs={{0,8},{1,9},{2,10},{3,11},{4,12},{5,13},{6,14},{7,15},{8,0},{9,1},... | collective-permute-start | bytes 98312 | tf_op jit(solution)/shard_map/ppermute | solution.py:540
  43.5 6.8 %collective-permute-start.22 = (f32[16,512]{1,0:T(8,128)S(1)}, f32[16,512]{1,0:T(8,128)S(1)}, u32[]{:S(2)}, u32[]{:S(2)}) collective-permute-start(f32[16,512]{1,0:T(8,128)S(1)} %get-tuple-element.134), channel_id=1, source_target_pairs={{0,1},{1,0},{2,3},{3,2},{4,5},{5,4},{6,7},{7,6},{8,16},{9,17},{10,... | collective-permute-start | bytes 98312 | tf_op jit(solution)/shard_map/ppermute | solution.py:540
  43.5 6.8 %collective-permute-start.23 = (f32[16,512]{1,0:T(8,128)S(1)}, f32[16,512]{1,0:T(8,128)S(1)}, u32[]{:S(2)}, u32[]{:S(2)}) collective-permute-start(f32[16,512]{1,0:T(8,128)S(1)} %get-tuple-element.135), channel_id=1, source_target_pairs={{0,1},{1,0},{2,3},{3,2},{4,5},{5,4},{6,7},{7,6},{8,9},{9,8},{10,11... | collective-permute-start | bytes 98312 | tf_op jit(solution)/shard_map/ppermute | solution.py:540
  44.9 11.7 %all-to-all-start.1 = ((f32[32,1,128]{2,1,0:T(1,128)}), f32[32,1,128]{2,1,0:T(1,128)S(1)}, u32[]{:S(2)}, u32[]{:S(2)}) async-start(f32[32,1,128]{2,1,0:T(1,128)} %get-tuple-element.121), calls=%async_computation.1 | async-start | bytes 32768 | tf_op jit(solution)/shard_map/all_to_all | solution.py:553
  50.7 5.9 %collective-permute-start.24 = (f32[8,512]{1,0:T(8,128)S(1)}, f32[8,512]{1,0:T(8,128)S(1)}, u32[]{:S(2)}, u32[]{:S(2)}) collective-permute-start(f32[8,512]{1,0:T(8,128)S(1)} %get-tuple-element.139), channel_id=1, source_target_pairs={{0,8},{1,2},{2,1},{3,4},{4,3},{5,6},{6,5},{7,15},{8,0},{9,10},{10,... | collective-permute-start | bytes 49160 | tf_op jit(solution)/shard_map/ppermute | solution.py:540
  52.6 4.1 %collective-permute-start.25 = (f32[8,512]{1,0:T(8,128)S(1)}, f32[8,512]{1,0:T(8,128)S(1)}, u32[]{:S(2)}, u32[]{:S(2)}) collective-permute-start(f32[8,512]{1,0:T(8,128)S(1)} %get-tuple-element.140), channel_id=1, source_target_pairs={{0,8},{1,9},{2,10},{3,11},{4,12},{5,13},{6,14},{7,15},{8,0},{9,1},... | collective-permute-start | bytes 49160 | tf_op jit(solution)/shard_map/ppermute | solution.py:540
  52.8 3.8 %collective-permute-start.26 = (f32[8,512]{1,0:T(8,128)S(1)}, f32[8,512]{1,0:T(8,128)S(1)}, u32[]{:S(2)}, u32[]{:S(2)}) collective-permute-start(f32[8,512]{1,0:T(8,128)S(1)} %get-tuple-element.141), channel_id=1, source_target_pairs={{0,1},{1,0},{2,3},{3,2},{4,5},{5,4},{6,7},{7,6},{8,16},{9,17},{10,... | collective-permute-start | bytes 49160 | tf_op jit(solution)/shard_map/ppermute | solution.py:540
  53.9 2.8 %collective-permute-start.27 = (f32[8,512]{1,0:T(8,128)S(1)}, f32[8,512]{1,0:T(8,128)S(1)}, u32[]{:S(2)}, u32[]{:S(2)}) collective-permute-start(f32[8,512]{1,0:T(8,128)S(1)} %get-tuple-element.142), channel_id=1, source_target_pairs={{0,1},{1,0},{2,3},{3,2},{4,5},{5,4},{6,7},{7,6},{8,9},{9,8},{10,11... | collective-permute-start | bytes 49160 | tf_op jit(solution)/shard_map/ppermute | solution.py:540

commit v6 on v5

--- a/solution.py
+++ b/solution.py
@@ -345,18 +345,21 @@
     along_z(b, xy, kz_out, diagonal_out, f1, f2, b1, b2, lanes, q_out)
 
 
-def dots_row(pairs, inverse, out):
-    width = out.shape[-1]
-    rows = []
-    for u, v in pairs:
-        product = sum(x * (y * m) for x, y, m in zip(u, v, inverse))
-        product = sum(product[:, i : i + width] for i in range(0, product.shape[1], width))
-        rows.append(jnp.sum(product, axis=0, keepdims=True))
-    rows += [jnp.zeros_like(rows[0])] * (-len(rows) % N)
-    sums = jnp.sum(jnp.concatenate(rows, 0), axis=1, keepdims=True)
-    shape = (len(rows), width)
+def dots_row(pairs, inverse, first=0):
+    shape = (N, LANES)
     lane = lax.broadcasted_iota(jnp.int32, shape, 1)
-    row = jnp.sum(jnp.where(lane == row_index(shape), sums, 0.0), axis=0, keepdims=True)
+    row = jnp.zeros(shape, f32)
+    scaled = {}
+    for i, (u, v) in enumerate(pairs):
+        if id(u) not in scaled:
+            scaled[id(u)] = [x * m for x, m in zip(u, inverse)]
+        product = sum(x * y for x, y in zip(scaled[id(u)], v))
+        product = sum(product[:, j : j + LANES] for j in range(0, product.shape[1], LANES))
+        row = jnp.where(lane == first + i, jnp.sum(product, axis=1, keepdims=True), row)
+    return jnp.sum(row, axis=0, keepdims=True)
+
+
+def for_all(row, out):
     for i in range(out.shape[0]):
         out[i] = row
 
@@ -370,14 +373,9 @@
     return jnp.concatenate([scalar] * (like.shape[1] // scalar.shape[1]), 1)
 
 
-def inner_pairs(b, r, s, w, z):
-    return [(b, r), (b, s), (b, w), (b, z), (w, r), (w, s), (r, z), (s, z), (w, w), (w, z), (z, z)]
-
-
-def steps(g):
-    br, bs, bw, bz, wr, ws, rz, sz, ww, wz, zz = g
+def steps(br, bs, bw, bz, wr, ws, zr, zs, ww, wz, zz):
     alpha = br / bs
-    omega = (wr - alpha * (ws + rz) + alpha * alpha * sz) / (
+    omega = (wr - alpha * (ws + zr) + alpha * alpha * zs) / (
         ww - 2.0 * alpha * wz + alpha * alpha * zz
     )
     rho_next = (br - alpha * bs) - omega * (bw - alpha * bz)
@@ -385,6 +383,44 @@
     return alpha, omega, beta
 
 
+def early_pairs(b, e):
+    return [(e[i], b) for i in range(6)] + [(e[i], e[j]) for i in range(6) for j in range(i, 6)]
+
+
+def late_pairs(b, e):
+    return [(e[i], b) for i in (6, 7)] + [(e[j], e[i]) for j in (6, 7) for i in range(j + 1)]
+
+
+EARLY = 27
+
+
+def last_steps(sums):
+    keys = early_pairs("b", range(6)) + late_pairs("b", range(8))
+    value = dict(zip(keys, sums))
+    g = lambda i, j: value[i, j] if (i, j) in value else value[j, i]
+    second = steps(
+        g(0, "b"), g(1, "b"), g(2, "b"), g(3, "b"),
+        g(2, 0), g(2, 1), g(3, 0), g(3, 1), g(2, 2), g(2, 3), g(3, 3),
+    )
+    alpha, omega, beta = second
+    one, cross = jnp.ones_like(alpha), alpha * omega
+    both = -alpha - beta * omega
+    r = {0: one, 1: -alpha, 2: -omega, 3: cross}
+    w = {2: one, 3: -alpha, 4: -omega, 5: cross}
+    s = {1: beta, 2: one, 3: both, 4: -omega, 5: cross}
+    z = {3: beta, 4: one, 5: both, 6: -omega, 7: cross}
+    with_b = lambda u: sum(c * g(i, "b") for i, c in u.items())
+    times = lambda u: {i: sum(c * g(i, j) for j, c in u.items()) for i in range(8)}
+    inner = lambda image, u: sum(c * image[i] for i, c in u.items())
+    gw, gz = times(w), times(z)
+    third = steps(
+        with_b(r), with_b(s), with_b(w), with_b(z),
+        inner(gw, r), inner(gw, s), inner(gz, r), inner(gz, s),
+        inner(gw, w), inner(gw, z), inner(gz, z),
+    )
+    return second, third
+
+
 def apply_kernel(sizes, q, x0, x1, y0, y1, kx, ky, advect, v_out, xy_out, *refs):
     pos = position()
     v = assemble(sizes, pos, q, (x0, x1, y0, y1))
@@ -396,16 +432,24 @@
     along_z(*refs)
 
 
-def first_dots_kernel(b, s, z, inverse, row):
-    b, s, z = tiles(b), tiles(s), tiles(z)
-    dots_row([(b, b), (b, s), (b, z), (s, s), (s, z), (z, z)], tiles(inverse), row)
+def first_dots_kernel(sizes, b, s, inverse, q, x0, x1, y0, y1, kx, ky, advect, z_out, xy_out, *refs):
+    *sends, row_out, low, high, row, sem = refs
+    pos = position()
+    z = assemble(sizes, pos, q, (x0, x1, y0, y1))
+    store(z_out, z)
+    b, s = tiles(b), tiles(s)
+    for_all(dots_row([(b, b), (b, s), (b, z), (s, s), (s, z), (z, z)], tiles(inverse)), row)
+    copy = pltpu.make_async_copy(row, row_out, sem)
+    copy.start()
+    operate(pos, z, kx, ky, advect, xy_out, sends, low, high)
+    copy.wait()
 
 
 def update_kernel(sizes, gathered, s, z, az, q, x0, x1, y0, y1, kx, ky, advect,
-                  z_out, aw_out, scalars, z_xy_out, aw_xy_out, *refs):
+                  z_out, aw_out, scalars, xy_out, *refs):
     pos = position()
     bb, bs, bz, ss, sz, zz = totals(gathered, 6)
-    values = steps((bb, bs, bs, bz, bs, ss, bz, sz, ss, sz, zz))
+    values = steps(bb, bs, bs, bz, bs, ss, bz, sz, ss, sz, zz)
     for i, value in enumerate(values):
         scalars[i : i + 1, :] = value
     alpha, omega, beta = (wide(value, s) for value in values)
@@ -415,15 +459,11 @@
     z_next = [aw[i] + beta * (z[i] - omega * az[i]) for i in range(N)]
     store(aw_out, aw)
     store(z_out, z_next)
-    sends, sides = refs[:4], refs[4:]
-    halves = [[ref.at[pl.ds(i * N, N)] for ref in sends] for i in range(2)]
-    operate(pos, z_next, kx, ky, advect, z_xy_out, halves[0], *sides)
-    operate(pos, aw, kx, ky, advect, aw_xy_out, halves[1], *sides)
-
-
-def update_rest_kernel(scalars, b, s, z, az, z_next, inverse, x_out, r_out, p_out, s_out, w_out, row):
+    operate(pos, z_next, kx, ky, advect, xy_out, refs[:4], *refs[4:])
+
+
+def update_rest_kernel(scalars, b, s, z, az, x_out, r_out, p_out, s_out, w_out):
     alpha, omega, beta = (wide(scalars[i : i + 1, :], s) for i in range(3))
-    fields = [], [], [], []
     for i in range(N):
         at = slice(N * i, N * i + N)
         b_, s_, z_, az_ = b[at, :], s[at, :], z[at, :], az[at, :]
@@ -431,60 +471,64 @@
         x_out[at, :] = alpha * b_ + omega * half
         r = half - omega * applied_half
         w = applied_half - omega * (z_ - alpha * az_)
-        s_next = w + beta * (s_ - omega * z_)
         p_out[at, :] = r + beta * (b_ - omega * s_)
-        r_out[at, :], w_out[at, :], s_out[at, :] = r, w, s_next
-        for values, value in zip(fields, (b_, r, s_next, w)):
-            values.append(value)
-    dots_row(inner_pairs(*fields, tiles(z_next)), tiles(inverse), row)
-
-
-def two_z_kernel(z, z_xy, aw, aw_xy, *refs):
-    *shared, z_q_out, aw_q_out = refs
+        r_out[at, :], w_out[at, :], s_out[at, :] = r, w, w + beta * (s_ - omega * z_)
+
+
+def two_z_kernel(z, z_xy, aw, kx, ky, advect, *refs):
+    *shared, z_q_out, aw_q_out, f0, f1, f2, f3, xy, low, high = refs
     along_z(z, z_xy, *shared, z_q_out)
-    along_z(aw, aw_xy, *shared, aw_q_out)
-
-
-def apply_two_kernel(sizes, z_q, aw_q, x0, x1, y0, y1, kx, ky, advect, az_out, aaw_out, xy_out, *refs):
+    operate(position(), tiles(aw), kx, ky, advect, xy, (f0, f1, f2, f3), low, high)
+    along_z(aw, xy, *shared, aw_q_out)
+
+
+def apply_beside_kernel(sizes, f0, f1, f2, f3, q, x0, x1, y0, y1, kx, ky, advect, v_out, xy_out, *refs):
+    sends, sides = refs[:4], refs[4:]
+    pos = position()
+    v = assemble(sizes, pos, q, (x0, x1, y0, y1))
+    store(v_out, v)
+    operate(pos, v, kx, ky, advect, xy_out, [ref.at[pl.ds(0, N)] for ref in sends], *sides)
+    for ref, face in zip(sends, (f0, f1, f2, f3)):
+        ref[N : 2 * N, :] = face[...]
+
+
+def early_dots_kernel(b, r, s, w, z, aw, az, inverse, row):
+    e = [tiles(ref) for ref in (r, s, w, z, aw, az)]
+    row[...] = dots_row(early_pairs(tiles(b), e), tiles(inverse))
+
+
+def late_dots_kernel(sizes, b, r, s, w, z, aw, az, inverse, early, aaz_q, aaw_q, x0, x1, y0, y1,
+                     aaw_out, aaz_out, row):
     pos = position()
     halves = [[ref.at[pl.ds(i * N, N)] for ref in (x0, x1, y0, y1)] for i in range(2)]
-    az = assemble(sizes, pos, z_q, halves[0])
-    store(az_out, az)
-    operate(pos, az, kx, ky, advect, xy_out, refs[:4], *refs[4:])
-    store(aaw_out, assemble(sizes, pos, aw_q, halves[1]))
-
-
-def second_kernel(sizes, gathered, b, x, r, p, s, w, z, az, aw, aaw, inverse, q, x0, x1, y0, y1,
-                  x_out, r_out, p_out, s_out, w_out, z_out, row):
-    pos = position()
-    alpha, omega, beta = (wide(value, s) for value in steps(totals(gathered, 11)))
-    aaz = assemble(sizes, pos, q, (x0, x1, y0, y1))
-    fields = [], [], [], []
+    aaz = assemble(sizes, pos, aaz_q, halves[0])
+    aaw = assemble(sizes, pos, aaw_q, halves[1])
+    store(aaz_out, aaz)
+    store(aaw_out, aaw)
+    e = [tiles(ref) for ref in (r, s, w, z, aw, az)] + [aaw, aaz]
+    for_all(early[...] + dots_row(late_pairs(tiles(b), e), tiles(inverse), EARLY), row)
+
+
+def last_kernel(gathered, x, p, r, s, w, z, aw, az, aaw, aaz, x_out, r_out):
+    second, third = last_steps(totals(gathered, EARLY + 17))
+    alpha, omega, beta = (wide(value, s) for value in second)
+    last_alpha, last_omega, _ = (wide(value, s) for value in third)
     for i in range(N):
         at = slice(N * i, N * i + N)
-        r_, s_, w_, z_, az_ = r[at, :], s[at, :], w[at, :], z[at, :], az[at, :]
-        applied_half = w_ - alpha * z_
+        p_, s_, z_, az_ = p[at, :], s[at, :], z[at, :], az[at, :]
+        half, applied_half = r[at, :] - alpha * s_, w[at, :] - alpha * z_
         applied_twice = aw[at, :] - alpha * az_
-        half = r_ - alpha * s_
         r_next = half - omega * applied_half
-        x_out[at, :] = x[at, :] + alpha * p[at, :] + omega * half
-        p_out[at, :] = r_next + beta * (p[at, :] - omega * s_)
         w_next = applied_half - omega * applied_twice
-        aw_next = applied_twice - omega * (aaw[at, :] - alpha * aaz[i])
+        aw_next = applied_twice - omega * (aaw[at, :] - alpha * aaz[at, :])
+        p_next = r_next + beta * (p_ - omega * s_)
         s_next = w_next + beta * (s_ - omega * z_)
         z_next = aw_next + beta * (z_ - omega * az_)
-        r_out[at, :], w_out[at, :], s_out[at, :], z_out[at, :] = r_next, w_next, s_next, z_next
-        for values, value in zip(fields, (r_next, s_next, w_next, z_next)):
-            values.append(value)
-    dots_row(inner_pairs(tiles(b), *fields), tiles(inverse), row)
-
-
-def last_kernel(gathered, r, p, s, w, z, x, x_out, r_out):
-    alpha, omega, _ = steps(totals(gathered, 11))
-    alpha, omega = wide(alpha, s), wide(omega, s)
-    half = r[...] - alpha * s[...]
-    x_out[...] = x[...] + alpha * p[...] + omega * half
-    r_out[...] = half - omega * (w[...] - alpha * z[...])
+        last_half = r_next - last_alpha * s_next
+        x_out[at, :] = (x[at, :] + alpha * p_ + omega * half) + (
+            last_alpha * p_next + last_omega * last_half
+        )
+        r_out[at, :] = last_half - last_omega * (w_next - last_alpha * z_next)
 
 
 def pairings(sizes):
@@ -521,14 +565,15 @@
     row = jax.ShapeDtypeStruct((devices, 1, 128), f32)
     scalars = jax.ShapeDtypeStruct((N, 128), f32)
     side = [pltpu.VMEM((N, size), f32)] * 2
-
-    def call(kernel, outs, *operands, scratch=(), hbm=0, limit=32, cost=0):
+    row_side = [pltpu.VMEM(row.shape, f32), pltpu.SemaphoreType.DMA]
+
+    def call(kernel, outs, *operands, scratch=(), hbm=0, limit=32, cost=0, hbm_out=0):
         specs = [HBM] * hbm + [VMEM] * (len(operands) - hbm)
         return pl.pallas_call(
             kernel,
             out_shape=outs,
             in_specs=specs,
-            out_specs=[VMEM] * len(outs),
+            out_specs=[VMEM] * (len(outs) - hbm_out) + [HBM] * hbm_out,
             scratch_shapes=list(scratch),
             compiler_params=pltpu.CompilerParams(vmem_limit_bytes=limit * 1024 * 1024),
             cost_estimate=pl.CostEstimate(flops=cost, bytes_accessed=cost, transcendentals=0)
@@ -595,33 +640,42 @@
         return v, q, recv
 
     s, q, recv = apply(q, recv)
-    z, q, recv = apply(q, recv)
-    (products,) = call(first_dots_kernel, [row], b, s, z, inverse, cost=COST)
+    z, xy, *parts, products = call(
+        functools.partial(first_dots_kernel, sizes), [field] * 2 + faces + [row],
+        b, s, inverse, q, *recv, *coefs, scratch=side + row_side, hbm_out=1,
+    )
     gathered = spread(products)
+    recv = swap(parts)
+    (q,) = call(z_kernel, [field], z, xy, *z_args, cost=COST)
     az, q, recv = apply(q, recv)
-    z_next, aw, values, z_xy, aw_xy, *parts = call(
+    z_next, aw, values, z_xy, *parts = call(
         functools.partial(update_kernel, sizes),
-        [field] * 2 + [scalars] + [field] * 2 + [struct(2 * N)] * 4,
+        [field] * 2 + [scalars] + [field] + faces,
         gathered, s, z, az, q, *recv, *coefs, scratch=side,
     )
     recv = swap(parts)
-    x, r, p, s, w, products = call(
-        update_rest_kernel, [field] * 5 + [row], values, b, s, z, az, z_next, inverse, cost=COST
-    )
-    gathered = spread(products)
+    x, r, p, s, w = call(update_rest_kernel, [field] * 5, values, b, s, z, az, cost=COST)
     z = z_next
-    z_q, aw_q = call(two_z_kernel, [field] * 2, z, z_xy, aw, aw_xy, *z_args, cost=COST)
-    az, aaw, xy, *parts = call(
-        functools.partial(apply_two_kernel, sizes), [field] * 3 + faces,
-        z_q, aw_q, *recv, *coefs, scratch=side,
+    z_q, aw_q, *aw_parts = call(
+        two_z_kernel, [field] * 2 + faces, z, z_xy, aw, *coefs, *z_args,
+        cost=COST, scratch=[pltpu.VMEM((rows, size), f32)] + side,
+    )
+    az, xy, *parts = call(
+        functools.partial(apply_beside_kernel, sizes), [field] * 2 + [struct(2 * N)] * 4,
+        *aw_parts, z_q, *recv, *coefs, scratch=side,
     )
     recv = swap(parts)
     (q,) = call(z_kernel, [field], az, xy, *z_args, cost=COST)
-    x, r, p, s, w, z, products = call(
-        functools.partial(second_kernel, sizes), [field] * 6 + [row],
-        gathered, b, x, r, p, s, w, z, az, aw, aaw, inverse, q, *recv,
-    )
-    x, r = call(last_kernel, [field] * 2, spread(products), r, p, s, w, z, x)
+    (early,) = call(
+        early_dots_kernel, [jax.ShapeDtypeStruct((1, LANES), f32)], b, r, s, w, z, aw, az, inverse, cost=COST
+    )
+    aaw, aaz, products = call(
+        functools.partial(late_dots_kernel, sizes), [field] * 2 + [row],
+        b, r, s, w, z, aw, az, inverse, early, q, aw_q, *recv,
+    )
+    x, r = call(
+        last_kernel, [field] * 2, spread(products), x, p, r, s, w, z, aw, az, aaw, aaz
+    )
     return x.reshape(shape), r.reshape(shape)
 
 

time: 69.7 us -> 64.1 us (0.920)
  starting transfers between devices: 32.5 us -> 26.8 us
  waiting for transfers between devices: 13.3 us -> 15.5 us
  blocking collectives: 11.5 us -> 10.2 us
  Pallas kernels: 11.2 us -> 10.4 us
    all_to_all x2 -> x1, starting transfers between devices: 8.02 us -> 2.84 us  [spread(): return lax.all_to_all(values, ('gx', 'gy'), 0, 0)]
    ppermute x28, waiting for transfers between devices: 8.4 us -> 13 us  [permute(): return lax.ppermute(values, ('gx', 'gy'), pairs)]
    all_to_all x2 -> x1, waiting for transfers between devices: 4.92 us -> 2.59 us  [spread(): return lax.all_to_all(values, ('gx', 'gy'), 0, 0)]
    all_to_all x1, blocking collectives: 11.5 us -> 10.2 us  [spread(): return lax.all_to_all(values, ('gx', 'gy'), 0, 0)]
    pallas_call x20, Pallas kernels: 11.2 us -> 10.4 us  [call(): pl.pallas_call(kernel, out_shape=outs, in_specs=specs, out_specs=[VMEM] *...]
  transfers between devices with their start and end apart: 30 -> 29, of which waited for: 7 -> 10; matrix products, arithmetic and copies ran while one was open for 0% -> 0% of each run, Pallas kernels for 9% -> 7%
where the time goes in v6:
time: 64.1 us; the launch traced here: 63.9 us
  starting transfers between devices  26.8 us (42%)
  waiting for transfers between devices  15.5 us (24%)
  Pallas kernels  10.4 us (16%)
  blocking collectives  10.2 us (16%)
  between operations  0.91 us (1%)
    ppermute x28, starting transfers between devices, permute(): return lax.ppermute(values, ('gx', 'gy'), pairs)  23.9 us
    ppermute x28, waiting for transfers between devices, permute(): return lax.ppermute(values, ('gx', 'gy'), pairs)  13 us
    pallas_call x20, Pallas kernels, call(): pl.pallas_call(kernel, out_shape=outs, in_specs=specs, out_specs=[VMEM] *...  10.4 us
    all_to_all x1, blocking collectives, spread(): return lax.all_to_all(values, ('gx', 'gy'), 0, 0)  10.2 us
    all_to_all x1, starting transfers between devices, spread(): return lax.all_to_all(values, ('gx', 'gy'), 0, 0)  2.84 us
    all_to_all x1, waiting for transfers between devices, spread(): return lax.all_to_all(values, ('gx', 'gy'), 0, 0)  2.59 us
  transfers between devices with their start and end apart: 29, of which 10 were waited for; matrix products, arithmetic and copies ran while one was open for 0% of the time, Pallas kernels for 7%

profile of v6, /device:TPU:0, one launch (start us, length us, event | category | flops | bytes accessed | tf_op | source)
XLA Modules:
  0.0 63.9 jit_solution(11620564060448985649)
XLA Ops:
  0.6 1.8 %shard_map.114 = (f32[24,512]{1,0:T(8,128)}, f32[24,512]{1,0:T(8,128)}) custom-call(f32[64,512]{1,0:T(8,128)} %bitcast.7, f32[64,512]{1,0:T(8,128)} %bitcast.9, s32[1,64]{1,0:T(1,128)} %bitcast.11, s32[1,64]{1,0:T(1,128)} %bitcast.13, f32[1,4]{1,0:T(1,128)} %bitcast.15), custom_call_target="tpu_custom_call" | custom-call | tf_op jit(solution)/shard_map/pallas_call | solution.py:572
  2.5 0.0 copy-start.7
  2.5 0.0 copy-start.8
  2.5 0.0 copy-start.9
  2.5 3.1 %collective-permute-start = (f32[24,512]{1,0:T(8,128)}, f32[24,512]{1,0:T(8,128)S(1)}, u32[]{:S(2)}, u32[]{:S(2)}) collective-permute-start(f32[24,512]{1,0:T(8,128)} %get-tuple-element.78), channel_id=1, source_target_pairs={{0,8},{1,2},{2,1},{3,4},{4,3},{5,6},{6,5},{7,15},{8,0},{9,10},{10,... | collective-permute-start | bytes 147464 | tf_op jit(solution)/shard_map/ppermute | solution.py:585
  5.6 0.0 collective-permute-start.1
  5.6 0.3 shard_map.113
  5.9 2.0 %collective-permute-done.odd = f32[24,512]{1,0:T(8,128)S(1)} collective-permute-done((f32[24,512]{1,0:T(8,128)}, f32[24,512]{1,0:T(8,128)S(1)}, u32[]{:S(2)}, u32[]{:S(2)}) %collective-permute-start) | collective-permute-done | bytes 49184 | tf_op jit(solution)/shard_map/ppermute | solution.py:585
  7.9 0.0 collective-permute-done.1.even
  7.9 0.1 collective-permute-start.2
  8.0 3.6 %collective-permute-start.3 = (f32[32,512]{1,0:T(8,128)S(1)}, f32[32,512]{1,0:T(8,128)S(1)}, u32[]{:S(2)}, u32[]{:S(2)}) collective-permute-start(f32[32,512]{1,0:T(8,128)S(1)} %get-tuple-element.85), channel_id=1, source_target_pairs={{0,8},{1,9},{2,10},{3,11},{4,12},{5,13},{6,14},{7,15},{8,0},{9,1},... | collective-permute-start | bytes 196616 | tf_op jit(solution)/shard_map/ppermute | solution.py:585
  11.6 0.4 shard_map.115
  12.0 1.9 %collective-permute-done.3.even = f32[32,512]{1,0:T(8,128)S(1)} collective-permute-done((f32[32,512]{1,0:T(8,128)S(1)}, f32[32,512]{1,0:T(8,128)S(1)}, u32[]{:S(2)}, u32[]{:S(2)}) %collective-permute-start.3) | collective-permute-done | bytes 65568 | tf_op jit(solution)/shard_map/ppermute | solution.py:585
  13.8 0.4 shard_map.117
  14.2 2.1 %collective-permute-start.4 = (f32[8,512]{1,0:T(8,128)S(1)}, f32[8,512]{1,0:T(8,128)S(1)}, u32[]{:S(2)}, u32[]{:S(2)}) collective-permute-start(f32[8,512]{1,0:T(8,128)S(1)} %get-tuple-element.91), channel_id=1, source_target_pairs={{0,8},{1,2},{2,1},{3,4},{4,3},{5,6},{6,5},{7,15},{8,0},{9,10},{10,... | collective-permute-start | bytes 49160 | tf_op jit(solution)/shard_map/ppermute | solution.py:585
  16.3 0.1 collective-permute-start.5
  16.4 1.3 %collective-permute-start.6 = (f32[8,512]{1,0:T(8,128)S(1)}, f32[8,512]{1,0:T(8,128)S(1)}, u32[]{:S(2)}, u32[]{:S(2)}) collective-permute-start(f32[8,512]{1,0:T(8,128)S(1)} %get-tuple-element.93), channel_id=1, source_target_pairs={{0,1},{1,0},{2,3},{3,2},{4,5},{5,4},{6,7},{7,6},{8,16},{9,17},{10,... | collective-permute-start | bytes 49160 | tf_op jit(solution)/shard_map/ppermute | solution.py:585
  17.7 0.0 collective-permute-start.7
  17.8 0.5 shard_map.118
  18.2 1.8 %collective-permute-done.5.x1 = f32[8,512]{1,0:T(8,128)S(1)} collective-permute-done((f32[8,512]{1,0:T(8,128)S(1)}, f32[8,512]{1,0:T(8,128)S(1)}, u32[]{:S(2)}, u32[]{:S(2)}) %collective-permute-start.5) | collective-permute-done | bytes 16416 | tf_op jit(solution)/shard_map/ppermute | solution.py:585
  20.1 0.0 collective-permute-done.6.y0
  20.1 0.0 collective-permute-done.7.y1
  20.1 0.4 shard_map.119
  20.5 0.1 collective-permute-start.10
  20.5 0.5 collective-permute-start.11
  21.0 2.0 %collective-permute-start.8 = (f32[8,512]{1,0:T(8,128)S(1)}, f32[8,512]{1,0:T(8,128)S(1)}, u32[]{:S(2)}, u32[]{:S(2)}) collective-permute-start(f32[8,512]{1,0:T(8,128)S(1)} %get-tuple-element.101), channel_id=1, source_target_pairs={{0,8},{1,2},{2,1},{3,4},{4,3},{5,6},{6,5},{7,15},{8,0},{9,10},{10,... | collective-permute-start | bytes 49160 | tf_op jit(solution)/shard_map/ppermute | solution.py:585
  23.1 0.0 collective-permute-start.9
  23.1 0.4 shard_map.120.q
  23.5 0.0 collective-permute-done.10.y0
  23.6 1.2 %collective-permute-done.8.x0 = f32[8,512]{1,0:T(8,128)S(1)} collective-permute-done((f32[8,512]{1,0:T(8,128)S(1)}, f32[8,512]{1,0:T(8,128)S(1)}, u32[]{:S(2)}, u32[]{:S(2)}) %collective-permute-start.8) | collective-permute-done | bytes 16416 | tf_op jit(solution)/shard_map/ppermute | solution.py:585
  24.8 2.0 %collective-permute-done.9.x1 = f32[8,512]{1,0:T(8,128)S(1)} collective-permute-done((f32[8,512]{1,0:T(8,128)S(1)}, f32[8,512]{1,0:T(8,128)S(1)}, u32[]{:S(2)}, u32[]{:S(2)}) %collective-permute-start.9) | collective-permute-done | bytes 16416 | tf_op jit(solution)/shard_map/ppermute | solution.py:585
  26.8 0.8 %shard_map.121 = (f32[64,512]{1,0:T(8,128)S(1)}, f32[64,512]{1,0:T(8,128)S(1)}, f32[8,512]{1,0:T(8,128)S(1)}, f32[8,512]{1,0:T(8,128)S(1)}, f32[8,512]{1,0:T(8,1...) custom-call(f32[64,512]{1,0:T(8,128)S(1)} %get-tuple-element.86.b, f32[64,512]{1,0:T(8,128)S(1)} %get-tuple-element.96.refs_0_.s, ...), custom_call_target="tpu_custom_call" | custom-call | tf_op jit(solution)/shard_map/pallas_call | solution.py:572
  27.6 0.2 collective-permute-start.12
  27.9 1.9 %collective-permute-start.13 = (f32[8,512]{1,0:T(8,128)S(1)}, f32[8,512]{1,0:T(8,128)S(1)}, u32[]{:S(2)}, u32[]{:S(2)}) collective-permute-start(f32[8,512]{1,0:T(8,128)S(1)} %get-tuple-element.109), channel_id=1, source_target_pairs={{0,8},{1,9},{2,10},{3,11},{4,12},{5,13},{6,14},{7,15},{8,0},{9,1},... | collective-permute-start | bytes 49160 | tf_op jit(solution)/shard_map/ppermute | solution.py:585
  29.7 0.0 collective-permute-start.14
  29.7 0.5 collective-permute-start.15
  30.2 2.8 %all-to-all-start = ((f32[32,1,128]{2,1,0:T(1,128)}), f32[32,1,128]{2,1,0:T(1,128)S(1)}, u32[]{:S(2)}, u32[]{:S(2)}) async-start(f32[32,1,128]{2,1,0:T(1,128)} %get-tuple-element.105), calls=%async_computation | async-start | bytes 32768 | tf_op jit(solution)/shard_map/all_to_all | solution.py:598
  33.1 0.5 shard_map.122.q
  33.5 0.0 collective-permute-done.13.x1
  33.6 0.4 shard_map.123
  34.0 1.8 %collective-permute-start.16 = (f32[8,512]{1,0:T(8,128)S(1)}, f32[8,512]{1,0:T(8,128)S(1)}, u32[]{:S(2)}, u32[]{:S(2)}) collective-permute-start(f32[8,512]{1,0:T(8,128)S(1)} %get-tuple-element.114), channel_id=1, source_target_pairs={{0,8},{1,2},{2,1},{3,4},{4,3},{5,6},{6,5},{7,15},{8,0},{9,10},{10,... | collective-permute-start | bytes 49160 | tf_op jit(solution)/shard_map/ppermute | solution.py:585
  35.8 0.3 collective-permute-start.17
  36.1 1.0 %collective-permute-start.18 = (f32[8,512]{1,0:T(8,128)S(1)}, f32[8,512]{1,0:T(8,128)S(1)}, u32[]{:S(2)}, u32[]{:S(2)}) collective-permute-start(f32[8,512]{1,0:T(8,128)S(1)} %get-tuple-element.116), channel_id=1, source_target_pairs={{0,1},{1,0},{2,3},{3,2},{4,5},{5,4},{6,7},{7,6},{8,16},{9,17},{10,... | collective-permute-start | bytes 49160 | tf_op jit(solution)/shard_map/ppermute | solution.py:585
  37.1 0.4 shard_map.124.q
  37.6 2.6 %all-to-all-done.gathered = f32[32,1,128]{2,1,0:T(1,128)S(1)} async-done(((f32[32,1,128]{2,1,0:T(1,128)}), f32[32,1,128]{2,1,0:T(1,128)S(1)}, u32[]{:S(2)}, u32[]{:S(2)}) %all-to-all-start) | async-done | bytes 16416 | tf_op jit(solution)/shard_map/all_to_all | solution.py:598
  40.2 0.5 shard_map.125
  40.7 1.5 %collective-permute-start.20 = (f32[8,512]{1,0:T(8,128)S(1)}, f32[8,512]{1,0:T(8,128)S(1)}, u32[]{:S(2)}, u32[]{:S(2)}) collective-permute-start(f32[8,512]{1,0:T(8,128)S(1)} %get-tuple-element.130), channel_id=1, source_target_pairs={{0,8},{1,2},{2,1},{3,4},{4,3},{5,6},{6,5},{7,15},{8,0},{9,10},{10,... | collective-permute-start | bytes 49160 | tf_op jit(solution)/shard_map/ppermute | solution.py:585
  42.1 0.6 collective-permute-start.21
  42.8 0.5 collective-permute-start.23
  43.3 0.9 %shard_map.127 = (f32[64,512]{1,0:T(8,128)S(1)}, f32[64,512]{1,0:T(8,128)S(1)}, f32[8,512]{1,0:T(8,128)S(1)}, f32[8,512]{1,0:T(8,128)S(1)}, f32[8,512]{1,0:T(8,128)S(1)}, /*index=5*/f32[8,512]{1,0:T(8,128)S(1)}) custom-call(f32[64,512]{1,0:T(8,128)S(1)} %get-tuple-element.122.z, f32[64,512]{1,0:T(8,128)S(1)} %get-tuple-element.124.z_xy, ...), custom_call_target="tpu_custom_call" | custom-call | flops 1048576 | bytes 1048576 | tf_op jit(solution)/shard_map/pallas_call | solution.py:572
  44.2 0.3 collective-permute-done.20.x0
  44.5 1.4 %collective-permute-done.21.x1 = f32[8,512]{1,0:T(8,128)S(1)} collective-permute-done((f32[8,512]{1,0:T(8,128)S(1)}, f32[8,512]{1,0:T(8,128)S(1)}, u32[]{:S(2)}, u32[]{:S(2)}) %collective-permute-start.21) | collective-permute-done | bytes 16416 | tf_op jit(solution)/shard_map/ppermute | solution.py:585
  45.9 0.4 shard_map.128
  46.3 2.1 %collective-permute-start.24 = (f32[16,512]{1,0:T(8,128)S(1)}, f32[16,512]{1,0:T(8,128)S(1)}, u32[]{:S(2)}, u32[]{:S(2)}) collective-permute-start(f32[16,512]{1,0:T(8,128)S(1)} %get-tuple-element.137), channel_id=1, source_target_pairs={{0,8},{1,2},{2,1},{3,4},{4,3},{5,6},{6,5},{7,15},{8,0},{9,10},{10,... | collective-permute-start | bytes 98312 | tf_op jit(solution)/shard_map/ppermute | solution.py:585
  48.3 0.1 collective-permute-start.25
  48.4 0.5 collective-permute-start.27
  48.9 0.1 shard_map.126
  49.0 0.5 shard_map.130.aaz_q
  49.5 0.4 shard_map.129.early
  49.9 0.4 collective-permute-done.24.x0
  50.3 2.0 %collective-permute-done.25.x1 = f32[16,512]{1,0:T(8,128)S(1)} collective-permute-done((f32[16,512]{1,0:T(8,128)S(1)}, f32[16,512]{1,0:T(8,128)S(1)}, u32[]{:S(2)}, u32[]{:S(2)}) %collective-permute-start.25) | collective-permute-done | bytes 32800 | tf_op jit(solution)/shard_map/ppermute | solution.py:585
  52.3 0.3 shard_map.131
  52.6 10.2 %all_to_all.10.gathered = f32[32,1,128]{2,1,0:T(1,128)S(1)} all-to-all(f32[32,1,128]{2,1,0:T(1,128)S(1)} %get-tuple-element.141), channel_id=1, replica_groups=mesh['gx'=4,'gy'=8] {'gx','gy'}, dimensions={0} | all-to-all | bytes 32768 | tf_op jit(solution)/shard_map/all_to_all | solution.py:598
  62.9 1.0 %shard_map.132 = (f32[64,512]{1,0:T(8,128)}, f32[64,512]{1,0:T(8,128)}) custom-call(f32[32,1,128]{2,1,0:T(1,128)S(1)} %all_to_all.10.gathered, f32[64,512]{1,0:T(8,128)S(1)} %get-tuple-element.142.x, f32[64,512]{1,0:T(8,128)S(1)} %get-tuple-element.143.p, f32[64,512]{1,0:T(8,128)S(1)} %get-tuple-element.119.r, f32[64,512]{1,0:T(8,128)S(1)} %get-tuple-element.120.s, ...), custom_call_target="tpu_custom_call" | custom-call | tf_op jit(solution)/shard_map/pallas_call | solution.py:572
  (35 shorter events, 0.1 us)
Async XLA Ops:
  0.6 5.0 %copy-start.5 = (f32[8,8,512]{2,1,0:T(8,128)S(1)}, f32[8,8,512]{2,1,0:T(8,128)}, u32[]{:S(2)}) copy-start(f32[8,8,512]{2,1,0:T(8,128)} %param.10) | copy-start | bytes 393220
  0.6 5.0 %copy-start.6 = (f32[8,8,512]{2,1,0:T(8,128)S(1)}, f32[8,8,512]{2,1,0:T(8,128)}, u32[]{:S(2)}) copy-start(f32[8,8,512]{2,1,0:T(8,128)} %param.11) | copy-start | bytes 393220
  2.5 3.2 %copy-start.7 = (s32[1,1,64]{2,1,0:T(1,128)S(1)}, s32[1,1,64]{2,1,0:T(1,128)}, u32[]{:S(2)}) copy-start(s32[1,1,64]{2,1,0:T(1,128)} %param.12) | copy-start | bytes 772
  2.5 3.2 %copy-start.8 = (s32[1,1,64]{2,1,0:T(1,128)S(1)}, s32[1,1,64]{2,1,0:T(1,128)}, u32[]{:S(2)}) copy-start(s32[1,1,64]{2,1,0:T(1,128)} %param.13) | copy-start | bytes 772
  2.5 3.1 %copy-start.9 = (f32[4]{0:T(128)S(1)}, f32[4]{0:T(128)}, u32[]{:S(2)}) copy-start(f32[4]{0:T(128)} %param.14) | copy-start | bytes 52
  2.5 5.4 %collective-permute-start = (f32[24,512]{1,0:T(8,128)}, f32[24,512]{1,0:T(8,128)S(1)}, u32[]{:S(2)}, u32[]{:S(2)}) collective-permute-start(f32[24,512]{1,0:T(8,128)} %get-tuple-element.78), channel_id=1, source_target_pairs={{0,8},{1,2},{2,1},{3,4},{4,3},{5,6},{6,5},{7,15},{8,0},{9,10},{10,... | collective-permute-start | bytes 147464 | tf_op jit(solution)/shard_map/ppermute | solution.py:585
  5.6 2.3 %collective-permute-start.1 = (f32[24,512]{1,0:T(8,128)}, f32[24,512]{1,0:T(8,128)S(1)}, u32[]{:S(2)}, u32[]{:S(2)}) collective-permute-start(f32[24,512]{1,0:T(8,128)} %get-tuple-element.79), channel_id=1, source_target_pairs={{0,1},{1,0},{2,3},{3,2},{4,5},{5,4},{6,7},{7,6},{8,9},{9,8},{10,11... | collective-permute-start | bytes 147464 | tf_op jit(solution)/shard_map/ppermute | solution.py:585
  7.9 3.7 %copy-start.4 = (f32[8,512]{1,0:T(8,128)S(1)}, f32[8,512]{1,0:T(8,128)}, u32[]{:S(2)}) copy-start(f32[8,512]{1,0:T(8,128)} %constant.14.clone.lanes.refs_8_.refs_6_) | copy-start | bytes 49156
  7.9 4.0 %collective-permute-start.2 = (f32[32,512]{1,0:T(8,128)S(1)}, f32[32,512]{1,0:T(8,128)S(1)}, u32[]{:S(2)}, u32[]{:S(2)}) collective-permute-start(f32[32,512]{1,0:T(8,128)S(1)} %get-tuple-element.84), channel_id=1, source_target_pairs={{0,1},{1,0},{2,3},{3,2},{4,5},{5,4},{6,7},{7,6},{8,16},{9,17},{10,... | collective-permute-start | bytes 196616 | tf_op jit(solution)/shard_map/ppermute | solution.py:585
  8.0 5.8 %collective-permute-start.3 = (f32[32,512]{1,0:T(8,128)S(1)}, f32[32,512]{1,0:T(8,128)S(1)}, u32[]{:S(2)}, u32[]{:S(2)}) collective-permute-start(f32[32,512]{1,0:T(8,128)S(1)} %get-tuple-element.85), channel_id=1, source_target_pairs={{0,8},{1,9},{2,10},{3,11},{4,12},{5,13},{6,14},{7,15},{8,0},{9,1},... | collective-permute-start | bytes 196616 | tf_op jit(solution)/shard_map/ppermute | solution.py:585
  13.8 3.9 %copy-start = (bf16[256,256]{1,0:T(8,128)(2,1)S(1)}, bf16[256,256]{1,0:T(8,128)(2,1)}, u32[]{:S(2)}) copy-start(bf16[256,256]{1,0:T(8,128)(2,1)} %constant.10.clone.f1.refs_4_.refs_2_) | copy-start | bytes 393220
  13.8 3.9 %copy-start.1 = (bf16[256,256]{1,0:T(8,128)(2,1)S(1)}, bf16[256,256]{1,0:T(8,128)(2,1)}, u32[]{:S(2)}) copy-start(bf16[256,256]{1,0:T(8,128)(2,1)} %constant.12.clone.b1.refs_6_.refs_4_) | copy-start | bytes 393220
  13.8 3.9 %copy-start.2 = (bf16[256,128]{1,0:T(8,128)(2,1)S(1)}, bf16[256,128]{1,0:T(8,128)(2,1)}, u32[]{:S(2)}) copy-start(bf16[256,128]{1,0:T(8,128)(2,1)} %constant.11.clone.f2.refs_5_.refs_3_) | copy-start | bytes 196612
  13.8 3.9 %copy-start.3 = (bf16[256,128]{1,0:T(8,128)(2,1)S(1)}, bf16[256,128]{1,0:T(8,128)(2,1)}, u32[]{:S(2)}) copy-start(bf16[256,128]{1,0:T(8,128)(2,1)} %constant.13.clone.b2.refs_7_.refs_5_) | copy-start | bytes 196612
  14.2 4.0 %collective-permute-start.4 = (f32[8,512]{1,0:T(8,128)S(1)}, f32[8,512]{1,0:T(8,128)S(1)}, u32[]{:S(2)}, u32[]{:S(2)}) collective-permute-start(f32[8,512]{1,0:T(8,128)S(1)} %get-tuple-element.91), channel_id=1, source_target_pairs={{0,8},{1,2},{2,1},{3,4},{4,3},{5,6},{6,5},{7,15},{8,0},{9,10},{10,... | collective-permute-start | bytes 49160 | tf_op jit(solution)/shard_map/ppermute | solution.py:585
  16.3 3.7 %collective-permute-start.5 = (f32[8,512]{1,0:T(8,128)S(1)}, f32[8,512]{1,0:T(8,128)S(1)}, u32[]{:S(2)}, u32[]{:S(2)}) collective-permute-start(f32[8,512]{1,0:T(8,128)S(1)} %get-tuple-element.92), channel_id=1, source_target_pairs={{0,8},{1,9},{2,10},{3,11},{4,12},{5,13},{6,14},{7,15},{8,0},{9,1},... | collective-permute-start | bytes 49160 | tf_op jit(solution)/shard_map/ppermute | solution.py:585
  16.4 3.7 %collective-permute-start.6 = (f32[8,512]{1,0:T(8,128)S(1)}, f32[8,512]{1,0:T(8,128)S(1)}, u32[]{:S(2)}, u32[]{:S(2)}) collective-permute-start(f32[8,512]{1,0:T(8,128)S(1)} %get-tuple-element.93), channel_id=1, source_target_pairs={{0,1},{1,0},{2,3},{3,2},{4,5},{5,4},{6,7},{7,6},{8,16},{9,17},{10,... | collective-permute-start | bytes 49160 | tf_op jit(solution)/shard_map/ppermute | solution.py:585
  17.7 2.3 %collective-permute-start.7 = (f32[8,512]{1,0:T(8,128)S(1)}, f32[8,512]{1,0:T(8,128)S(1)}, u32[]{:S(2)}, u32[]{:S(2)}) collective-permute-start(f32[8,512]{1,0:T(8,128)S(1)} %get-tuple-element.94), channel_id=1, source_target_pairs={{0,1},{1,0},{2,3},{3,2},{4,5},{5,4},{6,7},{7,6},{8,9},{9,8},{10,11... | collective-permute-start | bytes 49160 | tf_op jit(solution)/shard_map/ppermute | solution.py:585
  20.5 3.1 %collective-permute-start.10 = (f32[8,512]{1,0:T(8,128)S(1)}, f32[8,512]{1,0:T(8,128)S(1)}, u32[]{:S(2)}, u32[]{:S(2)}) collective-permute-start(f32[8,512]{1,0:T(8,128)S(1)} %get-tuple-element.103), channel_id=1, source_target_pairs={{0,1},{1,0},{2,3},{3,2},{4,5},{5,4},{6,7},{7,6},{8,16},{9,17},{10,... | collective-permute-start | bytes 49160 | tf_op jit(solution)/shard_map/ppermute | solution.py:585
  20.5 3.0 %collective-permute-start.11 = (f32[8,512]{1,0:T(8,128)S(1)}, f32[8,512]{1,0:T(8,128)S(1)}, u32[]{:S(2)}, u32[]{:S(2)}) collective-permute-start(f32[8,512]{1,0:T(8,128)S(1)} %get-tuple-element.104), channel_id=1, source_target_pairs={{0,1},{1,0},{2,3},{3,2},{4,5},{5,4},{6,7},{7,6},{8,9},{9,8},{10,11... | collective-permute-start | bytes 49160 | tf_op jit(solution)/shard_map/ppermute | solution.py:585
  21.0 3.7 %collective-permute-start.8 = (f32[8,512]{1,0:T(8,128)S(1)}, f32[8,512]{1,0:T(8,128)S(1)}, u32[]{:S(2)}, u32[]{:S(2)}) collective-permute-start(f32[8,512]{1,0:T(8,128)S(1)} %get-tuple-element.101), channel_id=1, source_target_pairs={{0,8},{1,2},{2,1},{3,4},{4,3},{5,6},{6,5},{7,15},{8,0},{9,10},{10,... | collective-permute-start | bytes 49160 | tf_op jit(solution)/shard_map/ppermute | solution.py:585
  23.1 3.7 %collective-permute-start.9 = (f32[8,512]{1,0:T(8,128)S(1)}, f32[8,512]{1,0:T(8,128)S(1)}, u32[]{:S(2)}, u32[]{:S(2)}) collective-permute-start(f32[8,512]{1,0:T(8,128)S(1)} %get-tuple-element.102), channel_id=1, source_target_pairs={{0,8},{1,9},{2,10},{3,11},{4,12},{5,13},{6,14},{7,15},{8,0},{9,1},... | collective-permute-start | bytes 49160 | tf_op jit(solution)/shard_map/ppermute | solution.py:585
  27.6 5.9 %collective-permute-start.12 = (f32[8,512]{1,0:T(8,128)S(1)}, f32[8,512]{1,0:T(8,128)S(1)}, u32[]{:S(2)}, u32[]{:S(2)}) collective-permute-start(f32[8,512]{1,0:T(8,128)S(1)} %get-tuple-element.108), channel_id=1, source_target_pairs={{0,8},{1,2},{2,1},{3,4},{4,3},{5,6},{6,5},{7,15},{8,0},{9,10},{10,... | collective-permute-start | bytes 49160 | tf_op jit(solution)/shard_map/ppermute | solution.py:585
  27.9 5.7 %collective-permute-start.13 = (f32[8,512]{1,0:T(8,128)S(1)}, f32[8,512]{1,0:T(8,128)S(1)}, u32[]{:S(2)}, u32[]{:S(2)}) collective-permute-start(f32[8,512]{1,0:T(8,128)S(1)} %get-tuple-element.109), channel_id=1, source_target_pairs={{0,8},{1,9},{2,10},{3,11},{4,12},{5,13},{6,14},{7,15},{8,0},{9,1},... | collective-permute-start | bytes 49160 | tf_op jit(solution)/shard_map/ppermute | solution.py:585
  29.7 3.8 %collective-permute-start.14 = (f32[8,512]{1,0:T(8,128)S(1)}, f32[8,512]{1,0:T(8,128)S(1)}, u32[]{:S(2)}, u32[]{:S(2)}) collective-permute-start(f32[8,512]{1,0:T(8,128)S(1)} %get-tuple-element.110), channel_id=1, source_target_pairs={{0,1},{1,0},{2,3},{3,2},{4,5},{5,4},{6,7},{7,6},{8,16},{9,17},{10,... | collective-permute-start | bytes 49160 | tf_op jit(solution)/shard_map/ppermute | solution.py:585
  29.7 3.9 %collective-permute-start.15 = (f32[8,512]{1,0:T(8,128)S(1)}, f32[8,512]{1,0:T(8,128)S(1)}, u32[]{:S(2)}, u32[]{:S(2)}) collective-permute-start(f32[8,512]{1,0:T(8,128)S(1)} %get-tuple-element.111), channel_id=1, source_target_pairs={{0,1},{1,0},{2,3},{3,2},{4,5},{5,4},{6,7},{7,6},{8,9},{9,8},{10,11... | collective-permute-start | bytes 49160 | tf_op jit(solution)/shard_map/ppermute | solution.py:585
  30.2 9.9 %all-to-all-start = ((f32[32,1,128]{2,1,0:T(1,128)}), f32[32,1,128]{2,1,0:T(1,128)S(1)}, u32[]{:S(2)}, u32[]{:S(2)}) async-start(f32[32,1,128]{2,1,0:T(1,128)} %get-tuple-element.105), calls=%async_computation | async-start | bytes 32768 | tf_op jit(solution)/shard_map/all_to_all | solution.py:598
  34.0 6.2 %collective-permute-start.16 = (f32[8,512]{1,0:T(8,128)S(1)}, f32[8,512]{1,0:T(8,128)S(1)}, u32[]{:S(2)}, u32[]{:S(2)}) collective-permute-start(f32[8,512]{1,0:T(8,128)S(1)} %get-tuple-element.114), channel_id=1, source_target_pairs={{0,8},{1,2},{2,1},{3,4},{4,3},{5,6},{6,5},{7,15},{8,0},{9,10},{10,... | collective-permute-start | bytes 49160 | tf_op jit(solution)/shard_map/ppermute | solution.py:585
  35.8 4.4 %collective-permute-start.17 = (f32[8,512]{1,0:T(8,128)S(1)}, f32[8,512]{1,0:T(8,128)S(1)}, u32[]{:S(2)}, u32[]{:S(2)}) collective-permute-start(f32[8,512]{1,0:T(8,128)S(1)} %get-tuple-element.115), channel_id=1, source_target_pairs={{0,8},{1,9},{2,10},{3,11},{4,12},{5,13},{6,14},{7,15},{8,0},{9,1},... | collective-permute-start | bytes 49160 | tf_op jit(solution)/shard_map/ppermute | solution.py:585
  36.1 4.1 %collective-permute-start.18 = (f32[8,512]{1,0:T(8,128)S(1)}, f32[8,512]{1,0:T(8,128)S(1)}, u32[]{:S(2)}, u32[]{:S(2)}) collective-permute-start(f32[8,512]{1,0:T(8,128)S(1)} %get-tuple-element.116), channel_id=1, source_target_pairs={{0,1},{1,0},{2,3},{3,2},{4,5},{5,4},{6,7},{7,6},{8,16},{9,17},{10,... | collective-permute-start | bytes 49160 | tf_op jit(solution)/shard_map/ppermute | solution.py:585
  37.1 3.1 %collective-permute-start.19 = (f32[8,512]{1,0:T(8,128)S(1)}, f32[8,512]{1,0:T(8,128)S(1)}, u32[]{:S(2)}, u32[]{:S(2)}) collective-permute-start(f32[8,512]{1,0:T(8,128)S(1)} %get-tuple-element.117), channel_id=1, source_target_pairs={{0,1},{1,0},{2,3},{3,2},{4,5},{5,4},{6,7},{7,6},{8,9},{9,8},{10,11... | collective-permute-start | bytes 49160 | tf_op jit(solution)/shard_map/ppermute | solution.py:585
  40.7 3.8 %collective-permute-start.20 = (f32[8,512]{1,0:T(8,128)S(1)}, f32[8,512]{1,0:T(8,128)S(1)}, u32[]{:S(2)}, u32[]{:S(2)}) collective-permute-start(f32[8,512]{1,0:T(8,128)S(1)} %get-tuple-element.130), channel_id=1, source_target_pairs={{0,8},{1,2},{2,1},{3,4},{4,3},{5,6},{6,5},{7,15},{8,0},{9,10},{10,... | collective-permute-start | bytes 49160 | tf_op jit(solution)/shard_map/ppermute | solution.py:585
  42.1 3.7 %collective-permute-start.21 = (f32[8,512]{1,0:T(8,128)S(1)}, f32[8,512]{1,0:T(8,128)S(1)}, u32[]{:S(2)}, u32[]{:S(2)}) collective-permute-start(f32[8,512]{1,0:T(8,128)S(1)} %get-tuple-element.131), channel_id=1, source_target_pairs={{0,8},{1,9},{2,10},{3,11},{4,12},{5,13},{6,14},{7,15},{8,0},{9,1},... | collective-permute-start | bytes 49160 | tf_op jit(solution)/shard_map/ppermute | solution.py:585
  42.8 3.1 %collective-permute-start.22 = (f32[8,512]{1,0:T(8,128)S(1)}, f32[8,512]{1,0:T(8,128)S(1)}, u32[]{:S(2)}, u32[]{:S(2)}) collective-permute-start(f32[8,512]{1,0:T(8,128)S(1)} %get-tuple-element.132), channel_id=1, source_target_pairs={{0,1},{1,0},{2,3},{3,2},{4,5},{5,4},{6,7},{7,6},{8,16},{9,17},{10,... | collective-permute-start | bytes 49160 | tf_op jit(solution)/shard_map/ppermute | solution.py:585
  42.8 3.1 %collective-permute-start.23 = (f32[8,512]{1,0:T(8,128)S(1)}, f32[8,512]{1,0:T(8,128)S(1)}, u32[]{:S(2)}, u32[]{:S(2)}) collective-permute-start(f32[8,512]{1,0:T(8,128)S(1)} %get-tuple-element.133), channel_id=1, source_target_pairs={{0,1},{1,0},{2,3},{3,2},{4,5},{5,4},{6,7},{7,6},{8,9},{9,8},{10,11... | collective-permute-start | bytes 49160 | tf_op jit(solution)/shard_map/ppermute | solution.py:585
  46.3 4.0 %collective-permute-start.24 = (f32[16,512]{1,0:T(8,128)S(1)}, f32[16,512]{1,0:T(8,128)S(1)}, u32[]{:S(2)}, u32[]{:S(2)}) collective-permute-start(f32[16,512]{1,0:T(8,128)S(1)} %get-tuple-element.137), channel_id=1, source_target_pairs={{0,8},{1,2},{2,1},{3,4},{4,3},{5,6},{6,5},{7,15},{8,0},{9,10},{10,... | collective-permute-start | bytes 98312 | tf_op jit(solution)/shard_map/ppermute | solution.py:585
  48.3 3.9 %collective-permute-start.25 = (f32[16,512]{1,0:T(8,128)S(1)}, f32[16,512]{1,0:T(8,128)S(1)}, u32[]{:S(2)}, u32[]{:S(2)}) collective-permute-start(f32[16,512]{1,0:T(8,128)S(1)} %get-tuple-element.138), channel_id=1, source_target_pairs={{0,8},{1,9},{2,10},{3,11},{4,12},{5,13},{6,14},{7,15},{8,0},{9,1},... | collective-permute-start | bytes 98312 | tf_op jit(solution)/shard_map/ppermute | solution.py:585
  48.4 3.8 %collective-permute-start.26 = (f32[16,512]{1,0:T(8,128)S(1)}, f32[16,512]{1,0:T(8,128)S(1)}, u32[]{:S(2)}, u32[]{:S(2)}) collective-permute-start(f32[16,512]{1,0:T(8,128)S(1)} %get-tuple-element.139), channel_id=1, source_target_pairs={{0,1},{1,0},{2,3},{3,2},{4,5},{5,4},{6,7},{7,6},{8,16},{9,17},{10,... | collective-permute-start | bytes 98312 | tf_op jit(solution)/shard_map/ppermute | solution.py:585
  48.4 3.8 %collective-permute-start.27 = (f32[16,512]{1,0:T(8,128)S(1)}, f32[16,512]{1,0:T(8,128)S(1)}, u32[]{:S(2)}, u32[]{:S(2)}) collective-permute-start(f32[16,512]{1,0:T(8,128)S(1)} %get-tuple-element.140), channel_id=1, source_target_pairs={{0,1},{1,0},{2,3},{3,2},{4,5},{5,4},{6,7},{7,6},{8,9},{9,8},{10,11... | collective-permute-start | bytes 98312 | tf_op jit(solution)/shard_map/ppermute | solution.py:585

commit v7 on v6

--- a/solution.py
+++ b/solution.py
@@ -383,6 +383,10 @@
     return alpha, omega, beta
 
 
+def second_pairs(b, r, s, w, z):
+    return [(w, b), (w, r), (w, s), (w, w), (w, z), (r, b), (r, z)]
+
+
 def early_pairs(b, e):
     return [(e[i], b) for i in range(6)] + [(e[i], e[j]) for i in range(6) for j in range(i, 6)]
 
@@ -391,24 +395,32 @@
     return [(e[i], b) for i in (6, 7)] + [(e[j], e[i]) for j in (6, 7) for i in range(j + 1)]
 
 
-EARLY = 27
-
-
-def last_steps(sums):
-    keys = early_pairs("b", range(6)) + late_pairs("b", range(8))
-    value = dict(zip(keys, sums))
+EARLY = 34
+LATE = 17
+
+
+def guess(scalars, like):
+    omega = wide(scalars[1:2, :], like)
+    return 2.0 * omega, omega
+
+
+def last_steps(sums, guessed_omega):
+    names = second_pairs(*"brswz") + early_pairs("b", range(6)) + late_pairs("b", range(8))
+    value = dict(zip(names, sums))
     g = lambda i, j: value[i, j] if (i, j) in value else value[j, i]
     second = steps(
-        g(0, "b"), g(1, "b"), g(2, "b"), g(3, "b"),
-        g(2, 0), g(2, 1), g(3, 0), g(3, 1), g(2, 2), g(2, 3), g(3, 3),
+        g("r", "b"), g(1, "b"), g("w", "b"), g(3, "b"),
+        g("w", "r"), g("w", "s"), g("r", "z"), g(1, 3), g("w", "w"), g("w", "z"), g(3, 3),
     )
     alpha, omega, beta = second
-    one, cross = jnp.ones_like(alpha), alpha * omega
-    both = -alpha - beta * omega
-    r = {0: one, 1: -alpha, 2: -omega, 3: cross}
-    w = {2: one, 3: -alpha, 4: -omega, 5: cross}
-    s = {1: beta, 2: one, 3: both, 4: -omega, 5: cross}
-    z = {3: beta, 4: one, 5: both, 6: -omega, 7: cross}
+    off_alpha, off_omega = alpha - 2.0 * guessed_omega, omega - guessed_omega
+    ratio = off_omega / guessed_omega
+    one, cross = jnp.ones_like(alpha), off_alpha * omega
+    both = -off_alpha - beta * omega
+    r = {0: one, 1: -off_alpha, 2: -off_omega, 3: cross, 4: -off_omega * guessed_omega}
+    w = {2: one, 3: -off_alpha, 4: -off_omega, 5: cross}
+    s = {1: beta, 2: one, 3: both, 4: -off_omega, 5: cross}
+    z = {3: beta, 4: -ratio, 5: both, 6: one + ratio, 7: cross}
     with_b = lambda u: sum(c * g(i, "b") for i, c in u.items())
     times = lambda u: {i: sum(c * g(i, j) for j, c in u.items()) for i in range(8)}
     inner = lambda image, u: sum(c * image[i] for i, c in u.items())
@@ -492,25 +504,40 @@
         ref[N : 2 * N, :] = face[...]
 
 
-def early_dots_kernel(b, r, s, w, z, aw, az, inverse, row):
-    e = [tiles(ref) for ref in (r, s, w, z, aw, az)]
-    row[...] = dots_row(early_pairs(tiles(b), e), tiles(inverse))
-
-
-def late_dots_kernel(sizes, b, r, s, w, z, aw, az, inverse, early, aaz_q, aaw_q, x0, x1, y0, y1,
-                     aaw_out, aaz_out, row):
+def early_dots_kernel(scalars, b, r, s, w, z, aw, az, inverse, near_r_out, y_out, au_out, row):
+    alpha, omega = guess(scalars, s)
+    au, y, near_r = [], [], []
+    for i in range(N):
+        at = slice(N * i, N * i + N)
+        u = w[at, :] - alpha * z[at, :]
+        au.append(aw[at, :] - alpha * az[at, :])
+        y.append(u - omega * au[i])
+        near_r.append((r[at, :] - alpha * s[at, :]) - omega * u)
+    store(near_r_out, near_r)
+    store(y_out, y)
+    store(au_out, au)
+    b, r, s, w, z, az = (tiles(ref) for ref in (b, r, s, w, z, az))
+    pairs = second_pairs(b, r, s, w, z) + early_pairs(b, [near_r, s, y, z, au, az])
+    row[...] = dots_row(pairs, tiles(inverse))
+
+
+def late_dots_kernel(sizes, scalars, b, near_r, s, y, z, au, az, inverse, early, aaz_q, aaw_q,
+                     x0, x1, y0, y1, aaw_out, aaz_out, row):
     pos = position()
     halves = [[ref.at[pl.ds(i * N, N)] for ref in (x0, x1, y0, y1)] for i in range(2)]
     aaz = assemble(sizes, pos, aaz_q, halves[0])
     aaw = assemble(sizes, pos, aaw_q, halves[1])
     store(aaz_out, aaz)
     store(aaw_out, aaw)
-    e = [tiles(ref) for ref in (r, s, w, z, aw, az)] + [aaw, aaz]
-    for_all(early[...] + dots_row(late_pairs(tiles(b), e), tiles(inverse), EARLY), row)
-
-
-def last_kernel(gathered, x, p, r, s, w, z, aw, az, aaw, aaz, x_out, r_out):
-    second, third = last_steps(totals(gathered, EARLY + 17))
+    alpha, omega = guess(scalars, s)
+    e = [tiles(ref) for ref in (near_r, s, y, z, au, az)]
+    ay = [e[4][i] - omega * (aaw[i] - alpha * aaz[i]) for i in range(N)]
+    pairs = late_pairs(tiles(b), e + [ay, aaz])
+    for_all(early[...] + dots_row(pairs, tiles(inverse), EARLY), row)
+
+
+def last_kernel(gathered, scalars, x, p, r, s, w, z, aw, az, aaw, aaz, x_out, r_out):
+    second, third = last_steps(totals(gathered, EARLY + LATE), scalars[1:2, :])
     alpha, omega, beta = (wide(value, s) for value in second)
     last_alpha, last_omega, _ = (wide(value, s) for value in third)
     for i in range(N):
@@ -666,15 +693,16 @@
     )
     recv = swap(parts)
     (q,) = call(z_kernel, [field], az, xy, *z_args, cost=COST)
-    (early,) = call(
-        early_dots_kernel, [jax.ShapeDtypeStruct((1, LANES), f32)], b, r, s, w, z, aw, az, inverse, cost=COST
+    near_r, y, au, early = call(
+        early_dots_kernel, [field] * 3 + [jax.ShapeDtypeStruct((1, LANES), f32)],
+        values, b, r, s, w, z, aw, az, inverse, cost=COST,
     )
     aaw, aaz, products = call(
         functools.partial(late_dots_kernel, sizes), [field] * 2 + [row],
-        b, r, s, w, z, aw, az, inverse, early, q, aw_q, *recv,
+        values, b, near_r, s, y, z, au, az, inverse, early, q, aw_q, *recv,
     )
     x, r = call(
-        last_kernel, [field] * 2, spread(products), x, p, r, s, w, z, aw, az, aaw, aaz
+        last_kernel, [field] * 2, spread(products), values, x, p, r, s, w, z, aw, az, aaw, aaz
     )
     return x.reshape(shape), r.reshape(shape)
 

time: 64.1 us -> 64.2 us (level)
    ppermute x28, waiting for transfers between devices: 13 us -> 12.3 us  [permute(): return lax.ppermute(values, ('gx', 'gy'), pairs)]
  transfers between devices with their start and end apart: 29 -> 29, of which waited for: 10 -> 10; matrix products, arithmetic and copies ran while one was open for 0% -> 0% of each run, Pallas kernels for 7% -> 8%
where the time goes in v7:
time: 64.2 us; the launch traced here: 64 us
  starting transfers between devices  27.4 us (43%)
  waiting for transfers between devices  14.9 us (23%)
  Pallas kernels  10.6 us (17%)
  blocking collectives  10.2 us (16%)
  between operations  0.89 us (1%)
    ppermute x28, starting transfers between devices, permute(): return lax.ppermute(values, ('gx', 'gy'), pairs)  24 us
    ppermute x28, waiting for transfers between devices, permute(): return lax.ppermute(values, ('gx', 'gy'), pairs)  12.3 us
    pallas_call x20, Pallas kernels, call(): pl.pallas_call(kernel, out_shape=outs, in_specs=specs, out_specs=[VMEM] *...  10.6 us
    all_to_all x1, blocking collectives, spread(): return lax.all_to_all(values, ('gx', 'gy'), 0, 0)  10.2 us
    all_to_all x1, starting transfers between devices, spread(): return lax.all_to_all(values, ('gx', 'gy'), 0, 0)  3.38 us
    all_to_all x1, waiting for transfers between devices, spread(): return lax.all_to_all(values, ('gx', 'gy'), 0, 0)  2.59 us
  transfers between devices with their start and end apart: 29, of which 10 were waited for; matrix products, arithmetic and copies ran while one was open for 0% of the time, Pallas kernels for 8%

profile of v7, /device:TPU:0, one launch (start us, length us, event | category | flops | bytes accessed | tf_op | source)
XLA Modules:
  0.0 64.0 jit_solution(15529577256754526301)
XLA Ops:
  0.6 1.8 %shard_map.114 = (f32[24,512]{1,0:T(8,128)}, f32[24,512]{1,0:T(8,128)}) custom-call(f32[64,512]{1,0:T(8,128)} %bitcast.7, f32[64,512]{1,0:T(8,128)} %bitcast.9, s32[1,64]{1,0:T(1,128)} %bitcast.11, s32[1,64]{1,0:T(1,128)} %bitcast.13, f32[1,4]{1,0:T(1,128)} %bitcast.15), custom_call_target="tpu_custom_call" | custom-call | tf_op jit(solution)/shard_map/pallas_call | solution.py:599
  2.5 0.0 copy-start.7
  2.5 0.0 copy-start.8
  2.5 0.0 copy-start.9
  2.5 3.1 %collective-permute-start = (f32[24,512]{1,0:T(8,128)}, f32[24,512]{1,0:T(8,128)S(1)}, u32[]{:S(2)}, u32[]{:S(2)}) collective-permute-start(f32[24,512]{1,0:T(8,128)} %get-tuple-element.82), channel_id=1, source_target_pairs={{0,8},{1,2},{2,1},{3,4},{4,3},{5,6},{6,5},{7,15},{8,0},{9,10},{10,... | collective-permute-start | bytes 147464 | tf_op jit(solution)/shard_map/ppermute | solution.py:612
  5.6 0.0 collective-permute-start.1
  5.6 0.3 shard_map.113
  5.9 2.0 %collective-permute-done.odd = f32[24,512]{1,0:T(8,128)S(1)} collective-permute-done((f32[24,512]{1,0:T(8,128)}, f32[24,512]{1,0:T(8,128)S(1)}, u32[]{:S(2)}, u32[]{:S(2)}) %collective-permute-start) | collective-permute-done | bytes 49184 | tf_op jit(solution)/shard_map/ppermute | solution.py:612
  7.9 0.0 collective-permute-done.1.even
  7.9 0.1 collective-permute-start.2
  8.0 3.6 %collective-permute-start.3 = (f32[32,512]{1,0:T(8,128)S(1)}, f32[32,512]{1,0:T(8,128)S(1)}, u32[]{:S(2)}, u32[]{:S(2)}) collective-permute-start(f32[32,512]{1,0:T(8,128)S(1)} %get-tuple-element.89), channel_id=1, source_target_pairs={{0,8},{1,9},{2,10},{3,11},{4,12},{5,13},{6,14},{7,15},{8,0},{9,1},... | collective-permute-start | bytes 196616 | tf_op jit(solution)/shard_map/ppermute | solution.py:612
  11.6 0.4 shard_map.115
  12.0 1.9 %collective-permute-done.3.even = f32[32,512]{1,0:T(8,128)S(1)} collective-permute-done((f32[32,512]{1,0:T(8,128)S(1)}, f32[32,512]{1,0:T(8,128)S(1)}, u32[]{:S(2)}, u32[]{:S(2)}) %collective-permute-start.3) | collective-permute-done | bytes 65568 | tf_op jit(solution)/shard_map/ppermute | solution.py:612
  13.8 0.4 shard_map.117
  14.2 2.1 %collective-permute-start.4 = (f32[8,512]{1,0:T(8,128)S(1)}, f32[8,512]{1,0:T(8,128)S(1)}, u32[]{:S(2)}, u32[]{:S(2)}) collective-permute-start(f32[8,512]{1,0:T(8,128)S(1)} %get-tuple-element.95), channel_id=1, source_target_pairs={{0,8},{1,2},{2,1},{3,4},{4,3},{5,6},{6,5},{7,15},{8,0},{9,10},{10,... | collective-permute-start | bytes 49160 | tf_op jit(solution)/shard_map/ppermute | solution.py:612
  16.3 0.1 collective-permute-start.5
  16.4 1.3 %collective-permute-start.6 = (f32[8,512]{1,0:T(8,128)S(1)}, f32[8,512]{1,0:T(8,128)S(1)}, u32[]{:S(2)}, u32[]{:S(2)}) collective-permute-start(f32[8,512]{1,0:T(8,128)S(1)} %get-tuple-element.97), channel_id=1, source_target_pairs={{0,1},{1,0},{2,3},{3,2},{4,5},{5,4},{6,7},{7,6},{8,16},{9,17},{10,... | collective-permute-start | bytes 49160 | tf_op jit(solution)/shard_map/ppermute | solution.py:612
  17.7 0.0 collective-permute-start.7
  17.8 0.5 shard_map.118
  18.2 1.8 %collective-permute-done.5.x1 = f32[8,512]{1,0:T(8,128)S(1)} collective-permute-done((f32[8,512]{1,0:T(8,128)S(1)}, f32[8,512]{1,0:T(8,128)S(1)}, u32[]{:S(2)}, u32[]{:S(2)}) %collective-permute-start.5) | collective-permute-done | bytes 16416 | tf_op jit(solution)/shard_map/ppermute | solution.py:612
  20.1 0.0 collective-permute-done.6.y0
  20.1 0.0 collective-permute-done.7.y1
  20.1 0.4 shard_map.119
  20.5 2.1 %collective-permute-start.8 = (f32[8,512]{1,0:T(8,128)S(1)}, f32[8,512]{1,0:T(8,128)S(1)}, u32[]{:S(2)}, u32[]{:S(2)}) collective-permute-start(f32[8,512]{1,0:T(8,128)S(1)} %get-tuple-element.105), channel_id=1, source_target_pairs={{0,8},{1,2},{2,1},{3,4},{4,3},{5,6},{6,5},{7,15},{8,0},{9,10},{10,... | collective-permute-start | bytes 49160 | tf_op jit(solution)/shard_map/ppermute | solution.py:612
  22.5 0.1 collective-permute-start.9
  22.6 0.5 collective-permute-start.11
  23.1 0.4 shard_map.120.q
  23.6 0.7 %collective-permute-done.8.x0 = f32[8,512]{1,0:T(8,128)S(1)} collective-permute-done((f32[8,512]{1,0:T(8,128)S(1)}, f32[8,512]{1,0:T(8,128)S(1)}, u32[]{:S(2)}, u32[]{:S(2)}) %collective-permute-start.8) | collective-permute-done | bytes 16416 | tf_op jit(solution)/shard_map/ppermute | solution.py:612
  24.3 2.0 %collective-permute-done.9.x1 = f32[8,512]{1,0:T(8,128)S(1)} collective-permute-done((f32[8,512]{1,0:T(8,128)S(1)}, f32[8,512]{1,0:T(8,128)S(1)}, u32[]{:S(2)}, u32[]{:S(2)}) %collective-permute-start.9) | collective-permute-done | bytes 16416 | tf_op jit(solution)/shard_map/ppermute | solution.py:612
  26.3 0.8 %shard_map.121 = (f32[64,512]{1,0:T(8,128)S(1)}, f32[64,512]{1,0:T(8,128)S(1)}, f32[8,512]{1,0:T(8,128)S(1)}, f32[8,512]{1,0:T(8,128)S(1)}, f32[8,512]{1,0:T(8,1...) custom-call(f32[64,512]{1,0:T(8,128)S(1)} %get-tuple-element.90.b, f32[64,512]{1,0:T(8,128)S(1)} %get-tuple-element.100.refs_0_.s, ...), custom_call_target="tpu_custom_call" | custom-call | tf_op jit(solution)/shard_map/pallas_call | solution.py:599
  27.1 2.1 %collective-permute-start.12 = (f32[8,512]{1,0:T(8,128)S(1)}, f32[8,512]{1,0:T(8,128)S(1)}, u32[]{:S(2)}, u32[]{:S(2)}) collective-permute-start(f32[8,512]{1,0:T(8,128)S(1)} %get-tuple-element.112), channel_id=1, source_target_pairs={{0,8},{1,2},{2,1},{3,4},{4,3},{5,6},{6,5},{7,15},{8,0},{9,10},{10,... | collective-permute-start | bytes 49160 | tf_op jit(solution)/shard_map/ppermute | solution.py:612
  29.2 0.1 collective-permute-start.13
  29.3 0.5 collective-permute-start.15
  29.8 3.4 %all-to-all-start = ((f32[32,1,128]{2,1,0:T(1,128)}), f32[32,1,128]{2,1,0:T(1,128)S(1)}, u32[]{:S(2)}, u32[]{:S(2)}) async-start(f32[32,1,128]{2,1,0:T(1,128)} %get-tuple-element.109), calls=%async_computation | async-start | bytes 32768 | tf_op jit(solution)/shard_map/all_to_all | solution.py:625
  33.2 0.5 shard_map.122.q
  33.6 0.0 collective-permute-done.14.y0
  33.7 0.4 shard_map.123
  34.1 1.8 %collective-permute-start.16 = (f32[8,512]{1,0:T(8,128)S(1)}, f32[8,512]{1,0:T(8,128)S(1)}, u32[]{:S(2)}, u32[]{:S(2)}) collective-permute-start(f32[8,512]{1,0:T(8,128)S(1)} %get-tuple-element.118), channel_id=1, source_target_pairs={{0,8},{1,2},{2,1},{3,4},{4,3},{5,6},{6,5},{7,15},{8,0},{9,10},{10,... | collective-permute-start | bytes 49160 | tf_op jit(solution)/shard_map/ppermute | solution.py:612
  35.9 0.3 collective-permute-start.17
  36.2 1.0 %collective-permute-start.18 = (f32[8,512]{1,0:T(8,128)S(1)}, f32[8,512]{1,0:T(8,128)S(1)}, u32[]{:S(2)}, u32[]{:S(2)}) collective-permute-start(f32[8,512]{1,0:T(8,128)S(1)} %get-tuple-element.120), channel_id=1, source_target_pairs={{0,1},{1,0},{2,3},{3,2},{4,5},{5,4},{6,7},{7,6},{8,16},{9,17},{10,... | collective-permute-start | bytes 49160 | tf_op jit(solution)/shard_map/ppermute | solution.py:612
  37.2 0.4 shard_map.124.q
  37.7 2.6 %all-to-all-done.gathered = f32[32,1,128]{2,1,0:T(1,128)S(1)} async-done(((f32[32,1,128]{2,1,0:T(1,128)}), f32[32,1,128]{2,1,0:T(1,128)S(1)}, u32[]{:S(2)}, u32[]{:S(2)}) %all-to-all-start) | async-done | bytes 16416 | tf_op jit(solution)/shard_map/all_to_all | solution.py:625
  40.2 0.0 collective-permute-done.16.x0
  40.3 0.0 collective-permute-done.17.x1
  40.3 0.0 collective-permute-done.18.y0
  40.3 0.5 shard_map.125
  40.8 1.4 %collective-permute-start.20 = (f32[8,512]{1,0:T(8,128)S(1)}, f32[8,512]{1,0:T(8,128)S(1)}, u32[]{:S(2)}, u32[]{:S(2)}) collective-permute-start(f32[8,512]{1,0:T(8,128)S(1)} %get-tuple-element.134), channel_id=1, source_target_pairs={{0,8},{1,2},{2,1},{3,4},{4,3},{5,6},{6,5},{7,15},{8,0},{9,10},{10,... | collective-permute-start | bytes 49160 | tf_op jit(solution)/shard_map/ppermute | solution.py:612
  42.2 0.6 collective-permute-start.21
  42.9 0.5 collective-permute-start.23
  43.4 0.9 %shard_map.127 = (f32[64,512]{1,0:T(8,128)S(1)}, f32[64,512]{1,0:T(8,128)S(1)}, f32[8,512]{1,0:T(8,128)S(1)}, f32[8,512]{1,0:T(8,128)S(1)}, f32[8,512]{1,0:T(8,128)S(1)}, /*index=5*/f32[8,512]{1,0:T(8,128)S(1)}) custom-call(f32[64,512]{1,0:T(8,128)S(1)} %get-tuple-element.126.z, f32[64,512]{1,0:T(8,128)S(1)} %get-tuple-element.128.z_xy, ...), custom_call_target="tpu_custom_call" | custom-call | flops 1048576 | bytes 1048576 | tf_op jit(solution)/shard_map/pallas_call | solution.py:599
  44.3 0.3 collective-permute-done.20.x0
  44.6 1.4 %collective-permute-done.21.x1 = f32[8,512]{1,0:T(8,128)S(1)} collective-permute-done((f32[8,512]{1,0:T(8,128)S(1)}, f32[8,512]{1,0:T(8,128)S(1)}, u32[]{:S(2)}, u32[]{:S(2)}) %collective-permute-start.21) | collective-permute-done | bytes 16416 | tf_op jit(solution)/shard_map/ppermute | solution.py:612
  46.0 0.4 shard_map.128
  46.4 2.1 %collective-permute-start.24 = (f32[16,512]{1,0:T(8,128)S(1)}, f32[16,512]{1,0:T(8,128)S(1)}, u32[]{:S(2)}, u32[]{:S(2)}) collective-permute-start(f32[16,512]{1,0:T(8,128)S(1)} %get-tuple-element.145), channel_id=1, source_target_pairs={{0,8},{1,2},{2,1},{3,4},{4,3},{5,6},{6,5},{7,15},{8,0},{9,10},{10,... | collective-permute-start | bytes 98312 | tf_op jit(solution)/shard_map/ppermute | solution.py:612
  48.4 0.1 collective-permute-start.25
  48.5 0.5 collective-permute-start.27
  49.0 0.1 shard_map.126
  49.1 0.5 shard_map.130.aaz_q
  49.6 0.6 shard_map.129
  50.2 0.2 collective-permute-done.24.x0
  50.3 2.0 %collective-permute-done.25.x1 = f32[16,512]{1,0:T(8,128)S(1)} collective-permute-done((f32[16,512]{1,0:T(8,128)S(1)}, f32[16,512]{1,0:T(8,128)S(1)}, u32[]{:S(2)}, u32[]{:S(2)}) %collective-permute-start.25) | collective-permute-done | bytes 32800 | tf_op jit(solution)/shard_map/ppermute | solution.py:612
  52.4 0.4 shard_map.131
  52.7 10.2 %all_to_all.10.gathered = f32[32,1,128]{2,1,0:T(1,128)S(1)} all-to-all(f32[32,1,128]{2,1,0:T(1,128)S(1)} %get-tuple-element.149), channel_id=1, replica_groups=mesh['gx'=4,'gy'=8] {'gx','gy'}, dimensions={0} | all-to-all | bytes 32768 | tf_op jit(solution)/shard_map/all_to_all | solution.py:625
  63.0 1.0 %shard_map.132 = (f32[64,512]{1,0:T(8,128)}, f32[64,512]{1,0:T(8,128)}) custom-call(f32[32,1,128]{2,1,0:T(1,128)S(1)} %all_to_all.10.gathered, f32[8,128]{1,0:T(8,128)S(1)} %get-tuple-element.122.scalars, f32[64,512]{1,0:T(8,128)S(1)} %get-tuple-element.150.x, f32[64,512]{1,0:T(8,128)S(1)} %get-tuple-element.151.p, f32[64,512]{1,0:T(8,128)S(1)} %get-tuple-element.123.r, ...), custom_call_target="tpu_custom_call" | custom-call | tf_op jit(solution)/shard_map/pallas_call | solution.py:599
  (35 shorter events, 0.1 us)
Async XLA Ops:
  0.6 5.0 %copy-start.5 = (f32[8,8,512]{2,1,0:T(8,128)S(1)}, f32[8,8,512]{2,1,0:T(8,128)}, u32[]{:S(2)}) copy-start(f32[8,8,512]{2,1,0:T(8,128)} %param.10) | copy-start | bytes 393220
  0.6 5.0 %copy-start.6 = (f32[8,8,512]{2,1,0:T(8,128)S(1)}, f32[8,8,512]{2,1,0:T(8,128)}, u32[]{:S(2)}) copy-start(f32[8,8,512]{2,1,0:T(8,128)} %param.11) | copy-start | bytes 393220
  2.5 3.2 %copy-start.7 = (s32[1,1,64]{2,1,0:T(1,128)S(1)}, s32[1,1,64]{2,1,0:T(1,128)}, u32[]{:S(2)}) copy-start(s32[1,1,64]{2,1,0:T(1,128)} %param.12) | copy-start | bytes 772
  2.5 3.2 %copy-start.8 = (s32[1,1,64]{2,1,0:T(1,128)S(1)}, s32[1,1,64]{2,1,0:T(1,128)}, u32[]{:S(2)}) copy-start(s32[1,1,64]{2,1,0:T(1,128)} %param.13) | copy-start | bytes 772
  2.5 3.1 %copy-start.9 = (f32[4]{0:T(128)S(1)}, f32[4]{0:T(128)}, u32[]{:S(2)}) copy-start(f32[4]{0:T(128)} %param.14) | copy-start | bytes 52
  2.5 5.4 %collective-permute-start = (f32[24,512]{1,0:T(8,128)}, f32[24,512]{1,0:T(8,128)S(1)}, u32[]{:S(2)}, u32[]{:S(2)}) collective-permute-start(f32[24,512]{1,0:T(8,128)} %get-tuple-element.82), channel_id=1, source_target_pairs={{0,8},{1,2},{2,1},{3,4},{4,3},{5,6},{6,5},{7,15},{8,0},{9,10},{10,... | collective-permute-start | bytes 147464 | tf_op jit(solution)/shard_map/ppermute | solution.py:612
  5.6 2.3 %collective-permute-start.1 = (f32[24,512]{1,0:T(8,128)}, f32[24,512]{1,0:T(8,128)S(1)}, u32[]{:S(2)}, u32[]{:S(2)}) collective-permute-start(f32[24,512]{1,0:T(8,128)} %get-tuple-element.83), channel_id=1, source_target_pairs={{0,1},{1,0},{2,3},{3,2},{4,5},{5,4},{6,7},{7,6},{8,9},{9,8},{10,11... | collective-permute-start | bytes 147464 | tf_op jit(solution)/shard_map/ppermute | solution.py:612
  7.9 3.7 %copy-start.4 = (f32[8,512]{1,0:T(8,128)S(1)}, f32[8,512]{1,0:T(8,128)}, u32[]{:S(2)}) copy-start(f32[8,512]{1,0:T(8,128)} %constant.14.clone.lanes.refs_8_.refs_6_) | copy-start | bytes 49156
  7.9 4.0 %collective-permute-start.2 = (f32[32,512]{1,0:T(8,128)S(1)}, f32[32,512]{1,0:T(8,128)S(1)}, u32[]{:S(2)}, u32[]{:S(2)}) collective-permute-start(f32[32,512]{1,0:T(8,128)S(1)} %get-tuple-element.88), channel_id=1, source_target_pairs={{0,1},{1,0},{2,3},{3,2},{4,5},{5,4},{6,7},{7,6},{8,16},{9,17},{10,... | collective-permute-start | bytes 196616 | tf_op jit(solution)/shard_map/ppermute | solution.py:612
  8.0 5.8 %collective-permute-start.3 = (f32[32,512]{1,0:T(8,128)S(1)}, f32[32,512]{1,0:T(8,128)S(1)}, u32[]{:S(2)}, u32[]{:S(2)}) collective-permute-start(f32[32,512]{1,0:T(8,128)S(1)} %get-tuple-element.89), channel_id=1, source_target_pairs={{0,8},{1,9},{2,10},{3,11},{4,12},{5,13},{6,14},{7,15},{8,0},{9,1},... | collective-permute-start | bytes 196616 | tf_op jit(solution)/shard_map/ppermute | solution.py:612
  13.8 3.9 %copy-start = (bf16[256,256]{1,0:T(8,128)(2,1)S(1)}, bf16[256,256]{1,0:T(8,128)(2,1)}, u32[]{:S(2)}) copy-start(bf16[256,256]{1,0:T(8,128)(2,1)} %constant.12.clone.b1.refs_6_.refs_4_) | copy-start | bytes 393220
  13.8 3.9 %copy-start.1 = (bf16[256,256]{1,0:T(8,128)(2,1)S(1)}, bf16[256,256]{1,0:T(8,128)(2,1)}, u32[]{:S(2)}) copy-start(bf16[256,256]{1,0:T(8,128)(2,1)} %constant.10.clone.f1.refs_4_.refs_2_) | copy-start | bytes 393220
  13.8 3.9 %copy-start.2 = (bf16[256,128]{1,0:T(8,128)(2,1)S(1)}, bf16[256,128]{1,0:T(8,128)(2,1)}, u32[]{:S(2)}) copy-start(bf16[256,128]{1,0:T(8,128)(2,1)} %constant.13.clone.b2.refs_7_.refs_5_) | copy-start | bytes 196612
  13.8 3.9 %copy-start.3 = (bf16[256,128]{1,0:T(8,128)(2,1)S(1)}, bf16[256,128]{1,0:T(8,128)(2,1)}, u32[]{:S(2)}) copy-start(bf16[256,128]{1,0:T(8,128)(2,1)} %constant.11.clone.f2.refs_5_.refs_3_) | copy-start | bytes 196612
  14.2 4.0 %collective-permute-start.4 = (f32[8,512]{1,0:T(8,128)S(1)}, f32[8,512]{1,0:T(8,128)S(1)}, u32[]{:S(2)}, u32[]{:S(2)}) collective-permute-start(f32[8,512]{1,0:T(8,128)S(1)} %get-tuple-element.95), channel_id=1, source_target_pairs={{0,8},{1,2},{2,1},{3,4},{4,3},{5,6},{6,5},{7,15},{8,0},{9,10},{10,... | collective-permute-start | bytes 49160 | tf_op jit(solution)/shard_map/ppermute | solution.py:612
  16.3 3.7 %collective-permute-start.5 = (f32[8,512]{1,0:T(8,128)S(1)}, f32[8,512]{1,0:T(8,128)S(1)}, u32[]{:S(2)}, u32[]{:S(2)}) collective-permute-start(f32[8,512]{1,0:T(8,128)S(1)} %get-tuple-element.96), channel_id=1, source_target_pairs={{0,8},{1,9},{2,10},{3,11},{4,12},{5,13},{6,14},{7,15},{8,0},{9,1},... | collective-permute-start | bytes 49160 | tf_op jit(solution)/shard_map/ppermute | solution.py:612
  16.4 3.7 %collective-permute-start.6 = (f32[8,512]{1,0:T(8,128)S(1)}, f32[8,512]{1,0:T(8,128)S(1)}, u32[]{:S(2)}, u32[]{:S(2)}) collective-permute-start(f32[8,512]{1,0:T(8,128)S(1)} %get-tuple-element.97), channel_id=1, source_target_pairs={{0,1},{1,0},{2,3},{3,2},{4,5},{5,4},{6,7},{7,6},{8,16},{9,17},{10,... | collective-permute-start | bytes 49160 | tf_op jit(solution)/shard_map/ppermute | solution.py:612
  17.7 2.3 %collective-permute-start.7 = (f32[8,512]{1,0:T(8,128)S(1)}, f32[8,512]{1,0:T(8,128)S(1)}, u32[]{:S(2)}, u32[]{:S(2)}) collective-permute-start(f32[8,512]{1,0:T(8,128)S(1)} %get-tuple-element.98), channel_id=1, source_target_pairs={{0,1},{1,0},{2,3},{3,2},{4,5},{5,4},{6,7},{7,6},{8,9},{9,8},{10,11... | collective-permute-start | bytes 49160 | tf_op jit(solution)/shard_map/ppermute | solution.py:612
  20.5 3.8 %collective-permute-start.8 = (f32[8,512]{1,0:T(8,128)S(1)}, f32[8,512]{1,0:T(8,128)S(1)}, u32[]{:S(2)}, u32[]{:S(2)}) collective-permute-start(f32[8,512]{1,0:T(8,128)S(1)} %get-tuple-element.105), channel_id=1, source_target_pairs={{0,8},{1,2},{2,1},{3,4},{4,3},{5,6},{6,5},{7,15},{8,0},{9,10},{10,... | collective-permute-start | bytes 49160 | tf_op jit(solution)/shard_map/ppermute | solution.py:612
  22.5 3.7 %collective-permute-start.9 = (f32[8,512]{1,0:T(8,128)S(1)}, f32[8,512]{1,0:T(8,128)S(1)}, u32[]{:S(2)}, u32[]{:S(2)}) collective-permute-start(f32[8,512]{1,0:T(8,128)S(1)} %get-tuple-element.106), channel_id=1, source_target_pairs={{0,8},{1,9},{2,10},{3,11},{4,12},{5,13},{6,14},{7,15},{8,0},{9,1},... | collective-permute-start | bytes 49160 | tf_op jit(solution)/shard_map/ppermute | solution.py:612
  22.6 3.7 %collective-permute-start.10 = (f32[8,512]{1,0:T(8,128)S(1)}, f32[8,512]{1,0:T(8,128)S(1)}, u32[]{:S(2)}, u32[]{:S(2)}) collective-permute-start(f32[8,512]{1,0:T(8,128)S(1)} %get-tuple-element.107), channel_id=1, source_target_pairs={{0,1},{1,0},{2,3},{3,2},{4,5},{5,4},{6,7},{7,6},{8,16},{9,17},{10,... | collective-permute-start | bytes 49160 | tf_op jit(solution)/shard_map/ppermute | solution.py:612
  22.6 3.7 %collective-permute-start.11 = (f32[8,512]{1,0:T(8,128)S(1)}, f32[8,512]{1,0:T(8,128)S(1)}, u32[]{:S(2)}, u32[]{:S(2)}) collective-permute-start(f32[8,512]{1,0:T(8,128)S(1)} %get-tuple-element.108), channel_id=1, source_target_pairs={{0,1},{1,0},{2,3},{3,2},{4,5},{5,4},{6,7},{7,6},{8,9},{9,8},{10,11... | collective-permute-start | bytes 49160 | tf_op jit(solution)/shard_map/ppermute | solution.py:612
  27.1 6.5 %collective-permute-start.12 = (f32[8,512]{1,0:T(8,128)S(1)}, f32[8,512]{1,0:T(8,128)S(1)}, u32[]{:S(2)}, u32[]{:S(2)}) collective-permute-start(f32[8,512]{1,0:T(8,128)S(1)} %get-tuple-element.112), channel_id=1, source_target_pairs={{0,8},{1,2},{2,1},{3,4},{4,3},{5,6},{6,5},{7,15},{8,0},{9,10},{10,... | collective-permute-start | bytes 49160 | tf_op jit(solution)/shard_map/ppermute | solution.py:612
  29.2 4.4 %collective-permute-start.13 = (f32[8,512]{1,0:T(8,128)S(1)}, f32[8,512]{1,0:T(8,128)S(1)}, u32[]{:S(2)}, u32[]{:S(2)}) collective-permute-start(f32[8,512]{1,0:T(8,128)S(1)} %get-tuple-element.113), channel_id=1, source_target_pairs={{0,8},{1,9},{2,10},{3,11},{4,12},{5,13},{6,14},{7,15},{8,0},{9,1},... | collective-permute-start | bytes 49160 | tf_op jit(solution)/shard_map/ppermute | solution.py:612
  29.3 4.4 %collective-permute-start.14 = (f32[8,512]{1,0:T(8,128)S(1)}, f32[8,512]{1,0:T(8,128)S(1)}, u32[]{:S(2)}, u32[]{:S(2)}) collective-permute-start(f32[8,512]{1,0:T(8,128)S(1)} %get-tuple-element.114), channel_id=1, source_target_pairs={{0,1},{1,0},{2,3},{3,2},{4,5},{5,4},{6,7},{7,6},{8,16},{9,17},{10,... | collective-permute-start | bytes 49160 | tf_op jit(solution)/shard_map/ppermute | solution.py:612
  29.3 4.4 %collective-permute-start.15 = (f32[8,512]{1,0:T(8,128)S(1)}, f32[8,512]{1,0:T(8,128)S(1)}, u32[]{:S(2)}, u32[]{:S(2)}) collective-permute-start(f32[8,512]{1,0:T(8,128)S(1)} %get-tuple-element.115), channel_id=1, source_target_pairs={{0,1},{1,0},{2,3},{3,2},{4,5},{5,4},{6,7},{7,6},{8,9},{9,8},{10,11... | collective-permute-start | bytes 49160 | tf_op jit(solution)/shard_map/ppermute | solution.py:612
  29.8 10.5 %all-to-all-start = ((f32[32,1,128]{2,1,0:T(1,128)}), f32[32,1,128]{2,1,0:T(1,128)S(1)}, u32[]{:S(2)}, u32[]{:S(2)}) async-start(f32[32,1,128]{2,1,0:T(1,128)} %get-tuple-element.109), calls=%async_computation | async-start | bytes 32768 | tf_op jit(solution)/shard_map/all_to_all | solution.py:625
  34.1 6.2 %collective-permute-start.16 = (f32[8,512]{1,0:T(8,128)S(1)}, f32[8,512]{1,0:T(8,128)S(1)}, u32[]{:S(2)}, u32[]{:S(2)}) collective-permute-start(f32[8,512]{1,0:T(8,128)S(1)} %get-tuple-element.118), channel_id=1, source_target_pairs={{0,8},{1,2},{2,1},{3,4},{4,3},{5,6},{6,5},{7,15},{8,0},{9,10},{10,... | collective-permute-start | bytes 49160 | tf_op jit(solution)/shard_map/ppermute | solution.py:612
  35.9 4.4 %collective-permute-start.17 = (f32[8,512]{1,0:T(8,128)S(1)}, f32[8,512]{1,0:T(8,128)S(1)}, u32[]{:S(2)}, u32[]{:S(2)}) collective-permute-start(f32[8,512]{1,0:T(8,128)S(1)} %get-tuple-element.119), channel_id=1, source_target_pairs={{0,8},{1,9},{2,10},{3,11},{4,12},{5,13},{6,14},{7,15},{8,0},{9,1},... | collective-permute-start | bytes 49160 | tf_op jit(solution)/shard_map/ppermute | solution.py:612
  36.2 4.1 %collective-permute-start.18 = (f32[8,512]{1,0:T(8,128)S(1)}, f32[8,512]{1,0:T(8,128)S(1)}, u32[]{:S(2)}, u32[]{:S(2)}) collective-permute-start(f32[8,512]{1,0:T(8,128)S(1)} %get-tuple-element.120), channel_id=1, source_target_pairs={{0,1},{1,0},{2,3},{3,2},{4,5},{5,4},{6,7},{7,6},{8,16},{9,17},{10,... | collective-permute-start | bytes 49160 | tf_op jit(solution)/shard_map/ppermute | solution.py:612
  37.2 3.1 %collective-permute-start.19 = (f32[8,512]{1,0:T(8,128)S(1)}, f32[8,512]{1,0:T(8,128)S(1)}, u32[]{:S(2)}, u32[]{:S(2)}) collective-permute-start(f32[8,512]{1,0:T(8,128)S(1)} %get-tuple-element.121), channel_id=1, source_target_pairs={{0,1},{1,0},{2,3},{3,2},{4,5},{5,4},{6,7},{7,6},{8,9},{9,8},{10,11... | collective-permute-start | bytes 49160 | tf_op jit(solution)/shard_map/ppermute | solution.py:612
  40.8 3.8 %collective-permute-start.20 = (f32[8,512]{1,0:T(8,128)S(1)}, f32[8,512]{1,0:T(8,128)S(1)}, u32[]{:S(2)}, u32[]{:S(2)}) collective-permute-start(f32[8,512]{1,0:T(8,128)S(1)} %get-tuple-element.134), channel_id=1, source_target_pairs={{0,8},{1,2},{2,1},{3,4},{4,3},{5,6},{6,5},{7,15},{8,0},{9,10},{10,... | collective-permute-start | bytes 49160 | tf_op jit(solution)/shard_map/ppermute | solution.py:612
  42.2 3.7 %collective-permute-start.21 = (f32[8,512]{1,0:T(8,128)S(1)}, f32[8,512]{1,0:T(8,128)S(1)}, u32[]{:S(2)}, u32[]{:S(2)}) collective-permute-start(f32[8,512]{1,0:T(8,128)S(1)} %get-tuple-element.135), channel_id=1, source_target_pairs={{0,8},{1,9},{2,10},{3,11},{4,12},{5,13},{6,14},{7,15},{8,0},{9,1},... | collective-permute-start | bytes 49160 | tf_op jit(solution)/shard_map/ppermute | solution.py:612
  42.9 3.1 %collective-permute-start.22 = (f32[8,512]{1,0:T(8,128)S(1)}, f32[8,512]{1,0:T(8,128)S(1)}, u32[]{:S(2)}, u32[]{:S(2)}) collective-permute-start(f32[8,512]{1,0:T(8,128)S(1)} %get-tuple-element.136), channel_id=1, source_target_pairs={{0,1},{1,0},{2,3},{3,2},{4,5},{5,4},{6,7},{7,6},{8,16},{9,17},{10,... | collective-permute-start | bytes 49160 | tf_op jit(solution)/shard_map/ppermute | solution.py:612
  42.9 3.1 %collective-permute-start.23 = (f32[8,512]{1,0:T(8,128)S(1)}, f32[8,512]{1,0:T(8,128)S(1)}, u32[]{:S(2)}, u32[]{:S(2)}) collective-permute-start(f32[8,512]{1,0:T(8,128)S(1)} %get-tuple-element.137), channel_id=1, source_target_pairs={{0,1},{1,0},{2,3},{3,2},{4,5},{5,4},{6,7},{7,6},{8,9},{9,8},{10,11... | collective-permute-start | bytes 49160 | tf_op jit(solution)/shard_map/ppermute | solution.py:612
  46.4 4.0 %collective-permute-start.24 = (f32[16,512]{1,0:T(8,128)S(1)}, f32[16,512]{1,0:T(8,128)S(1)}, u32[]{:S(2)}, u32[]{:S(2)}) collective-permute-start(f32[16,512]{1,0:T(8,128)S(1)} %get-tuple-element.145), channel_id=1, source_target_pairs={{0,8},{1,2},{2,1},{3,4},{4,3},{5,6},{6,5},{7,15},{8,0},{9,10},{10,... | collective-permute-start | bytes 98312 | tf_op jit(solution)/shard_map/ppermute | solution.py:612
  48.4 3.9 %collective-permute-start.25 = (f32[16,512]{1,0:T(8,128)S(1)}, f32[16,512]{1,0:T(8,128)S(1)}, u32[]{:S(2)}, u32[]{:S(2)}) collective-permute-start(f32[16,512]{1,0:T(8,128)S(1)} %get-tuple-element.146), channel_id=1, source_target_pairs={{0,8},{1,9},{2,10},{3,11},{4,12},{5,13},{6,14},{7,15},{8,0},{9,1},... | collective-permute-start | bytes 98312 | tf_op jit(solution)/shard_map/ppermute | solution.py:612
  48.5 3.8 %collective-permute-start.26 = (f32[16,512]{1,0:T(8,128)S(1)}, f32[16,512]{1,0:T(8,128)S(1)}, u32[]{:S(2)}, u32[]{:S(2)}) collective-permute-start(f32[16,512]{1,0:T(8,128)S(1)} %get-tuple-element.147), channel_id=1, source_target_pairs={{0,1},{1,0},{2,3},{3,2},{4,5},{5,4},{6,7},{7,6},{8,16},{9,17},{10,... | collective-permute-start | bytes 98312 | tf_op jit(solution)/shard_map/ppermute | solution.py:612
  48.5 3.8 %collective-permute-start.27 = (f32[16,512]{1,0:T(8,128)S(1)}, f32[16,512]{1,0:T(8,128)S(1)}, u32[]{:S(2)}, u32[]{:S(2)}) collective-permute-start(f32[16,512]{1,0:T(8,128)S(1)} %get-tuple-element.148), channel_id=1, source_target_pairs={{0,1},{1,0},{2,3},{3,2},{4,5},{5,4},{6,7},{7,6},{8,9},{9,8},{10,11... | collective-permute-start | bytes 98312 | tf_op jit(solution)/shard_map/ppermute | solution.py:612

commit v8 on v7

--- a/solution.py
+++ b/solution.py
@@ -457,80 +457,65 @@
     copy.wait()
 
 
-def update_kernel(sizes, gathered, s, z, az, q, x0, x1, y0, y1, kx, ky, advect,
-                  z_out, aw_out, scalars, xy_out, *refs):
-    pos = position()
+def first_steps_kernel(_, gathered, scalars):
     bb, bs, bz, ss, sz, zz = totals(gathered, 6)
-    values = steps(bb, bs, bs, bz, bs, ss, bz, sz, ss, sz, zz)
-    for i, value in enumerate(values):
+    for i, value in enumerate(steps(bb, bs, bs, bz, bs, ss, bz, sz, ss, sz, zz)):
         scalars[i : i + 1, :] = value
-    alpha, omega, beta = (wide(value, s) for value in values)
-    aaz = assemble(sizes, pos, q, (x0, x1, y0, y1))
-    z, az = tiles(z), tiles(az)
-    aw = [(z[i] - alpha * az[i]) - omega * (az[i] - alpha * aaz[i]) for i in range(N)]
-    z_next = [aw[i] + beta * (z[i] - omega * az[i]) for i in range(N)]
-    store(aw_out, aw)
-    store(z_out, z_next)
-    operate(pos, z_next, kx, ky, advect, xy_out, refs[:4], *refs[4:])
-
-
-def update_rest_kernel(scalars, b, s, z, az, x_out, r_out, p_out, s_out, w_out):
+
+
+def update_kernel(sizes, scalars, az, aaz, q, x0, x1, y0, y1, kx, ky, advect,
+                  az_out, aaw_out, xy_out, *refs):
+    pos = position()
+    alpha, omega, beta = (wide(scalars[i : i + 1, :], az) for i in range(3))
+    aaaz = assemble(sizes, pos, q, (x0, x1, y0, y1))
+    az, aaz = tiles(az), tiles(aaz)
+    aaw = [(az[i] - alpha * aaz[i]) - omega * (aaz[i] - alpha * aaaz[i]) for i in range(N)]
+    az_next = [aaw[i] + beta * (az[i] - omega * aaz[i]) for i in range(N)]
+    store(aaw_out, aaw)
+    store(az_out, az_next)
+    operate(pos, az_next, kx, ky, advect, xy_out, refs[:4], *refs[4:])
+
+
+def update_rest_kernel(scalars, b, s, z, az, aaz, az_next, inverse,
+                       x_out, r_out, p_out, s_out, w_out, z_out, aw_out, near_r_out, y_out, au_out, row):
     alpha, omega, beta = (wide(scalars[i : i + 1, :], s) for i in range(3))
+    near_alpha, near_omega = guess(scalars, s)
+    fields = [[] for _ in range(9)]
     for i in range(N):
         at = slice(N * i, N * i + N)
         b_, s_, z_, az_ = b[at, :], s[at, :], z[at, :], az[at, :]
         half, applied_half = b_ - alpha * s_, s_ - alpha * z_
+        applied_twice = z_ - alpha * az_
         x_out[at, :] = alpha * b_ + omega * half
         r = half - omega * applied_half
-        w = applied_half - omega * (z_ - alpha * az_)
+        w = applied_half - omega * applied_twice
+        aw = applied_twice - omega * (az_ - alpha * aaz[at, :])
+        s_next = w + beta * (s_ - omega * z_)
+        z_next = aw + beta * (z_ - omega * az_)
         p_out[at, :] = r + beta * (b_ - omega * s_)
-        r_out[at, :], w_out[at, :], s_out[at, :] = r, w, w + beta * (s_ - omega * z_)
-
-
-def two_z_kernel(z, z_xy, aw, kx, ky, advect, *refs):
-    *shared, z_q_out, aw_q_out, f0, f1, f2, f3, xy, low, high = refs
-    along_z(z, z_xy, *shared, z_q_out)
-    operate(position(), tiles(aw), kx, ky, advect, xy, (f0, f1, f2, f3), low, high)
-    along_z(aw, xy, *shared, aw_q_out)
-
-
-def apply_beside_kernel(sizes, f0, f1, f2, f3, q, x0, x1, y0, y1, kx, ky, advect, v_out, xy_out, *refs):
-    sends, sides = refs[:4], refs[4:]
-    pos = position()
-    v = assemble(sizes, pos, q, (x0, x1, y0, y1))
-    store(v_out, v)
-    operate(pos, v, kx, ky, advect, xy_out, [ref.at[pl.ds(0, N)] for ref in sends], *sides)
-    for ref, face in zip(sends, (f0, f1, f2, f3)):
-        ref[N : 2 * N, :] = face[...]
-
-
-def early_dots_kernel(scalars, b, r, s, w, z, aw, az, inverse, near_r_out, y_out, au_out, row):
-    alpha, omega = guess(scalars, s)
-    au, y, near_r = [], [], []
-    for i in range(N):
-        at = slice(N * i, N * i + N)
-        u = w[at, :] - alpha * z[at, :]
-        au.append(aw[at, :] - alpha * az[at, :])
-        y.append(u - omega * au[i])
-        near_r.append((r[at, :] - alpha * s[at, :]) - omega * u)
-    store(near_r_out, near_r)
-    store(y_out, y)
-    store(au_out, au)
-    b, r, s, w, z, az = (tiles(ref) for ref in (b, r, s, w, z, az))
-    pairs = second_pairs(b, r, s, w, z) + early_pairs(b, [near_r, s, y, z, au, az])
+        u = w - near_alpha * z_next
+        au = aw - near_alpha * az_next[at, :]
+        y = u - near_omega * au
+        near_r = (r - near_alpha * s_next) - near_omega * u
+        outs = r_out, s_out, w_out, z_out, aw_out, near_r_out, y_out, au_out
+        values = r, s_next, w, z_next, aw, near_r, y, au
+        for out, value in zip(outs, values):
+            out[at, :] = value
+        for kept, value in zip(fields, (b_, r, s_next, w, z_next, near_r, y, au, az_next[at, :])):
+            kept.append(value)
+    b_, r, s_next, w, z_next, near_r, y, au, az_ = fields
+    pairs = second_pairs(b_, r, s_next, w, z_next)
+    pairs += early_pairs(b_, [near_r, s_next, y, z_next, au, az_])
     row[...] = dots_row(pairs, tiles(inverse))
 
 
-def late_dots_kernel(sizes, scalars, b, near_r, s, y, z, au, az, inverse, early, aaz_q, aaw_q,
-                     x0, x1, y0, y1, aaw_out, aaz_out, row):
-    pos = position()
-    halves = [[ref.at[pl.ds(i * N, N)] for ref in (x0, x1, y0, y1)] for i in range(2)]
-    aaz = assemble(sizes, pos, aaz_q, halves[0])
-    aaw = assemble(sizes, pos, aaw_q, halves[1])
+def late_dots_kernel(sizes, scalars, b, near_r, s, y, z, au, az, aaw, inverse, early, q,
+                     x0, x1, y0, y1, aaz_out, row):
+    aaz = assemble(sizes, position(), q, (x0, x1, y0, y1))
     store(aaz_out, aaz)
-    store(aaw_out, aaw)
     alpha, omega = guess(scalars, s)
     e = [tiles(ref) for ref in (near_r, s, y, z, au, az)]
+    aaw = tiles(aaw)
     ay = [e[4][i] - omega * (aaw[i] - alpha * aaz[i]) for i in range(N)]
     pairs = late_pairs(tiles(b), e + [ay, aaz])
     for_all(early[...] + dots_row(pairs, tiles(inverse), EARLY), row)
@@ -675,31 +660,23 @@
     recv = swap(parts)
     (q,) = call(z_kernel, [field], z, xy, *z_args, cost=COST)
     az, q, recv = apply(q, recv)
-    z_next, aw, values, z_xy, *parts = call(
+    aaz, q, recv = apply(q, recv)
+    (values,) = call(first_steps_kernel, [scalars], q, gathered, cost=COST)
+    az_next, aaw, xy, *parts = call(
         functools.partial(update_kernel, sizes),
-        [field] * 2 + [scalars] + [field] + faces,
-        gathered, s, z, az, q, *recv, *coefs, scratch=side,
+        [field] * 3 + faces,
+        values, az, aaz, q, *recv, *coefs, scratch=side,
     )
     recv = swap(parts)
-    x, r, p, s, w = call(update_rest_kernel, [field] * 5, values, b, s, z, az, cost=COST)
-    z = z_next
-    z_q, aw_q, *aw_parts = call(
-        two_z_kernel, [field] * 2 + faces, z, z_xy, aw, *coefs, *z_args,
-        cost=COST, scratch=[pltpu.VMEM((rows, size), f32)] + side,
-    )
-    az, xy, *parts = call(
-        functools.partial(apply_beside_kernel, sizes), [field] * 2 + [struct(2 * N)] * 4,
-        *aw_parts, z_q, *recv, *coefs, scratch=side,
-    )
-    recv = swap(parts)
-    (q,) = call(z_kernel, [field], az, xy, *z_args, cost=COST)
-    near_r, y, au, early = call(
-        early_dots_kernel, [field] * 3 + [jax.ShapeDtypeStruct((1, LANES), f32)],
-        values, b, r, s, w, z, aw, az, inverse, cost=COST,
-    )
-    aaw, aaz, products = call(
-        functools.partial(late_dots_kernel, sizes), [field] * 2 + [row],
-        values, b, near_r, s, y, z, au, az, inverse, early, q, aw_q, *recv,
+    (q,) = call(z_kernel, [field], az_next, xy, *z_args, cost=COST)
+    x, r, p, s, w, z, aw, near_r, y, au, early = call(
+        update_rest_kernel, [field] * 10 + [jax.ShapeDtypeStruct((1, LANES), f32)],
+        values, b, s, z, az, aaz, az_next, inverse, cost=COST,
+    )
+    az = az_next
+    aaz, products = call(
+        functools.partial(late_dots_kernel, sizes), [field, row],
+        values, b, near_r, s, y, z, au, az, aaw, inverse, early, q, *recv,
     )
     x, r = call(
         last_kernel, [field] * 2, spread(products), values, x, p, r, s, w, z, aw, az, aaw, aaz

time: 64.2 us -> 63.9 us (level)
  transfers between devices with their start and end apart: 29 -> 29, of which waited for: 10 -> 9; matrix products, arithmetic and copies ran while one was open for 0% -> 0% of each run, Pallas kernels for 8% -> 7%
where the time goes in v8:
time: 63.9 us; the launch traced here: 63.7 us
  starting transfers between devices  27.4 us (43%)
  waiting for transfers between devices  15 us (23%)
  Pallas kernels  10.2 us (16%)
  blocking collectives  10.2 us (16%)
  between operations  0.92 us (1%)
    ppermute x28, starting transfers between devices, permute(): return lax.ppermute(values, ('gx', 'gy'), pairs)  24 us
    ppermute x28, waiting for transfers between devices, permute(): return lax.ppermute(values, ('gx', 'gy'), pairs)  12.4 us
    all_to_all x1, blocking collectives, spread(): return lax.all_to_all(values, ('gx', 'gy'), 0, 0)  10.2 us
    pallas_call x20, Pallas kernels, call(): pl.pallas_call(kernel, out_shape=outs, in_specs=specs, out_specs=[VMEM] *...  10.2 us
    all_to_all x1, starting transfers between devices, spread(): return lax.all_to_all(values, ('gx', 'gy'), 0, 0)  3.38 us
    all_to_all x1, waiting for transfers between devices, spread(): return lax.all_to_all(values, ('gx', 'gy'), 0, 0)  2.59 us
  transfers between devices with their start and end apart: 29, of which 9 were waited for; matrix products, arithmetic and copies ran while one was open for 0% of the time, Pallas kernels for 7%

profile of v8, /device:TPU:0, one launch (start us, length us, event | category | flops | bytes accessed | tf_op | source)
XLA Modules:
  0.0 63.7 jit_solution(5674945772751506696)
XLA Ops:
  0.6 1.8 %shard_map.114 = (f32[24,512]{1,0:T(8,128)}, f32[24,512]{1,0:T(8,128)}) custom-call(f32[64,512]{1,0:T(8,128)} %bitcast.7, f32[64,512]{1,0:T(8,128)} %bitcast.9, s32[1,64]{1,0:T(1,128)} %bitcast.11, s32[1,64]{1,0:T(1,128)} %bitcast.13, f32[1,4]{1,0:T(1,128)} %bitcast.15), custom_call_target="tpu_custom_call" | custom-call | tf_op jit(solution)/shard_map/pallas_call | solution.py:584
  2.5 0.0 copy-start.7
  2.5 0.0 copy-start.8
  2.5 0.0 copy-start.9
  2.5 3.1 %collective-permute-start = (f32[24,512]{1,0:T(8,128)}, f32[24,512]{1,0:T(8,128)S(1)}, u32[]{:S(2)}, u32[]{:S(2)}) collective-permute-start(f32[24,512]{1,0:T(8,128)} %get-tuple-element.76), channel_id=1, source_target_pairs={{0,8},{1,2},{2,1},{3,4},{4,3},{5,6},{6,5},{7,15},{8,0},{9,10},{10,... | collective-permute-start | bytes 147464 | tf_op jit(solution)/shard_map/ppermute | solution.py:597
  5.6 0.0 collective-permute-start.1
  5.6 0.3 shard_map.113
  5.9 2.0 %collective-permute-done.odd = f32[24,512]{1,0:T(8,128)S(1)} collective-permute-done((f32[24,512]{1,0:T(8,128)}, f32[24,512]{1,0:T(8,128)S(1)}, u32[]{:S(2)}, u32[]{:S(2)}) %collective-permute-start) | collective-permute-done | bytes 49184 | tf_op jit(solution)/shard_map/ppermute | solution.py:597
  7.9 0.0 collective-permute-done.1.even
  7.9 0.1 collective-permute-start.2
  8.0 3.6 %collective-permute-start.3 = (f32[32,512]{1,0:T(8,128)S(1)}, f32[32,512]{1,0:T(8,128)S(1)}, u32[]{:S(2)}, u32[]{:S(2)}) collective-permute-start(f32[32,512]{1,0:T(8,128)S(1)} %get-tuple-element.83), channel_id=1, source_target_pairs={{0,8},{1,9},{2,10},{3,11},{4,12},{5,13},{6,14},{7,15},{8,0},{9,1},... | collective-permute-start | bytes 196616 | tf_op jit(solution)/shard_map/ppermute | solution.py:597
  11.6 0.4 shard_map.115
  12.0 1.9 %collective-permute-done.3.even = f32[32,512]{1,0:T(8,128)S(1)} collective-permute-done((f32[32,512]{1,0:T(8,128)S(1)}, f32[32,512]{1,0:T(8,128)S(1)}, u32[]{:S(2)}, u32[]{:S(2)}) %collective-permute-start.3) | collective-permute-done | bytes 65568 | tf_op jit(solution)/shard_map/ppermute | solution.py:597
  13.8 0.4 shard_map.117
  14.2 2.1 %collective-permute-start.4 = (f32[8,512]{1,0:T(8,128)S(1)}, f32[8,512]{1,0:T(8,128)S(1)}, u32[]{:S(2)}, u32[]{:S(2)}) collective-permute-start(f32[8,512]{1,0:T(8,128)S(1)} %get-tuple-element.89), channel_id=1, source_target_pairs={{0,8},{1,2},{2,1},{3,4},{4,3},{5,6},{6,5},{7,15},{8,0},{9,10},{10,... | collective-permute-start | bytes 49160 | tf_op jit(solution)/shard_map/ppermute | solution.py:597
  16.3 0.1 collective-permute-start.5
  16.4 1.3 %collective-permute-start.6 = (f32[8,512]{1,0:T(8,128)S(1)}, f32[8,512]{1,0:T(8,128)S(1)}, u32[]{:S(2)}, u32[]{:S(2)}) collective-permute-start(f32[8,512]{1,0:T(8,128)S(1)} %get-tuple-element.91), channel_id=1, source_target_pairs={{0,1},{1,0},{2,3},{3,2},{4,5},{5,4},{6,7},{7,6},{8,16},{9,17},{10,... | collective-permute-start | bytes 49160 | tf_op jit(solution)/shard_map/ppermute | solution.py:597
  17.7 0.0 collective-permute-start.7
  17.8 0.5 shard_map.118
  18.2 1.8 %collective-permute-done.5.x1 = f32[8,512]{1,0:T(8,128)S(1)} collective-permute-done((f32[8,512]{1,0:T(8,128)S(1)}, f32[8,512]{1,0:T(8,128)S(1)}, u32[]{:S(2)}, u32[]{:S(2)}) %collective-permute-start.5) | collective-permute-done | bytes 16416 | tf_op jit(solution)/shard_map/ppermute | solution.py:597
  20.1 0.0 collective-permute-done.6.y0
  20.1 0.0 collective-permute-done.7.y1
  20.1 0.4 shard_map.119
  20.5 2.1 %collective-permute-start.8 = (f32[8,512]{1,0:T(8,128)S(1)}, f32[8,512]{1,0:T(8,128)S(1)}, u32[]{:S(2)}, u32[]{:S(2)}) collective-permute-start(f32[8,512]{1,0:T(8,128)S(1)} %get-tuple-element.99), channel_id=1, source_target_pairs={{0,8},{1,2},{2,1},{3,4},{4,3},{5,6},{6,5},{7,15},{8,0},{9,10},{10,... | collective-permute-start | bytes 49160 | tf_op jit(solution)/shard_map/ppermute | solution.py:597
  22.5 0.1 collective-permute-start.9
  22.6 0.5 collective-permute-start.11
  23.1 0.4 shard_map.120.q
  23.6 0.7 %collective-permute-done.8.x0 = f32[8,512]{1,0:T(8,128)S(1)} collective-permute-done((f32[8,512]{1,0:T(8,128)S(1)}, f32[8,512]{1,0:T(8,128)S(1)}, u32[]{:S(2)}, u32[]{:S(2)}) %collective-permute-start.8) | collective-permute-done | bytes 16416 | tf_op jit(solution)/shard_map/ppermute | solution.py:597
  24.3 2.0 %collective-permute-done.9.x1 = f32[8,512]{1,0:T(8,128)S(1)} collective-permute-done((f32[8,512]{1,0:T(8,128)S(1)}, f32[8,512]{1,0:T(8,128)S(1)}, u32[]{:S(2)}, u32[]{:S(2)}) %collective-permute-start.9) | collective-permute-done | bytes 16416 | tf_op jit(solution)/shard_map/ppermute | solution.py:597
  26.3 0.8 %shard_map.121 = (f32[64,512]{1,0:T(8,128)S(1)}, f32[64,512]{1,0:T(8,128)S(1)}, f32[8,512]{1,0:T(8,128)S(1)}, f32[8,512]{1,0:T(8,128)S(1)}, f32[8,512]{1,0:T(8,1...) custom-call(f32[64,512]{1,0:T(8,128)S(1)} %get-tuple-element.84.b, f32[64,512]{1,0:T(8,128)S(1)} %get-tuple-element.94.refs_0_.s, ...), custom_call_target="tpu_custom_call" | custom-call | tf_op jit(solution)/shard_map/pallas_call | solution.py:584
  27.1 2.1 %collective-permute-start.12 = (f32[8,512]{1,0:T(8,128)S(1)}, f32[8,512]{1,0:T(8,128)S(1)}, u32[]{:S(2)}, u32[]{:S(2)}) collective-permute-start(f32[8,512]{1,0:T(8,128)S(1)} %get-tuple-element.105), channel_id=1, source_target_pairs={{0,8},{1,2},{2,1},{3,4},{4,3},{5,6},{6,5},{7,15},{8,0},{9,10},{10,... | collective-permute-start | bytes 49160 | tf_op jit(solution)/shard_map/ppermute | solution.py:597
  29.2 0.1 collective-permute-start.13
  29.3 0.5 collective-permute-start.15
  29.8 0.4 shard_map.122.q
  30.2 0.7 %collective-permute-done.12.x0 = f32[8,512]{1,0:T(8,128)S(1)} collective-permute-done((f32[8,512]{1,0:T(8,128)S(1)}, f32[8,512]{1,0:T(8,128)S(1)}, u32[]{:S(2)}, u32[]{:S(2)}) %collective-permute-start.12) | collective-permute-done | bytes 16416 | tf_op jit(solution)/shard_map/ppermute | solution.py:597
  30.9 2.0 %collective-permute-done.13.x1 = f32[8,512]{1,0:T(8,128)S(1)} collective-permute-done((f32[8,512]{1,0:T(8,128)S(1)}, f32[8,512]{1,0:T(8,128)S(1)}, u32[]{:S(2)}, u32[]{:S(2)}) %collective-permute-start.13) | collective-permute-done | bytes 16416 | tf_op jit(solution)/shard_map/ppermute | solution.py:597
  32.9 0.0 collective-permute-done.14.y0
  32.9 0.0 collective-permute-done.15.y1
  32.9 0.4 shard_map.123
  33.3 2.1 %collective-permute-start.16 = (f32[8,512]{1,0:T(8,128)S(1)}, f32[8,512]{1,0:T(8,128)S(1)}, u32[]{:S(2)}, u32[]{:S(2)}) collective-permute-start(f32[8,512]{1,0:T(8,128)S(1)} %get-tuple-element.111), channel_id=1, source_target_pairs={{0,8},{1,2},{2,1},{3,4},{4,3},{5,6},{6,5},{7,15},{8,0},{9,10},{10,... | collective-permute-start | bytes 49160 | tf_op jit(solution)/shard_map/ppermute | solution.py:597
  35.4 0.1 collective-permute-start.17
  35.5 0.0 collective-permute-start.18
  35.5 0.5 collective-permute-start.19
  36.0 3.4 %all-to-all-start = ((f32[32,1,128]{2,1,0:T(1,128)}), f32[32,1,128]{2,1,0:T(1,128)S(1)}, u32[]{:S(2)}, u32[]{:S(2)}) async-start(f32[32,1,128]{2,1,0:T(1,128)} %get-tuple-element.117), calls=%async_computation | async-start | bytes 32768 | tf_op jit(solution)/shard_map/all_to_all | solution.py:610
  39.4 0.5 shard_map.124.q
  39.8 0.0 collective-permute-done.17.x1
  39.9 0.4 shard_map.125
  40.3 1.8 %collective-permute-start.20 = (f32[8,512]{1,0:T(8,128)S(1)}, f32[8,512]{1,0:T(8,128)S(1)}, u32[]{:S(2)}, u32[]{:S(2)}) collective-permute-start(f32[8,512]{1,0:T(8,128)S(1)} %get-tuple-element.118), channel_id=1, source_target_pairs={{0,8},{1,2},{2,1},{3,4},{4,3},{5,6},{6,5},{7,15},{8,0},{9,10},{10,... | collective-permute-start | bytes 49160 | tf_op jit(solution)/shard_map/ppermute | solution.py:597
  42.1 0.3 collective-permute-start.21
  42.4 1.0 %collective-permute-start.22 = (f32[8,512]{1,0:T(8,128)S(1)}, f32[8,512]{1,0:T(8,128)S(1)}, u32[]{:S(2)}, u32[]{:S(2)}) collective-permute-start(f32[8,512]{1,0:T(8,128)S(1)} %get-tuple-element.120), channel_id=1, source_target_pairs={{0,1},{1,0},{2,3},{3,2},{4,5},{5,4},{6,7},{7,6},{8,16},{9,17},{10,... | collective-permute-start | bytes 49160 | tf_op jit(solution)/shard_map/ppermute | solution.py:597
  43.4 0.4 shard_map.126._.q
  43.9 2.6 %all-to-all-done.gathered = f32[32,1,128]{2,1,0:T(1,128)S(1)} async-done(((f32[32,1,128]{2,1,0:T(1,128)}), f32[32,1,128]{2,1,0:T(1,128)S(1)}, u32[]{:S(2)}, u32[]{:S(2)}) %all-to-all-start) | async-done | bytes 16416 | tf_op jit(solution)/shard_map/all_to_all | solution.py:610
  46.5 0.1 shard_map.127.scalars
  46.6 0.4 shard_map.128
  47.1 1.3 %collective-permute-start.24 = (f32[8,512]{1,0:T(8,128)S(1)}, f32[8,512]{1,0:T(8,128)S(1)}, u32[]{:S(2)}, u32[]{:S(2)}) collective-permute-start(f32[8,512]{1,0:T(8,128)S(1)} %get-tuple-element.131), channel_id=1, source_target_pairs={{0,8},{1,2},{2,1},{3,4},{4,3},{5,6},{6,5},{7,15},{8,0},{9,10},{10,... | collective-permute-start | bytes 49160 | tf_op jit(solution)/shard_map/ppermute | solution.py:597
  48.4 0.8 %collective-permute-start.25 = (f32[8,512]{1,0:T(8,128)S(1)}, f32[8,512]{1,0:T(8,128)S(1)}, u32[]{:S(2)}, u32[]{:S(2)}) collective-permute-start(f32[8,512]{1,0:T(8,128)S(1)} %get-tuple-element.132), channel_id=1, source_target_pairs={{0,8},{1,9},{2,10},{3,11},{4,12},{5,13},{6,14},{7,15},{8,0},{9,1},... | collective-permute-start | bytes 49160 | tf_op jit(solution)/shard_map/ppermute | solution.py:597
  49.2 0.5 collective-permute-start.27
  49.7 0.7 %shard_map.129 = (f32[64,512]{1,0:T(8,128)S(1)}, f32[64,512]{1,0:T(8,128)S(1)}, f32[64,512]{1,0:T(8,128)S(1)}, f32[64,512]{1,0:T(8,128)S(1)}, f32[64,512]{1,0:T(...) custom-call(f32[8,128]{1,0:T(8,128)S(1)} %shard_map.127.scalars, ...), custom_call_target="tpu_custom_call" | custom-call | flops 1048576 | bytes 1048576 | tf_op jit(solution)/shard_map/pallas_call | solution.py:584
  50.4 0.5 shard_map.130.q
  50.8 0.0 collective-permute-done.24.x0
  50.9 1.2 %collective-permute-done.25.x1 = f32[8,512]{1,0:T(8,128)S(1)} collective-permute-done((f32[8,512]{1,0:T(8,128)S(1)}, f32[8,512]{1,0:T(8,128)S(1)}, u32[]{:S(2)}, u32[]{:S(2)}) %collective-permute-start.25) | collective-permute-done | bytes 16416 | tf_op jit(solution)/shard_map/ppermute | solution.py:597
  52.1 0.3 shard_map.131
  52.4 10.2 %all_to_all.10.gathered = f32[32,1,128]{2,1,0:T(1,128)S(1)} all-to-all(f32[32,1,128]{2,1,0:T(1,128)S(1)} %get-tuple-element.135), channel_id=1, replica_groups=mesh['gx'=4,'gy'=8] {'gx','gy'}, dimensions={0} | all-to-all | bytes 32768 | tf_op jit(solution)/shard_map/all_to_all | solution.py:610
  62.7 1.0 %shard_map.132 = (f32[64,512]{1,0:T(8,128)}, f32[64,512]{1,0:T(8,128)}) custom-call(f32[32,1,128]{2,1,0:T(1,128)S(1)} %all_to_all.10.gathered, f32[8,128]{1,0:T(8,128)S(1)} %shard_map.127.scalars, f32[64,512]{1,0:T(8,128)S(1)} %get-tuple-element.136.x, f32[64,512]{1,0:T(8,128)S(1)} %get-tuple-element.137.p, f32[64,512]{1,0:T(8,128)S(1)} %get-tuple-element.138.r, ...), custom_call_target="tpu_custom_call" | custom-call | tf_op jit(solution)/shard_map/pallas_call | solution.py:584
  (35 shorter events, 0.1 us)
Async XLA Ops:
  0.6 5.0 %copy-start.5 = (f32[8,8,512]{2,1,0:T(8,128)S(1)}, f32[8,8,512]{2,1,0:T(8,128)}, u32[]{:S(2)}) copy-start(f32[8,8,512]{2,1,0:T(8,128)} %param.10) | copy-start | bytes 393220
  0.6 5.0 %copy-start.6 = (f32[8,8,512]{2,1,0:T(8,128)S(1)}, f32[8,8,512]{2,1,0:T(8,128)}, u32[]{:S(2)}) copy-start(f32[8,8,512]{2,1,0:T(8,128)} %param.11) | copy-start | bytes 393220
  2.5 3.2 %copy-start.7 = (s32[1,1,64]{2,1,0:T(1,128)S(1)}, s32[1,1,64]{2,1,0:T(1,128)}, u32[]{:S(2)}) copy-start(s32[1,1,64]{2,1,0:T(1,128)} %param.12) | copy-start | bytes 772
  2.5 3.2 %copy-start.8 = (s32[1,1,64]{2,1,0:T(1,128)S(1)}, s32[1,1,64]{2,1,0:T(1,128)}, u32[]{:S(2)}) copy-start(s32[1,1,64]{2,1,0:T(1,128)} %param.13) | copy-start | bytes 772
  2.5 3.1 %copy-start.9 = (f32[4]{0:T(128)S(1)}, f32[4]{0:T(128)}, u32[]{:S(2)}) copy-start(f32[4]{0:T(128)} %param.14) | copy-start | bytes 52
  2.5 5.4 %collective-permute-start = (f32[24,512]{1,0:T(8,128)}, f32[24,512]{1,0:T(8,128)S(1)}, u32[]{:S(2)}, u32[]{:S(2)}) collective-permute-start(f32[24,512]{1,0:T(8,128)} %get-tuple-element.76), channel_id=1, source_target_pairs={{0,8},{1,2},{2,1},{3,4},{4,3},{5,6},{6,5},{7,15},{8,0},{9,10},{10,... | collective-permute-start | bytes 147464 | tf_op jit(solution)/shard_map/ppermute | solution.py:597
  5.6 2.3 %collective-permute-start.1 = (f32[24,512]{1,0:T(8,128)}, f32[24,512]{1,0:T(8,128)S(1)}, u32[]{:S(2)}, u32[]{:S(2)}) collective-permute-start(f32[24,512]{1,0:T(8,128)} %get-tuple-element.77), channel_id=1, source_target_pairs={{0,1},{1,0},{2,3},{3,2},{4,5},{5,4},{6,7},{7,6},{8,9},{9,8},{10,11... | collective-permute-start | bytes 147464 | tf_op jit(solution)/shard_map/ppermute | solution.py:597
  7.9 3.7 %copy-start.4 = (f32[8,512]{1,0:T(8,128)S(1)}, f32[8,512]{1,0:T(8,128)}, u32[]{:S(2)}) copy-start(f32[8,512]{1,0:T(8,128)} %constant.14.clone.lanes.refs_8_) | copy-start | bytes 49156
  7.9 4.0 %collective-permute-start.2 = (f32[32,512]{1,0:T(8,128)S(1)}, f32[32,512]{1,0:T(8,128)S(1)}, u32[]{:S(2)}, u32[]{:S(2)}) collective-permute-start(f32[32,512]{1,0:T(8,128)S(1)} %get-tuple-element.82), channel_id=1, source_target_pairs={{0,1},{1,0},{2,3},{3,2},{4,5},{5,4},{6,7},{7,6},{8,16},{9,17},{10,... | collective-permute-start | bytes 196616 | tf_op jit(solution)/shard_map/ppermute | solution.py:597
  8.0 5.8 %collective-permute-start.3 = (f32[32,512]{1,0:T(8,128)S(1)}, f32[32,512]{1,0:T(8,128)S(1)}, u32[]{:S(2)}, u32[]{:S(2)}) collective-permute-start(f32[32,512]{1,0:T(8,128)S(1)} %get-tuple-element.83), channel_id=1, source_target_pairs={{0,8},{1,9},{2,10},{3,11},{4,12},{5,13},{6,14},{7,15},{8,0},{9,1},... | collective-permute-start | bytes 196616 | tf_op jit(solution)/shard_map/ppermute | solution.py:597
  13.8 3.9 %copy-start = (bf16[256,256]{1,0:T(8,128)(2,1)S(1)}, bf16[256,256]{1,0:T(8,128)(2,1)}, u32[]{:S(2)}) copy-start(bf16[256,256]{1,0:T(8,128)(2,1)} %constant.12.clone.b1.refs_6_) | copy-start | bytes 393220
  13.8 3.9 %copy-start.1 = (bf16[256,256]{1,0:T(8,128)(2,1)S(1)}, bf16[256,256]{1,0:T(8,128)(2,1)}, u32[]{:S(2)}) copy-start(bf16[256,256]{1,0:T(8,128)(2,1)} %constant.10.clone.f1.refs_4_) | copy-start | bytes 393220
  13.8 3.9 %copy-start.2 = (bf16[256,128]{1,0:T(8,128)(2,1)S(1)}, bf16[256,128]{1,0:T(8,128)(2,1)}, u32[]{:S(2)}) copy-start(bf16[256,128]{1,0:T(8,128)(2,1)} %constant.13.clone.b2.refs_7_) | copy-start | bytes 196612
  13.8 3.9 %copy-start.3 = (bf16[256,128]{1,0:T(8,128)(2,1)S(1)}, bf16[256,128]{1,0:T(8,128)(2,1)}, u32[]{:S(2)}) copy-start(bf16[256,128]{1,0:T(8,128)(2,1)} %constant.11.clone.f2.refs_5_) | copy-start | bytes 196612
  14.2 4.0 %collective-permute-start.4 = (f32[8,512]{1,0:T(8,128)S(1)}, f32[8,512]{1,0:T(8,128)S(1)}, u32[]{:S(2)}, u32[]{:S(2)}) collective-permute-start(f32[8,512]{1,0:T(8,128)S(1)} %get-tuple-element.89), channel_id=1, source_target_pairs={{0,8},{1,2},{2,1},{3,4},{4,3},{5,6},{6,5},{7,15},{8,0},{9,10},{10,... | collective-permute-start | bytes 49160 | tf_op jit(solution)/shard_map/ppermute | solution.py:597
  16.3 3.7 %collective-permute-start.5 = (f32[8,512]{1,0:T(8,128)S(1)}, f32[8,512]{1,0:T(8,128)S(1)}, u32[]{:S(2)}, u32[]{:S(2)}) collective-permute-start(f32[8,512]{1,0:T(8,128)S(1)} %get-tuple-element.90), channel_id=1, source_target_pairs={{0,8},{1,9},{2,10},{3,11},{4,12},{5,13},{6,14},{7,15},{8,0},{9,1},... | collective-permute-start | bytes 49160 | tf_op jit(solution)/shard_map/ppermute | solution.py:597
  16.4 3.7 %collective-permute-start.6 = (f32[8,512]{1,0:T(8,128)S(1)}, f32[8,512]{1,0:T(8,128)S(1)}, u32[]{:S(2)}, u32[]{:S(2)}) collective-permute-start(f32[8,512]{1,0:T(8,128)S(1)} %get-tuple-element.91), channel_id=1, source_target_pairs={{0,1},{1,0},{2,3},{3,2},{4,5},{5,4},{6,7},{7,6},{8,16},{9,17},{10,... | collective-permute-start | bytes 49160 | tf_op jit(solution)/shard_map/ppermute | solution.py:597
  17.7 2.3 %collective-permute-start.7 = (f32[8,512]{1,0:T(8,128)S(1)}, f32[8,512]{1,0:T(8,128)S(1)}, u32[]{:S(2)}, u32[]{:S(2)}) collective-permute-start(f32[8,512]{1,0:T(8,128)S(1)} %get-tuple-element.92), channel_id=1, source_target_pairs={{0,1},{1,0},{2,3},{3,2},{4,5},{5,4},{6,7},{7,6},{8,9},{9,8},{10,11... | collective-permute-start | bytes 49160 | tf_op jit(solution)/shard_map/ppermute | solution.py:597
  20.5 3.8 %collective-permute-start.8 = (f32[8,512]{1,0:T(8,128)S(1)}, f32[8,512]{1,0:T(8,128)S(1)}, u32[]{:S(2)}, u32[]{:S(2)}) collective-permute-start(f32[8,512]{1,0:T(8,128)S(1)} %get-tuple-element.99), channel_id=1, source_target_pairs={{0,8},{1,2},{2,1},{3,4},{4,3},{5,6},{6,5},{7,15},{8,0},{9,10},{10,... | collective-permute-start | bytes 49160 | tf_op jit(solution)/shard_map/ppermute | solution.py:597
  22.5 3.7 %collective-permute-start.9 = (f32[8,512]{1,0:T(8,128)S(1)}, f32[8,512]{1,0:T(8,128)S(1)}, u32[]{:S(2)}, u32[]{:S(2)}) collective-permute-start(f32[8,512]{1,0:T(8,128)S(1)} %get-tuple-element.100), channel_id=1, source_target_pairs={{0,8},{1,9},{2,10},{3,11},{4,12},{5,13},{6,14},{7,15},{8,0},{9,1},... | collective-permute-start | bytes 49160 | tf_op jit(solution)/shard_map/ppermute | solution.py:597
  22.6 3.7 %collective-permute-start.10 = (f32[8,512]{1,0:T(8,128)S(1)}, f32[8,512]{1,0:T(8,128)S(1)}, u32[]{:S(2)}, u32[]{:S(2)}) collective-permute-start(f32[8,512]{1,0:T(8,128)S(1)} %get-tuple-element.101), channel_id=1, source_target_pairs={{0,1},{1,0},{2,3},{3,2},{4,5},{5,4},{6,7},{7,6},{8,16},{9,17},{10,... | collective-permute-start | bytes 49160 | tf_op jit(solution)/shard_map/ppermute | solution.py:597
  22.6 3.7 %collective-permute-start.11 = (f32[8,512]{1,0:T(8,128)S(1)}, f32[8,512]{1,0:T(8,128)S(1)}, u32[]{:S(2)}, u32[]{:S(2)}) collective-permute-start(f32[8,512]{1,0:T(8,128)S(1)} %get-tuple-element.102), channel_id=1, source_target_pairs={{0,1},{1,0},{2,3},{3,2},{4,5},{5,4},{6,7},{7,6},{8,9},{9,8},{10,11... | collective-permute-start | bytes 49160 | tf_op jit(solution)/shard_map/ppermute | solution.py:597
  27.1 3.8 %collective-permute-start.12 = (f32[8,512]{1,0:T(8,128)S(1)}, f32[8,512]{1,0:T(8,128)S(1)}, u32[]{:S(2)}, u32[]{:S(2)}) collective-permute-start(f32[8,512]{1,0:T(8,128)S(1)} %get-tuple-element.105), channel_id=1, source_target_pairs={{0,8},{1,2},{2,1},{3,4},{4,3},{5,6},{6,5},{7,15},{8,0},{9,10},{10,... | collective-permute-start | bytes 49160 | tf_op jit(solution)/shard_map/ppermute | solution.py:597
  29.2 3.7 %collective-permute-start.13 = (f32[8,512]{1,0:T(8,128)S(1)}, f32[8,512]{1,0:T(8,128)S(1)}, u32[]{:S(2)}, u32[]{:S(2)}) collective-permute-start(f32[8,512]{1,0:T(8,128)S(1)} %get-tuple-element.106), channel_id=1, source_target_pairs={{0,8},{1,9},{2,10},{3,11},{4,12},{5,13},{6,14},{7,15},{8,0},{9,1},... | collective-permute-start | bytes 49160 | tf_op jit(solution)/shard_map/ppermute | solution.py:597
  29.3 3.7 %collective-permute-start.14 = (f32[8,512]{1,0:T(8,128)S(1)}, f32[8,512]{1,0:T(8,128)S(1)}, u32[]{:S(2)}, u32[]{:S(2)}) collective-permute-start(f32[8,512]{1,0:T(8,128)S(1)} %get-tuple-element.107), channel_id=1, source_target_pairs={{0,1},{1,0},{2,3},{3,2},{4,5},{5,4},{6,7},{7,6},{8,16},{9,17},{10,... | collective-permute-start | bytes 49160 | tf_op jit(solution)/shard_map/ppermute | solution.py:597
  29.3 3.7 %collective-permute-start.15 = (f32[8,512]{1,0:T(8,128)S(1)}, f32[8,512]{1,0:T(8,128)S(1)}, u32[]{:S(2)}, u32[]{:S(2)}) collective-permute-start(f32[8,512]{1,0:T(8,128)S(1)} %get-tuple-element.108), channel_id=1, source_target_pairs={{0,1},{1,0},{2,3},{3,2},{4,5},{5,4},{6,7},{7,6},{8,9},{9,8},{10,11... | collective-permute-start | bytes 49160 | tf_op jit(solution)/shard_map/ppermute | solution.py:597
  33.3 6.5 %collective-permute-start.16 = (f32[8,512]{1,0:T(8,128)S(1)}, f32[8,512]{1,0:T(8,128)S(1)}, u32[]{:S(2)}, u32[]{:S(2)}) collective-permute-start(f32[8,512]{1,0:T(8,128)S(1)} %get-tuple-element.111), channel_id=1, source_target_pairs={{0,8},{1,2},{2,1},{3,4},{4,3},{5,6},{6,5},{7,15},{8,0},{9,10},{10,... | collective-permute-start | bytes 49160 | tf_op jit(solution)/shard_map/ppermute | solution.py:597
  35.4 4.4 %collective-permute-start.17 = (f32[8,512]{1,0:T(8,128)S(1)}, f32[8,512]{1,0:T(8,128)S(1)}, u32[]{:S(2)}, u32[]{:S(2)}) collective-permute-start(f32[8,512]{1,0:T(8,128)S(1)} %get-tuple-element.112), channel_id=1, source_target_pairs={{0,8},{1,9},{2,10},{3,11},{4,12},{5,13},{6,14},{7,15},{8,0},{9,1},... | collective-permute-start | bytes 49160 | tf_op jit(solution)/shard_map/ppermute | solution.py:597
  35.5 4.4 %collective-permute-start.18 = (f32[8,512]{1,0:T(8,128)S(1)}, f32[8,512]{1,0:T(8,128)S(1)}, u32[]{:S(2)}, u32[]{:S(2)}) collective-permute-start(f32[8,512]{1,0:T(8,128)S(1)} %get-tuple-element.113), channel_id=1, source_target_pairs={{0,1},{1,0},{2,3},{3,2},{4,5},{5,4},{6,7},{7,6},{8,16},{9,17},{10,... | collective-permute-start | bytes 49160 | tf_op jit(solution)/shard_map/ppermute | solution.py:597
  35.5 4.4 %collective-permute-start.19 = (f32[8,512]{1,0:T(8,128)S(1)}, f32[8,512]{1,0:T(8,128)S(1)}, u32[]{:S(2)}, u32[]{:S(2)}) collective-permute-start(f32[8,512]{1,0:T(8,128)S(1)} %get-tuple-element.114), channel_id=1, source_target_pairs={{0,1},{1,0},{2,3},{3,2},{4,5},{5,4},{6,7},{7,6},{8,9},{9,8},{10,11... | collective-permute-start | bytes 49160 | tf_op jit(solution)/shard_map/ppermute | solution.py:597
  36.0 10.5 %all-to-all-start = ((f32[32,1,128]{2,1,0:T(1,128)}), f32[32,1,128]{2,1,0:T(1,128)S(1)}, u32[]{:S(2)}, u32[]{:S(2)}) async-start(f32[32,1,128]{2,1,0:T(1,128)} %get-tuple-element.117), calls=%async_computation | async-start | bytes 32768 | tf_op jit(solution)/shard_map/all_to_all | solution.py:610
  40.3 6.3 %collective-permute-start.20 = (f32[8,512]{1,0:T(8,128)S(1)}, f32[8,512]{1,0:T(8,128)S(1)}, u32[]{:S(2)}, u32[]{:S(2)}) collective-permute-start(f32[8,512]{1,0:T(8,128)S(1)} %get-tuple-element.118), channel_id=1, source_target_pairs={{0,8},{1,2},{2,1},{3,4},{4,3},{5,6},{6,5},{7,15},{8,0},{9,10},{10,... | collective-permute-start | bytes 49160 | tf_op jit(solution)/shard_map/ppermute | solution.py:597
  42.1 4.5 %collective-permute-start.21 = (f32[8,512]{1,0:T(8,128)S(1)}, f32[8,512]{1,0:T(8,128)S(1)}, u32[]{:S(2)}, u32[]{:S(2)}) collective-permute-start(f32[8,512]{1,0:T(8,128)S(1)} %get-tuple-element.119), channel_id=1, source_target_pairs={{0,8},{1,9},{2,10},{3,11},{4,12},{5,13},{6,14},{7,15},{8,0},{9,1},... | collective-permute-start | bytes 49160 | tf_op jit(solution)/shard_map/ppermute | solution.py:597
  42.4 4.2 %collective-permute-start.22 = (f32[8,512]{1,0:T(8,128)S(1)}, f32[8,512]{1,0:T(8,128)S(1)}, u32[]{:S(2)}, u32[]{:S(2)}) collective-permute-start(f32[8,512]{1,0:T(8,128)S(1)} %get-tuple-element.120), channel_id=1, source_target_pairs={{0,1},{1,0},{2,3},{3,2},{4,5},{5,4},{6,7},{7,6},{8,16},{9,17},{10,... | collective-permute-start | bytes 49160 | tf_op jit(solution)/shard_map/ppermute | solution.py:597
  43.4 3.2 %collective-permute-start.23 = (f32[8,512]{1,0:T(8,128)S(1)}, f32[8,512]{1,0:T(8,128)S(1)}, u32[]{:S(2)}, u32[]{:S(2)}) collective-permute-start(f32[8,512]{1,0:T(8,128)S(1)} %get-tuple-element.121), channel_id=1, source_target_pairs={{0,1},{1,0},{2,3},{3,2},{4,5},{5,4},{6,7},{7,6},{8,9},{9,8},{10,11... | collective-permute-start | bytes 49160 | tf_op jit(solution)/shard_map/ppermute | solution.py:597
  47.1 3.8 %collective-permute-start.24 = (f32[8,512]{1,0:T(8,128)S(1)}, f32[8,512]{1,0:T(8,128)S(1)}, u32[]{:S(2)}, u32[]{:S(2)}) collective-permute-start(f32[8,512]{1,0:T(8,128)S(1)} %get-tuple-element.131), channel_id=1, source_target_pairs={{0,8},{1,2},{2,1},{3,4},{4,3},{5,6},{6,5},{7,15},{8,0},{9,10},{10,... | collective-permute-start | bytes 49160 | tf_op jit(solution)/shard_map/ppermute | solution.py:597
  48.4 3.7 %collective-permute-start.25 = (f32[8,512]{1,0:T(8,128)S(1)}, f32[8,512]{1,0:T(8,128)S(1)}, u32[]{:S(2)}, u32[]{:S(2)}) collective-permute-start(f32[8,512]{1,0:T(8,128)S(1)} %get-tuple-element.132), channel_id=1, source_target_pairs={{0,8},{1,9},{2,10},{3,11},{4,12},{5,13},{6,14},{7,15},{8,0},{9,1},... | collective-permute-start | bytes 49160 | tf_op jit(solution)/shard_map/ppermute | solution.py:597
  49.2 3.0 %collective-permute-start.26 = (f32[8,512]{1,0:T(8,128)S(1)}, f32[8,512]{1,0:T(8,128)S(1)}, u32[]{:S(2)}, u32[]{:S(2)}) collective-permute-start(f32[8,512]{1,0:T(8,128)S(1)} %get-tuple-element.133), channel_id=1, source_target_pairs={{0,1},{1,0},{2,3},{3,2},{4,5},{5,4},{6,7},{7,6},{8,16},{9,17},{10,... | collective-permute-start | bytes 49160 | tf_op jit(solution)/shard_map/ppermute | solution.py:597
  49.2 3.0 %collective-permute-start.27 = (f32[8,512]{1,0:T(8,128)S(1)}, f32[8,512]{1,0:T(8,128)S(1)}, u32[]{:S(2)}, u32[]{:S(2)}) collective-permute-start(f32[8,512]{1,0:T(8,128)S(1)} %get-tuple-element.134), channel_id=1, source_target_pairs={{0,1},{1,0},{2,3},{3,2},{4,5},{5,4},{6,7},{7,6},{8,9},{9,8},{10,11... | collective-permute-start | bytes 49160 | tf_op jit(solution)/shard_map/ppermute | solution.py:597

commit v9 on v8

--- a/solution.py
+++ b/solution.py
@@ -444,16 +444,13 @@
     along_z(*refs)
 
 
-def first_dots_kernel(sizes, b, s, inverse, q, x0, x1, y0, y1, kx, ky, advect, z_out, xy_out, *refs):
-    *sends, row_out, low, high, row, sem = refs
-    pos = position()
-    z = assemble(sizes, pos, q, (x0, x1, y0, y1))
-    store(z_out, z)
-    b, s = tiles(b), tiles(s)
-    for_all(dots_row([(b, b), (b, s), (b, z), (s, s), (s, z), (z, z)], tiles(inverse)), row)
+def z_dots_kernel(b, s, inverse, z, *refs):
+    *shared, row_out, row, sem = refs
+    b, s, z_ = tiles(b), tiles(s), tiles(z)
+    for_all(dots_row([(b, b), (b, s), (b, z_), (s, s), (s, z_), (z_, z_)], tiles(inverse)), row)
     copy = pltpu.make_async_copy(row, row_out, sem)
     copy.start()
-    operate(pos, z, kx, ky, advect, xy_out, sends, low, high)
+    along_z(z, *shared)
     copy.wait()
 
 
@@ -652,13 +649,15 @@
         return v, q, recv
 
     s, q, recv = apply(q, recv)
-    z, xy, *parts, products = call(
-        functools.partial(first_dots_kernel, sizes), [field] * 2 + faces + [row],
-        b, s, inverse, q, *recv, *coefs, scratch=side + row_side, hbm_out=1,
+    z, xy, *parts = call(
+        functools.partial(apply_kernel, sizes), [field] * 2 + faces, q, *recv, *coefs, scratch=side
+    )
+    recv = swap(parts)
+    q, products = call(
+        z_dots_kernel, [field, row], b, s, inverse, z, xy, *z_args,
+        cost=COST, scratch=row_side, hbm_out=1,
     )
     gathered = spread(products)
-    recv = swap(parts)
-    (q,) = call(z_kernel, [field], z, xy, *z_args, cost=COST)
     az, q, recv = apply(q, recv)
     aaz, q, recv = apply(q, recv)
     (values,) = call(first_steps_kernel, [scalars], q, gathered, cost=COST)

time: 63.9 us -> 63.5 us (level)
  transfers between devices with their start and end apart: 29 -> 29, of which waited for: 9 -> 9; matrix products, arithmetic and copies ran while one was open for 0% -> 0% of each run, Pallas kernels for 7% -> 8%
where the time goes in v9:
time: 63.5 us; the launch traced here: 63.3 us
  starting transfers between devices  27.4 us (43%)
  waiting for transfers between devices  14.4 us (23%)
  Pallas kernels  10.3 us (16%)
  blocking collectives  10.2 us (16%)
  between operations  0.91 us (1%)
    ppermute x28, starting transfers between devices, permute(): return lax.ppermute(values, ('gx', 'gy'), pairs)  24 us
    ppermute x28, waiting for transfers between devices, permute(): return lax.ppermute(values, ('gx', 'gy'), pairs)  11.8 us
    pallas_call x20, Pallas kernels, call(): pl.pallas_call(kernel, out_shape=outs, in_specs=specs, out_specs=[VMEM] *...  10.3 us
    all_to_all x1, blocking collectives, spread(): return lax.all_to_all(values, ('gx', 'gy'), 0, 0)  10.2 us
    all_to_all x1, starting transfers between devices, spread(): return lax.all_to_all(values, ('gx', 'gy'), 0, 0)  3.38 us
    all_to_all x1, waiting for transfers between devices, spread(): return lax.all_to_all(values, ('gx', 'gy'), 0, 0)  2.59 us
  transfers between devices with their start and end apart: 29, of which 9 were waited for; matrix products, arithmetic and copies ran while one was open for 0% of the time, Pallas kernels for 8%

profile of v9, /device:TPU:0, one launch (start us, length us, event | category | flops | bytes accessed | tf_op | source)
XLA Modules:
  0.0 63.3 jit_solution(16679638014488884747)
XLA Ops:
  0.6 1.8 %shard_map.114 = (f32[24,512]{1,0:T(8,128)}, f32[24,512]{1,0:T(8,128)}) custom-call(f32[64,512]{1,0:T(8,128)} %bitcast.7, f32[64,512]{1,0:T(8,128)} %bitcast.9, s32[1,64]{1,0:T(1,128)} %bitcast.11, s32[1,64]{1,0:T(1,128)} %bitcast.13, f32[1,4]{1,0:T(1,128)} %bitcast.15), custom_call_target="tpu_custom_call" | custom-call | tf_op jit(solution)/shard_map/pallas_call | solution.py:581
  2.5 0.0 copy-start.7
  2.5 0.0 copy-start.8
  2.5 0.0 copy-start.9
  2.5 3.1 %collective-permute-start = (f32[24,512]{1,0:T(8,128)}, f32[24,512]{1,0:T(8,128)S(1)}, u32[]{:S(2)}, u32[]{:S(2)}) collective-permute-start(f32[24,512]{1,0:T(8,128)} %get-tuple-element.77), channel_id=1, source_target_pairs={{0,8},{1,2},{2,1},{3,4},{4,3},{5,6},{6,5},{7,15},{8,0},{9,10},{10,... | collective-permute-start | bytes 147464 | tf_op jit(solution)/shard_map/ppermute | solution.py:594
  5.6 0.0 collective-permute-start.1
  5.6 0.3 shard_map.113
  5.9 2.0 %collective-permute-done.odd = f32[24,512]{1,0:T(8,128)S(1)} collective-permute-done((f32[24,512]{1,0:T(8,128)}, f32[24,512]{1,0:T(8,128)S(1)}, u32[]{:S(2)}, u32[]{:S(2)}) %collective-permute-start) | collective-permute-done | bytes 49184 | tf_op jit(solution)/shard_map/ppermute | solution.py:594
  7.9 0.0 collective-permute-done.1.even
  7.9 0.1 collective-permute-start.2
  8.0 3.6 %collective-permute-start.3 = (f32[32,512]{1,0:T(8,128)S(1)}, f32[32,512]{1,0:T(8,128)S(1)}, u32[]{:S(2)}, u32[]{:S(2)}) collective-permute-start(f32[32,512]{1,0:T(8,128)S(1)} %get-tuple-element.84), channel_id=1, source_target_pairs={{0,8},{1,9},{2,10},{3,11},{4,12},{5,13},{6,14},{7,15},{8,0},{9,1},... | collective-permute-start | bytes 196616 | tf_op jit(solution)/shard_map/ppermute | solution.py:594
  11.6 0.4 shard_map.115
  12.0 1.9 %collective-permute-done.3.even = f32[32,512]{1,0:T(8,128)S(1)} collective-permute-done((f32[32,512]{1,0:T(8,128)S(1)}, f32[32,512]{1,0:T(8,128)S(1)}, u32[]{:S(2)}, u32[]{:S(2)}) %collective-permute-start.3) | collective-permute-done | bytes 65568 | tf_op jit(solution)/shard_map/ppermute | solution.py:594
  13.8 0.4 shard_map.117
  14.2 2.1 %collective-permute-start.4 = (f32[8,512]{1,0:T(8,128)S(1)}, f32[8,512]{1,0:T(8,128)S(1)}, u32[]{:S(2)}, u32[]{:S(2)}) collective-permute-start(f32[8,512]{1,0:T(8,128)S(1)} %get-tuple-element.90), channel_id=1, source_target_pairs={{0,8},{1,2},{2,1},{3,4},{4,3},{5,6},{6,5},{7,15},{8,0},{9,10},{10,... | collective-permute-start | bytes 49160 | tf_op jit(solution)/shard_map/ppermute | solution.py:594
  16.3 0.1 collective-permute-start.5
  16.4 1.3 %collective-permute-start.6 = (f32[8,512]{1,0:T(8,128)S(1)}, f32[8,512]{1,0:T(8,128)S(1)}, u32[]{:S(2)}, u32[]{:S(2)}) collective-permute-start(f32[8,512]{1,0:T(8,128)S(1)} %get-tuple-element.92), channel_id=1, source_target_pairs={{0,1},{1,0},{2,3},{3,2},{4,5},{5,4},{6,7},{7,6},{8,16},{9,17},{10,... | collective-permute-start | bytes 49160 | tf_op jit(solution)/shard_map/ppermute | solution.py:594
  17.7 0.0 collective-permute-start.7
  17.8 0.5 shard_map.118
  18.2 1.8 %collective-permute-done.5.x1 = f32[8,512]{1,0:T(8,128)S(1)} collective-permute-done((f32[8,512]{1,0:T(8,128)S(1)}, f32[8,512]{1,0:T(8,128)S(1)}, u32[]{:S(2)}, u32[]{:S(2)}) %collective-permute-start.5) | collective-permute-done | bytes 16416 | tf_op jit(solution)/shard_map/ppermute | solution.py:594
  20.1 0.0 collective-permute-done.6.y0
  20.1 0.0 collective-permute-done.7.y1
  20.1 0.4 shard_map.119
  20.5 2.1 %collective-permute-start.8 = (f32[8,512]{1,0:T(8,128)S(1)}, f32[8,512]{1,0:T(8,128)S(1)}, u32[]{:S(2)}, u32[]{:S(2)}) collective-permute-start(f32[8,512]{1,0:T(8,128)S(1)} %get-tuple-element.100), channel_id=1, source_target_pairs={{0,8},{1,2},{2,1},{3,4},{4,3},{5,6},{6,5},{7,15},{8,0},{9,10},{10,... | collective-permute-start | bytes 49160 | tf_op jit(solution)/shard_map/ppermute | solution.py:594
  22.5 0.1 collective-permute-start.9
  22.6 0.5 collective-permute-start.11
  23.1 0.4 shard_map.120.q
  23.6 0.7 %collective-permute-done.8.x0 = f32[8,512]{1,0:T(8,128)S(1)} collective-permute-done((f32[8,512]{1,0:T(8,128)S(1)}, f32[8,512]{1,0:T(8,128)S(1)}, u32[]{:S(2)}, u32[]{:S(2)}) %collective-permute-start.8) | collective-permute-done | bytes 16416 | tf_op jit(solution)/shard_map/ppermute | solution.py:594
  24.3 2.0 %collective-permute-done.9.x1 = f32[8,512]{1,0:T(8,128)S(1)} collective-permute-done((f32[8,512]{1,0:T(8,128)S(1)}, f32[8,512]{1,0:T(8,128)S(1)}, u32[]{:S(2)}, u32[]{:S(2)}) %collective-permute-start.9) | collective-permute-done | bytes 16416 | tf_op jit(solution)/shard_map/ppermute | solution.py:594
  26.3 0.4 shard_map.121
  26.7 2.1 %collective-permute-start.12 = (f32[8,512]{1,0:T(8,128)S(1)}, f32[8,512]{1,0:T(8,128)S(1)}, u32[]{:S(2)}, u32[]{:S(2)}) collective-permute-start(f32[8,512]{1,0:T(8,128)S(1)} %get-tuple-element.107), channel_id=1, source_target_pairs={{0,8},{1,2},{2,1},{3,4},{4,3},{5,6},{6,5},{7,15},{8,0},{9,10},{10,... | collective-permute-start | bytes 49160 | tf_op jit(solution)/shard_map/ppermute | solution.py:594
  28.7 0.1 collective-permute-start.13
  28.8 0.0 collective-permute-start.14
  28.8 0.5 collective-permute-start.15
  29.3 1.0 %shard_map.122 = (f32[64,512]{1,0:T(8,128)S(1)}, f32[32,1,128]{2,1,0:T(1,128)}) custom-call(f32[64,512]{1,0:T(8,128)S(1)} %get-tuple-element.85.b, f32[64,512]{1,0:T(8,128)S(1)} %get-tuple-element.95.refs_0_.s, f32[64,512]{1,0:T(8,128)S(1)} %get-tuple-element.96.inverse, f32[64,512]{1,0:T(8,128)S(1)} %get-tuple-element.104.z, ...), custom_call_target="tpu_custom_call" | custom-call | flops 1048576 | bytes 1048576 | tf_op jit(solution)/shard_map/pallas_call | solution.py:581
  30.3 0.1 collective-permute-done.12.x0
  30.5 2.0 %collective-permute-done.13.x1 = f32[8,512]{1,0:T(8,128)S(1)} collective-permute-done((f32[8,512]{1,0:T(8,128)S(1)}, f32[8,512]{1,0:T(8,128)S(1)}, u32[]{:S(2)}, u32[]{:S(2)}) %collective-permute-start.13) | collective-permute-done | bytes 16416 | tf_op jit(solution)/shard_map/ppermute | solution.py:594
  32.5 0.0 collective-permute-done.14.y0
  32.5 0.0 collective-permute-done.15.y1
  32.5 0.4 shard_map.123
  32.9 2.1 %collective-permute-start.16 = (f32[8,512]{1,0:T(8,128)S(1)}, f32[8,512]{1,0:T(8,128)S(1)}, u32[]{:S(2)}, u32[]{:S(2)}) collective-permute-start(f32[8,512]{1,0:T(8,128)S(1)} %get-tuple-element.113), channel_id=1, source_target_pairs={{0,8},{1,2},{2,1},{3,4},{4,3},{5,6},{6,5},{7,15},{8,0},{9,10},{10,... | collective-permute-start | bytes 49160 | tf_op jit(solution)/shard_map/ppermute | solution.py:594
  34.9 0.1 collective-permute-start.17
  35.0 0.0 collective-permute-start.18
  35.0 0.5 collective-permute-start.19
  35.5 3.4 %all-to-all-start = ((f32[32,1,128]{2,1,0:T(1,128)}), f32[32,1,128]{2,1,0:T(1,128)S(1)}, u32[]{:S(2)}, u32[]{:S(2)}) async-start(f32[32,1,128]{2,1,0:T(1,128)} %get-tuple-element.119), calls=%async_computation | async-start | bytes 32768 | tf_op jit(solution)/shard_map/all_to_all | solution.py:607
  38.9 0.5 shard_map.124.q
  39.4 0.4 shard_map.125
  39.8 1.8 %collective-permute-start.20 = (f32[8,512]{1,0:T(8,128)S(1)}, f32[8,512]{1,0:T(8,128)S(1)}, u32[]{:S(2)}, u32[]{:S(2)}) collective-permute-start(f32[8,512]{1,0:T(8,128)S(1)} %get-tuple-element.120), channel_id=1, source_target_pairs={{0,8},{1,2},{2,1},{3,4},{4,3},{5,6},{6,5},{7,15},{8,0},{9,10},{10,... | collective-permute-start | bytes 49160 | tf_op jit(solution)/shard_map/ppermute | solution.py:594
  41.6 0.3 collective-permute-start.21
  41.9 1.0 %collective-permute-start.22 = (f32[8,512]{1,0:T(8,128)S(1)}, f32[8,512]{1,0:T(8,128)S(1)}, u32[]{:S(2)}, u32[]{:S(2)}) collective-permute-start(f32[8,512]{1,0:T(8,128)S(1)} %get-tuple-element.122), channel_id=1, source_target_pairs={{0,1},{1,0},{2,3},{3,2},{4,5},{5,4},{6,7},{7,6},{8,16},{9,17},{10,... | collective-permute-start | bytes 49160 | tf_op jit(solution)/shard_map/ppermute | solution.py:594
  43.0 0.4 shard_map.126._.q
  43.4 2.6 %all-to-all-done.gathered = f32[32,1,128]{2,1,0:T(1,128)S(1)} async-done(((f32[32,1,128]{2,1,0:T(1,128)}), f32[32,1,128]{2,1,0:T(1,128)S(1)}, u32[]{:S(2)}, u32[]{:S(2)}) %all-to-all-start) | async-done | bytes 16416 | tf_op jit(solution)/shard_map/all_to_all | solution.py:607
  46.0 0.1 shard_map.127.scalars
  46.2 0.4 shard_map.128
  46.6 1.3 %collective-permute-start.24 = (f32[8,512]{1,0:T(8,128)S(1)}, f32[8,512]{1,0:T(8,128)S(1)}, u32[]{:S(2)}, u32[]{:S(2)}) collective-permute-start(f32[8,512]{1,0:T(8,128)S(1)} %get-tuple-element.133), channel_id=1, source_target_pairs={{0,8},{1,2},{2,1},{3,4},{4,3},{5,6},{6,5},{7,15},{8,0},{9,10},{10,... | collective-permute-start | bytes 49160 | tf_op jit(solution)/shard_map/ppermute | solution.py:594
  47.9 0.8 %collective-permute-start.25 = (f32[8,512]{1,0:T(8,128)S(1)}, f32[8,512]{1,0:T(8,128)S(1)}, u32[]{:S(2)}, u32[]{:S(2)}) collective-permute-start(f32[8,512]{1,0:T(8,128)S(1)} %get-tuple-element.134), channel_id=1, source_target_pairs={{0,8},{1,9},{2,10},{3,11},{4,12},{5,13},{6,14},{7,15},{8,0},{9,1},... | collective-permute-start | bytes 49160 | tf_op jit(solution)/shard_map/ppermute | solution.py:594
  48.7 0.5 collective-permute-start.27
  49.2 0.7 %shard_map.129 = (f32[64,512]{1,0:T(8,128)S(1)}, f32[64,512]{1,0:T(8,128)S(1)}, f32[64,512]{1,0:T(8,128)S(1)}, f32[64,512]{1,0:T(8,128)S(1)}, f32[64,512]{1,0:T(...) custom-call(f32[8,128]{1,0:T(8,128)S(1)} %shard_map.127.scalars, ...), custom_call_target="tpu_custom_call" | custom-call | flops 1048576 | bytes 1048576 | tf_op jit(solution)/shard_map/pallas_call | solution.py:581
  49.9 0.5 shard_map.130.q
  50.4 0.0 collective-permute-done.24.x0
  50.4 1.2 %collective-permute-done.25.x1 = f32[8,512]{1,0:T(8,128)S(1)} collective-permute-done((f32[8,512]{1,0:T(8,128)S(1)}, f32[8,512]{1,0:T(8,128)S(1)}, u32[]{:S(2)}, u32[]{:S(2)}) %collective-permute-start.25) | collective-permute-done | bytes 16416 | tf_op jit(solution)/shard_map/ppermute | solution.py:594
  51.7 0.3 shard_map.131
  52.0 10.2 %all_to_all.10.gathered = f32[32,1,128]{2,1,0:T(1,128)S(1)} all-to-all(f32[32,1,128]{2,1,0:T(1,128)S(1)} %get-tuple-element.137), channel_id=1, replica_groups=mesh['gx'=4,'gy'=8] {'gx','gy'}, dimensions={0} | all-to-all | bytes 32768 | tf_op jit(solution)/shard_map/all_to_all | solution.py:607
  62.2 1.0 %shard_map.132 = (f32[64,512]{1,0:T(8,128)}, f32[64,512]{1,0:T(8,128)}) custom-call(f32[32,1,128]{2,1,0:T(1,128)S(1)} %all_to_all.10.gathered, f32[8,128]{1,0:T(8,128)S(1)} %shard_map.127.scalars, f32[64,512]{1,0:T(8,128)S(1)} %get-tuple-element.138.x, f32[64,512]{1,0:T(8,128)S(1)} %get-tuple-element.139.p, f32[64,512]{1,0:T(8,128)S(1)} %get-tuple-element.140.r, ...), custom_call_target="tpu_custom_call" | custom-call | tf_op jit(solution)/shard_map/pallas_call | solution.py:581
  (35 shorter events, 0.1 us)
Async XLA Ops:
  0.6 5.0 %copy-start.5 = (f32[8,8,512]{2,1,0:T(8,128)S(1)}, f32[8,8,512]{2,1,0:T(8,128)}, u32[]{:S(2)}) copy-start(f32[8,8,512]{2,1,0:T(8,128)} %param.10) | copy-start | bytes 393220
  0.6 5.0 %copy-start.6 = (f32[8,8,512]{2,1,0:T(8,128)S(1)}, f32[8,8,512]{2,1,0:T(8,128)}, u32[]{:S(2)}) copy-start(f32[8,8,512]{2,1,0:T(8,128)} %param.11) | copy-start | bytes 393220
  2.5 3.2 %copy-start.7 = (s32[1,1,64]{2,1,0:T(1,128)S(1)}, s32[1,1,64]{2,1,0:T(1,128)}, u32[]{:S(2)}) copy-start(s32[1,1,64]{2,1,0:T(1,128)} %param.12) | copy-start | bytes 772
  2.5 3.2 %copy-start.8 = (s32[1,1,64]{2,1,0:T(1,128)S(1)}, s32[1,1,64]{2,1,0:T(1,128)}, u32[]{:S(2)}) copy-start(s32[1,1,64]{2,1,0:T(1,128)} %param.13) | copy-start | bytes 772
  2.5 3.1 %copy-start.9 = (f32[4]{0:T(128)S(1)}, f32[4]{0:T(128)}, u32[]{:S(2)}) copy-start(f32[4]{0:T(128)} %param.14) | copy-start | bytes 52
  2.5 5.4 %collective-permute-start = (f32[24,512]{1,0:T(8,128)}, f32[24,512]{1,0:T(8,128)S(1)}, u32[]{:S(2)}, u32[]{:S(2)}) collective-permute-start(f32[24,512]{1,0:T(8,128)} %get-tuple-element.77), channel_id=1, source_target_pairs={{0,8},{1,2},{2,1},{3,4},{4,3},{5,6},{6,5},{7,15},{8,0},{9,10},{10,... | collective-permute-start | bytes 147464 | tf_op jit(solution)/shard_map/ppermute | solution.py:594
  5.6 2.3 %collective-permute-start.1 = (f32[24,512]{1,0:T(8,128)}, f32[24,512]{1,0:T(8,128)S(1)}, u32[]{:S(2)}, u32[]{:S(2)}) collective-permute-start(f32[24,512]{1,0:T(8,128)} %get-tuple-element.78), channel_id=1, source_target_pairs={{0,1},{1,0},{2,3},{3,2},{4,5},{5,4},{6,7},{7,6},{8,9},{9,8},{10,11... | collective-permute-start | bytes 147464 | tf_op jit(solution)/shard_map/ppermute | solution.py:594
  7.9 3.7 %copy-start.4 = (f32[8,512]{1,0:T(8,128)S(1)}, f32[8,512]{1,0:T(8,128)}, u32[]{:S(2)}) copy-start(f32[8,512]{1,0:T(8,128)} %constant.14.clone.lanes.refs_8_.refs_7_) | copy-start | bytes 49156
  7.9 4.0 %collective-permute-start.2 = (f32[32,512]{1,0:T(8,128)S(1)}, f32[32,512]{1,0:T(8,128)S(1)}, u32[]{:S(2)}, u32[]{:S(2)}) collective-permute-start(f32[32,512]{1,0:T(8,128)S(1)} %get-tuple-element.83), channel_id=1, source_target_pairs={{0,1},{1,0},{2,3},{3,2},{4,5},{5,4},{6,7},{7,6},{8,16},{9,17},{10,... | collective-permute-start | bytes 196616 | tf_op jit(solution)/shard_map/ppermute | solution.py:594
  8.0 5.8 %collective-permute-start.3 = (f32[32,512]{1,0:T(8,128)S(1)}, f32[32,512]{1,0:T(8,128)S(1)}, u32[]{:S(2)}, u32[]{:S(2)}) collective-permute-start(f32[32,512]{1,0:T(8,128)S(1)} %get-tuple-element.84), channel_id=1, source_target_pairs={{0,8},{1,9},{2,10},{3,11},{4,12},{5,13},{6,14},{7,15},{8,0},{9,1},... | collective-permute-start | bytes 196616 | tf_op jit(solution)/shard_map/ppermute | solution.py:594
  13.8 3.9 %copy-start = (bf16[256,256]{1,0:T(8,128)(2,1)S(1)}, bf16[256,256]{1,0:T(8,128)(2,1)}, u32[]{:S(2)}) copy-start(bf16[256,256]{1,0:T(8,128)(2,1)} %constant.12.clone.b1.refs_6_.refs_5_) | copy-start | bytes 393220
  13.8 3.9 %copy-start.1 = (bf16[256,256]{1,0:T(8,128)(2,1)S(1)}, bf16[256,256]{1,0:T(8,128)(2,1)}, u32[]{:S(2)}) copy-start(bf16[256,256]{1,0:T(8,128)(2,1)} %constant.10.clone.f1.refs_4_.refs_3_) | copy-start | bytes 393220
  13.8 3.9 %copy-start.2 = (bf16[256,128]{1,0:T(8,128)(2,1)S(1)}, bf16[256,128]{1,0:T(8,128)(2,1)}, u32[]{:S(2)}) copy-start(bf16[256,128]{1,0:T(8,128)(2,1)} %constant.13.clone.b2.refs_7_.refs_6_) | copy-start | bytes 196612
  13.8 3.9 %copy-start.3 = (bf16[256,128]{1,0:T(8,128)(2,1)S(1)}, bf16[256,128]{1,0:T(8,128)(2,1)}, u32[]{:S(2)}) copy-start(bf16[256,128]{1,0:T(8,128)(2,1)} %constant.11.clone.f2.refs_5_.refs_4_) | copy-start | bytes 196612
  14.2 4.0 %collective-permute-start.4 = (f32[8,512]{1,0:T(8,128)S(1)}, f32[8,512]{1,0:T(8,128)S(1)}, u32[]{:S(2)}, u32[]{:S(2)}) collective-permute-start(f32[8,512]{1,0:T(8,128)S(1)} %get-tuple-element.90), channel_id=1, source_target_pairs={{0,8},{1,2},{2,1},{3,4},{4,3},{5,6},{6,5},{7,15},{8,0},{9,10},{10,... | collective-permute-start | bytes 49160 | tf_op jit(solution)/shard_map/ppermute | solution.py:594
  16.3 3.7 %collective-permute-start.5 = (f32[8,512]{1,0:T(8,128)S(1)}, f32[8,512]{1,0:T(8,128)S(1)}, u32[]{:S(2)}, u32[]{:S(2)}) collective-permute-start(f32[8,512]{1,0:T(8,128)S(1)} %get-tuple-element.91), channel_id=1, source_target_pairs={{0,8},{1,9},{2,10},{3,11},{4,12},{5,13},{6,14},{7,15},{8,0},{9,1},... | collective-permute-start | bytes 49160 | tf_op jit(solution)/shard_map/ppermute | solution.py:594
  16.4 3.7 %collective-permute-start.6 = (f32[8,512]{1,0:T(8,128)S(1)}, f32[8,512]{1,0:T(8,128)S(1)}, u32[]{:S(2)}, u32[]{:S(2)}) collective-permute-start(f32[8,512]{1,0:T(8,128)S(1)} %get-tuple-element.92), channel_id=1, source_target_pairs={{0,1},{1,0},{2,3},{3,2},{4,5},{5,4},{6,7},{7,6},{8,16},{9,17},{10,... | collective-permute-start | bytes 49160 | tf_op jit(solution)/shard_map/ppermute | solution.py:594
  17.7 2.3 %collective-permute-start.7 = (f32[8,512]{1,0:T(8,128)S(1)}, f32[8,512]{1,0:T(8,128)S(1)}, u32[]{:S(2)}, u32[]{:S(2)}) collective-permute-start(f32[8,512]{1,0:T(8,128)S(1)} %get-tuple-element.93), channel_id=1, source_target_pairs={{0,1},{1,0},{2,3},{3,2},{4,5},{5,4},{6,7},{7,6},{8,9},{9,8},{10,11... | collective-permute-start | bytes 49160 | tf_op jit(solution)/shard_map/ppermute | solution.py:594
  20.5 3.8 %collective-permute-start.8 = (f32[8,512]{1,0:T(8,128)S(1)}, f32[8,512]{1,0:T(8,128)S(1)}, u32[]{:S(2)}, u32[]{:S(2)}) collective-permute-start(f32[8,512]{1,0:T(8,128)S(1)} %get-tuple-element.100), channel_id=1, source_target_pairs={{0,8},{1,2},{2,1},{3,4},{4,3},{5,6},{6,5},{7,15},{8,0},{9,10},{10,... | collective-permute-start | bytes 49160 | tf_op jit(solution)/shard_map/ppermute | solution.py:594
  22.5 3.7 %collective-permute-start.9 = (f32[8,512]{1,0:T(8,128)S(1)}, f32[8,512]{1,0:T(8,128)S(1)}, u32[]{:S(2)}, u32[]{:S(2)}) collective-permute-start(f32[8,512]{1,0:T(8,128)S(1)} %get-tuple-element.101), channel_id=1, source_target_pairs={{0,8},{1,9},{2,10},{3,11},{4,12},{5,13},{6,14},{7,15},{8,0},{9,1},... | collective-permute-start | bytes 49160 | tf_op jit(solution)/shard_map/ppermute | solution.py:594
  22.6 3.7 %collective-permute-start.10 = (f32[8,512]{1,0:T(8,128)S(1)}, f32[8,512]{1,0:T(8,128)S(1)}, u32[]{:S(2)}, u32[]{:S(2)}) collective-permute-start(f32[8,512]{1,0:T(8,128)S(1)} %get-tuple-element.102), channel_id=1, source_target_pairs={{0,1},{1,0},{2,3},{3,2},{4,5},{5,4},{6,7},{7,6},{8,16},{9,17},{10,... | collective-permute-start | bytes 49160 | tf_op jit(solution)/shard_map/ppermute | solution.py:594
  22.6 3.7 %collective-permute-start.11 = (f32[8,512]{1,0:T(8,128)S(1)}, f32[8,512]{1,0:T(8,128)S(1)}, u32[]{:S(2)}, u32[]{:S(2)}) collective-permute-start(f32[8,512]{1,0:T(8,128)S(1)} %get-tuple-element.103), channel_id=1, source_target_pairs={{0,1},{1,0},{2,3},{3,2},{4,5},{5,4},{6,7},{7,6},{8,9},{9,8},{10,11... | collective-permute-start | bytes 49160 | tf_op jit(solution)/shard_map/ppermute | solution.py:594
  26.7 3.8 %collective-permute-start.12 = (f32[8,512]{1,0:T(8,128)S(1)}, f32[8,512]{1,0:T(8,128)S(1)}, u32[]{:S(2)}, u32[]{:S(2)}) collective-permute-start(f32[8,512]{1,0:T(8,128)S(1)} %get-tuple-element.107), channel_id=1, source_target_pairs={{0,8},{1,2},{2,1},{3,4},{4,3},{5,6},{6,5},{7,15},{8,0},{9,10},{10,... | collective-permute-start | bytes 49160 | tf_op jit(solution)/shard_map/ppermute | solution.py:594
  28.7 3.7 %collective-permute-start.13 = (f32[8,512]{1,0:T(8,128)S(1)}, f32[8,512]{1,0:T(8,128)S(1)}, u32[]{:S(2)}, u32[]{:S(2)}) collective-permute-start(f32[8,512]{1,0:T(8,128)S(1)} %get-tuple-element.108), channel_id=1, source_target_pairs={{0,8},{1,9},{2,10},{3,11},{4,12},{5,13},{6,14},{7,15},{8,0},{9,1},... | collective-permute-start | bytes 49160 | tf_op jit(solution)/shard_map/ppermute | solution.py:594
  28.8 3.7 %collective-permute-start.14 = (f32[8,512]{1,0:T(8,128)S(1)}, f32[8,512]{1,0:T(8,128)S(1)}, u32[]{:S(2)}, u32[]{:S(2)}) collective-permute-start(f32[8,512]{1,0:T(8,128)S(1)} %get-tuple-element.109), channel_id=1, source_target_pairs={{0,1},{1,0},{2,3},{3,2},{4,5},{5,4},{6,7},{7,6},{8,16},{9,17},{10,... | collective-permute-start | bytes 49160 | tf_op jit(solution)/shard_map/ppermute | solution.py:594
  28.8 3.7 %collective-permute-start.15 = (f32[8,512]{1,0:T(8,128)S(1)}, f32[8,512]{1,0:T(8,128)S(1)}, u32[]{:S(2)}, u32[]{:S(2)}) collective-permute-start(f32[8,512]{1,0:T(8,128)S(1)} %get-tuple-element.110), channel_id=1, source_target_pairs={{0,1},{1,0},{2,3},{3,2},{4,5},{5,4},{6,7},{7,6},{8,9},{9,8},{10,11... | collective-permute-start | bytes 49160 | tf_op jit(solution)/shard_map/ppermute | solution.py:594
  32.9 6.5 %collective-permute-start.16 = (f32[8,512]{1,0:T(8,128)S(1)}, f32[8,512]{1,0:T(8,128)S(1)}, u32[]{:S(2)}, u32[]{:S(2)}) collective-permute-start(f32[8,512]{1,0:T(8,128)S(1)} %get-tuple-element.113), channel_id=1, source_target_pairs={{0,8},{1,2},{2,1},{3,4},{4,3},{5,6},{6,5},{7,15},{8,0},{9,10},{10,... | collective-permute-start | bytes 49160 | tf_op jit(solution)/shard_map/ppermute | solution.py:594
  34.9 4.4 %collective-permute-start.17 = (f32[8,512]{1,0:T(8,128)S(1)}, f32[8,512]{1,0:T(8,128)S(1)}, u32[]{:S(2)}, u32[]{:S(2)}) collective-permute-start(f32[8,512]{1,0:T(8,128)S(1)} %get-tuple-element.114), channel_id=1, source_target_pairs={{0,8},{1,9},{2,10},{3,11},{4,12},{5,13},{6,14},{7,15},{8,0},{9,1},... | collective-permute-start | bytes 49160 | tf_op jit(solution)/shard_map/ppermute | solution.py:594
  35.0 4.4 %collective-permute-start.18 = (f32[8,512]{1,0:T(8,128)S(1)}, f32[8,512]{1,0:T(8,128)S(1)}, u32[]{:S(2)}, u32[]{:S(2)}) collective-permute-start(f32[8,512]{1,0:T(8,128)S(1)} %get-tuple-element.115), channel_id=1, source_target_pairs={{0,1},{1,0},{2,3},{3,2},{4,5},{5,4},{6,7},{7,6},{8,16},{9,17},{10,... | collective-permute-start | bytes 49160 | tf_op jit(solution)/shard_map/ppermute | solution.py:594
  35.0 4.4 %collective-permute-start.19 = (f32[8,512]{1,0:T(8,128)S(1)}, f32[8,512]{1,0:T(8,128)S(1)}, u32[]{:S(2)}, u32[]{:S(2)}) collective-permute-start(f32[8,512]{1,0:T(8,128)S(1)} %get-tuple-element.116), channel_id=1, source_target_pairs={{0,1},{1,0},{2,3},{3,2},{4,5},{5,4},{6,7},{7,6},{8,9},{9,8},{10,11... | collective-permute-start | bytes 49160 | tf_op jit(solution)/shard_map/ppermute | solution.py:594
  35.5 10.5 %all-to-all-start = ((f32[32,1,128]{2,1,0:T(1,128)}), f32[32,1,128]{2,1,0:T(1,128)S(1)}, u32[]{:S(2)}, u32[]{:S(2)}) async-start(f32[32,1,128]{2,1,0:T(1,128)} %get-tuple-element.119), calls=%async_computation | async-start | bytes 32768 | tf_op jit(solution)/shard_map/all_to_all | solution.py:607
  39.8 6.3 %collective-permute-start.20 = (f32[8,512]{1,0:T(8,128)S(1)}, f32[8,512]{1,0:T(8,128)S(1)}, u32[]{:S(2)}, u32[]{:S(2)}) collective-permute-start(f32[8,512]{1,0:T(8,128)S(1)} %get-tuple-element.120), channel_id=1, source_target_pairs={{0,8},{1,2},{2,1},{3,4},{4,3},{5,6},{6,5},{7,15},{8,0},{9,10},{10,... | collective-permute-start | bytes 49160 | tf_op jit(solution)/shard_map/ppermute | solution.py:594
  41.6 4.5 %collective-permute-start.21 = (f32[8,512]{1,0:T(8,128)S(1)}, f32[8,512]{1,0:T(8,128)S(1)}, u32[]{:S(2)}, u32[]{:S(2)}) collective-permute-start(f32[8,512]{1,0:T(8,128)S(1)} %get-tuple-element.121), channel_id=1, source_target_pairs={{0,8},{1,9},{2,10},{3,11},{4,12},{5,13},{6,14},{7,15},{8,0},{9,1},... | collective-permute-start | bytes 49160 | tf_op jit(solution)/shard_map/ppermute | solution.py:594
  41.9 4.2 %collective-permute-start.22 = (f32[8,512]{1,0:T(8,128)S(1)}, f32[8,512]{1,0:T(8,128)S(1)}, u32[]{:S(2)}, u32[]{:S(2)}) collective-permute-start(f32[8,512]{1,0:T(8,128)S(1)} %get-tuple-element.122), channel_id=1, source_target_pairs={{0,1},{1,0},{2,3},{3,2},{4,5},{5,4},{6,7},{7,6},{8,16},{9,17},{10,... | collective-permute-start | bytes 49160 | tf_op jit(solution)/shard_map/ppermute | solution.py:594
  43.0 3.2 %collective-permute-start.23 = (f32[8,512]{1,0:T(8,128)S(1)}, f32[8,512]{1,0:T(8,128)S(1)}, u32[]{:S(2)}, u32[]{:S(2)}) collective-permute-start(f32[8,512]{1,0:T(8,128)S(1)} %get-tuple-element.123), channel_id=1, source_target_pairs={{0,1},{1,0},{2,3},{3,2},{4,5},{5,4},{6,7},{7,6},{8,9},{9,8},{10,11... | collective-permute-start | bytes 49160 | tf_op jit(solution)/shard_map/ppermute | solution.py:594
  46.6 3.8 %collective-permute-start.24 = (f32[8,512]{1,0:T(8,128)S(1)}, f32[8,512]{1,0:T(8,128)S(1)}, u32[]{:S(2)}, u32[]{:S(2)}) collective-permute-start(f32[8,512]{1,0:T(8,128)S(1)} %get-tuple-element.133), channel_id=1, source_target_pairs={{0,8},{1,2},{2,1},{3,4},{4,3},{5,6},{6,5},{7,15},{8,0},{9,10},{10,... | collective-permute-start | bytes 49160 | tf_op jit(solution)/shard_map/ppermute | solution.py:594
  47.9 3.7 %collective-permute-start.25 = (f32[8,512]{1,0:T(8,128)S(1)}, f32[8,512]{1,0:T(8,128)S(1)}, u32[]{:S(2)}, u32[]{:S(2)}) collective-permute-start(f32[8,512]{1,0:T(8,128)S(1)} %get-tuple-element.134), channel_id=1, source_target_pairs={{0,8},{1,9},{2,10},{3,11},{4,12},{5,13},{6,14},{7,15},{8,0},{9,1},... | collective-permute-start | bytes 49160 | tf_op jit(solution)/shard_map/ppermute | solution.py:594
  48.7 3.0 %collective-permute-start.26 = (f32[8,512]{1,0:T(8,128)S(1)}, f32[8,512]{1,0:T(8,128)S(1)}, u32[]{:S(2)}, u32[]{:S(2)}) collective-permute-start(f32[8,512]{1,0:T(8,128)S(1)} %get-tuple-element.135), channel_id=1, source_target_pairs={{0,1},{1,0},{2,3},{3,2},{4,5},{5,4},{6,7},{7,6},{8,16},{9,17},{10,... | collective-permute-start | bytes 49160 | tf_op jit(solution)/shard_map/ppermute | solution.py:594
  48.7 3.0 %collective-permute-start.27 = (f32[8,512]{1,0:T(8,128)S(1)}, f32[8,512]{1,0:T(8,128)S(1)}, u32[]{:S(2)}, u32[]{:S(2)}) collective-permute-start(f32[8,512]{1,0:T(8,128)S(1)} %get-tuple-element.136), channel_id=1, source_target_pairs={{0,1},{1,0},{2,3},{3,2},{4,5},{5,4},{6,7},{7,6},{8,9},{9,8},{10,11... | collective-permute-start | bytes 49160 | tf_op jit(solution)/shard_map/ppermute | solution.py:594

commit v10 on v9

--- a/solution.py
+++ b/solution.py
@@ -220,7 +220,8 @@
             field[N * a : N * a + N, :] + place(low, high, N * i + a, row)
             for i, field in enumerate((ws, wk, robin))
         ]
-        sides.append(jnp.concatenate(part + [wk[N * a : N * a + N, :]], 0))
+        part[1] = wk[N * a : N * a + N, :]
+        sides.append(jnp.concatenate(part + [low[N + a : N + a + 1], high[N + a : N + a + 1]], 0))
     send(pos, 0, sides[0], sides[1], even_out, odd_out)
 
 
@@ -326,7 +327,7 @@
     b, ky = tiles(b_in), tiles(ky_in)
     for a, side in ((0, low), (N - 1, high)):
         b[a] += fold_z(side[0:N], lanes)
-        ky[a] += fold_z(side[3 * N : 4 * N], lanes)
+        ky[a] += fold_z(side[N : 2 * N], lanes)
     store(b_out, b)
     store(ky_out, ky)
     operate(pos, b, kx, ky_out, advect, xy_out, refs[:4], *refs[4:])
@@ -340,7 +341,8 @@
     diagonal_out[...] = diagonal_in[...]
     for a, side in ((0, low), (N - 1, high)):
         at = slice(N * a, N * a + N)
-        kz_out[at, :] += side[N : 2 * N]
+        ends = place(side[3 * N : 3 * N + 1], side[3 * N + 1 : 3 * N + 2], 0, row_index((N, side.shape[1])))
+        kz_out[at, :] += side[N : 2 * N] + ends
         diagonal_out[at, :] += fold_z(side[2 * N : 3 * N], lanes)
     along_z(b, xy, kz_out, diagonal_out, f1, f2, b1, b2, lanes, q_out)
 
@@ -621,7 +623,7 @@
     recv = exchange(y_pairs, *parts)
     ws, wk, robin = call(functools.partial(whole_field_kernel, sizes), [field] * 3, *given, cost=COST)
     parts = call(
-        functools.partial(fold_y_kernel, sizes), [struct(4 * N)] * 2, ws, wk, robin, *recv
+        functools.partial(fold_y_kernel, sizes), [struct(3 * N + 2)] * 2, ws, wk, robin, *recv
     )
     b, kx, ky, kz, advect, diagonal, inverse = call(
         functools.partial(prepare_kernel, sizes), [field] * 7, ws, wk, robin, *recv, lanes,

time: 63.5 us -> 63.5 us (level)
  no operation moved by 1% of the time
where the time goes in v10:
time: 63.5 us; the launch traced here: 63.3 us
  starting transfers between devices  27.4 us (43%)
  waiting for transfers between devices  14.4 us (23%)
  Pallas kernels  10.3 us (16%)
  blocking collectives  10.2 us (16%)
  between operations  0.91 us (1%)
    ppermute x28, starting transfers between devices, permute(): return lax.ppermute(values, ('gx', 'gy'), pairs)  24 us
    ppermute x28, waiting for transfers between devices, permute(): return lax.ppermute(values, ('gx', 'gy'), pairs)  11.8 us
    pallas_call x20, Pallas kernels, call(): pl.pallas_call(kernel, out_shape=outs, in_specs=specs, out_specs=[VMEM] *...  10.3 us
    all_to_all x1, blocking collectives, spread(): return lax.all_to_all(values, ('gx', 'gy'), 0, 0)  10.2 us
    all_to_all x1, starting transfers between devices, spread(): return lax.all_to_all(values, ('gx', 'gy'), 0, 0)  3.38 us
    all_to_all x1, waiting for transfers between devices, spread(): return lax.all_to_all(values, ('gx', 'gy'), 0, 0)  2.59 us
  transfers between devices with their start and end apart: 29, of which 9 were waited for; matrix products, arithmetic and copies ran while one was open for 0% of the time, Pallas kernels for 8%

profile of v10, /device:TPU:0, one launch (start us, length us, event | category | flops | bytes accessed | tf_op | source)
XLA Modules:
  0.0 63.3 jit_solution(15776764535266157299)
XLA Ops:
  0.6 1.8 %shard_map.114 = (f32[24,512]{1,0:T(8,128)}, f32[24,512]{1,0:T(8,128)}) custom-call(f32[64,512]{1,0:T(8,128)} %bitcast.7, f32[64,512]{1,0:T(8,128)} %bitcast.9, s32[1,64]{1,0:T(1,128)} %bitcast.11, s32[1,64]{1,0:T(1,128)} %bitcast.13, f32[1,4]{1,0:T(1,128)} %bitcast.15), custom_call_target="tpu_custom_call" | custom-call | tf_op jit(solution)/shard_map/pallas_call | solution.py:583
  2.5 0.0 copy-start.7
  2.5 0.0 copy-start.8
  2.5 0.0 copy-start.9
  2.5 3.1 %collective-permute-start = (f32[24,512]{1,0:T(8,128)}, f32[24,512]{1,0:T(8,128)S(1)}, u32[]{:S(2)}, u32[]{:S(2)}) collective-permute-start(f32[24,512]{1,0:T(8,128)} %get-tuple-element.77), channel_id=1, source_target_pairs={{0,8},{1,2},{2,1},{3,4},{4,3},{5,6},{6,5},{7,15},{8,0},{9,10},{10,... | collective-permute-start | bytes 147464 | tf_op jit(solution)/shard_map/ppermute | solution.py:596
  5.6 0.0 collective-permute-start.1
  5.6 0.3 shard_map.113
  5.9 2.0 %collective-permute-done.odd = f32[24,512]{1,0:T(8,128)S(1)} collective-permute-done((f32[24,512]{1,0:T(8,128)}, f32[24,512]{1,0:T(8,128)S(1)}, u32[]{:S(2)}, u32[]{:S(2)}) %collective-permute-start) | collective-permute-done | bytes 49184 | tf_op jit(solution)/shard_map/ppermute | solution.py:596
  7.9 0.0 collective-permute-done.1.even
  7.9 0.1 collective-permute-start.2
  8.0 3.6 %collective-permute-start.3 = (f32[26,512]{1,0:T(8,128)S(1)}, f32[26,512]{1,0:T(8,128)S(1)}, u32[]{:S(2)}, u32[]{:S(2)}) collective-permute-start(f32[26,512]{1,0:T(8,128)S(1)} %get-tuple-element.84), channel_id=1, source_target_pairs={{0,8},{1,9},{2,10},{3,11},{4,12},{5,13},{6,14},{7,15},{8,0},{9,1},... | collective-permute-start | bytes 159752 | tf_op jit(solution)/shard_map/ppermute | solution.py:596
  11.6 0.4 shard_map.115
  11.9 0.0 collective-permute-done.2.odd
  12.0 1.9 %collective-permute-done.3.even = f32[26,512]{1,0:T(8,128)S(1)} collective-permute-done((f32[26,512]{1,0:T(8,128)S(1)}, f32[26,512]{1,0:T(8,128)S(1)}, u32[]{:S(2)}, u32[]{:S(2)}) %collective-permute-start.3) | collective-permute-done | bytes 53280 | tf_op jit(solution)/shard_map/ppermute | solution.py:596
  13.8 0.4 shard_map.117
  14.2 2.1 %collective-permute-start.4 = (f32[8,512]{1,0:T(8,128)S(1)}, f32[8,512]{1,0:T(8,128)S(1)}, u32[]{:S(2)}, u32[]{:S(2)}) collective-permute-start(f32[8,512]{1,0:T(8,128)S(1)} %get-tuple-element.90), channel_id=1, source_target_pairs={{0,8},{1,2},{2,1},{3,4},{4,3},{5,6},{6,5},{7,15},{8,0},{9,10},{10,... | collective-permute-start | bytes 49160 | tf_op jit(solution)/shard_map/ppermute | solution.py:596
  16.3 0.1 collective-permute-start.5
  16.4 1.3 %collective-permute-start.6 = (f32[8,512]{1,0:T(8,128)S(1)}, f32[8,512]{1,0:T(8,128)S(1)}, u32[]{:S(2)}, u32[]{:S(2)}) collective-permute-start(f32[8,512]{1,0:T(8,128)S(1)} %get-tuple-element.92), channel_id=1, source_target_pairs={{0,1},{1,0},{2,3},{3,2},{4,5},{5,4},{6,7},{7,6},{8,16},{9,17},{10,... | collective-permute-start | bytes 49160 | tf_op jit(solution)/shard_map/ppermute | solution.py:596
  17.8 0.5 shard_map.118
  18.2 0.0 collective-permute-done.4.x0
  18.2 1.8 %collective-permute-done.5.x1 = f32[8,512]{1,0:T(8,128)S(1)} collective-permute-done((f32[8,512]{1,0:T(8,128)S(1)}, f32[8,512]{1,0:T(8,128)S(1)}, u32[]{:S(2)}, u32[]{:S(2)}) %collective-permute-start.5) | collective-permute-done | bytes 16416 | tf_op jit(solution)/shard_map/ppermute | solution.py:596
  20.1 0.4 shard_map.119
  20.5 2.1 %collective-permute-start.8 = (f32[8,512]{1,0:T(8,128)S(1)}, f32[8,512]{1,0:T(8,128)S(1)}, u32[]{:S(2)}, u32[]{:S(2)}) collective-permute-start(f32[8,512]{1,0:T(8,128)S(1)} %get-tuple-element.100), channel_id=1, source_target_pairs={{0,8},{1,2},{2,1},{3,4},{4,3},{5,6},{6,5},{7,15},{8,0},{9,10},{10,... | collective-permute-start | bytes 49160 | tf_op jit(solution)/shard_map/ppermute | solution.py:596
  22.5 0.1 collective-permute-start.9
  22.6 0.0 collective-permute-start.10
  22.6 0.5 collective-permute-start.11
  23.1 0.4 shard_map.120.q
  23.6 0.7 %collective-permute-done.8.x0 = f32[8,512]{1,0:T(8,128)S(1)} collective-permute-done((f32[8,512]{1,0:T(8,128)S(1)}, f32[8,512]{1,0:T(8,128)S(1)}, u32[]{:S(2)}, u32[]{:S(2)}) %collective-permute-start.8) | collective-permute-done | bytes 16416 | tf_op jit(solution)/shard_map/ppermute | solution.py:596
  24.3 2.0 %collective-permute-done.9.x1 = f32[8,512]{1,0:T(8,128)S(1)} collective-permute-done((f32[8,512]{1,0:T(8,128)S(1)}, f32[8,512]{1,0:T(8,128)S(1)}, u32[]{:S(2)}, u32[]{:S(2)}) %collective-permute-start.9) | collective-permute-done | bytes 16416 | tf_op jit(solution)/shard_map/ppermute | solution.py:596
  26.3 0.0 collective-permute-done.10.y0
  26.3 0.0 collective-permute-done.11.y1
  26.3 0.4 shard_map.121
  26.7 2.1 %collective-permute-start.12 = (f32[8,512]{1,0:T(8,128)S(1)}, f32[8,512]{1,0:T(8,128)S(1)}, u32[]{:S(2)}, u32[]{:S(2)}) collective-permute-start(f32[8,512]{1,0:T(8,128)S(1)} %get-tuple-element.107), channel_id=1, source_target_pairs={{0,8},{1,2},{2,1},{3,4},{4,3},{5,6},{6,5},{7,15},{8,0},{9,10},{10,... | collective-permute-start | bytes 49160 | tf_op jit(solution)/shard_map/ppermute | solution.py:596
  28.7 0.1 collective-permute-start.13
  28.8 0.0 collective-permute-start.14
  28.8 0.5 collective-permute-start.15
  29.3 1.0 %shard_map.122 = (f32[64,512]{1,0:T(8,128)S(1)}, f32[32,1,128]{2,1,0:T(1,128)}) custom-call(f32[64,512]{1,0:T(8,128)S(1)} %get-tuple-element.85.b, f32[64,512]{1,0:T(8,128)S(1)} %get-tuple-element.95.refs_0_.s, f32[64,512]{1,0:T(8,128)S(1)} %get-tuple-element.96.inverse, f32[64,512]{1,0:T(8,128)S(1)} %get-tuple-element.104.z, ...), custom_call_target="tpu_custom_call" | custom-call | flops 1048576 | bytes 1048576 | tf_op jit(solution)/shard_map/pallas_call | solution.py:583
  30.3 0.1 collective-permute-done.12.x0
  30.5 2.0 %collective-permute-done.13.x1 = f32[8,512]{1,0:T(8,128)S(1)} collective-permute-done((f32[8,512]{1,0:T(8,128)S(1)}, f32[8,512]{1,0:T(8,128)S(1)}, u32[]{:S(2)}, u32[]{:S(2)}) %collective-permute-start.13) | collective-permute-done | bytes 16416 | tf_op jit(solution)/shard_map/ppermute | solution.py:596
  32.5 0.4 shard_map.123
  32.9 2.1 %collective-permute-start.16 = (f32[8,512]{1,0:T(8,128)S(1)}, f32[8,512]{1,0:T(8,128)S(1)}, u32[]{:S(2)}, u32[]{:S(2)}) collective-permute-start(f32[8,512]{1,0:T(8,128)S(1)} %get-tuple-element.113), channel_id=1, source_target_pairs={{0,8},{1,2},{2,1},{3,4},{4,3},{5,6},{6,5},{7,15},{8,0},{9,10},{10,... | collective-permute-start | bytes 49160 | tf_op jit(solution)/shard_map/ppermute | solution.py:596
  34.9 0.1 collective-permute-start.17
  35.0 0.5 collective-permute-start.19
  35.5 3.4 %all-to-all-start = ((f32[32,1,128]{2,1,0:T(1,128)}), f32[32,1,128]{2,1,0:T(1,128)S(1)}, u32[]{:S(2)}, u32[]{:S(2)}) async-start(f32[32,1,128]{2,1,0:T(1,128)} %get-tuple-element.119), calls=%async_computation | async-start | bytes 32768 | tf_op jit(solution)/shard_map/all_to_all | solution.py:609
  38.9 0.5 shard_map.124.q
  39.4 0.0 collective-permute-done.16.x0
  39.4 0.4 shard_map.125
  39.8 1.8 %collective-permute-start.20 = (f32[8,512]{1,0:T(8,128)S(1)}, f32[8,512]{1,0:T(8,128)S(1)}, u32[]{:S(2)}, u32[]{:S(2)}) collective-permute-start(f32[8,512]{1,0:T(8,128)S(1)} %get-tuple-element.120), channel_id=1, source_target_pairs={{0,8},{1,2},{2,1},{3,4},{4,3},{5,6},{6,5},{7,15},{8,0},{9,10},{10,... | collective-permute-start | bytes 49160 | tf_op jit(solution)/shard_map/ppermute | solution.py:596
  41.6 0.3 collective-permute-start.21
  41.9 1.0 %collective-permute-start.22 = (f32[8,512]{1,0:T(8,128)S(1)}, f32[8,512]{1,0:T(8,128)S(1)}, u32[]{:S(2)}, u32[]{:S(2)}) collective-permute-start(f32[8,512]{1,0:T(8,128)S(1)} %get-tuple-element.122), channel_id=1, source_target_pairs={{0,1},{1,0},{2,3},{3,2},{4,5},{5,4},{6,7},{7,6},{8,16},{9,17},{10,... | collective-permute-start | bytes 49160 | tf_op jit(solution)/shard_map/ppermute | solution.py:596
  43.0 0.4 shard_map.126._.q
  43.4 2.6 %all-to-all-done.gathered = f32[32,1,128]{2,1,0:T(1,128)S(1)} async-done(((f32[32,1,128]{2,1,0:T(1,128)}), f32[32,1,128]{2,1,0:T(1,128)S(1)}, u32[]{:S(2)}, u32[]{:S(2)}) %all-to-all-start) | async-done | bytes 16416 | tf_op jit(solution)/shard_map/all_to_all | solution.py:609
  46.0 0.1 shard_map.127.scalars
  46.2 0.4 shard_map.128
  46.6 1.3 %collective-permute-start.24 = (f32[8,512]{1,0:T(8,128)S(1)}, f32[8,512]{1,0:T(8,128)S(1)}, u32[]{:S(2)}, u32[]{:S(2)}) collective-permute-start(f32[8,512]{1,0:T(8,128)S(1)} %get-tuple-element.133), channel_id=1, source_target_pairs={{0,8},{1,2},{2,1},{3,4},{4,3},{5,6},{6,5},{7,15},{8,0},{9,10},{10,... | collective-permute-start | bytes 49160 | tf_op jit(solution)/shard_map/ppermute | solution.py:596
  47.9 0.8 %collective-permute-start.25 = (f32[8,512]{1,0:T(8,128)S(1)}, f32[8,512]{1,0:T(8,128)S(1)}, u32[]{:S(2)}, u32[]{:S(2)}) collective-permute-start(f32[8,512]{1,0:T(8,128)S(1)} %get-tuple-element.134), channel_id=1, source_target_pairs={{0,8},{1,9},{2,10},{3,11},{4,12},{5,13},{6,14},{7,15},{8,0},{9,1},... | collective-permute-start | bytes 49160 | tf_op jit(solution)/shard_map/ppermute | solution.py:596
  48.7 0.5 collective-permute-start.27
  49.2 0.7 %shard_map.129 = (f32[64,512]{1,0:T(8,128)S(1)}, f32[64,512]{1,0:T(8,128)S(1)}, f32[64,512]{1,0:T(8,128)S(1)}, f32[64,512]{1,0:T(8,128)S(1)}, f32[64,512]{1,0:T(...) custom-call(f32[8,128]{1,0:T(8,128)S(1)} %shard_map.127.scalars, ...), custom_call_target="tpu_custom_call" | custom-call | flops 1048576 | bytes 1048576 | tf_op jit(solution)/shard_map/pallas_call | solution.py:583
  49.9 0.5 shard_map.130.q
  50.4 0.0 collective-permute-done.24.x0
  50.4 1.2 %collective-permute-done.25.x1 = f32[8,512]{1,0:T(8,128)S(1)} collective-permute-done((f32[8,512]{1,0:T(8,128)S(1)}, f32[8,512]{1,0:T(8,128)S(1)}, u32[]{:S(2)}, u32[]{:S(2)}) %collective-permute-start.25) | collective-permute-done | bytes 16416 | tf_op jit(solution)/shard_map/ppermute | solution.py:596
  51.7 0.3 shard_map.131
  52.0 10.2 %all_to_all.10.gathered = f32[32,1,128]{2,1,0:T(1,128)S(1)} all-to-all(f32[32,1,128]{2,1,0:T(1,128)S(1)} %get-tuple-element.137), channel_id=1, replica_groups=mesh['gx'=4,'gy'=8] {'gx','gy'}, dimensions={0} | all-to-all | bytes 32768 | tf_op jit(solution)/shard_map/all_to_all | solution.py:609
  62.2 1.0 %shard_map.132 = (f32[64,512]{1,0:T(8,128)}, f32[64,512]{1,0:T(8,128)}) custom-call(f32[32,1,128]{2,1,0:T(1,128)S(1)} %all_to_all.10.gathered, f32[8,128]{1,0:T(8,128)S(1)} %shard_map.127.scalars, f32[64,512]{1,0:T(8,128)S(1)} %get-tuple-element.138.x, f32[64,512]{1,0:T(8,128)S(1)} %get-tuple-element.139.p, f32[64,512]{1,0:T(8,128)S(1)} %get-tuple-element.140.r, ...), custom_call_target="tpu_custom_call" | custom-call | tf_op jit(solution)/shard_map/pallas_call | solution.py:583
  (35 shorter events, 0.1 us)
Async XLA Ops:
  0.6 5.0 %copy-start.5 = (f32[8,8,512]{2,1,0:T(8,128)S(1)}, f32[8,8,512]{2,1,0:T(8,128)}, u32[]{:S(2)}) copy-start(f32[8,8,512]{2,1,0:T(8,128)} %param.10) | copy-start | bytes 393220
  0.6 5.0 %copy-start.6 = (f32[8,8,512]{2,1,0:T(8,128)S(1)}, f32[8,8,512]{2,1,0:T(8,128)}, u32[]{:S(2)}) copy-start(f32[8,8,512]{2,1,0:T(8,128)} %param.11) | copy-start | bytes 393220
  2.5 3.2 %copy-start.7 = (s32[1,1,64]{2,1,0:T(1,128)S(1)}, s32[1,1,64]{2,1,0:T(1,128)}, u32[]{:S(2)}) copy-start(s32[1,1,64]{2,1,0:T(1,128)} %param.12) | copy-start | bytes 772
  2.5 3.2 %copy-start.8 = (s32[1,1,64]{2,1,0:T(1,128)S(1)}, s32[1,1,64]{2,1,0:T(1,128)}, u32[]{:S(2)}) copy-start(s32[1,1,64]{2,1,0:T(1,128)} %param.13) | copy-start | bytes 772
  2.5 3.1 %copy-start.9 = (f32[4]{0:T(128)S(1)}, f32[4]{0:T(128)}, u32[]{:S(2)}) copy-start(f32[4]{0:T(128)} %param.14) | copy-start | bytes 52
  2.5 5.4 %collective-permute-start = (f32[24,512]{1,0:T(8,128)}, f32[24,512]{1,0:T(8,128)S(1)}, u32[]{:S(2)}, u32[]{:S(2)}) collective-permute-start(f32[24,512]{1,0:T(8,128)} %get-tuple-element.77), channel_id=1, source_target_pairs={{0,8},{1,2},{2,1},{3,4},{4,3},{5,6},{6,5},{7,15},{8,0},{9,10},{10,... | collective-permute-start | bytes 147464 | tf_op jit(solution)/shard_map/ppermute | solution.py:596
  5.6 2.3 %collective-permute-start.1 = (f32[24,512]{1,0:T(8,128)}, f32[24,512]{1,0:T(8,128)S(1)}, u32[]{:S(2)}, u32[]{:S(2)}) collective-permute-start(f32[24,512]{1,0:T(8,128)} %get-tuple-element.78), channel_id=1, source_target_pairs={{0,1},{1,0},{2,3},{3,2},{4,5},{5,4},{6,7},{7,6},{8,9},{9,8},{10,11... | collective-permute-start | bytes 147464 | tf_op jit(solution)/shard_map/ppermute | solution.py:596
  7.9 3.7 %copy-start.4 = (f32[8,512]{1,0:T(8,128)S(1)}, f32[8,512]{1,0:T(8,128)}, u32[]{:S(2)}) copy-start(f32[8,512]{1,0:T(8,128)} %constant.14.clone.lanes.refs_8_.refs_7_) | copy-start | bytes 49156
  7.9 4.0 %collective-permute-start.2 = (f32[26,512]{1,0:T(8,128)S(1)}, f32[26,512]{1,0:T(8,128)S(1)}, u32[]{:S(2)}, u32[]{:S(2)}) collective-permute-start(f32[26,512]{1,0:T(8,128)S(1)} %get-tuple-element.83), channel_id=1, source_target_pairs={{0,1},{1,0},{2,3},{3,2},{4,5},{5,4},{6,7},{7,6},{8,16},{9,17},{10,... | collective-permute-start | bytes 159752 | tf_op jit(solution)/shard_map/ppermute | solution.py:596
  8.0 5.8 %collective-permute-start.3 = (f32[26,512]{1,0:T(8,128)S(1)}, f32[26,512]{1,0:T(8,128)S(1)}, u32[]{:S(2)}, u32[]{:S(2)}) collective-permute-start(f32[26,512]{1,0:T(8,128)S(1)} %get-tuple-element.84), channel_id=1, source_target_pairs={{0,8},{1,9},{2,10},{3,11},{4,12},{5,13},{6,14},{7,15},{8,0},{9,1},... | collective-permute-start | bytes 159752 | tf_op jit(solution)/shard_map/ppermute | solution.py:596
  13.8 3.9 %copy-start = (bf16[256,256]{1,0:T(8,128)(2,1)S(1)}, bf16[256,256]{1,0:T(8,128)(2,1)}, u32[]{:S(2)}) copy-start(bf16[256,256]{1,0:T(8,128)(2,1)} %constant.12.clone.b1.refs_6_.refs_5_) | copy-start | bytes 393220
  13.8 3.9 %copy-start.1 = (bf16[256,256]{1,0:T(8,128)(2,1)S(1)}, bf16[256,256]{1,0:T(8,128)(2,1)}, u32[]{:S(2)}) copy-start(bf16[256,256]{1,0:T(8,128)(2,1)} %constant.10.clone.f1.refs_4_.refs_3_) | copy-start | bytes 393220
  13.8 3.9 %copy-start.2 = (bf16[256,128]{1,0:T(8,128)(2,1)S(1)}, bf16[256,128]{1,0:T(8,128)(2,1)}, u32[]{:S(2)}) copy-start(bf16[256,128]{1,0:T(8,128)(2,1)} %constant.13.clone.b2.refs_7_.refs_6_) | copy-start | bytes 196612
  13.8 3.9 %copy-start.3 = (bf16[256,128]{1,0:T(8,128)(2,1)S(1)}, bf16[256,128]{1,0:T(8,128)(2,1)}, u32[]{:S(2)}) copy-start(bf16[256,128]{1,0:T(8,128)(2,1)} %constant.11.clone.f2.refs_5_.refs_4_) | copy-start | bytes 196612
  14.2 4.0 %collective-permute-start.4 = (f32[8,512]{1,0:T(8,128)S(1)}, f32[8,512]{1,0:T(8,128)S(1)}, u32[]{:S(2)}, u32[]{:S(2)}) collective-permute-start(f32[8,512]{1,0:T(8,128)S(1)} %get-tuple-element.90), channel_id=1, source_target_pairs={{0,8},{1,2},{2,1},{3,4},{4,3},{5,6},{6,5},{7,15},{8,0},{9,10},{10,... | collective-permute-start | bytes 49160 | tf_op jit(solution)/shard_map/ppermute | solution.py:596
  16.3 3.7 %collective-permute-start.5 = (f32[8,512]{1,0:T(8,128)S(1)}, f32[8,512]{1,0:T(8,128)S(1)}, u32[]{:S(2)}, u32[]{:S(2)}) collective-permute-start(f32[8,512]{1,0:T(8,128)S(1)} %get-tuple-element.91), channel_id=1, source_target_pairs={{0,8},{1,9},{2,10},{3,11},{4,12},{5,13},{6,14},{7,15},{8,0},{9,1},... | collective-permute-start | bytes 49160 | tf_op jit(solution)/shard_map/ppermute | solution.py:596
  16.4 3.7 %collective-permute-start.6 = (f32[8,512]{1,0:T(8,128)S(1)}, f32[8,512]{1,0:T(8,128)S(1)}, u32[]{:S(2)}, u32[]{:S(2)}) collective-permute-start(f32[8,512]{1,0:T(8,128)S(1)} %get-tuple-element.92), channel_id=1, source_target_pairs={{0,1},{1,0},{2,3},{3,2},{4,5},{5,4},{6,7},{7,6},{8,16},{9,17},{10,... | collective-permute-start | bytes 49160 | tf_op jit(solution)/shard_map/ppermute | solution.py:596
  17.7 2.3 %collective-permute-start.7 = (f32[8,512]{1,0:T(8,128)S(1)}, f32[8,512]{1,0:T(8,128)S(1)}, u32[]{:S(2)}, u32[]{:S(2)}) collective-permute-start(f32[8,512]{1,0:T(8,128)S(1)} %get-tuple-element.93), channel_id=1, source_target_pairs={{0,1},{1,0},{2,3},{3,2},{4,5},{5,4},{6,7},{7,6},{8,9},{9,8},{10,11... | collective-permute-start | bytes 49160 | tf_op jit(solution)/shard_map/ppermute | solution.py:596
  20.5 3.8 %collective-permute-start.8 = (f32[8,512]{1,0:T(8,128)S(1)}, f32[8,512]{1,0:T(8,128)S(1)}, u32[]{:S(2)}, u32[]{:S(2)}) collective-permute-start(f32[8,512]{1,0:T(8,128)S(1)} %get-tuple-element.100), channel_id=1, source_target_pairs={{0,8},{1,2},{2,1},{3,4},{4,3},{5,6},{6,5},{7,15},{8,0},{9,10},{10,... | collective-permute-start | bytes 49160 | tf_op jit(solution)/shard_map/ppermute | solution.py:596
  22.5 3.7 %collective-permute-start.9 = (f32[8,512]{1,0:T(8,128)S(1)}, f32[8,512]{1,0:T(8,128)S(1)}, u32[]{:S(2)}, u32[]{:S(2)}) collective-permute-start(f32[8,512]{1,0:T(8,128)S(1)} %get-tuple-element.101), channel_id=1, source_target_pairs={{0,8},{1,9},{2,10},{3,11},{4,12},{5,13},{6,14},{7,15},{8,0},{9,1},... | collective-permute-start | bytes 49160 | tf_op jit(solution)/shard_map/ppermute | solution.py:596
  22.6 3.7 %collective-permute-start.10 = (f32[8,512]{1,0:T(8,128)S(1)}, f32[8,512]{1,0:T(8,128)S(1)}, u32[]{:S(2)}, u32[]{:S(2)}) collective-permute-start(f32[8,512]{1,0:T(8,128)S(1)} %get-tuple-element.102), channel_id=1, source_target_pairs={{0,1},{1,0},{2,3},{3,2},{4,5},{5,4},{6,7},{7,6},{8,16},{9,17},{10,... | collective-permute-start | bytes 49160 | tf_op jit(solution)/shard_map/ppermute | solution.py:596
  22.6 3.7 %collective-permute-start.11 = (f32[8,512]{1,0:T(8,128)S(1)}, f32[8,512]{1,0:T(8,128)S(1)}, u32[]{:S(2)}, u32[]{:S(2)}) collective-permute-start(f32[8,512]{1,0:T(8,128)S(1)} %get-tuple-element.103), channel_id=1, source_target_pairs={{0,1},{1,0},{2,3},{3,2},{4,5},{5,4},{6,7},{7,6},{8,9},{9,8},{10,11... | collective-permute-start | bytes 49160 | tf_op jit(solution)/shard_map/ppermute | solution.py:596
  26.7 3.8 %collective-permute-start.12 = (f32[8,512]{1,0:T(8,128)S(1)}, f32[8,512]{1,0:T(8,128)S(1)}, u32[]{:S(2)}, u32[]{:S(2)}) collective-permute-start(f32[8,512]{1,0:T(8,128)S(1)} %get-tuple-element.107), channel_id=1, source_target_pairs={{0,8},{1,2},{2,1},{3,4},{4,3},{5,6},{6,5},{7,15},{8,0},{9,10},{10,... | collective-permute-start | bytes 49160 | tf_op jit(solution)/shard_map/ppermute | solution.py:596
  28.7 3.7 %collective-permute-start.13 = (f32[8,512]{1,0:T(8,128)S(1)}, f32[8,512]{1,0:T(8,128)S(1)}, u32[]{:S(2)}, u32[]{:S(2)}) collective-permute-start(f32[8,512]{1,0:T(8,128)S(1)} %get-tuple-element.108), channel_id=1, source_target_pairs={{0,8},{1,9},{2,10},{3,11},{4,12},{5,13},{6,14},{7,15},{8,0},{9,1},... | collective-permute-start | bytes 49160 | tf_op jit(solution)/shard_map/ppermute | solution.py:596
  28.8 3.7 %collective-permute-start.14 = (f32[8,512]{1,0:T(8,128)S(1)}, f32[8,512]{1,0:T(8,128)S(1)}, u32[]{:S(2)}, u32[]{:S(2)}) collective-permute-start(f32[8,512]{1,0:T(8,128)S(1)} %get-tuple-element.109), channel_id=1, source_target_pairs={{0,1},{1,0},{2,3},{3,2},{4,5},{5,4},{6,7},{7,6},{8,16},{9,17},{10,... | collective-permute-start | bytes 49160 | tf_op jit(solution)/shard_map/ppermute | solution.py:596
  28.8 3.7 %collective-permute-start.15 = (f32[8,512]{1,0:T(8,128)S(1)}, f32[8,512]{1,0:T(8,128)S(1)}, u32[]{:S(2)}, u32[]{:S(2)}) collective-permute-start(f32[8,512]{1,0:T(8,128)S(1)} %get-tuple-element.110), channel_id=1, source_target_pairs={{0,1},{1,0},{2,3},{3,2},{4,5},{5,4},{6,7},{7,6},{8,9},{9,8},{10,11... | collective-permute-start | bytes 49160 | tf_op jit(solution)/shard_map/ppermute | solution.py:596
  32.9 6.5 %collective-permute-start.16 = (f32[8,512]{1,0:T(8,128)S(1)}, f32[8,512]{1,0:T(8,128)S(1)}, u32[]{:S(2)}, u32[]{:S(2)}) collective-permute-start(f32[8,512]{1,0:T(8,128)S(1)} %get-tuple-element.113), channel_id=1, source_target_pairs={{0,8},{1,2},{2,1},{3,4},{4,3},{5,6},{6,5},{7,15},{8,0},{9,10},{10,... | collective-permute-start | bytes 49160 | tf_op jit(solution)/shard_map/ppermute | solution.py:596
  34.9 4.4 %collective-permute-start.17 = (f32[8,512]{1,0:T(8,128)S(1)}, f32[8,512]{1,0:T(8,128)S(1)}, u32[]{:S(2)}, u32[]{:S(2)}) collective-permute-start(f32[8,512]{1,0:T(8,128)S(1)} %get-tuple-element.114), channel_id=1, source_target_pairs={{0,8},{1,9},{2,10},{3,11},{4,12},{5,13},{6,14},{7,15},{8,0},{9,1},... | collective-permute-start | bytes 49160 | tf_op jit(solution)/shard_map/ppermute | solution.py:596
  35.0 4.4 %collective-permute-start.18 = (f32[8,512]{1,0:T(8,128)S(1)}, f32[8,512]{1,0:T(8,128)S(1)}, u32[]{:S(2)}, u32[]{:S(2)}) collective-permute-start(f32[8,512]{1,0:T(8,128)S(1)} %get-tuple-element.115), channel_id=1, source_target_pairs={{0,1},{1,0},{2,3},{3,2},{4,5},{5,4},{6,7},{7,6},{8,16},{9,17},{10,... | collective-permute-start | bytes 49160 | tf_op jit(solution)/shard_map/ppermute | solution.py:596
  35.0 4.4 %collective-permute-start.19 = (f32[8,512]{1,0:T(8,128)S(1)}, f32[8,512]{1,0:T(8,128)S(1)}, u32[]{:S(2)}, u32[]{:S(2)}) collective-permute-start(f32[8,512]{1,0:T(8,128)S(1)} %get-tuple-element.116), channel_id=1, source_target_pairs={{0,1},{1,0},{2,3},{3,2},{4,5},{5,4},{6,7},{7,6},{8,9},{9,8},{10,11... | collective-permute-start | bytes 49160 | tf_op jit(solution)/shard_map/ppermute | solution.py:596
  35.5 10.5 %all-to-all-start = ((f32[32,1,128]{2,1,0:T(1,128)}), f32[32,1,128]{2,1,0:T(1,128)S(1)}, u32[]{:S(2)}, u32[]{:S(2)}) async-start(f32[32,1,128]{2,1,0:T(1,128)} %get-tuple-element.119), calls=%async_computation | async-start | bytes 32768 | tf_op jit(solution)/shard_map/all_to_all | solution.py:609
  39.8 6.3 %collective-permute-start.20 = (f32[8,512]{1,0:T(8,128)S(1)}, f32[8,512]{1,0:T(8,128)S(1)}, u32[]{:S(2)}, u32[]{:S(2)}) collective-permute-start(f32[8,512]{1,0:T(8,128)S(1)} %get-tuple-element.120), channel_id=1, source_target_pairs={{0,8},{1,2},{2,1},{3,4},{4,3},{5,6},{6,5},{7,15},{8,0},{9,10},{10,... | collective-permute-start | bytes 49160 | tf_op jit(solution)/shard_map/ppermute | solution.py:596
  41.6 4.5 %collective-permute-start.21 = (f32[8,512]{1,0:T(8,128)S(1)}, f32[8,512]{1,0:T(8,128)S(1)}, u32[]{:S(2)}, u32[]{:S(2)}) collective-permute-start(f32[8,512]{1,0:T(8,128)S(1)} %get-tuple-element.121), channel_id=1, source_target_pairs={{0,8},{1,9},{2,10},{3,11},{4,12},{5,13},{6,14},{7,15},{8,0},{9,1},... | collective-permute-start | bytes 49160 | tf_op jit(solution)/shard_map/ppermute | solution.py:596
  41.9 4.2 %collective-permute-start.22 = (f32[8,512]{1,0:T(8,128)S(1)}, f32[8,512]{1,0:T(8,128)S(1)}, u32[]{:S(2)}, u32[]{:S(2)}) collective-permute-start(f32[8,512]{1,0:T(8,128)S(1)} %get-tuple-element.122), channel_id=1, source_target_pairs={{0,1},{1,0},{2,3},{3,2},{4,5},{5,4},{6,7},{7,6},{8,16},{9,17},{10,... | collective-permute-start | bytes 49160 | tf_op jit(solution)/shard_map/ppermute | solution.py:596
  42.9 3.2 %collective-permute-start.23 = (f32[8,512]{1,0:T(8,128)S(1)}, f32[8,512]{1,0:T(8,128)S(1)}, u32[]{:S(2)}, u32[]{:S(2)}) collective-permute-start(f32[8,512]{1,0:T(8,128)S(1)} %get-tuple-element.123), channel_id=1, source_target_pairs={{0,1},{1,0},{2,3},{3,2},{4,5},{5,4},{6,7},{7,6},{8,9},{9,8},{10,11... | collective-permute-start | bytes 49160 | tf_op jit(solution)/shard_map/ppermute | solution.py:596
  46.6 3.8 %collective-permute-start.24 = (f32[8,512]{1,0:T(8,128)S(1)}, f32[8,512]{1,0:T(8,128)S(1)}, u32[]{:S(2)}, u32[]{:S(2)}) collective-permute-start(f32[8,512]{1,0:T(8,128)S(1)} %get-tuple-element.133), channel_id=1, source_target_pairs={{0,8},{1,2},{2,1},{3,4},{4,3},{5,6},{6,5},{7,15},{8,0},{9,10},{10,... | collective-permute-start | bytes 49160 | tf_op jit(solution)/shard_map/ppermute | solution.py:596
  47.9 3.7 %collective-permute-start.25 = (f32[8,512]{1,0:T(8,128)S(1)}, f32[8,512]{1,0:T(8,128)S(1)}, u32[]{:S(2)}, u32[]{:S(2)}) collective-permute-start(f32[8,512]{1,0:T(8,128)S(1)} %get-tuple-element.134), channel_id=1, source_target_pairs={{0,8},{1,9},{2,10},{3,11},{4,12},{5,13},{6,14},{7,15},{8,0},{9,1},... | collective-permute-start | bytes 49160 | tf_op jit(solution)/shard_map/ppermute | solution.py:596
  48.7 3.0 %collective-permute-start.26 = (f32[8,512]{1,0:T(8,128)S(1)}, f32[8,512]{1,0:T(8,128)S(1)}, u32[]{:S(2)}, u32[]{:S(2)}) collective-permute-start(f32[8,512]{1,0:T(8,128)S(1)} %get-tuple-element.135), channel_id=1, source_target_pairs={{0,1},{1,0},{2,3},{3,2},{4,5},{5,4},{6,7},{7,6},{8,16},{9,17},{10,... | collective-permute-start | bytes 49160 | tf_op jit(solution)/shard_map/ppermute | solution.py:596
  48.7 3.0 %collective-permute-start.27 = (f32[8,512]{1,0:T(8,128)S(1)}, f32[8,512]{1,0:T(8,128)S(1)}, u32[]{:S(2)}, u32[]{:S(2)}) collective-permute-start(f32[8,512]{1,0:T(8,128)S(1)} %get-tuple-element.136), channel_id=1, source_target_pairs={{0,1},{1,0},{2,3},{3,2},{4,5},{5,4},{6,7},{7,6},{8,9},{9,8},{10,11... | collective-permute-start | bytes 49160 | tf_op jit(solution)/shard_map/ppermute | solution.py:596

commit v11 on v9

--- a/solution.py
+++ b/solution.py
@@ -388,14 +388,14 @@
 
 
 def early_pairs(b, e):
-    return [(e[i], b) for i in range(6)] + [(e[i], e[j]) for i in range(6) for j in range(i, 6)]
+    return [(e[i], b) for i in range(6)] + [(e[i], e[j]) for i in range(6) for j in range(max(i, 2), 6)]
 
 
 def late_pairs(b, e):
     return [(e[i], b) for i in (6, 7)] + [(e[j], e[i]) for j in (6, 7) for i in range(j + 1)]
 
 
-EARLY = 34
+EARLY = 31
 LATE = 17
 
 

time: 63.5 us -> 63.5 us (level)
  no operation moved by 1% of the time
where the time goes in v11:
time: 63.5 us; the launch traced here: 63.3 us
  starting transfers between devices  27.4 us (43%)
  waiting for transfers between devices  14.4 us (23%)
  Pallas kernels  10.3 us (16%)
  blocking collectives  10.2 us (16%)
  between operations  0.91 us (1%)
    ppermute x28, starting transfers between devices, permute(): return lax.ppermute(values, ('gx', 'gy'), pairs)  24 us
    ppermute x28, waiting for transfers between devices, permute(): return lax.ppermute(values, ('gx', 'gy'), pairs)  11.8 us
    pallas_call x20, Pallas kernels, call(): pl.pallas_call(kernel, out_shape=outs, in_specs=specs, out_specs=[VMEM] *...  10.3 us
    all_to_all x1, blocking collectives, spread(): return lax.all_to_all(values, ('gx', 'gy'), 0, 0)  10.2 us
    all_to_all x1, starting transfers between devices, spread(): return lax.all_to_all(values, ('gx', 'gy'), 0, 0)  3.38 us
    all_to_all x1, waiting for transfers between devices, spread(): return lax.all_to_all(values, ('gx', 'gy'), 0, 0)  2.59 us
  transfers between devices with their start and end apart: 29, of which 9 were waited for; matrix products, arithmetic and copies ran while one was open for 0% of the time, Pallas kernels for 8%

profile of v11, /device:TPU:0, one launch (start us, length us, event | category | flops | bytes accessed | tf_op | source)
XLA Modules:
  0.0 63.3 jit_solution(17934657593317245998)
XLA Ops:
  0.6 1.8 %shard_map.114 = (f32[24,512]{1,0:T(8,128)}, f32[24,512]{1,0:T(8,128)}) custom-call(f32[64,512]{1,0:T(8,128)} %bitcast.7, f32[64,512]{1,0:T(8,128)} %bitcast.9, s32[1,64]{1,0:T(1,128)} %bitcast.11, s32[1,64]{1,0:T(1,128)} %bitcast.13, f32[1,4]{1,0:T(1,128)} %bitcast.15), custom_call_target="tpu_custom_call" | custom-call | tf_op jit(solution)/shard_map/pallas_call | solution.py:581
  2.5 0.0 copy-start.7
  2.5 0.0 copy-start.8
  2.5 0.0 copy-start.9
  2.5 3.1 %collective-permute-start = (f32[24,512]{1,0:T(8,128)}, f32[24,512]{1,0:T(8,128)S(1)}, u32[]{:S(2)}, u32[]{:S(2)}) collective-permute-start(f32[24,512]{1,0:T(8,128)} %get-tuple-element.77), channel_id=1, source_target_pairs={{0,8},{1,2},{2,1},{3,4},{4,3},{5,6},{6,5},{7,15},{8,0},{9,10},{10,... | collective-permute-start | bytes 147464 | tf_op jit(solution)/shard_map/ppermute | solution.py:594
  5.6 0.0 collective-permute-start.1
  5.6 0.3 shard_map.113
  5.9 2.0 %collective-permute-done.odd = f32[24,512]{1,0:T(8,128)S(1)} collective-permute-done((f32[24,512]{1,0:T(8,128)}, f32[24,512]{1,0:T(8,128)S(1)}, u32[]{:S(2)}, u32[]{:S(2)}) %collective-permute-start) | collective-permute-done | bytes 49184 | tf_op jit(solution)/shard_map/ppermute | solution.py:594
  7.9 0.0 collective-permute-done.1.even
  7.9 0.1 collective-permute-start.2
  8.0 3.6 %collective-permute-start.3 = (f32[32,512]{1,0:T(8,128)S(1)}, f32[32,512]{1,0:T(8,128)S(1)}, u32[]{:S(2)}, u32[]{:S(2)}) collective-permute-start(f32[32,512]{1,0:T(8,128)S(1)} %get-tuple-element.84), channel_id=1, source_target_pairs={{0,8},{1,9},{2,10},{3,11},{4,12},{5,13},{6,14},{7,15},{8,0},{9,1},... | collective-permute-start | bytes 196616 | tf_op jit(solution)/shard_map/ppermute | solution.py:594
  11.6 0.4 shard_map.115
  12.0 1.9 %collective-permute-done.3.even = f32[32,512]{1,0:T(8,128)S(1)} collective-permute-done((f32[32,512]{1,0:T(8,128)S(1)}, f32[32,512]{1,0:T(8,128)S(1)}, u32[]{:S(2)}, u32[]{:S(2)}) %collective-permute-start.3) | collective-permute-done | bytes 65568 | tf_op jit(solution)/shard_map/ppermute | solution.py:594
  13.8 0.4 shard_map.117
  14.2 2.1 %collective-permute-start.4 = (f32[8,512]{1,0:T(8,128)S(1)}, f32[8,512]{1,0:T(8,128)S(1)}, u32[]{:S(2)}, u32[]{:S(2)}) collective-permute-start(f32[8,512]{1,0:T(8,128)S(1)} %get-tuple-element.90), channel_id=1, source_target_pairs={{0,8},{1,2},{2,1},{3,4},{4,3},{5,6},{6,5},{7,15},{8,0},{9,10},{10,... | collective-permute-start | bytes 49160 | tf_op jit(solution)/shard_map/ppermute | solution.py:594
  16.3 0.1 collective-permute-start.5
  16.4 1.3 %collective-permute-start.6 = (f32[8,512]{1,0:T(8,128)S(1)}, f32[8,512]{1,0:T(8,128)S(1)}, u32[]{:S(2)}, u32[]{:S(2)}) collective-permute-start(f32[8,512]{1,0:T(8,128)S(1)} %get-tuple-element.92), channel_id=1, source_target_pairs={{0,1},{1,0},{2,3},{3,2},{4,5},{5,4},{6,7},{7,6},{8,16},{9,17},{10,... | collective-permute-start | bytes 49160 | tf_op jit(solution)/shard_map/ppermute | solution.py:594
  17.7 0.0 collective-permute-start.7
  17.8 0.5 shard_map.118
  18.2 1.8 %collective-permute-done.5.x1 = f32[8,512]{1,0:T(8,128)S(1)} collective-permute-done((f32[8,512]{1,0:T(8,128)S(1)}, f32[8,512]{1,0:T(8,128)S(1)}, u32[]{:S(2)}, u32[]{:S(2)}) %collective-permute-start.5) | collective-permute-done | bytes 16416 | tf_op jit(solution)/shard_map/ppermute | solution.py:594
  20.1 0.0 collective-permute-done.6.y0
  20.1 0.0 collective-permute-done.7.y1
  20.1 0.4 shard_map.119
  20.5 2.1 %collective-permute-start.8 = (f32[8,512]{1,0:T(8,128)S(1)}, f32[8,512]{1,0:T(8,128)S(1)}, u32[]{:S(2)}, u32[]{:S(2)}) collective-permute-start(f32[8,512]{1,0:T(8,128)S(1)} %get-tuple-element.100), channel_id=1, source_target_pairs={{0,8},{1,2},{2,1},{3,4},{4,3},{5,6},{6,5},{7,15},{8,0},{9,10},{10,... | collective-permute-start | bytes 49160 | tf_op jit(solution)/shard_map/ppermute | solution.py:594
  22.5 0.1 collective-permute-start.9
  22.6 0.5 collective-permute-start.11
  23.1 0.4 shard_map.120.q
  23.6 0.7 %collective-permute-done.8.x0 = f32[8,512]{1,0:T(8,128)S(1)} collective-permute-done((f32[8,512]{1,0:T(8,128)S(1)}, f32[8,512]{1,0:T(8,128)S(1)}, u32[]{:S(2)}, u32[]{:S(2)}) %collective-permute-start.8) | collective-permute-done | bytes 16416 | tf_op jit(solution)/shard_map/ppermute | solution.py:594
  24.3 2.0 %collective-permute-done.9.x1 = f32[8,512]{1,0:T(8,128)S(1)} collective-permute-done((f32[8,512]{1,0:T(8,128)S(1)}, f32[8,512]{1,0:T(8,128)S(1)}, u32[]{:S(2)}, u32[]{:S(2)}) %collective-permute-start.9) | collective-permute-done | bytes 16416 | tf_op jit(solution)/shard_map/ppermute | solution.py:594
  26.3 0.4 shard_map.121
  26.7 2.1 %collective-permute-start.12 = (f32[8,512]{1,0:T(8,128)S(1)}, f32[8,512]{1,0:T(8,128)S(1)}, u32[]{:S(2)}, u32[]{:S(2)}) collective-permute-start(f32[8,512]{1,0:T(8,128)S(1)} %get-tuple-element.107), channel_id=1, source_target_pairs={{0,8},{1,2},{2,1},{3,4},{4,3},{5,6},{6,5},{7,15},{8,0},{9,10},{10,... | collective-permute-start | bytes 49160 | tf_op jit(solution)/shard_map/ppermute | solution.py:594
  28.7 0.1 collective-permute-start.13
  28.8 0.0 collective-permute-start.14
  28.8 0.5 collective-permute-start.15
  29.3 1.0 %shard_map.122 = (f32[64,512]{1,0:T(8,128)S(1)}, f32[32,1,128]{2,1,0:T(1,128)}) custom-call(f32[64,512]{1,0:T(8,128)S(1)} %get-tuple-element.85.b, f32[64,512]{1,0:T(8,128)S(1)} %get-tuple-element.95.refs_0_.s, f32[64,512]{1,0:T(8,128)S(1)} %get-tuple-element.96.inverse, f32[64,512]{1,0:T(8,128)S(1)} %get-tuple-element.104.z, ...), custom_call_target="tpu_custom_call" | custom-call | flops 1048576 | bytes 1048576 | tf_op jit(solution)/shard_map/pallas_call | solution.py:581
  30.3 0.1 collective-permute-done.12.x0
  30.5 2.0 %collective-permute-done.13.x1 = f32[8,512]{1,0:T(8,128)S(1)} collective-permute-done((f32[8,512]{1,0:T(8,128)S(1)}, f32[8,512]{1,0:T(8,128)S(1)}, u32[]{:S(2)}, u32[]{:S(2)}) %collective-permute-start.13) | collective-permute-done | bytes 16416 | tf_op jit(solution)/shard_map/ppermute | solution.py:594
  32.5 0.0 collective-permute-done.14.y0
  32.5 0.0 collective-permute-done.15.y1
  32.5 0.4 shard_map.123
  32.9 2.1 %collective-permute-start.16 = (f32[8,512]{1,0:T(8,128)S(1)}, f32[8,512]{1,0:T(8,128)S(1)}, u32[]{:S(2)}, u32[]{:S(2)}) collective-permute-start(f32[8,512]{1,0:T(8,128)S(1)} %get-tuple-element.113), channel_id=1, source_target_pairs={{0,8},{1,2},{2,1},{3,4},{4,3},{5,6},{6,5},{7,15},{8,0},{9,10},{10,... | collective-permute-start | bytes 49160 | tf_op jit(solution)/shard_map/ppermute | solution.py:594
  34.9 0.1 collective-permute-start.17
  35.0 0.0 collective-permute-start.18
  35.0 0.5 collective-permute-start.19
  35.5 3.4 %all-to-all-start = ((f32[32,1,128]{2,1,0:T(1,128)}), f32[32,1,128]{2,1,0:T(1,128)S(1)}, u32[]{:S(2)}, u32[]{:S(2)}) async-start(f32[32,1,128]{2,1,0:T(1,128)} %get-tuple-element.119), calls=%async_computation | async-start | bytes 32768 | tf_op jit(solution)/shard_map/all_to_all | solution.py:607
  38.9 0.5 shard_map.124.q
  39.4 0.4 shard_map.125
  39.8 1.8 %collective-permute-start.20 = (f32[8,512]{1,0:T(8,128)S(1)}, f32[8,512]{1,0:T(8,128)S(1)}, u32[]{:S(2)}, u32[]{:S(2)}) collective-permute-start(f32[8,512]{1,0:T(8,128)S(1)} %get-tuple-element.120), channel_id=1, source_target_pairs={{0,8},{1,2},{2,1},{3,4},{4,3},{5,6},{6,5},{7,15},{8,0},{9,10},{10,... | collective-permute-start | bytes 49160 | tf_op jit(solution)/shard_map/ppermute | solution.py:594
  41.6 0.3 collective-permute-start.21
  41.9 1.0 %collective-permute-start.22 = (f32[8,512]{1,0:T(8,128)S(1)}, f32[8,512]{1,0:T(8,128)S(1)}, u32[]{:S(2)}, u32[]{:S(2)}) collective-permute-start(f32[8,512]{1,0:T(8,128)S(1)} %get-tuple-element.122), channel_id=1, source_target_pairs={{0,1},{1,0},{2,3},{3,2},{4,5},{5,4},{6,7},{7,6},{8,16},{9,17},{10,... | collective-permute-start | bytes 49160 | tf_op jit(solution)/shard_map/ppermute | solution.py:594
  43.0 0.4 shard_map.126._.q
  43.4 2.6 %all-to-all-done.gathered = f32[32,1,128]{2,1,0:T(1,128)S(1)} async-done(((f32[32,1,128]{2,1,0:T(1,128)}), f32[32,1,128]{2,1,0:T(1,128)S(1)}, u32[]{:S(2)}, u32[]{:S(2)}) %all-to-all-start) | async-done | bytes 16416 | tf_op jit(solution)/shard_map/all_to_all | solution.py:607
  46.0 0.1 shard_map.127.scalars
  46.2 0.4 shard_map.128
  46.6 1.3 %collective-permute-start.24 = (f32[8,512]{1,0:T(8,128)S(1)}, f32[8,512]{1,0:T(8,128)S(1)}, u32[]{:S(2)}, u32[]{:S(2)}) collective-permute-start(f32[8,512]{1,0:T(8,128)S(1)} %get-tuple-element.133), channel_id=1, source_target_pairs={{0,8},{1,2},{2,1},{3,4},{4,3},{5,6},{6,5},{7,15},{8,0},{9,10},{10,... | collective-permute-start | bytes 49160 | tf_op jit(solution)/shard_map/ppermute | solution.py:594
  47.9 0.8 %collective-permute-start.25 = (f32[8,512]{1,0:T(8,128)S(1)}, f32[8,512]{1,0:T(8,128)S(1)}, u32[]{:S(2)}, u32[]{:S(2)}) collective-permute-start(f32[8,512]{1,0:T(8,128)S(1)} %get-tuple-element.134), channel_id=1, source_target_pairs={{0,8},{1,9},{2,10},{3,11},{4,12},{5,13},{6,14},{7,15},{8,0},{9,1},... | collective-permute-start | bytes 49160 | tf_op jit(solution)/shard_map/ppermute | solution.py:594
  48.7 0.5 collective-permute-start.27
  49.2 0.7 %shard_map.129 = (f32[64,512]{1,0:T(8,128)S(1)}, f32[64,512]{1,0:T(8,128)S(1)}, f32[64,512]{1,0:T(8,128)S(1)}, f32[64,512]{1,0:T(8,128)S(1)}, f32[64,512]{1,0:T(...) custom-call(f32[8,128]{1,0:T(8,128)S(1)} %shard_map.127.scalars, ...), custom_call_target="tpu_custom_call" | custom-call | flops 1048576 | bytes 1048576 | tf_op jit(solution)/shard_map/pallas_call | solution.py:581
  49.9 0.5 shard_map.130.q
  50.4 0.0 collective-permute-done.24.x0
  50.4 1.2 %collective-permute-done.25.x1 = f32[8,512]{1,0:T(8,128)S(1)} collective-permute-done((f32[8,512]{1,0:T(8,128)S(1)}, f32[8,512]{1,0:T(8,128)S(1)}, u32[]{:S(2)}, u32[]{:S(2)}) %collective-permute-start.25) | collective-permute-done | bytes 16416 | tf_op jit(solution)/shard_map/ppermute | solution.py:594
  51.7 0.3 shard_map.131
  52.0 10.2 %all_to_all.10.gathered = f32[32,1,128]{2,1,0:T(1,128)S(1)} all-to-all(f32[32,1,128]{2,1,0:T(1,128)S(1)} %get-tuple-element.137), channel_id=1, replica_groups=mesh['gx'=4,'gy'=8] {'gx','gy'}, dimensions={0} | all-to-all | bytes 32768 | tf_op jit(solution)/shard_map/all_to_all | solution.py:607
  62.2 1.0 %shard_map.132 = (f32[64,512]{1,0:T(8,128)}, f32[64,512]{1,0:T(8,128)}) custom-call(f32[32,1,128]{2,1,0:T(1,128)S(1)} %all_to_all.10.gathered, f32[8,128]{1,0:T(8,128)S(1)} %shard_map.127.scalars, f32[64,512]{1,0:T(8,128)S(1)} %get-tuple-element.138.x, f32[64,512]{1,0:T(8,128)S(1)} %get-tuple-element.139.p, f32[64,512]{1,0:T(8,128)S(1)} %get-tuple-element.140.r, ...), custom_call_target="tpu_custom_call" | custom-call | tf_op jit(solution)/shard_map/pallas_call | solution.py:581
  (35 shorter events, 0.1 us)
Async XLA Ops:
  0.6 5.0 %copy-start.5 = (f32[8,8,512]{2,1,0:T(8,128)S(1)}, f32[8,8,512]{2,1,0:T(8,128)}, u32[]{:S(2)}) copy-start(f32[8,8,512]{2,1,0:T(8,128)} %param.10) | copy-start | bytes 393220
  0.6 5.0 %copy-start.6 = (f32[8,8,512]{2,1,0:T(8,128)S(1)}, f32[8,8,512]{2,1,0:T(8,128)}, u32[]{:S(2)}) copy-start(f32[8,8,512]{2,1,0:T(8,128)} %param.11) | copy-start | bytes 393220
  2.5 3.2 %copy-start.7 = (s32[1,1,64]{2,1,0:T(1,128)S(1)}, s32[1,1,64]{2,1,0:T(1,128)}, u32[]{:S(2)}) copy-start(s32[1,1,64]{2,1,0:T(1,128)} %param.12) | copy-start | bytes 772
  2.5 3.2 %copy-start.8 = (s32[1,1,64]{2,1,0:T(1,128)S(1)}, s32[1,1,64]{2,1,0:T(1,128)}, u32[]{:S(2)}) copy-start(s32[1,1,64]{2,1,0:T(1,128)} %param.13) | copy-start | bytes 772
  2.5 3.1 %copy-start.9 = (f32[4]{0:T(128)S(1)}, f32[4]{0:T(128)}, u32[]{:S(2)}) copy-start(f32[4]{0:T(128)} %param.14) | copy-start | bytes 52
  2.5 5.4 %collective-permute-start = (f32[24,512]{1,0:T(8,128)}, f32[24,512]{1,0:T(8,128)S(1)}, u32[]{:S(2)}, u32[]{:S(2)}) collective-permute-start(f32[24,512]{1,0:T(8,128)} %get-tuple-element.77), channel_id=1, source_target_pairs={{0,8},{1,2},{2,1},{3,4},{4,3},{5,6},{6,5},{7,15},{8,0},{9,10},{10,... | collective-permute-start | bytes 147464 | tf_op jit(solution)/shard_map/ppermute | solution.py:594
  5.6 2.3 %collective-permute-start.1 = (f32[24,512]{1,0:T(8,128)}, f32[24,512]{1,0:T(8,128)S(1)}, u32[]{:S(2)}, u32[]{:S(2)}) collective-permute-start(f32[24,512]{1,0:T(8,128)} %get-tuple-element.78), channel_id=1, source_target_pairs={{0,1},{1,0},{2,3},{3,2},{4,5},{5,4},{6,7},{7,6},{8,9},{9,8},{10,11... | collective-permute-start | bytes 147464 | tf_op jit(solution)/shard_map/ppermute | solution.py:594
  7.9 3.7 %copy-start.4 = (f32[8,512]{1,0:T(8,128)S(1)}, f32[8,512]{1,0:T(8,128)}, u32[]{:S(2)}) copy-start(f32[8,512]{1,0:T(8,128)} %constant.14.clone.lanes.refs_8_.refs_7_) | copy-start | bytes 49156
  7.9 4.0 %collective-permute-start.2 = (f32[32,512]{1,0:T(8,128)S(1)}, f32[32,512]{1,0:T(8,128)S(1)}, u32[]{:S(2)}, u32[]{:S(2)}) collective-permute-start(f32[32,512]{1,0:T(8,128)S(1)} %get-tuple-element.83), channel_id=1, source_target_pairs={{0,1},{1,0},{2,3},{3,2},{4,5},{5,4},{6,7},{7,6},{8,16},{9,17},{10,... | collective-permute-start | bytes 196616 | tf_op jit(solution)/shard_map/ppermute | solution.py:594
  8.0 5.8 %collective-permute-start.3 = (f32[32,512]{1,0:T(8,128)S(1)}, f32[32,512]{1,0:T(8,128)S(1)}, u32[]{:S(2)}, u32[]{:S(2)}) collective-permute-start(f32[32,512]{1,0:T(8,128)S(1)} %get-tuple-element.84), channel_id=1, source_target_pairs={{0,8},{1,9},{2,10},{3,11},{4,12},{5,13},{6,14},{7,15},{8,0},{9,1},... | collective-permute-start | bytes 196616 | tf_op jit(solution)/shard_map/ppermute | solution.py:594
  13.8 3.9 %copy-start = (bf16[256,256]{1,0:T(8,128)(2,1)S(1)}, bf16[256,256]{1,0:T(8,128)(2,1)}, u32[]{:S(2)}) copy-start(bf16[256,256]{1,0:T(8,128)(2,1)} %constant.12.clone.b1.refs_6_.refs_5_) | copy-start | bytes 393220
  13.8 3.9 %copy-start.1 = (bf16[256,256]{1,0:T(8,128)(2,1)S(1)}, bf16[256,256]{1,0:T(8,128)(2,1)}, u32[]{:S(2)}) copy-start(bf16[256,256]{1,0:T(8,128)(2,1)} %constant.10.clone.f1.refs_4_.refs_3_) | copy-start | bytes 393220
  13.8 3.9 %copy-start.2 = (bf16[256,128]{1,0:T(8,128)(2,1)S(1)}, bf16[256,128]{1,0:T(8,128)(2,1)}, u32[]{:S(2)}) copy-start(bf16[256,128]{1,0:T(8,128)(2,1)} %constant.13.clone.b2.refs_7_.refs_6_) | copy-start | bytes 196612
  13.8 3.9 %copy-start.3 = (bf16[256,128]{1,0:T(8,128)(2,1)S(1)}, bf16[256,128]{1,0:T(8,128)(2,1)}, u32[]{:S(2)}) copy-start(bf16[256,128]{1,0:T(8,128)(2,1)} %constant.11.clone.f2.refs_5_.refs_4_) | copy-start | bytes 196612
  14.2 4.0 %collective-permute-start.4 = (f32[8,512]{1,0:T(8,128)S(1)}, f32[8,512]{1,0:T(8,128)S(1)}, u32[]{:S(2)}, u32[]{:S(2)}) collective-permute-start(f32[8,512]{1,0:T(8,128)S(1)} %get-tuple-element.90), channel_id=1, source_target_pairs={{0,8},{1,2},{2,1},{3,4},{4,3},{5,6},{6,5},{7,15},{8,0},{9,10},{10,... | collective-permute-start | bytes 49160 | tf_op jit(solution)/shard_map/ppermute | solution.py:594
  16.3 3.7 %collective-permute-start.5 = (f32[8,512]{1,0:T(8,128)S(1)}, f32[8,512]{1,0:T(8,128)S(1)}, u32[]{:S(2)}, u32[]{:S(2)}) collective-permute-start(f32[8,512]{1,0:T(8,128)S(1)} %get-tuple-element.91), channel_id=1, source_target_pairs={{0,8},{1,9},{2,10},{3,11},{4,12},{5,13},{6,14},{7,15},{8,0},{9,1},... | collective-permute-start | bytes 49160 | tf_op jit(solution)/shard_map/ppermute | solution.py:594
  16.4 3.7 %collective-permute-start.6 = (f32[8,512]{1,0:T(8,128)S(1)}, f32[8,512]{1,0:T(8,128)S(1)}, u32[]{:S(2)}, u32[]{:S(2)}) collective-permute-start(f32[8,512]{1,0:T(8,128)S(1)} %get-tuple-element.92), channel_id=1, source_target_pairs={{0,1},{1,0},{2,3},{3,2},{4,5},{5,4},{6,7},{7,6},{8,16},{9,17},{10,... | collective-permute-start | bytes 49160 | tf_op jit(solution)/shard_map/ppermute | solution.py:594
  17.7 2.3 %collective-permute-start.7 = (f32[8,512]{1,0:T(8,128)S(1)}, f32[8,512]{1,0:T(8,128)S(1)}, u32[]{:S(2)}, u32[]{:S(2)}) collective-permute-start(f32[8,512]{1,0:T(8,128)S(1)} %get-tuple-element.93), channel_id=1, source_target_pairs={{0,1},{1,0},{2,3},{3,2},{4,5},{5,4},{6,7},{7,6},{8,9},{9,8},{10,11... | collective-permute-start | bytes 49160 | tf_op jit(solution)/shard_map/ppermute | solution.py:594
  20.5 3.8 %collective-permute-start.8 = (f32[8,512]{1,0:T(8,128)S(1)}, f32[8,512]{1,0:T(8,128)S(1)}, u32[]{:S(2)}, u32[]{:S(2)}) collective-permute-start(f32[8,512]{1,0:T(8,128)S(1)} %get-tuple-element.100), channel_id=1, source_target_pairs={{0,8},{1,2},{2,1},{3,4},{4,3},{5,6},{6,5},{7,15},{8,0},{9,10},{10,... | collective-permute-start | bytes 49160 | tf_op jit(solution)/shard_map/ppermute | solution.py:594
  22.5 3.7 %collective-permute-start.9 = (f32[8,512]{1,0:T(8,128)S(1)}, f32[8,512]{1,0:T(8,128)S(1)}, u32[]{:S(2)}, u32[]{:S(2)}) collective-permute-start(f32[8,512]{1,0:T(8,128)S(1)} %get-tuple-element.101), channel_id=1, source_target_pairs={{0,8},{1,9},{2,10},{3,11},{4,12},{5,13},{6,14},{7,15},{8,0},{9,1},... | collective-permute-start | bytes 49160 | tf_op jit(solution)/shard_map/ppermute | solution.py:594
  22.6 3.7 %collective-permute-start.10 = (f32[8,512]{1,0:T(8,128)S(1)}, f32[8,512]{1,0:T(8,128)S(1)}, u32[]{:S(2)}, u32[]{:S(2)}) collective-permute-start(f32[8,512]{1,0:T(8,128)S(1)} %get-tuple-element.102), channel_id=1, source_target_pairs={{0,1},{1,0},{2,3},{3,2},{4,5},{5,4},{6,7},{7,6},{8,16},{9,17},{10,... | collective-permute-start | bytes 49160 | tf_op jit(solution)/shard_map/ppermute | solution.py:594
  22.6 3.7 %collective-permute-start.11 = (f32[8,512]{1,0:T(8,128)S(1)}, f32[8,512]{1,0:T(8,128)S(1)}, u32[]{:S(2)}, u32[]{:S(2)}) collective-permute-start(f32[8,512]{1,0:T(8,128)S(1)} %get-tuple-element.103), channel_id=1, source_target_pairs={{0,1},{1,0},{2,3},{3,2},{4,5},{5,4},{6,7},{7,6},{8,9},{9,8},{10,11... | collective-permute-start | bytes 49160 | tf_op jit(solution)/shard_map/ppermute | solution.py:594
  26.7 3.8 %collective-permute-start.12 = (f32[8,512]{1,0:T(8,128)S(1)}, f32[8,512]{1,0:T(8,128)S(1)}, u32[]{:S(2)}, u32[]{:S(2)}) collective-permute-start(f32[8,512]{1,0:T(8,128)S(1)} %get-tuple-element.107), channel_id=1, source_target_pairs={{0,8},{1,2},{2,1},{3,4},{4,3},{5,6},{6,5},{7,15},{8,0},{9,10},{10,... | collective-permute-start | bytes 49160 | tf_op jit(solution)/shard_map/ppermute | solution.py:594
  28.7 3.7 %collective-permute-start.13 = (f32[8,512]{1,0:T(8,128)S(1)}, f32[8,512]{1,0:T(8,128)S(1)}, u32[]{:S(2)}, u32[]{:S(2)}) collective-permute-start(f32[8,512]{1,0:T(8,128)S(1)} %get-tuple-element.108), channel_id=1, source_target_pairs={{0,8},{1,9},{2,10},{3,11},{4,12},{5,13},{6,14},{7,15},{8,0},{9,1},... | collective-permute-start | bytes 49160 | tf_op jit(solution)/shard_map/ppermute | solution.py:594
  28.8 3.7 %collective-permute-start.14 = (f32[8,512]{1,0:T(8,128)S(1)}, f32[8,512]{1,0:T(8,128)S(1)}, u32[]{:S(2)}, u32[]{:S(2)}) collective-permute-start(f32[8,512]{1,0:T(8,128)S(1)} %get-tuple-element.109), channel_id=1, source_target_pairs={{0,1},{1,0},{2,3},{3,2},{4,5},{5,4},{6,7},{7,6},{8,16},{9,17},{10,... | collective-permute-start | bytes 49160 | tf_op jit(solution)/shard_map/ppermute | solution.py:594
  28.8 3.7 %collective-permute-start.15 = (f32[8,512]{1,0:T(8,128)S(1)}, f32[8,512]{1,0:T(8,128)S(1)}, u32[]{:S(2)}, u32[]{:S(2)}) collective-permute-start(f32[8,512]{1,0:T(8,128)S(1)} %get-tuple-element.110), channel_id=1, source_target_pairs={{0,1},{1,0},{2,3},{3,2},{4,5},{5,4},{6,7},{7,6},{8,9},{9,8},{10,11... | collective-permute-start | bytes 49160 | tf_op jit(solution)/shard_map/ppermute | solution.py:594
  32.9 6.5 %collective-permute-start.16 = (f32[8,512]{1,0:T(8,128)S(1)}, f32[8,512]{1,0:T(8,128)S(1)}, u32[]{:S(2)}, u32[]{:S(2)}) collective-permute-start(f32[8,512]{1,0:T(8,128)S(1)} %get-tuple-element.113), channel_id=1, source_target_pairs={{0,8},{1,2},{2,1},{3,4},{4,3},{5,6},{6,5},{7,15},{8,0},{9,10},{10,... | collective-permute-start | bytes 49160 | tf_op jit(solution)/shard_map/ppermute | solution.py:594
  34.9 4.4 %collective-permute-start.17 = (f32[8,512]{1,0:T(8,128)S(1)}, f32[8,512]{1,0:T(8,128)S(1)}, u32[]{:S(2)}, u32[]{:S(2)}) collective-permute-start(f32[8,512]{1,0:T(8,128)S(1)} %get-tuple-element.114), channel_id=1, source_target_pairs={{0,8},{1,9},{2,10},{3,11},{4,12},{5,13},{6,14},{7,15},{8,0},{9,1},... | collective-permute-start | bytes 49160 | tf_op jit(solution)/shard_map/ppermute | solution.py:594
  35.0 4.4 %collective-permute-start.18 = (f32[8,512]{1,0:T(8,128)S(1)}, f32[8,512]{1,0:T(8,128)S(1)}, u32[]{:S(2)}, u32[]{:S(2)}) collective-permute-start(f32[8,512]{1,0:T(8,128)S(1)} %get-tuple-element.115), channel_id=1, source_target_pairs={{0,1},{1,0},{2,3},{3,2},{4,5},{5,4},{6,7},{7,6},{8,16},{9,17},{10,... | collective-permute-start | bytes 49160 | tf_op jit(solution)/shard_map/ppermute | solution.py:594
  35.0 4.4 %collective-permute-start.19 = (f32[8,512]{1,0:T(8,128)S(1)}, f32[8,512]{1,0:T(8,128)S(1)}, u32[]{:S(2)}, u32[]{:S(2)}) collective-permute-start(f32[8,512]{1,0:T(8,128)S(1)} %get-tuple-element.116), channel_id=1, source_target_pairs={{0,1},{1,0},{2,3},{3,2},{4,5},{5,4},{6,7},{7,6},{8,9},{9,8},{10,11... | collective-permute-start | bytes 49160 | tf_op jit(solution)/shard_map/ppermute | solution.py:594
  35.5 10.5 %all-to-all-start = ((f32[32,1,128]{2,1,0:T(1,128)}), f32[32,1,128]{2,1,0:T(1,128)S(1)}, u32[]{:S(2)}, u32[]{:S(2)}) async-start(f32[32,1,128]{2,1,0:T(1,128)} %get-tuple-element.119), calls=%async_computation | async-start | bytes 32768 | tf_op jit(solution)/shard_map/all_to_all | solution.py:607
  39.8 6.3 %collective-permute-start.20 = (f32[8,512]{1,0:T(8,128)S(1)}, f32[8,512]{1,0:T(8,128)S(1)}, u32[]{:S(2)}, u32[]{:S(2)}) collective-permute-start(f32[8,512]{1,0:T(8,128)S(1)} %get-tuple-element.120), channel_id=1, source_target_pairs={{0,8},{1,2},{2,1},{3,4},{4,3},{5,6},{6,5},{7,15},{8,0},{9,10},{10,... | collective-permute-start | bytes 49160 | tf_op jit(solution)/shard_map/ppermute | solution.py:594
  41.6 4.5 %collective-permute-start.21 = (f32[8,512]{1,0:T(8,128)S(1)}, f32[8,512]{1,0:T(8,128)S(1)}, u32[]{:S(2)}, u32[]{:S(2)}) collective-permute-start(f32[8,512]{1,0:T(8,128)S(1)} %get-tuple-element.121), channel_id=1, source_target_pairs={{0,8},{1,9},{2,10},{3,11},{4,12},{5,13},{6,14},{7,15},{8,0},{9,1},... | collective-permute-start | bytes 49160 | tf_op jit(solution)/shard_map/ppermute | solution.py:594
  41.9 4.2 %collective-permute-start.22 = (f32[8,512]{1,0:T(8,128)S(1)}, f32[8,512]{1,0:T(8,128)S(1)}, u32[]{:S(2)}, u32[]{:S(2)}) collective-permute-start(f32[8,512]{1,0:T(8,128)S(1)} %get-tuple-element.122), channel_id=1, source_target_pairs={{0,1},{1,0},{2,3},{3,2},{4,5},{5,4},{6,7},{7,6},{8,16},{9,17},{10,... | collective-permute-start | bytes 49160 | tf_op jit(solution)/shard_map/ppermute | solution.py:594
  43.0 3.2 %collective-permute-start.23 = (f32[8,512]{1,0:T(8,128)S(1)}, f32[8,512]{1,0:T(8,128)S(1)}, u32[]{:S(2)}, u32[]{:S(2)}) collective-permute-start(f32[8,512]{1,0:T(8,128)S(1)} %get-tuple-element.123), channel_id=1, source_target_pairs={{0,1},{1,0},{2,3},{3,2},{4,5},{5,4},{6,7},{7,6},{8,9},{9,8},{10,11... | collective-permute-start | bytes 49160 | tf_op jit(solution)/shard_map/ppermute | solution.py:594
  46.6 3.8 %collective-permute-start.24 = (f32[8,512]{1,0:T(8,128)S(1)}, f32[8,512]{1,0:T(8,128)S(1)}, u32[]{:S(2)}, u32[]{:S(2)}) collective-permute-start(f32[8,512]{1,0:T(8,128)S(1)} %get-tuple-element.133), channel_id=1, source_target_pairs={{0,8},{1,2},{2,1},{3,4},{4,3},{5,6},{6,5},{7,15},{8,0},{9,10},{10,... | collective-permute-start | bytes 49160 | tf_op jit(solution)/shard_map/ppermute | solution.py:594
  47.9 3.7 %collective-permute-start.25 = (f32[8,512]{1,0:T(8,128)S(1)}, f32[8,512]{1,0:T(8,128)S(1)}, u32[]{:S(2)}, u32[]{:S(2)}) collective-permute-start(f32[8,512]{1,0:T(8,128)S(1)} %get-tuple-element.134), channel_id=1, source_target_pairs={{0,8},{1,9},{2,10},{3,11},{4,12},{5,13},{6,14},{7,15},{8,0},{9,1},... | collective-permute-start | bytes 49160 | tf_op jit(solution)/shard_map/ppermute | solution.py:594
  48.7 3.0 %collective-permute-start.26 = (f32[8,512]{1,0:T(8,128)S(1)}, f32[8,512]{1,0:T(8,128)S(1)}, u32[]{:S(2)}, u32[]{:S(2)}) collective-permute-start(f32[8,512]{1,0:T(8,128)S(1)} %get-tuple-element.135), channel_id=1, source_target_pairs={{0,1},{1,0},{2,3},{3,2},{4,5},{5,4},{6,7},{7,6},{8,16},{9,17},{10,... | collective-permute-start | bytes 49160 | tf_op jit(solution)/shard_map/ppermute | solution.py:594
  48.7 3.0 %collective-permute-start.27 = (f32[8,512]{1,0:T(8,128)S(1)}, f32[8,512]{1,0:T(8,128)S(1)}, u32[]{:S(2)}, u32[]{:S(2)}) collective-permute-start(f32[8,512]{1,0:T(8,128)S(1)} %get-tuple-element.136), channel_id=1, source_target_pairs={{0,1},{1,0},{2,3},{3,2},{4,5},{5,4},{6,7},{7,6},{8,9},{9,8},{10,11... | collective-permute-start | bytes 49160 | tf_op jit(solution)/shard_map/ppermute | solution.py:594
